TPU v7x, 32 devices: a whole 2x2x4 slice. The times are simulated.
32 devices in a mesh: grp: 4 (over y, x), own: 8 (over z, core).
Axes of the slice: x: 2, y: 2, z: 4, core: 2. Of those that a mesh axis runs over, the one named last changes fastest.
Arguments:
- arrivals: bfloat16 [16384, 512], P(('grp', 'own')), may hold values from -6 to 6
- home_owner: int32 [16384, 1], P(('grp', 'own')), may hold values from 0 to 7; in each aligned block of 512 rows (0 to 511, 512 to 1023, ...) at most 128 rows name the same one
- cluster_slot: int32 [16384], P(('grp', 'own')), may hold values from 0 to 255
- bank: bfloat16 [2048, 32, 512], P('own'), may hold values from -6 to 6
- members: int32 [2048], P('own'), may hold values from 1 to 32
- centroid_sum: float32 [2048, 512], P('own'), may hold values from -1.6 to 1.6
Outputs:
- best_cosine: float32 [16384], P(('grp', 'own'))
- centroids: float32 [2048, 512], P('own')
Inputs may be any that keep to these rules, and one draw needn't show every extreme that they name: `home_owner`: among the 512 rows of one device no value appears more than 128 times, and some value appears exactly 128 times.
All inputs are finite; a program needn't handle non-finite values.
Results may differ from a plain program's by a relative error of at most 0.0017.
Values may be sent and summed in bfloat16 or wider, within the bound.
No kernel may reach another device: no remote copies, remote signals or barrier semaphores. Data moves between devices by JAX's collectives and lax.ppermute only.
A program may use at most 64 MiB of HBM per device.

v0:
```python
import jax
import jax.numpy as jnp
from jax import lax
from jax.sharding import PartitionSpec as P

epsilon = 1e-06


def normalize_rows(total):
    return total / jnp.sqrt(jnp.sum(total * total, axis=1, keepdims=True) + epsilon)


def body(arrivals, home_owner, cluster_slot, bank, members, centroid_sum):
    owners = lax.axis_size("own")
    local_rows = arrivals.shape[0]
    width = arrivals.shape[1]
    local_clusters = bank.shape[0]
    block_depth = bank.shape[1]
    capacity = 2 * local_rows // owners
    total_slots = owners * capacity
    values = arrivals.astype(jnp.float32)
    unit_rows = (
        values / jnp.sqrt(jnp.sum(values * values, axis=1, keepdims=True) + epsilon)
    ).astype(jnp.bfloat16)
    target = home_owner[:, 0]
    target_hit = target[:, None] == jnp.arange(owners, dtype=jnp.int32)[None, :]
    row_iota = jnp.arange(local_rows, dtype=jnp.int32)
    strictly_below = (row_iota[:, None] > row_iota[None, :]).astype(jnp.bfloat16)
    earlier = jnp.dot(
        strictly_below, target_hit.astype(jnp.bfloat16), preferred_element_type=jnp.float32
    )
    placed = jnp.sum(jnp.where(target_hit, earlier, 0.0), axis=1).astype(jnp.int32)
    slot_index = target * capacity + placed
    slot_iota = jnp.arange(total_slots, dtype=jnp.int32)
    slot_match = slot_iota[:, None] == slot_index[None, :]
    send_rows = (
        jnp.dot(slot_match.astype(jnp.bfloat16), unit_rows, preferred_element_type=jnp.float32)
        .astype(jnp.bfloat16)
        .reshape(owners, capacity, width)
    )
    send_slot = (jnp.sum(jnp.where(slot_match, cluster_slot[None, :] + 1, 0), axis=1) - 1).reshape(
        owners, capacity
    )
    bank_flat = bank.reshape(local_clusters * block_depth, width)
    bank_norm = jnp.sqrt(
        jnp.einsum("rd,rd->r", bank_flat, bank_flat, preferred_element_type=jnp.float32) + epsilon
    )
    column_cluster = jnp.arange(local_clusters * block_depth, dtype=jnp.int32) // block_depth
    column_depth = jnp.arange(local_clusters * block_depth, dtype=jnp.int32) % block_depth
    member_hit = (
        jnp.arange(local_clusters, dtype=jnp.int32)[:, None] == column_cluster[None, :]
    ).astype(jnp.int32)
    column_members = jnp.sum(member_hit * members[:, None], axis=0)
    column_live = column_depth < column_members
    column_code = jnp.where(column_live, column_cluster, -2)

    def score_tile(query, chosen):
        dot_raw = lax.dot_general(
            query, bank_flat, (((1,), (1,)), ((), ())), preferred_element_type=jnp.float32
        )
        cosine = dot_raw / bank_norm[None, :]
        is_valid = column_code[None, :] == chosen[:, None]
        return jnp.max(jnp.where(is_valid, cosine, -3.0), axis=1)

    got_rows, got_slot = (
        lax.all_to_all(send_rows, "own", split_axis=0, concat_axis=0, tiled=True),
        lax.all_to_all(send_slot, "own", split_axis=0, concat_axis=0, tiled=True),
    )
    flat_rows = got_rows.reshape(total_slots, width)
    flat_slot = got_slot.reshape(total_slots)
    count = flat_rows.shape[0]
    tile = min(256, count)
    tiles = count // tile

    def mapped_tile(inputs):
        return score_tile(inputs[0], inputs[1])

    flat_best = lax.map(
        mapped_tile, (flat_rows.reshape(tiles, tile, width), flat_slot.reshape(tiles, tile))
    ).reshape(count)
    returned = lax.all_to_all(
        flat_best.reshape(owners, capacity), "own", split_axis=0, concat_axis=0, tiled=True
    )
    best_cosine = jnp.sum(
        jnp.where(slot_match, returned.reshape(total_slots)[:, None], 0.0), axis=0
    )
    cluster_hit = (
        jnp.arange(local_clusters, dtype=jnp.int32)[:, None] == flat_slot[None, :]
    ).astype(jnp.bfloat16)
    partial_value = jnp.dot(cluster_hit, flat_rows, preferred_element_type=jnp.float32)
    summed = lax.psum(partial_value, "grp")
    centroids = normalize_rows(centroid_sum + summed)
    return (best_cosine, centroids)


def solution(mesh):
    return jax.shard_map(
        body,
        mesh=mesh,
        in_specs=(
            P(("grp", "own"), None),
            P(("grp", "own"), None),
            P(("grp", "own")),
            P("own", None, None),
            P("own"),
            P("own", None),
        ),
        out_specs=(P(("grp", "own")), P("own", None)),
        check_vma=False,
    )
```

profile of v0, /device:TPU:0, one launch (start us, length us, event | category | flops | bytes accessed | tf_op | source)
XLA Modules:
  0.0 106.5 jit_solution(4100137262812214495)
XLA Ops:
  7.2 0.0 copy-start.1
  7.2 1.0 fusion.6
  8.2 0.7 convert_add_fusion
  8.9 0.3 select_reduce_fusion.3
  9.2 0.6 broadcast_add_fusion
  9.8 6.3 %all-to-all-start = ((s32[8,1,128]{2,1,0:T(1,128)}), s32[8,1,128]{2,1,0:T(1,128)S(1)}, u32[]{:S(2)}, u32[]{:S(2)}) async-start(s32[8,1,128]{2,1,0:T(1,128)} %bitcast.4), calls=%async_computation | async-start | bytes 8192 | tf_op jit(solution)/shard_map/all_to_all | solution.py:67
  16.1 1.2 %fusion.7 = f32[512]{0:T(512)S(1)} fusion(bf16[512,512]{1,0:T(8,128)(2,1)} %param.8), kind=kLoop, calls=%fused_computation.18 | loop fusion | flops 785920 | bytes 526336 | tf_op jit(solution)/shard_map/reduce_sum | solution.py:23
  17.3 2.8 %fusion.5 = bf16[1024,512]{1,0:T(8,128)(2,1)} fusion(s32[512]{0:T(512)S(1)} %get-tuple-element.56, bf16[512,512]{1,0:T(8,128)(2,1)} %param.8, f32[512]{0:T(512)S(1)} %add_sqrt_fusion.1), kind=kOutput, calls=%fused_computation.13 | convolution fusion | flops 538705920 | bytes 1576960 | tf_op jit(solution)/shard_map/dot_general | solution.py:37
  20.2 1.4 %all-to-all-done = s32[8,1,128]{2,1,0:T(1,128)S(1)} async-done(((s32[8,1,128]{2,1,0:T(1,128)}), s32[8,1,128]{2,1,0:T(1,128)S(1)}, u32[]{:S(2)}, u32[]{:S(2)}) %all-to-all-start) | async-done | bytes 4128 | tf_op jit(solution)/shard_map/all_to_all | solution.py:67
  21.6 3.7 %all-to-all-start.1 = ((bf16[8,128,512]{2,1,0:T(8,128)(2,1)}), bf16[8,128,512]{2,1,0:T(8,128)(2,1)S(1)}, u32[]{:S(2)}, u32[]{:S(2)}) async-start(bf16[8,128,512]{2,1,0:T(8,128)(2,1)} %bitcast.5), calls=%async_computation.1 | async-start | bytes 2097152 | tf_op jit(solution)/shard_map/all_to_all | solution.py:66
  25.3 0.0 all-reduce.2.cloned.1.call-start
  25.4 0.0 copy-done.1
  25.4 1.4 %select_reduce_fusion.1 = s32[8192]{0:T(1024)S(1)} fusion(s32[256]{0:T(256)S(1)} %copy-done.1, s32[8192]{0:T(1024)S(1)} %add_select_fusion), kind=kLoop, calls=%fused_computation.7 | loop fusion | flops 6283264 | bytes 66560 | tf_op jit(solution)/shard_map/reduce_sum | solution.py:53
  26.8 5.1 %fusion.3 = f32[8192]{0:T(1024)S(1)} fusion(bf16[256,32,512]{2,1,0:T(8,128)(2,1)} %param.11), kind=kLoop, calls=%fused_computation.6 | loop fusion | flops 12574720 | bytes 8421376 | tf_op jit(solution)/shard_map/rd,rd->r/dot_general | solution.py:46
  31.9 0.5 broadcast.84
  32.5 0.7 reduce.5
  33.1 18.8 %all-to-all-done.1 = bf16[8,128,512]{2,1,0:T(8,128)(2,1)S(1)} async-done(((bf16[8,128,512]{2,1,0:T(8,128)(2,1)}), bf16[8,128,512]{2,1,0:T(8,128)(2,1)S(1)}, u32[]{:S(2)}, u32[]{:S(2)}) %all-to-all-start.1) | async-done | bytes 1048608 | tf_op jit(solution)/shard_map/all_to_all | solution.py:66
  51.9 1.2 %fusion.10 = f32[256,512]{1,0:T(8,128)} fusion(bf16[1024,512]{1,0:T(8,128)(2,1)S(1)} %bitcast.25, s32[1024]{0:T(1024)S(1)} %bitcast.29), kind=kOutput, calls=%fused_computation.23 | convolution fusion | flops 268697600 | bytes 1576960 | tf_op jit(solution)/shard_map/dot_general | solution.py:90
  53.1 0.0 all-reduce.2.cloned.1.call-update
  53.2 0.0 copy-start
  53.2 24.2 %while.10 = (s32[]{:T(128)}, f32[4,256]{1,0:T(4,128)S(1)}, s32[8192]{0:T(1024)S(1)}, s32[4,256]{1,0:T(4,128)S(1)}, bf16[4,256,512]{2,1,0:T(8,128)(2,1)S(1)}, /*i...) while((s32[]{:T(128)}, f32[4,256]{1,0:T(4,128)S(1)}, s32[8192]{0:T(1024)S(1)}, ...), condition=%wide.region_6.7_spmd, body=%wide.region_4.6_spmd.sunk | while | flops 2155872000 | bytes 8722537 | solution.py:78
  53.2 6.0 %select_reduce_fusion.5 = f32[256]{0:T(256)S(1)} fusion(bf16[8192,512]{1,0:T(8,128)(2,1)} %get-tuple-element.124, f32[8192]{0:T(1024)S(1)} %get-tuple-element.125, s32[8192]{0:T(1024)S(1)} %get-tuple-element.121, s32[256]{0:T(256)S(1)} %bitcast.28, bf16[4,256,512]{2,1,0:T(8,128)(2,1)S(1)} %get-tuple-element.123, s32[]{:T(128)} %get-tuple-element.110), kind=kOutput, calls=%fused_computation.clone.1 | convolution fusion | flops 2155872000 | bytes 8718340 | tf_op jit(solution)/shard_map/while/body/eval_jaxpr/dot_general | solution.py:58
  59.3 6.0 %select_reduce_fusion.5 = f32[256]{0:T(256)S(1)} fusion(bf16[8192,512]{1,0:T(8,128)(2,1)} %get-tuple-element.124, f32[8192]{0:T(1024)S(1)} %get-tuple-element.125, s32[8192]{0:T(1024)S(1)} %get-tuple-element.121, s32[256]{0:T(256)S(1)} %bitcast.28, bf16[4,256,512]{2,1,0:T(8,128)(2,1)S(1)} %get-tuple-element.123, s32[]{:T(128)} %get-tuple-element.110), kind=kOutput, calls=%fused_computation.clone.1 | convolution fusion | flops 2155872000 | bytes 8718340 | tf_op jit(solution)/shard_map/while/body/eval_jaxpr/dot_general | solution.py:58
  65.3 6.0 %select_reduce_fusion.5 = f32[256]{0:T(256)S(1)} fusion(bf16[8192,512]{1,0:T(8,128)(2,1)} %get-tuple-element.124, f32[8192]{0:T(1024)S(1)} %get-tuple-element.125, s32[8192]{0:T(1024)S(1)} %get-tuple-element.121, s32[256]{0:T(256)S(1)} %bitcast.28, bf16[4,256,512]{2,1,0:T(8,128)(2,1)S(1)} %get-tuple-element.123, s32[]{:T(128)} %get-tuple-element.110), kind=kOutput, calls=%fused_computation.clone.1 | convolution fusion | flops 2155872000 | bytes 8718340 | tf_op jit(solution)/shard_map/while/body/eval_jaxpr/dot_general | solution.py:58
  71.3 6.0 %select_reduce_fusion.5 = f32[256]{0:T(256)S(1)} fusion(bf16[8192,512]{1,0:T(8,128)(2,1)} %get-tuple-element.124, f32[8192]{0:T(1024)S(1)} %get-tuple-element.125, s32[8192]{0:T(1024)S(1)} %get-tuple-element.121, s32[256]{0:T(256)S(1)} %bitcast.28, bf16[4,256,512]{2,1,0:T(8,128)(2,1)S(1)} %get-tuple-element.123, s32[]{:T(128)} %get-tuple-element.110), kind=kOutput, calls=%fused_computation.clone.1 | convolution fusion | flops 2155872000 | bytes 8718340 | tf_op jit(solution)/shard_map/while/body/eval_jaxpr/dot_general | solution.py:58
  77.4 7.9 %all_to_all.20 = f32[8,1,128]{2,1,0:T(1,128)S(1)} all-to-all(f32[8,1,128]{2,1,0:T(1,128)S(1)} %all_to_all.15), channel_id=1, replica_groups=mesh['grp'=4,'own'=8] {'own'}, dimensions={0} | all-to-all | bytes 8192 | tf_op jit(solution)/shard_map/all_to_all | solution.py:81
  85.3 0.9 select_reduce_fusion.2
  86.2 11.3 %all-reduce.2.cloned.1.call-done = f32[256,512]{1,0:T(8,128)} async-done(((f32[256,512]{1,0:T(8,128)}), f32[256,512]{1,0:T(8,128)}) %all-reduce.2.cloned.1.call-update) | async-done | bytes 524304 | tf_op jit(solution)/shard_map/psum | solution.py:91
  97.6 0.0 copy-done
  97.6 1.2 %multiply_reduce_fusion = (f32[256]{0:T(256)S(1)}, f32[256,512]{1,0:T(8,128)S(1)}) fusion(f32[256,512]{1,0:T(8,128)S(1)} %copy-done, f32[256,512]{1,0:T(8,128)} %all-reduce.2.cloned.1.call-done), kind=kLoop, calls=%fused_computation.24 | loop fusion | flops 392960 | bytes 1573888 | tf_op jit(solution)/shard_map/reduce_sum | solution.py:10
  98.8 0.9 broadcast_divide_fusion
  (16 shorter events, 0.3 us)
Async XLA Ops:
  7.2 18.2 %copy-start.1 = (s32[256]{0:T(256)S(1)}, s32[256]{0:T(256)}, u32[]{:S(2)}) copy-start(s32[256]{0:T(256)} %param.12) | copy-start | bytes 3076
  9.8 11.8 %all-to-all-start = ((s32[8,1,128]{2,1,0:T(1,128)}), s32[8,1,128]{2,1,0:T(1,128)S(1)}, u32[]{:S(2)}, u32[]{:S(2)}) async-start(s32[8,1,128]{2,1,0:T(1,128)} %bitcast.4), calls=%async_computation | async-start | bytes 8192 | tf_op jit(solution)/shard_map/all_to_all | solution.py:67
  21.6 30.3 %all-to-all-start.1 = ((bf16[8,128,512]{2,1,0:T(8,128)(2,1)}), bf16[8,128,512]{2,1,0:T(8,128)(2,1)S(1)}, u32[]{:S(2)}, u32[]{:S(2)}) async-start(bf16[8,128,512]{2,1,0:T(8,128)(2,1)} %bitcast.5), calls=%async_computation.1 | async-start | bytes 2097152 | tf_op jit(solution)/shard_map/all_to_all | solution.py:66
  25.3 72.3 %all-reduce.2.cloned.1.call-start = ((), (), s32[]{:S(2)}) async-start(), calls=%async_computation.3 | async-start | bytes 1048576 | tf_op jit(solution)/shard_map/psum | solution.py:91
  53.2 44.4 %copy-start = (f32[256,512]{1,0:T(8,128)S(1)}, f32[256,512]{1,0:T(8,128)}, u32[]{:S(2)}) copy-start(f32[256,512]{1,0:T(8,128)} %param.13) | copy-start | bytes 1572868
Sparse Core Ops, SparseCore 0:
  53.3 44.2 all-reduce.1
where the time goes:
time: 107 us
  waiting for transfers between devices  31.5 us (29%)
  matrix products  29 us (27%)
  between operations  14.1 us (13%)
  other arithmetic  13 us (12%)
  starting transfers between devices  10.1 us (9%)
  blocking collectives  7.92 us (7%)
    dot_general x4, matrix products, score_tile(): lax.dot_general(query, bank_flat, (((1,), (1,)), ((), ())), preferred_ele...  23.9 us
    all_to_all x1, waiting for transfers between devices, body(): lax.all_to_all(send_rows, 'own', split_axis=0, concat_axis=0, tiled=True)  18.8 us
    psum x1, waiting for transfers between devices, body(): summed = lax.psum(partial_value, 'grp')  11.3 us
    all_to_all x1, blocking collectives, body(): lax.all_to_all(flat_best.reshape(owners, capacity), 'own', split_axis=0,...  7.92 us
    all_to_all x1, starting transfers between devices, body(): lax.all_to_all(send_slot, 'own', split_axis=0, concat_axis=0, tiled=True)  6.33 us
    dot_general x1, other arithmetic, body(): jnp.einsum('rd,rd->r', bank_flat, bank_flat, preferred_element_type=jnp.f...  5.11 us
    all_to_all x1, starting transfers between devices, body(): lax.all_to_all(send_rows, 'own', split_axis=0, concat_axis=0, tiled=True)  3.7 us
    dot_general x1, matrix products, body(): jnp.dot(slot_match.astype(jnp.bfloat16), unit_rows, preferred_element_typ...  2.84 us
  transfers between devices with their start and end apart: 3, of which 3 were waited for; matrix products, arithmetic and copies ran while one was open for 35% of the time, Pallas kernels for 0%

commit v1 on v0

v1 whole, which is shorter than its diff:
```python
import functools

import jax
import jax.numpy as jnp
from jax import lax
from jax.experimental import pallas as pl
from jax.experimental.pallas import tpu as pltpu
from jax.sharding import PartitionSpec as P

epsilon = 1e-06
LANES = 128
INFO_ROWS = 16
CODE_BASE = 128
VMEM_BYTES = 40 * 1024 * 1024


def whole_vmem():
    return pl.BlockSpec(memory_space=pltpu.VMEM)


def params():
    return pltpu.CompilerParams(vmem_limit_bytes=VMEM_BYTES)


def pack_kernel(owners, capacity, me_ref, owner_ref, slot_ref, rows_ref, index_ref, *message_refs):
    rows = rows_ref.shape[0]
    width = rows_ref.shape[1]
    peer = owner_ref[...] ^ me_ref[0]
    peer_hit = lax.broadcasted_iota(jnp.int32, (owners, rows), 0) == peer
    earlier_mask = (
        lax.broadcasted_iota(jnp.int32, (rows, rows), 0)
        < lax.broadcasted_iota(jnp.int32, (rows, rows), 1)
    )
    earlier = jnp.dot(
        peer_hit.astype(jnp.float32).astype(jnp.bfloat16),
        earlier_mask.astype(jnp.float32).astype(jnp.bfloat16),
        preferred_element_type=jnp.float32,
    )
    placed = jnp.sum(jnp.where(peer_hit, earlier, 0.0), axis=0, keepdims=True).astype(jnp.int32)
    index = peer * capacity + placed
    index_ref[...] = index
    slot = slot_ref[...]
    code_row = lax.broadcasted_iota(jnp.int32, (INFO_ROWS, rows), 0)
    codes = jnp.where(
        code_row == 0,
        slot // CODE_BASE + 1,
        jnp.where(code_row == 1, slot % CODE_BASE, 0),
    )
    codes = codes.astype(jnp.float32).astype(jnp.bfloat16)
    values = rows_ref[...]
    per_dot = max(1, 256 // capacity)
    for first in range(0, owners, per_dot):
        count = min(per_dot, owners - first)
        place = lax.broadcasted_iota(jnp.int32, (count * capacity, rows), 0) + first * capacity
        match = (place == index).astype(jnp.float32).astype(jnp.bfloat16)
        packed = jnp.dot(match, values, preferred_element_type=jnp.float32).astype(jnp.bfloat16)
        info = lax.dot_general(
            codes, match, (((1,), (1,)), ((), ())), preferred_element_type=jnp.float32
        )
        for offset in range(count):
            message = message_refs[first + offset]
            low = offset * capacity
            for part in range(width // LANES):
                message[pl.ds(part * capacity, capacity), :] = packed[
                    low : low + capacity, part * LANES : (part + 1) * LANES
                ]
            piece = info[:, low : low + capacity]
            if capacity < LANES:
                piece = jnp.concatenate(
                    [piece, jnp.zeros((INFO_ROWS, LANES - capacity), jnp.float32)], axis=1
                )
            message[pl.ds(width // LANES * capacity, INFO_ROWS), :] = piece.astype(jnp.bfloat16)


def read_messages(message_refs, capacity, width):
    units, slots = [], []
    for message in message_refs:
        values = jnp.concatenate(
            [
                message[pl.ds(part * capacity, capacity), :].astype(jnp.float32)
                for part in range(width // LANES)
            ],
            axis=1,
        )
        norm = jnp.sqrt(jnp.sum(values * values, axis=1, keepdims=True) + epsilon)
        units.append((values / norm).astype(jnp.bfloat16))
        info = message[pl.ds(width // LANES * capacity, INFO_ROWS), :].astype(jnp.float32)
        slots.append((info[0:1, :capacity] - 1.0) * CODE_BASE + info[1:2, :capacity])
    return jnp.concatenate(units, axis=0), jnp.concatenate(slots, axis=1).astype(jnp.int32)


def cluster_onehot(slots, clusters):
    hit = lax.broadcasted_iota(jnp.int32, (clusters, slots.shape[1]), 0) == slots
    return hit.astype(jnp.float32).astype(jnp.bfloat16)


def early_sum_kernel(messages, capacity, *refs):
    message_refs, total_ref = refs[:messages], refs[messages]
    clusters, width = total_ref.shape
    units, slots = read_messages(message_refs, capacity, width)
    total_ref[...] = jnp.dot(
        cluster_onehot(slots, clusters), units, preferred_element_type=jnp.float32
    )


def late_sum_kernel(messages, capacity, parts, me_ref, *refs):
    message_refs, early_ref = refs[:messages], refs[messages]
    part_refs, total_ref = refs[messages + 1 : -1], refs[-1]
    clusters, width = total_ref.shape
    units, slots = read_messages(message_refs, capacity, width)
    total_ref[...] = early_ref[...] + jnp.dot(
        cluster_onehot(slots, clusters), units, preferred_element_type=jnp.float32
    )
    share = clusters // parts
    for offset in range(parts):
        start = pl.multiple_of((me_ref[0] ^ offset) * share, share)
        part_refs[offset][...] = total_ref[pl.ds(start, share), :].astype(part_refs[offset].dtype)


def score_kernel(messages, capacity, bank_ref, norm_ref, members_ref, *refs):
    message_refs = refs[:messages]
    best_refs = refs[messages : 2 * messages]
    unit_ref, slot_ref, picked_ref = refs[2 * messages :]
    step = pl.program_id(0)
    block_clusters, depth, width = bank_ref.shape
    clusters = norm_ref.shape[1]

    @pl.when(step == 0)
    def _():
        units, slots = read_messages(message_refs, capacity, width)
        unit_ref[...] = units.T
        slot_ref[...] = slots
        picked_ref[...] = jnp.zeros_like(picked_ref)

    dots = jnp.dot(
        bank_ref[...].reshape(block_clusters * depth, width),
        unit_ref[...],
        preferred_element_type=jnp.float32,
    )
    wanted = slot_ref[...] - step * block_clusters
    picked = picked_ref[...]
    for cluster in range(block_clusters):
        picked = jnp.where(
            wanted == cluster, dots[cluster * depth : (cluster + 1) * depth, :], picked
        )
    picked_ref[...] = picked

    @pl.when(step == pl.num_programs(0) - 1)
    def _():
        norm = norm_ref[...]
        high = norm.astype(jnp.bfloat16)
        rest = norm - high.astype(jnp.float32)
        middle = rest.astype(jnp.bfloat16)
        low = (rest - middle.astype(jnp.float32)).astype(jnp.bfloat16)
        member_rows = jnp.broadcast_to(
            members_ref[...].astype(jnp.float32), (INFO_ROWS, clusters)
        ).astype(jnp.bfloat16)
        table = jnp.concatenate([high, middle, low, member_rows], axis=0)
        chosen = jnp.dot(
            table, cluster_onehot(slot_ref[...], clusters), preferred_element_type=jnp.float32
        )
        chosen_norm = chosen[:depth] + chosen[depth : 2 * depth] + chosen[2 * depth : 3 * depth]
        chosen_members = chosen[3 * depth : 3 * depth + 1]
        place = lax.broadcasted_iota(jnp.int32, picked_ref.shape, 0).astype(jnp.float32)
        cosine = jnp.where(place < chosen_members, picked_ref[...] / chosen_norm, -3.0)
        best = jnp.max(cosine, axis=0, keepdims=True)
        for number in range(messages):
            best_refs[number][...] = best[:, number * capacity : (number + 1) * capacity]


def finish_kernel(parts, me_ref, stored_ref, *refs):
    out_ref = refs[-1]
    share = out_ref.shape[0]
    start = pl.multiple_of(me_ref[0] * share, share)
    total = stored_ref[pl.ds(start, share), :]
    for number in range(parts):
        total = total + refs[number][...].astype(jnp.float32)
    out_ref[...] = total / jnp.sqrt(jnp.sum(total * total, axis=1, keepdims=True) + epsilon)


def join_kernel(parts, me_ref, *refs):
    out_ref = refs[-1]
    share = refs[0].shape[0]
    for offset in range(parts):
        start = pl.multiple_of((me_ref[0] ^ offset) * share, share)
        out_ref[pl.ds(start, share), :] = refs[offset][...]


def unpack_kernel(owners, capacity, index_ref, *refs):
    out_ref = refs[-1]
    rows = index_ref.shape[1]
    best = jnp.concatenate([refs[number][...] for number in range(owners)], axis=1)
    high = best.astype(jnp.bfloat16)
    rest = best - high.astype(jnp.float32)
    middle = rest.astype(jnp.bfloat16)
    low = (rest - middle.astype(jnp.float32)).astype(jnp.bfloat16)
    row = lax.broadcasted_iota(jnp.int32, (INFO_ROWS, owners * capacity), 0)
    table = jnp.where(
        row == 0,
        high.astype(jnp.float32),
        jnp.where(
            row == 1,
            middle.astype(jnp.float32),
            jnp.where(row == 2, low.astype(jnp.float32), 0.0),
        ),
    ).astype(jnp.bfloat16)
    place = lax.broadcasted_iota(jnp.int32, (owners * capacity, rows), 0)
    match = (place == index_ref[...]).astype(jnp.float32).astype(jnp.bfloat16)
    spread = jnp.dot(table, match, preferred_element_type=jnp.float32)
    out_ref[...] = spread[0:1] + spread[1:2] + spread[2:3]


def exchange(value, axis, offset):
    size = lax.axis_size(axis)
    return lax.ppermute(value, axis, [(device, device ^ offset) for device in range(size)])


def body(arrivals, home_owner, cluster_slot, bank, members, centroid_sum):
    owners = lax.axis_size("own")
    parts = lax.axis_size("grp")
    rows, width = arrivals.shape
    clusters, depth = bank.shape[0], bank.shape[1]
    capacity = 2 * rows // owners
    message_rows = width // LANES * capacity + INFO_ROWS
    own_index = lax.axis_index("own").astype(jnp.int32).reshape(1)
    grp_index = lax.axis_index("grp").astype(jnp.int32).reshape(1)
    smem = pl.BlockSpec(memory_space=pltpu.SMEM)

    packed = pl.pallas_call(
        functools.partial(pack_kernel, owners, capacity),
        out_shape=[jax.ShapeDtypeStruct((1, rows), jnp.int32)]
        + [jax.ShapeDtypeStruct((message_rows, LANES), jnp.bfloat16)] * owners,
        in_specs=[smem] + [whole_vmem()] * 3,
        out_specs=[whole_vmem()] * (owners + 1),
        compiler_params=params(),
        name="pack",
    )(own_index, home_owner.reshape(1, rows), cluster_slot.reshape(1, rows), arrivals)
    index, messages = packed[0], packed[1:]

    got = [messages[0]] + [None] * (owners - 1)
    for offset in list(range(owners // 2, owners)) + list(range(owners // 2 - 1, 0, -1)):
        got[offset] = exchange(messages[offset], "own", offset)

    widened = bank.astype(jnp.float32)
    bank_norm = jnp.sqrt(jnp.sum(widened * widened, axis=2) + epsilon).T
    member_row = members.reshape(1, clusters)

    def score(group):
        count = len(group)
        block = min(clusters, 32)
        return pl.pallas_call(
            functools.partial(score_kernel, count, capacity),
            grid=(clusters // block,),
            out_shape=[jax.ShapeDtypeStruct((1, capacity), jnp.float32)] * count,
            in_specs=[
                pl.BlockSpec((block, depth, width), lambda i: (i, 0, 0)),
                pl.BlockSpec((depth, clusters), lambda i: (0, 0)),
                pl.BlockSpec((1, clusters), lambda i: (0, 0)),
            ]
            + [pl.BlockSpec((message_rows, LANES), lambda i: (0, 0))] * count,
            out_specs=[pl.BlockSpec((1, capacity), lambda i: (0, 0))] * count,
            scratch_shapes=[
                pltpu.VMEM((width, count * capacity), jnp.bfloat16),
                pltpu.VMEM((1, count * capacity), jnp.int32),
                pltpu.VMEM((depth, count * capacity), jnp.float32),
            ],
            compiler_params=params(),
            cost_estimate=pl.CostEstimate(
                flops=2 * clusters * depth * width * count * capacity,
                bytes_accessed=2 * clusters * depth * width,
                transcendentals=0,
            ),
            name="score",
        )(bank, bank_norm, member_row, *group)

    half, late = owners // 2, 3 * owners // 4
    best = [None] * owners

    def send_back(first, results):
        for number, value in enumerate(results):
            offset = first + number
            best[offset] = value if offset == 0 else exchange(value, "own", offset)

    send_back(0, score(got[:half]))
    send_back(half, score(got[half:late]))
    early = pl.pallas_call(
        functools.partial(early_sum_kernel, late, capacity),
        out_shape=jax.ShapeDtypeStruct((clusters, width), jnp.float32),
        in_specs=[whole_vmem()] * late,
        out_specs=whole_vmem(),
        compiler_params=params(),
        name="early_sum",
    )(*got[:late])
    share = clusters // parts
    summed = pl.pallas_call(
        functools.partial(late_sum_kernel, owners - late, capacity, parts),
        out_shape=[jax.ShapeDtypeStruct((share, width), jnp.float32)] * parts,
        in_specs=[smem] + [whole_vmem()] * (owners - late + 1),
        out_specs=[whole_vmem()] * parts,
        scratch_shapes=[pltpu.VMEM((clusters, width), jnp.float32)],
        compiler_params=params(),
        name="late_sum",
    )(grp_index, *got[late:], early)
    terms = [summed[0]] + [exchange(summed[k], "grp", k) for k in range(1, parts)]
    send_back(late, score(got[late:]))
    own_share = pl.pallas_call(
        functools.partial(finish_kernel, parts),
        out_shape=jax.ShapeDtypeStruct((share, width), jnp.float32),
        in_specs=[smem] + [whole_vmem()] * (parts + 1),
        out_specs=whole_vmem(),
        compiler_params=params(),
        name="finish",
    )(grp_index, centroid_sum, *terms)
    shares = [own_share] + [exchange(own_share, "grp", k) for k in range(1, parts)]
    best_cosine = pl.pallas_call(
        functools.partial(unpack_kernel, owners, capacity),
        out_shape=jax.ShapeDtypeStruct((1, rows), jnp.float32),
        in_specs=[whole_vmem()] * (owners + 1),
        out_specs=whole_vmem(),
        compiler_params=params(),
        name="unpack",
    )(index, *best).reshape(rows)
    centroids = pl.pallas_call(
        functools.partial(join_kernel, parts),
        out_shape=jax.ShapeDtypeStruct((clusters, width), jnp.float32),
        in_specs=[smem] + [whole_vmem()] * parts,
        out_specs=whole_vmem(),
        compiler_params=params(),
        name="join",
    )(grp_index, *shares)
    return (best_cosine, centroids)


def solution(mesh):
    return jax.shard_map(
        body,
        mesh=mesh,
        in_specs=(
            P(("grp", "own"), None),
            P(("grp", "own"), None),
            P(("grp", "own")),
            P("own", None, None),
            P("own"),
            P("own", None),
        ),
        out_specs=(P(("grp", "own")), P("own", None)),
        check_vma=False,
    )
```

time: 107 us -> 70 us (0.65)
  matrix products: 29 us -> 0 us
  waiting for transfers between devices: 31.5 us -> 4.98 us
  Pallas kernels: 0 us -> 18.2 us
  starting transfers between devices: 10.1 us -> 27.8 us
  between operations: 14.1 us -> 0.8 us
  local copies, waits for them, and re-layouts: 0.73 us -> 12.6 us
  blocking collectives: 7.92 us -> 0 us
  other arithmetic: 13 us -> 5.26 us
    dot_general x7 -> x0, matrix products: 29 us -> none  [the longest x4 23.9 us: score_tile(): lax.dot_general(query, bank_flat, (((1,), (1,)), ((), ())), preferred_ele...]
    ppermute x0 -> x20, starting transfers between devices: none -> 27.8 us  [exchange(): lax.ppermute(value, axis, [(device, device ^ offset) for device in range(...]
    all_to_all x2 -> x0, waiting for transfers between devices: 20.2 us -> none  [the longest x1 18.8 us: body(): lax.all_to_all(send_rows, 'own', split_axis=0, concat_axis=0, tiled=True)]
    pallas_call x0 -> x9, Pallas kernels: none -> 18.2 us  [the longest x3 14.3 us: score(): pl.pallas_call(functools.partial(score_kernel, count, capacity), grid=(cl...]
    unnamed x4 -> x16, local copies, waits for them, and re-layouts: 0.01 us -> 12.6 us
    psum x1 -> x0, waiting for transfers between devices: 11.3 us -> none  [body(): summed = lax.psum(partial_value, 'grp')]
    all_to_all x2 -> x0, starting transfers between devices: 10 us -> none  [the longest x1 6.33 us: body(): lax.all_to_all(send_slot, 'own', split_axis=0, concat_axis=0, tiled=True)]
    all_to_all x1 -> x0, blocking collectives: 7.92 us -> none  [body(): lax.all_to_all(flat_best.reshape(owners, capacity), 'own', split_axis=0,...]
  transfers between devices with their start and end apart: 3 -> 20, of which waited for: 3 -> 3; matrix products, arithmetic and copies ran while one was open for 35% -> 8% of each run, Pallas kernels for 0% -> 23%
where the time goes in v1:
time: 70 us; the launch traced here: 69.7 us
  starting transfers between devices  27.8 us (40%)
  Pallas kernels  18.2 us (26%)
  local copies, waits for them, and re-layouts  12.6 us (18%)
  other arithmetic  5.26 us (8%)
  waiting for transfers between devices  4.98 us (7%)
  between operations  0.8 us (1%)
    ppermute x20, starting transfers between devices, exchange(): lax.ppermute(value, axis, [(device, device ^ offset) for device in range(...  27.8 us
    pallas_call x3, Pallas kernels, score(): pl.pallas_call(functools.partial(score_kernel, count, capacity), grid=(cl...  14.3 us
    unnamed x16, local copies, waits for them, and re-layouts  12.6 us
    reduce_sum x1, other arithmetic, body(): bank_norm = jnp.sqrt(jnp.sum(widened * widened, axis=2) + epsilon).T  5.23 us
    ppermute x20, waiting for transfers between devices, exchange(): lax.ppermute(value, axis, [(device, device ^ offset) for device in range(...  4.98 us
  transfers between devices with their start and end apart: 20, of which 3 were waited for; matrix products, arithmetic and copies ran while one was open for 8% of the time, Pallas kernels for 23%

profile of v1, /device:TPU:0, one launch (start us, length us, event | category | flops | bytes accessed | tf_op | source)
XLA Modules:
  0.0 69.7 jit_solution(3178440187104483548)
XLA Ops:
  0.7 1.0 %copy-done.3 = bf16[512,512]{1,0:T(8,128)(2,1)S(1)} copy-done((bf16[512,512]{1,0:T(8,128)(2,1)S(1)}, bf16[512,512]{1,0:T(8,128)(2,1)}, u32[]{:S(2)}) %copy-start.3) | copy-done | bytes 524312
  1.7 0.7 copy-done.6
  2.4 0.7 copy-done.7
  3.1 1.1 %pack.1 = (s32[1,512]{1,0:T(1,128)S(1)}, bf16[528,128]{1,0:T(8,128)(2,1)S(1)}, bf16[528,128]{1,0:T(8,128)(2,1)S(1)}, bf16[528,128]{1,0:T(8,128)(2,1)S(1)}, bf16[...) custom-call(s32[1]{0:T(128)} %bitcast.me_ref, ...), custom_call_target="tpu_custom_call" | custom-call | tf_op jit(solution)/shard_map/pack/pallas_call | solution.py:229
  4.2 0.5 collective-permute-start
  4.7 2.6 %collective-permute-start.1 = (bf16[528,128]{1,0:T(8,128)(2,1)S(1)}, bf16[528,128]{1,0:T(8,128)(2,1)S(1)}, u32[]{:S(2)}, u32[]{:S(2)}) collective-permute-start(bf16[528,128]{1,0:T(8,128)(2,1)S(1)} %get-tuple-element.26), channel_id=1, source_target_pairs={{0,2},{1,3},{2,0},{3,1},{4,6},{5,7},{6,4},{7,5},{8,10},{9,11},{10,... | collective-permute-start | bytes 405512 | tf_op jit(solution)/shard_map/ppermute | solution.py:215
  7.4 2.8 %collective-permute-start.6 = (bf16[528,128]{1,0:T(8,128)(2,1)S(1)}, bf16[528,128]{1,0:T(8,128)(2,1)S(1)}, u32[]{:S(2)}, u32[]{:S(2)}) collective-permute-start(bf16[528,128]{1,0:T(8,128)(2,1)S(1)} %get-tuple-element.32), channel_id=1, source_target_pairs={{0,4},{1,5},{2,6},{3,7},{4,0},{5,1},{6,2},{7,3},{8,12},{9,13},{10,... | collective-permute-start | bytes 405512 | tf_op jit(solution)/shard_map/ppermute | solution.py:215
  10.2 5.2 %multiply_reduce_fusion = f32[256,32]{1,0:T(8,128)S(1)} fusion(bf16[256,32,512]{2,1,0:T(8,128)(2,1)} %bank_ref.5), kind=kLoop, calls=%fused_computation | loop fusion | flops 12574720 | bytes 8421376 | tf_op jit(solution)/shard_map/reduce_sum | solution.py:245
  15.5 3.7 %collective-permute-start.10 = (bf16[528,128]{1,0:T(8,128)(2,1)S(1)}, bf16[528,128]{1,0:T(8,128)(2,1)S(1)}, u32[]{:S(2)}, u32[]{:S(2)}) collective-permute-start(bf16[528,128]{1,0:T(8,128)(2,1)S(1)} %get-tuple-element.36), channel_id=1, source_target_pairs={{0,6},{1,7},{2,4},{3,5},{4,2},{5,3},{6,0},{7,1},{8,14},{9,15},{10,... | collective-permute-start | bytes 405512 | tf_op jit(solution)/shard_map/ppermute | solution.py:215
  19.5 3.4 %copy-done = bf16[256,32,512]{2,1,0:T(8,128)(2,1)S(1)} copy-done((bf16[256,32,512]{2,1,0:T(8,128)(2,1)S(1)}, bf16[256,32,512]{2,1,0:T(8,128)(2,1)}, u32[]{:S(2)}) %copy-start) | copy-done | bytes 8388632
  22.9 6.3 %score.3 = (f32[1,128]{1,0:T(1,128)S(1)}, f32[1,128]{1,0:T(1,128)S(1)}, f32[1,128]{1,0:T(1,128)S(1)}, f32[1,128]{1,0:T(1,128)S(1)}) custom-call(bf16[256,32,512]{2,1,0:T(8,128)(2,1)S(1)} %copy-done, f32[32,256]{1,0:T(8,128)S(1)} %sqrt_bitcast_fusion.norm_ref, s32[1,256]{1,0:T(1,128)S(1)} %bitcast.8, bf16[528,128]{1,0:T(8,128)(2,1)S(1)} %get-tuple-element.24.refs_0_, ...), custom_call_target="tpu_custom_call" | custom-call | flops 4294967296 | bytes 8388608 | tf_op jit(solution)/shard_map/score/pallas_call | solution.py:251
  29.2 0.4 collective-permute-start.3
  29.7 0.6 early_sum.1.refs_2_
  30.3 0.4 late_sum.1
  30.7 1.7 %collective-permute-start.14 = (f32[64,512]{1,0:T(8,128)S(1)}, f32[64,512]{1,0:T(8,128)S(1)}, u32[]{:S(2)}, u32[]{:S(2)}) collective-permute-start(f32[64,512]{1,0:T(8,128)S(1)} %get-tuple-element.41), channel_id=1, source_target_pairs={{0,8},{8,0},{16,24},{24,16},{1,9},{9,1},{17,25},{25,17},{2,10},{10... | collective-permute-start | bytes 393224 | tf_op jit(solution)/shard_map/ppermute | solution.py:215
  32.4 1.5 %collective-permute-start.15 = (f32[64,512]{1,0:T(8,128)S(1)}, f32[64,512]{1,0:T(8,128)S(1)}, u32[]{:S(2)}, u32[]{:S(2)}) collective-permute-start(f32[64,512]{1,0:T(8,128)S(1)} %get-tuple-element.42), channel_id=1, source_target_pairs={{0,16},{8,24},{16,0},{24,8},{1,17},{9,25},{17,1},{25,9},{2,18},{10... | collective-permute-start | bytes 393224 | tf_op jit(solution)/shard_map/ppermute | solution.py:215
  33.9 0.3 collective-permute-start.16
  34.3 3.4 %copy-done.1 = bf16[256,32,512]{2,1,0:T(8,128)(2,1)S(1)} copy-done((bf16[256,32,512]{2,1,0:T(8,128)(2,1)S(1)}, bf16[256,32,512]{2,1,0:T(8,128)(2,1)}, u32[]{:S(2)}) %copy-start.1) | copy-done | bytes 8388632
  37.6 4.0 %score.4 = (f32[1,128]{1,0:T(1,128)S(1)}, f32[1,128]{1,0:T(1,128)S(1)}) custom-call(bf16[256,32,512]{2,1,0:T(8,128)(2,1)S(1)} %copy-done.1, f32[32,256]{1,0:T(8,128)S(1)} %sqrt_bitcast_fusion.norm_ref, s32[1,256]{1,0:T(1,128)S(1)} %bitcast.9, bf16[528,128]{1,0:T(8,128)(2,1)S(1)} %collective-permute-done.6.refs_0_.refs_4_, ...), custom_call_target="tpu_custom_call" | custom-call | flops 2147483648 | bytes 8388608 | tf_op jit(solution)/shard_map/score/pallas_call | solution.py:251
  41.6 3.6 %collective-permute-start.5 = (f32[1,128]{1,0:T(1,128)S(1)}, f32[1,128]{1,0:T(1,128)S(1)}, u32[]{:S(2)}, u32[]{:S(2)}) collective-permute-start(f32[1,128]{1,0:T(1,128)S(1)} %get-tuple-element.31), channel_id=1, source_target_pairs={{0,3},{1,2},{2,1},{3,0},{4,7},{5,6},{6,5},{7,4},{8,11},{9,10},{10,... | collective-permute-start | bytes 1544 | tf_op jit(solution)/shard_map/ppermute | solution.py:215
  45.2 3.1 %collective-permute-start.8 = (f32[1,128]{1,0:T(1,128)S(1)}, f32[1,128]{1,0:T(1,128)S(1)}, u32[]{:S(2)}, u32[]{:S(2)}) collective-permute-start(f32[1,128]{1,0:T(1,128)S(1)} %get-tuple-element.34), channel_id=1, source_target_pairs={{0,4},{1,5},{2,6},{3,7},{4,0},{5,1},{6,2},{7,3},{8,12},{9,13},{10,... | collective-permute-start | bytes 1544 | tf_op jit(solution)/shard_map/ppermute | solution.py:215
  48.3 0.9 %collective-permute-start.9 = (f32[1,128]{1,0:T(1,128)S(1)}, f32[1,128]{1,0:T(1,128)S(1)}, u32[]{:S(2)}, u32[]{:S(2)}) collective-permute-start(f32[1,128]{1,0:T(1,128)S(1)} %get-tuple-element.35), channel_id=1, source_target_pairs={{0,5},{1,4},{2,7},{3,6},{4,1},{5,0},{6,3},{7,2},{8,13},{9,12},{10,... | collective-permute-start | bytes 1544 | tf_op jit(solution)/shard_map/ppermute | solution.py:215
  49.4 1.5 %collective-permute-start.17 = (f32[64,512]{1,0:T(8,128)S(1)}, f32[64,512]{1,0:T(8,128)S(1)}, u32[]{:S(2)}, u32[]{:S(2)}) collective-permute-start(f32[64,512]{1,0:T(8,128)S(1)} %finish.1.refs_0_), channel_id=1, source_target_pairs={{0,8},{8,0},{16,24},{24,16},{1,9},{9,1},{17,25},{25,17},{2,10},{10... | collective-permute-start | bytes 393224 | tf_op jit(solution)/shard_map/ppermute | solution.py:215
  50.9 1.5 %collective-permute-start.18 = (f32[64,512]{1,0:T(8,128)S(1)}, f32[64,512]{1,0:T(8,128)S(1)}, u32[]{:S(2)}, u32[]{:S(2)}) collective-permute-start(f32[64,512]{1,0:T(8,128)S(1)} %finish.1.refs_0_), channel_id=1, source_target_pairs={{0,16},{8,24},{16,0},{24,8},{1,17},{9,25},{17,1},{25,9},{2,18},{10... | collective-permute-start | bytes 393224 | tf_op jit(solution)/shard_map/ppermute | solution.py:215
  52.4 0.5 collective-permute-start.19
  52.9 3.4 %copy-done.2 = bf16[256,32,512]{2,1,0:T(8,128)(2,1)S(1)} copy-done((bf16[256,32,512]{2,1,0:T(8,128)(2,1)S(1)}, bf16[256,32,512]{2,1,0:T(8,128)(2,1)}, u32[]{:S(2)}) %copy-start.2) | copy-done | bytes 8388632
  56.3 4.0 %score.5 = (f32[1,128]{1,0:T(1,128)S(1)}, f32[1,128]{1,0:T(1,128)S(1)}) custom-call(bf16[256,32,512]{2,1,0:T(8,128)(2,1)S(1)} %copy-done.2, f32[32,256]{1,0:T(8,128)S(1)} %sqrt_bitcast_fusion.norm_ref, s32[1,256]{1,0:T(1,128)S(1)} %bitcast.10, bf16[528,128]{1,0:T(8,128)(2,1)S(1)} %collective-permute-done.10.refs_0_, ...), custom_call_target="tpu_custom_call" | custom-call | flops 2147483648 | bytes 8388608 | tf_op jit(solution)/shard_map/score/pallas_call | solution.py:251
  60.3 2.9 %collective-permute-start.12 = (f32[1,128]{1,0:T(1,128)S(1)}, f32[1,128]{1,0:T(1,128)S(1)}, u32[]{:S(2)}, u32[]{:S(2)}) collective-permute-start(f32[1,128]{1,0:T(1,128)S(1)} %get-tuple-element.38), channel_id=1, source_target_pairs={{0,6},{1,7},{2,4},{3,5},{4,2},{5,3},{6,0},{7,1},{8,14},{9,15},{10,... | collective-permute-start | bytes 1544 | tf_op jit(solution)/shard_map/ppermute | solution.py:215
  63.2 2.5 %collective-permute-done.12.refs_6_ = f32[1,128]{1,0:T(1,128)S(1)} collective-permute-done((f32[1,128]{1,0:T(1,128)S(1)}, f32[1,128]{1,0:T(1,128)S(1)}, u32[]{:S(2)}, u32[]{:S(2)}) %collective-permute-start.12) | collective-permute-done | bytes 544 | tf_op jit(solution)/shard_map/ppermute | solution.py:215
  65.7 2.3 %collective-permute-done.13.refs_7_ = f32[1,128]{1,0:T(1,128)S(1)} collective-permute-done((f32[1,128]{1,0:T(1,128)S(1)}, f32[1,128]{1,0:T(1,128)S(1)}, u32[]{:S(2)}, u32[]{:S(2)}) %collective-permute-start.13) | collective-permute-done | bytes 544 | tf_op jit(solution)/shard_map/ppermute | solution.py:215
  68.0 0.8 %unpack.1 = f32[1,512]{1,0:T(1,128)} custom-call(s32[1,512]{1,0:T(1,128)S(1)} %get-tuple-element.23.index_ref, f32[1,128]{1,0:T(1,128)S(1)} %get-tuple-element.28.refs_0_, f32[1,128]{1,0:T(1,128)S(1)} %collective-permute-done.3.refs_1_, f32[1,128]{1,0:T(1,128)S(1)} %collective-permute-done.4.refs_2_, f32[1,128]{1,0:T(1,128)S(1)} %collective-permute-done.5.refs_3_, ...), custom_call_target="tpu_custom_call" | custom-call | tf_op jit(solution)/shard_map/unpack/pallas_call | solution.py:315
  68.8 0.8 %join.1 = f32[256,512]{1,0:T(8,128)} custom-call(s32[1]{0:T(128)} %bitcast.6.me_ref, f32[64,512]{1,0:T(8,128)S(1)} %finish.1.refs_0_, f32[64,512]{1,0:T(8,128)S(1)} %collective-permute-done.17.refs_1_, f32[64,512]{1,0:T(8,128)S(1)} %collective-permute-done.18.refs_2_, f32[64,512]{1,0:T(8,128)S(1)} %collective-permute-done.19.refs_3_), custom_call_target="tpu_custom_call" | custom-call | tf_op jit(solution)/shard_map/join/pallas_call | solution.py:323
  (36 shorter events, 0.7 us)
Async XLA Ops:
  0.6 18.9 %copy-start.5 = (s32[256]{0:T(256)S(1)}, s32[256]{0:T(256)}, u32[]{:S(2)}) copy-start(s32[256]{0:T(256)} %param.10) | copy-start | bytes 3076
  0.6 1.0 %copy-start.3 = (bf16[512,512]{1,0:T(8,128)(2,1)S(1)}, bf16[512,512]{1,0:T(8,128)(2,1)}, u32[]{:S(2)}) copy-start(bf16[512,512]{1,0:T(8,128)(2,1)} %rows_ref.1) | copy-start | bytes 1572868
  1.7 0.7 copy-start.6
  2.4 0.7 copy-start.7
  4.2 11.3 %collective-permute-start = (bf16[528,128]{1,0:T(8,128)(2,1)S(1)}, bf16[528,128]{1,0:T(8,128)(2,1)S(1)}, u32[]{:S(2)}, u32[]{:S(2)}) collective-permute-start(bf16[528,128]{1,0:T(8,128)(2,1)S(1)} %get-tuple-element.25), channel_id=1, source_target_pairs={{0,1},{1,0},{2,3},{3,2},{4,5},{5,4},{6,7},{7,6},{8,9},{9,8},{10,11... | collective-permute-start | bytes 405512 | tf_op jit(solution)/shard_map/ppermute | solution.py:215
  4.7 14.5 %collective-permute-start.1 = (bf16[528,128]{1,0:T(8,128)(2,1)S(1)}, bf16[528,128]{1,0:T(8,128)(2,1)S(1)}, u32[]{:S(2)}, u32[]{:S(2)}) collective-permute-start(bf16[528,128]{1,0:T(8,128)(2,1)S(1)} %get-tuple-element.26), channel_id=1, source_target_pairs={{0,2},{1,3},{2,0},{3,1},{4,6},{5,7},{6,4},{7,5},{8,10},{9,11},{10,... | collective-permute-start | bytes 405512 | tf_op jit(solution)/shard_map/ppermute | solution.py:215
  7.4 12.1 %collective-permute-start.2 = (bf16[528,128]{1,0:T(8,128)(2,1)S(1)}, bf16[528,128]{1,0:T(8,128)(2,1)S(1)}, u32[]{:S(2)}, u32[]{:S(2)}) collective-permute-start(bf16[528,128]{1,0:T(8,128)(2,1)S(1)} %get-tuple-element.27), channel_id=1, source_target_pairs={{0,3},{1,2},{2,1},{3,0},{4,7},{5,6},{6,5},{7,4},{8,11},{9,10},{10,... | collective-permute-start | bytes 405512 | tf_op jit(solution)/shard_map/ppermute | solution.py:215
  7.4 22.2 %collective-permute-start.6 = (bf16[528,128]{1,0:T(8,128)(2,1)S(1)}, bf16[528,128]{1,0:T(8,128)(2,1)S(1)}, u32[]{:S(2)}, u32[]{:S(2)}) collective-permute-start(bf16[528,128]{1,0:T(8,128)(2,1)S(1)} %get-tuple-element.32), channel_id=1, source_target_pairs={{0,4},{1,5},{2,6},{3,7},{4,0},{5,1},{6,2},{7,3},{8,12},{9,13},{10,... | collective-permute-start | bytes 405512 | tf_op jit(solution)/shard_map/ppermute | solution.py:215
  10.2 19.5 %collective-permute-start.7 = (bf16[528,128]{1,0:T(8,128)(2,1)S(1)}, bf16[528,128]{1,0:T(8,128)(2,1)S(1)}, u32[]{:S(2)}, u32[]{:S(2)}) collective-permute-start(bf16[528,128]{1,0:T(8,128)(2,1)S(1)} %get-tuple-element.33), channel_id=1, source_target_pairs={{0,5},{1,4},{2,7},{3,6},{4,1},{5,0},{6,3},{7,2},{8,13},{9,12},{10,... | collective-permute-start | bytes 405512 | tf_op jit(solution)/shard_map/ppermute | solution.py:215
  15.5 14.7 %collective-permute-start.10 = (bf16[528,128]{1,0:T(8,128)(2,1)S(1)}, bf16[528,128]{1,0:T(8,128)(2,1)S(1)}, u32[]{:S(2)}, u32[]{:S(2)}) collective-permute-start(bf16[528,128]{1,0:T(8,128)(2,1)S(1)} %get-tuple-element.36), channel_id=1, source_target_pairs={{0,6},{1,7},{2,4},{3,5},{4,2},{5,3},{6,0},{7,1},{8,14},{9,15},{10,... | collective-permute-start | bytes 405512 | tf_op jit(solution)/shard_map/ppermute | solution.py:215
  19.2 11.1 %collective-permute-start.11 = (bf16[528,128]{1,0:T(8,128)(2,1)S(1)}, bf16[528,128]{1,0:T(8,128)(2,1)S(1)}, u32[]{:S(2)}, u32[]{:S(2)}) collective-permute-start(bf16[528,128]{1,0:T(8,128)(2,1)S(1)} %get-tuple-element.37), channel_id=1, source_target_pairs={{0,7},{1,6},{2,5},{3,4},{4,3},{5,2},{6,1},{7,0},{8,15},{9,14},{10,... | collective-permute-start | bytes 405512 | tf_op jit(solution)/shard_map/ppermute | solution.py:215
  19.5 3.4 %copy-start = (bf16[256,32,512]{2,1,0:T(8,128)(2,1)S(1)}, bf16[256,32,512]{2,1,0:T(8,128)(2,1)}, u32[]{:S(2)}) copy-start(bf16[256,32,512]{2,1,0:T(8,128)(2,1)} %bank_ref.5) | copy-start | bytes 25165828
  29.2 20.0 %copy-start.4 = (f32[256,512]{1,0:T(8,128)S(1)}, f32[256,512]{1,0:T(8,128)}, u32[]{:S(2)}) copy-start(f32[256,512]{1,0:T(8,128)} %stored_ref.1) | copy-start | bytes 1572868
  29.2 20.2 %collective-permute-start.3 = (f32[1,128]{1,0:T(1,128)S(1)}, f32[1,128]{1,0:T(1,128)S(1)}, u32[]{:S(2)}, u32[]{:S(2)}) collective-permute-start(f32[1,128]{1,0:T(1,128)S(1)} %get-tuple-element.29), channel_id=1, source_target_pairs={{0,1},{1,0},{2,3},{3,2},{4,5},{5,4},{6,7},{7,6},{8,9},{9,8},{10,11... | collective-permute-start | bytes 1544 | tf_op jit(solution)/shard_map/ppermute | solution.py:215
  29.6 21.3 %collective-permute-start.4 = (f32[1,128]{1,0:T(1,128)S(1)}, f32[1,128]{1,0:T(1,128)S(1)}, u32[]{:S(2)}, u32[]{:S(2)}) collective-permute-start(f32[1,128]{1,0:T(1,128)S(1)} %get-tuple-element.30), channel_id=1, source_target_pairs={{0,2},{1,3},{2,0},{3,1},{4,6},{5,7},{6,4},{7,5},{8,10},{9,11},{10,... | collective-permute-start | bytes 1544 | tf_op jit(solution)/shard_map/ppermute | solution.py:215
  30.7 10.9 %collective-permute-start.14 = (f32[64,512]{1,0:T(8,128)S(1)}, f32[64,512]{1,0:T(8,128)S(1)}, u32[]{:S(2)}, u32[]{:S(2)}) collective-permute-start(f32[64,512]{1,0:T(8,128)S(1)} %get-tuple-element.41), channel_id=1, source_target_pairs={{0,8},{8,0},{16,24},{24,16},{1,9},{9,1},{17,25},{25,17},{2,10},{10... | collective-permute-start | bytes 393224 | tf_op jit(solution)/shard_map/ppermute | solution.py:215
  32.4 12.9 %collective-permute-start.15 = (f32[64,512]{1,0:T(8,128)S(1)}, f32[64,512]{1,0:T(8,128)S(1)}, u32[]{:S(2)}, u32[]{:S(2)}) collective-permute-start(f32[64,512]{1,0:T(8,128)S(1)} %get-tuple-element.42), channel_id=1, source_target_pairs={{0,16},{8,24},{16,0},{24,8},{1,17},{9,25},{17,1},{25,9},{2,18},{10... | collective-permute-start | bytes 393224 | tf_op jit(solution)/shard_map/ppermute | solution.py:215
  33.9 14.4 %collective-permute-start.16 = (f32[64,512]{1,0:T(8,128)S(1)}, f32[64,512]{1,0:T(8,128)S(1)}, u32[]{:S(2)}, u32[]{:S(2)}) collective-permute-start(f32[64,512]{1,0:T(8,128)S(1)} %get-tuple-element.43), channel_id=1, source_target_pairs={{0,24},{8,16},{16,8},{24,0},{1,25},{9,17},{17,9},{25,1},{2,26},{10... | collective-permute-start | bytes 393224 | tf_op jit(solution)/shard_map/ppermute | solution.py:215
  34.3 3.4 %copy-start.1 = (bf16[256,32,512]{2,1,0:T(8,128)(2,1)S(1)}, bf16[256,32,512]{2,1,0:T(8,128)(2,1)}, u32[]{:S(2)}) copy-start(bf16[256,32,512]{2,1,0:T(8,128)(2,1)} %bank_ref.5) | copy-start | bytes 25165828
  41.6 10.8 %collective-permute-start.5 = (f32[1,128]{1,0:T(1,128)S(1)}, f32[1,128]{1,0:T(1,128)S(1)}, u32[]{:S(2)}, u32[]{:S(2)}) collective-permute-start(f32[1,128]{1,0:T(1,128)S(1)} %get-tuple-element.31), channel_id=1, source_target_pairs={{0,3},{1,2},{2,1},{3,0},{4,7},{5,6},{6,5},{7,4},{8,11},{9,10},{10,... | collective-permute-start | bytes 1544 | tf_op jit(solution)/shard_map/ppermute | solution.py:215
  45.2 15.1 %collective-permute-start.8 = (f32[1,128]{1,0:T(1,128)S(1)}, f32[1,128]{1,0:T(1,128)S(1)}, u32[]{:S(2)}, u32[]{:S(2)}) collective-permute-start(f32[1,128]{1,0:T(1,128)S(1)} %get-tuple-element.34), channel_id=1, source_target_pairs={{0,4},{1,5},{2,6},{3,7},{4,0},{5,1},{6,2},{7,3},{8,12},{9,13},{10,... | collective-permute-start | bytes 1544 | tf_op jit(solution)/shard_map/ppermute | solution.py:215
  48.3 14.9 %collective-permute-start.9 = (f32[1,128]{1,0:T(1,128)S(1)}, f32[1,128]{1,0:T(1,128)S(1)}, u32[]{:S(2)}, u32[]{:S(2)}) collective-permute-start(f32[1,128]{1,0:T(1,128)S(1)} %get-tuple-element.35), channel_id=1, source_target_pairs={{0,5},{1,4},{2,7},{3,6},{4,1},{5,0},{6,3},{7,2},{8,13},{9,12},{10,... | collective-permute-start | bytes 1544 | tf_op jit(solution)/shard_map/ppermute | solution.py:215
  49.4 19.5 %collective-permute-start.17 = (f32[64,512]{1,0:T(8,128)S(1)}, f32[64,512]{1,0:T(8,128)S(1)}, u32[]{:S(2)}, u32[]{:S(2)}) collective-permute-start(f32[64,512]{1,0:T(8,128)S(1)} %finish.1.refs_0_), channel_id=1, source_target_pairs={{0,8},{8,0},{16,24},{24,16},{1,9},{9,1},{17,25},{25,17},{2,10},{10... | collective-permute-start | bytes 393224 | tf_op jit(solution)/shard_map/ppermute | solution.py:215
  50.9 17.9 %collective-permute-start.18 = (f32[64,512]{1,0:T(8,128)S(1)}, f32[64,512]{1,0:T(8,128)S(1)}, u32[]{:S(2)}, u32[]{:S(2)}) collective-permute-start(f32[64,512]{1,0:T(8,128)S(1)} %finish.1.refs_0_), channel_id=1, source_target_pairs={{0,16},{8,24},{16,0},{24,8},{1,17},{9,25},{17,1},{25,9},{2,18},{10... | collective-permute-start | bytes 393224 | tf_op jit(solution)/shard_map/ppermute | solution.py:215
  52.4 16.4 %collective-permute-start.19 = (f32[64,512]{1,0:T(8,128)S(1)}, f32[64,512]{1,0:T(8,128)S(1)}, u32[]{:S(2)}, u32[]{:S(2)}) collective-permute-start(f32[64,512]{1,0:T(8,128)S(1)} %finish.1.refs_0_), channel_id=1, source_target_pairs={{0,24},{8,16},{16,8},{24,0},{1,25},{9,17},{17,9},{25,1},{2,26},{10... | collective-permute-start | bytes 393224 | tf_op jit(solution)/shard_map/ppermute | solution.py:215
  52.9 3.4 %copy-start.2 = (bf16[256,32,512]{2,1,0:T(8,128)(2,1)S(1)}, bf16[256,32,512]{2,1,0:T(8,128)(2,1)}, u32[]{:S(2)}) copy-start(bf16[256,32,512]{2,1,0:T(8,128)(2,1)} %bank_ref.5) | copy-start | bytes 25165828
  60.3 5.4 %collective-permute-start.12 = (f32[1,128]{1,0:T(1,128)S(1)}, f32[1,128]{1,0:T(1,128)S(1)}, u32[]{:S(2)}, u32[]{:S(2)}) collective-permute-start(f32[1,128]{1,0:T(1,128)S(1)} %get-tuple-element.38), channel_id=1, source_target_pairs={{0,6},{1,7},{2,4},{3,5},{4,2},{5,3},{6,0},{7,1},{8,14},{9,15},{10,... | collective-permute-start | bytes 1544 | tf_op jit(solution)/shard_map/ppermute | solution.py:215
  63.2 4.8 %collective-permute-start.13 = (f32[1,128]{1,0:T(1,128)S(1)}, f32[1,128]{1,0:T(1,128)S(1)}, u32[]{:S(2)}, u32[]{:S(2)}) collective-permute-start(f32[1,128]{1,0:T(1,128)S(1)} %get-tuple-element.39), channel_id=1, source_target_pairs={{0,7},{1,6},{2,5},{3,4},{4,3},{5,2},{6,1},{7,0},{8,15},{9,14},{10,... | collective-permute-start | bytes 1544 | tf_op jit(solution)/shard_map/ppermute | solution.py:215

commit v2 on v1

v2 whole, which is shorter than its diff:
```python
import functools

import jax
import jax.numpy as jnp
from jax import lax
from jax.experimental import pallas as pl
from jax.experimental.pallas import tpu as pltpu
from jax.sharding import PartitionSpec as P

epsilon = 1e-06
LANES = 128
INFO_ROWS = 16
CODE_BASE = 128
CORES = 2
LARGE_VMEM = 50 * 1024 * 1024
SMALL_VMEM = 32 * 1024 * 1024


def whole_vmem():
    return pl.BlockSpec(memory_space=pltpu.VMEM)


def params():
    return pltpu.CompilerParams(vmem_limit_bytes=LARGE_VMEM)


def small_params():
    return pltpu.CompilerParams(vmem_limit_bytes=SMALL_VMEM)


def place_rows(owners, owner):
    rows = owner.shape[1]
    hit = lax.broadcasted_iota(jnp.int32, (owners, rows), 0) == owner
    earlier_mask = (
        lax.broadcasted_iota(jnp.int32, (rows, rows), 0)
        < lax.broadcasted_iota(jnp.int32, (rows, rows), 1)
    )
    earlier = jnp.dot(
        hit.astype(jnp.float32).astype(jnp.bfloat16),
        earlier_mask.astype(jnp.float32).astype(jnp.bfloat16),
        preferred_element_type=jnp.float32,
    )
    return jnp.sum(jnp.where(hit, earlier, 0.0), axis=0, keepdims=True).astype(jnp.int32)


def pack_kernel(owners, capacity, me_ref, *refs):
    sources, return_ref, message_refs = (refs[0:3], refs[3:6]), refs[6], refs[7:]
    chips = owners // CORES
    for source, (owner_ref, slot_ref, rows_ref) in enumerate(sources):
        owner, slot, values = owner_ref[...], slot_ref[...], rows_ref[...]
        rows, width = values.shape
        placed = place_rows(owners, owner)
        if source == 0:
            return_ref[...] = owner * capacity + placed
        peer = owner ^ me_ref[0]
        index = jnp.where(peer % CORES == 0, peer // CORES * capacity + placed, -1)
        code_row = lax.broadcasted_iota(jnp.int32, (INFO_ROWS, rows), 0)
        codes = jnp.where(
            code_row == 0,
            slot // CODE_BASE + 1,
            jnp.where(code_row == 1, slot % CODE_BASE, 0),
        )
        place = lax.broadcasted_iota(jnp.int32, (chips * capacity, rows), 0)
        match = (place == index).astype(jnp.float32).astype(jnp.bfloat16)
        packed = jnp.dot(match, values, preferred_element_type=jnp.float32).astype(jnp.bfloat16)
        info = lax.dot_general(
            codes.astype(jnp.float32).astype(jnp.bfloat16),
            match,
            (((1,), (1,)), ((), ())),
            preferred_element_type=jnp.float32,
        ).astype(jnp.bfloat16)
        for chip, message in enumerate(message_refs):
            low = chip * capacity
            for part in range(width // LANES):
                message[pl.ds((part * CORES + source) * capacity, capacity), :] = packed[
                    low : low + capacity, part * LANES : (part + 1) * LANES
                ]
            piece = info[:, low : low + capacity]
            if capacity < LANES:
                piece = jnp.concatenate(
                    [piece, jnp.zeros((INFO_ROWS, LANES - capacity), jnp.bfloat16)], axis=1
                )
            start = width // LANES * CORES * capacity + source * INFO_ROWS
            message[pl.ds(start, INFO_ROWS), :] = piece


def norm_kernel(bank_ref, after_ref, norm_ref):
    values = bank_ref[...].astype(jnp.float32)
    square = jnp.sum(values * values, axis=2, keepdims=True)
    shape = values.shape[:2] + (LANES,)
    own_lane = lax.broadcasted_iota(jnp.int32, shape, 2) == lax.broadcasted_iota(
        jnp.int32, shape, 1
    )
    norm_ref[...] = jnp.sqrt(jnp.sum(jnp.where(own_lane, square, 0.0), axis=1) + epsilon)


def read_messages(message_refs, capacity, width):
    units, slots = [], []
    count = CORES * capacity
    for message in message_refs:
        values = jnp.concatenate(
            [
                message[pl.ds(part * count, count), :].astype(jnp.float32)
                for part in range(width // LANES)
            ],
            axis=1,
        )
        norm = jnp.sqrt(jnp.sum(values * values, axis=1, keepdims=True) + epsilon)
        units.append((values / norm).astype(jnp.bfloat16))
        for source in range(CORES):
            start = width // LANES * count + source * INFO_ROWS
            info = message[pl.ds(start, INFO_ROWS), :].astype(jnp.float32)
            slots.append((info[0:1, :capacity] - 1.0) * CODE_BASE + info[1:2, :capacity])
    return jnp.concatenate(units, axis=0), jnp.concatenate(slots, axis=1).astype(jnp.int32)


def cluster_onehot(slots, clusters):
    hit = lax.broadcasted_iota(jnp.int32, (clusters, slots.shape[1]), 0) == slots
    return hit.astype(jnp.float32).astype(jnp.bfloat16)


def early_sum_kernel(messages, capacity, *refs):
    message_refs, total_ref = refs[:messages], refs[-1]
    clusters, width = total_ref.shape
    units, slots = read_messages(message_refs, capacity, width)
    total_ref[...] = jnp.dot(
        cluster_onehot(slots, clusters), units, preferred_element_type=jnp.float32
    )


def late_sum_kernel(messages, capacity, *refs):
    message_refs, early_ref = refs[:messages], refs[messages]
    total_ref, sent_ref = refs[-2:]
    clusters, width = total_ref.shape
    units, slots = read_messages(message_refs, capacity, width)
    total = early_ref[...] + jnp.dot(
        cluster_onehot(slots, clusters), units, preferred_element_type=jnp.float32
    )
    total_ref[...] = total
    sent_ref[...] = total.astype(sent_ref.dtype)


def split_exactly(value):
    high = value.astype(jnp.bfloat16)
    rest = value - high.astype(jnp.float32)
    middle = rest.astype(jnp.bfloat16)
    low = (rest - middle.astype(jnp.float32)).astype(jnp.bfloat16)
    return high, middle, low


def score_kernel(messages, earlier, capacity, me_ref, bank_ref, norm_ref, members_ref, *refs):
    message_refs = refs[:messages]
    earlier_refs = refs[messages : messages + earlier]
    best_ref, unit_ref, slot_ref, picked_ref = refs[messages + earlier :]
    step = pl.program_id(0)
    block_clusters, depth, width = bank_ref.shape
    clusters = norm_ref.shape[0]

    @pl.when(step == 0)
    def _():
        units, slots = read_messages(message_refs, capacity, width)
        unit_ref[...] = units.T
        slot_ref[...] = slots
        picked_ref[...] = jnp.zeros_like(picked_ref)

    dots = jnp.dot(
        bank_ref[...].reshape(block_clusters * depth, width),
        unit_ref[...],
        preferred_element_type=jnp.float32,
    )
    wanted = slot_ref[...] - step * block_clusters
    picked = picked_ref[...]
    for cluster in range(block_clusters):
        picked = jnp.where(
            wanted == cluster, dots[cluster * depth : (cluster + 1) * depth, :], picked
        )
    picked_ref[...] = picked

    @pl.when(step == pl.num_programs(0) - 1)
    def _():
        onehot = cluster_onehot(slot_ref[...], clusters)
        terms = [
            lax.dot_general(
                term, onehot, (((0,), (0,)), ((), ())), preferred_element_type=jnp.float32
            )[:depth]
            for term in split_exactly(norm_ref[...])
        ]
        chosen_norm = terms[0] + terms[1] + terms[2]
        member_rows = jnp.broadcast_to(
            members_ref[...].astype(jnp.float32), (INFO_ROWS, clusters)
        ).astype(jnp.bfloat16)
        chosen_members = jnp.dot(member_rows, onehot, preferred_element_type=jnp.float32)[0:1]
        place = lax.broadcasted_iota(jnp.int32, picked_ref.shape, 0).astype(jnp.float32)
        cosine = jnp.where(place < chosen_members, picked_ref[...] / chosen_norm, -3.0)
        best = jnp.max(cosine, axis=0, keepdims=True)
        if not earlier:
            for number in range(CORES * messages):
                best_ref[pl.ds(number, 1), :] = best[
                    :, number * capacity : (number + 1) * capacity
                ]
            return
        offset = 0
        for group in earlier_refs:
            for number in range(group.shape[0]):
                best_ref[pl.ds(me_ref[0] ^ offset, 1), :] = group[pl.ds(number, 1), :]
                offset += 1
        for number in range(CORES * messages):
            best_ref[pl.ds(me_ref[0] ^ (offset + number), 1), :] = best[
                :, number * capacity : (number + 1) * capacity
            ]


def finish_kernel(stored_ref, own_ref, *refs):
    out_ref = refs[-1]
    total = stored_ref[...] + own_ref[...]
    for term in refs[:-1]:
        total = total + term[...].astype(jnp.float32)
    out_ref[...] = total / jnp.sqrt(jnp.sum(total * total, axis=1, keepdims=True) + epsilon)


def unpack_kernel(index_ref, best_ref, out_ref):
    owners, capacity = best_ref.shape
    rows = index_ref.shape[1]
    best = jnp.concatenate([best_ref[pl.ds(number, 1), :] for number in range(owners)], axis=1)
    row = lax.broadcasted_iota(jnp.int32, (INFO_ROWS, owners * capacity), 0)
    table = jnp.zeros(row.shape, jnp.float32)
    for number, term in enumerate(split_exactly(best)):
        table = jnp.where(row == number, term.astype(jnp.float32), table)
    place = lax.broadcasted_iota(jnp.int32, (owners * capacity, rows), 0)
    match = (place == index_ref[...]).astype(jnp.float32).astype(jnp.bfloat16)
    spread = jnp.dot(table.astype(jnp.bfloat16), match, preferred_element_type=jnp.float32)
    out_ref[...] = spread[0:1] + spread[1:2] + spread[2:3]


def exchange(value, axis, offset):
    size = lax.axis_size(axis)
    return lax.ppermute(value, axis, [(device, device ^ offset) for device in range(size)])


def body(arrivals, home_owner, cluster_slot, bank, members, centroid_sum):
    owners = lax.axis_size("own")
    parts = lax.axis_size("grp")
    rows, width = arrivals.shape
    clusters, depth = bank.shape[0], bank.shape[1]
    capacity = 2 * rows // owners
    chips = owners // CORES
    message_rows = (width // LANES * capacity + INFO_ROWS) * CORES
    own_index = lax.axis_index("own").astype(jnp.int32).reshape(1)
    smem = pl.BlockSpec(memory_space=pltpu.SMEM)
    anywhere = pl.BlockSpec(memory_space=pl.ANY)
    message = jax.ShapeDtypeStruct((message_rows, LANES), jnp.bfloat16)
    half, late = chips // 2, 3 * chips // 4
    block = min(clusters, 32)

    def whole(shape):
        return pl.BlockSpec(shape, lambda i: (0,) * len(shape))

    own_rows = (home_owner.reshape(1, rows), cluster_slot.reshape(1, rows), arrivals)
    other_rows = [exchange(value, "own", 1) for value in own_rows[::-1]][::-1]
    row_specs = [whole((1, rows)), whole((1, rows)), whole((rows, width))]
    return_index, *sent = pl.pallas_call(
        functools.partial(pack_kernel, owners, capacity),
        grid=(1,),
        out_shape=[jax.ShapeDtypeStruct((1, rows), jnp.int32)] + [message] * chips,
        in_specs=[smem] + row_specs * 2,
        out_specs=[whole((1, rows))] + [whole((message_rows, LANES))] * chips,
        compiler_params=params(),
        name="pack",
    )(own_index, *own_rows, *other_rows)
    got = [sent[0]] + [None] * (chips - 1)
    for chip in list(range(half, chips)) + list(range(half - 1, 0, -1)):
        got[chip] = exchange(sent[chip], "own", chip * CORES)

    bank_norm = pl.pallas_call(
        norm_kernel,
        grid=(clusters // block,),
        out_shape=jax.ShapeDtypeStruct((clusters, LANES), jnp.float32),
        in_specs=[pl.BlockSpec((block, depth, width), lambda i: (i, 0, 0)), anywhere],
        out_specs=pl.BlockSpec((block, LANES), lambda i: (i, 0)),
        compiler_params=params(),
        cost_estimate=pl.CostEstimate(
            flops=2 * clusters * depth * width,
            bytes_accessed=2 * clusters * depth * width,
            transcendentals=0,
        ),
        name="bank_norm",
    )(bank, return_index)

    member_row = members.reshape(1, clusters)

    def score(group, earlier):
        count = len(group)
        result_rows = owners if earlier else CORES * count
        return pl.pallas_call(
            functools.partial(score_kernel, count, len(earlier), capacity),
            grid=(clusters // block,),
            out_shape=jax.ShapeDtypeStruct((result_rows, capacity), jnp.float32),
            in_specs=[
                smem,
                pl.BlockSpec((block, depth, width), lambda i: (i, 0, 0)),
                whole((clusters, LANES)),
                whole((1, clusters)),
            ]
            + [whole((message_rows, LANES))] * count
            + [whole(value.shape) for value in earlier],
            out_specs=whole((result_rows, capacity)),
            scratch_shapes=[
                pltpu.VMEM((width, CORES * count * capacity), jnp.bfloat16),
                pltpu.VMEM((1, CORES * count * capacity), jnp.int32),
                pltpu.VMEM((depth, CORES * count * capacity), jnp.float32),
            ],
            compiler_params=params(),
            cost_estimate=pl.CostEstimate(
                flops=2 * clusters * depth * width * CORES * count * capacity,
                bytes_accessed=2 * clusters * depth * width,
                transcendentals=0,
            ),
            name="score",
        )(own_index, bank, bank_norm, member_row, *group, *earlier)

    first_best = score(got[:half], [])
    second_best = score(got[half:late], [])
    sums = jax.ShapeDtypeStruct((clusters, width), jnp.float32)
    early = pl.pallas_call(
        functools.partial(early_sum_kernel, half, capacity),
        out_shape=sums,
        in_specs=[whole_vmem()] * half + [anywhere],
        out_specs=whole_vmem(),
        compiler_params=small_params(),
        name="early_sum",
    )(*got[:half], first_best)
    own_sum, sent_sum = pl.pallas_call(
        functools.partial(late_sum_kernel, chips - half, capacity),
        out_shape=[sums, jax.ShapeDtypeStruct((clusters, width), jnp.bfloat16)],
        in_specs=[whole_vmem()] * (chips - half + 1),
        out_specs=[whole_vmem()] * 2,
        compiler_params=small_params(),
        name="late_sum",
    )(*got[half:], early)
    terms = [exchange(sent_sum, "grp", offset) for offset in range(1, parts)]
    best = score(got[late:], [first_best, second_best])
    returned = lax.all_to_all(best, "own", split_axis=0, concat_axis=0, tiled=True)
    centroids = pl.pallas_call(
        finish_kernel,
        out_shape=sums,
        in_specs=[whole_vmem()] * (parts + 1),
        out_specs=whole_vmem(),
        compiler_params=small_params(),
        name="finish",
    )(centroid_sum, own_sum, *terms)
    best_cosine = pl.pallas_call(
        unpack_kernel,
        out_shape=jax.ShapeDtypeStruct((1, rows), jnp.float32),
        in_specs=[whole_vmem()] * 2,
        out_specs=whole_vmem(),
        compiler_params=small_params(),
        name="unpack",
    )(return_index, returned).reshape(rows)
    return (best_cosine, centroids)


def solution(mesh):
    return jax.shard_map(
        body,
        mesh=mesh,
        in_specs=(
            P(("grp", "own"), None),
            P(("grp", "own"), None),
            P(("grp", "own")),
            P("own", None, None),
            P("own"),
            P("own", None),
        ),
        out_specs=(P(("grp", "own")), P("own", None)),
        check_vma=False,
    )
```

time: 70 us -> 67.9 us (0.970)
  Pallas kernels: 18.2 us -> 36.2 us
  starting transfers between devices: 27.8 us -> 10.1 us
  local copies, waits for them, and re-layouts: 12.6 us -> 2.42 us
  blocking collectives: 0 us -> 9.28 us
  other arithmetic: 5.26 us -> 0 us
  waiting for transfers between devices: 4.98 us -> 8.35 us
    pallas_call x9, Pallas kernels: 18.2 us -> 36.2 us  [the longest x3 25.2 us: score(): pl.pallas_call(functools.partial(score_kernel, count, len(earlier), capac...]
    ppermute x20 -> x9, starting transfers between devices: 27.8 us -> 10.1 us  [exchange(): lax.ppermute(value, axis, [(device, device ^ offset) for device in range(...]
    unnamed x16 -> x10, local copies, waits for them, and re-layouts: 12.6 us -> 2.42 us
    all_to_all x0 -> x1, blocking collectives: none -> 9.28 us  [body(): lax.all_to_all(best, 'own', split_axis=0, concat_axis=0, tiled=True)]
    reduce_sum x1 -> x0, other arithmetic: 5.23 us -> none  [body(): bank_norm = jnp.sqrt(jnp.sum(widened * widened, axis=2) + epsilon).T]
    ppermute x20 -> x9, waiting for transfers between devices: 4.98 us -> 8.35 us  [exchange(): lax.ppermute(value, axis, [(device, device ^ offset) for device in range(...]
  transfers between devices with their start and end apart: 20 -> 9, of which waited for: 3 -> 2; matrix products, arithmetic and copies ran while one was open for 8% -> 0% of each run, Pallas kernels for 23% -> 50%
where the time goes in v2:
time: 67.9 us; the launch traced here: 67.1 us
  Pallas kernels  36.2 us (53%)
  starting transfers between devices  10.1 us (15%)
  blocking collectives  9.28 us (14%)
  waiting for transfers between devices  8.35 us (12%)
  local copies, waits for them, and re-layouts  2.42 us (4%)
  between operations  0.74 us (1%)
    pallas_call x3, Pallas kernels, score(): pl.pallas_call(functools.partial(score_kernel, count, len(earlier), capac...  25.2 us
    ppermute x9, starting transfers between devices, exchange(): lax.ppermute(value, axis, [(device, device ^ offset) for device in range(...  10.1 us
    all_to_all x1, blocking collectives, body(): lax.all_to_all(best, 'own', split_axis=0, concat_axis=0, tiled=True)  9.28 us
    ppermute x9, waiting for transfers between devices, exchange(): lax.ppermute(value, axis, [(device, device ^ offset) for device in range(...  8.35 us
    pallas_call x1, Pallas kernels, body(): pl.pallas_call(norm_kernel, grid=(clusters // block,), out_shape=jax.Shap...  6.77 us
    unnamed x10, local copies, waits for them, and re-layouts  2.42 us
  transfers between devices with their start and end apart: 9, of which 2 were waited for; matrix products, arithmetic and copies ran while one was open for 0% of the time, Pallas kernels for 50%

profile of v2, /device:TPU:0, one launch (start us, length us, event | category | flops | bytes accessed | tf_op | source)
XLA Modules:
  0.0 67.1 jit_solution(6896836308909861821)
XLA Ops:
  0.6 0.5 collective-permute-start.2
  1.2 0.1 collective-permute-start
  1.2 0.4 collective-permute-start.1
  1.7 1.2 %collective-permute-done.refs_3_ = s32[1,512]{1,0:T(1,128)S(1)} collective-permute-done((s32[1,512]{1,0:T(1,128)}, s32[1,512]{1,0:T(1,128)S(1)}, u32[]{:S(2)}, u32[]{:S(2)}) %collective-permute-start) | collective-permute-done | bytes 2080 | tf_op jit(solution)/shard_map/ppermute | solution.py:237
  2.9 0.0 collective-permute-done.1.refs_4_
  2.9 0.0 collective-permute-done.2.refs_5_
  2.9 1.0 %copy-done = bf16[512,512]{1,0:T(8,128)(2,1)S(1)} copy-done((bf16[512,512]{1,0:T(8,128)(2,1)S(1)}, bf16[512,512]{1,0:T(8,128)(2,1)}, u32[]{:S(2)}) %copy-start) | copy-done | bytes 524312
  4.0 0.7 %copy-done.3 = s32[512,1]{0,1:T(1,128)S(1)} copy-done((s32[512,1]{0,1:T(1,128)S(1)}, s32[512,1]{0,1:T(1,128)}, u32[]{:S(2)}) %copy-start.3) | copy-done | bytes 2072
  4.6 0.7 %copy-done.4 = s32[512]{0:T(512)S(1)} copy-done((s32[512]{0:T(512)S(1)}, s32[512]{0:T(512)}, u32[]{:S(2)}) %copy-start.4) | copy-done | bytes 2072
  5.3 1.2 %pack.1 = (s32[1,512]{1,0:T(1,128)S(1)}, bf16[1056,128]{1,0:T(8,128)(2,1)S(1)}, bf16[1056,128]{1,0:T(8,128)(2,1)S(1)}, bf16[1056,128]{1,0:T(8,128)(2,1)S(1)}, bf16[1056,128]{1,0:T(8,128)(2,1)S(1)}) custom-call(s32[1]{0:T(128)} %bitcast.me_ref, s32[1,512]{1,0:T(1,128)S(1)} %bitcast.15, s32[1,512]{1,0:T(1,128)S(1)} %bitcast.17, bf16[512,512]{1,0:T(8,128)(2,1)S(1)} %copy-done, ...), custom_call_target="tpu_custom_call" | custom-call | tf_op jit(solution)/shard_map/pack/pallas_call | solution.py:261
  6.6 2.9 %collective-permute-start.4 = (bf16[1056,128]{1,0:T(8,128)(2,1)S(1)}, bf16[1056,128]{1,0:T(8,128)(2,1)S(1)}, u32[]{:S(2)}, u32[]{:S(2)}) collective-permute-start(bf16[1056,128]{1,0:T(8,128)(2,1)S(1)} %get-tuple-element.12), channel_id=1, source_target_pairs={{0,2},{1,3},{2,0},{3,1},{4,6},{5,7},{6,4},{7,5},{8,10},{9,11},{10,... | collective-permute-start | bytes 811016 | tf_op jit(solution)/shard_map/ppermute | solution.py:237
  9.5 2.5 %collective-permute-start.3 = (bf16[1056,128]{1,0:T(8,128)(2,1)S(1)}, bf16[1056,128]{1,0:T(8,128)(2,1)S(1)}, u32[]{:S(2)}, u32[]{:S(2)}) collective-permute-start(bf16[1056,128]{1,0:T(8,128)(2,1)S(1)} %get-tuple-element.10), channel_id=1, source_target_pairs={{0,6},{1,7},{2,4},{3,5},{4,2},{5,3},{6,0},{7,1},{8,14},{9,15},{10,... | collective-permute-start | bytes 811016 | tf_op jit(solution)/shard_map/ppermute | solution.py:237
  12.0 0.1 collective-permute-start.5
  12.1 6.8 %bank_norm.1.norm_ref = f32[256,128]{1,0:T(8,128)S(1)} custom-call(bf16[256,32,512]{2,1,0:T(8,128)(2,1)} %bank_ref.7, s32[1,512]{1,0:T(1,128)S(1)} %get-tuple-element.9.after_ref.index_ref), custom_call_target="tpu_custom_call" | custom-call | flops 8388608 | bytes 8388608 | tf_op jit(solution)/shard_map/bank_norm/pallas_call | solution.py:274
  18.9 0.0 collective-permute-done.4.refs_1_
  18.9 9.5 %score.3.refs_1_.refs_2_ = f32[4,128]{1,0:T(4,128)S(1)} custom-call(s32[1]{0:T(128)} %bitcast.me_ref, bf16[256,32,512]{2,1,0:T(8,128)(2,1)} %bank_ref.7, f32[256,128]{1,0:T(8,128)S(1)} %bank_norm.1.norm_ref, s32[1,256]{1,0:T(1,128)S(1)} %bitcast.11, bf16[1056,128]{1,0:T(8,128)(2,1)S(1)} %get-tuple-element.11.refs_0_, ...), custom_call_target="tpu_custom_call" | custom-call | flops 4294967296 | bytes 8388608 | tf_op jit(solution)/shard_map/score/pallas_call | solution.py:294
  28.4 0.5 early_sum.1.refs_2_
  28.9 0.0 collective-permute-done.3.refs_0_.refs_1_
  28.9 7.1 %collective-permute-done.5.refs_0_ = bf16[1056,128]{1,0:T(8,128)(2,1)S(1)} collective-permute-done((bf16[1056,128]{1,0:T(8,128)(2,1)S(1)}, bf16[1056,128]{1,0:T(8,128)(2,1)S(1)}, u32[]{:S(2)}, u32[]{:S(2)}) %collective-permute-start.5) | collective-permute-done | bytes 270368 | tf_op jit(solution)/shard_map/ppermute | solution.py:237
  36.0 0.5 late_sum.1
  36.5 0.0 copy-start.1
  36.5 1.6 %collective-permute-start.6 = (bf16[256,512]{1,0:T(8,128)(2,1)S(1)}, bf16[256,512]{1,0:T(8,128)(2,1)S(1)}, u32[]{:S(2)}, u32[]{:S(2)}) collective-permute-start(bf16[256,512]{1,0:T(8,128)(2,1)S(1)} %get-tuple-element.15), channel_id=1, source_target_pairs={{0,8},{8,0},{16,24},{24,16},{1,9},{9,1},{17,25},{25,17},{2,10},{10... | collective-permute-start | bytes 786440 | tf_op jit(solution)/shard_map/ppermute | solution.py:237
  38.1 1.5 %collective-permute-start.7 = (bf16[256,512]{1,0:T(8,128)(2,1)S(1)}, bf16[256,512]{1,0:T(8,128)(2,1)S(1)}, u32[]{:S(2)}, u32[]{:S(2)}) collective-permute-start(bf16[256,512]{1,0:T(8,128)(2,1)S(1)} %get-tuple-element.15), channel_id=1, source_target_pairs={{0,16},{8,24},{16,0},{24,8},{1,17},{9,25},{17,1},{25,9},{2,18},{10... | collective-permute-start | bytes 786440 | tf_op jit(solution)/shard_map/ppermute | solution.py:237
  39.6 0.5 collective-permute-start.8
  40.1 7.9 %score.4.refs_2_ = f32[2,128]{1,0:T(2,128)S(1)} custom-call(s32[1]{0:T(128)} %bitcast.me_ref, bf16[256,32,512]{2,1,0:T(8,128)(2,1)} %bank_ref.7, f32[256,128]{1,0:T(8,128)S(1)} %bank_norm.1.norm_ref, s32[1,256]{1,0:T(1,128)S(1)} %bitcast.12, bf16[1056,128]{1,0:T(8,128)(2,1)S(1)} %collective-permute-done.5.refs_0_), custom_call_target="tpu_custom_call" | custom-call | flops 2147483648 | bytes 8388608 | tf_op jit(solution)/shard_map/score/pallas_call | solution.py:294
  48.0 7.9 %score.5 = f32[8,128]{1,0:T(8,128)S(1)} custom-call(s32[1]{0:T(128)} %bitcast.me_ref, bf16[256,32,512]{2,1,0:T(8,128)(2,1)} %bank_ref.7, f32[256,128]{1,0:T(8,128)S(1)} %bank_norm.1.norm_ref, s32[1,256]{1,0:T(1,128)S(1)} %bitcast.13, bf16[1056,128]{1,0:T(8,128)(2,1)S(1)} %collective-permute-done.3.refs_0_.refs_1_, f32[4,128]{1,0:T(4,128)S(1)} %score.3.refs_1_.refs_2_, ...), custom_call_target="tpu_custom_call" | custom-call | flops 2147483648 | bytes 8388608 | tf_op jit(solution)/shard_map/score/pallas_call | solution.py:294
  55.9 9.3 %all_to_all.11 = f32[8,1,128]{2,1,0:T(1,128)S(1)} all-to-all(f32[8,1,128]{2,1,0:T(1,128)S(1)} %bitcast.9), channel_id=1, replica_groups=mesh['grp'=4,'own'=8] {'own'}, dimensions={0} | all-to-all | bytes 8192 | tf_op jit(solution)/shard_map/all_to_all | solution.py:342
  65.2 0.8 %unpack.1 = f32[1,512]{1,0:T(1,128)} custom-call(s32[1,512]{1,0:T(1,128)S(1)} %get-tuple-element.9.after_ref.index_ref, f32[8,128]{1,0:T(8,128)S(1)} %bitcast.10), custom_call_target="tpu_custom_call" | custom-call | tf_op jit(solution)/shard_map/unpack/pallas_call | solution.py:351
  66.0 0.0 collective-permute-done.6.refs_0_
  66.0 0.0 collective-permute-done.7.refs_1_
  66.0 0.0 collective-permute-done.8.refs_2_
  66.0 1.0 %finish.1 = f32[256,512]{1,0:T(8,128)} custom-call(f32[256,512]{1,0:T(8,128)S(1)} %copy-done.1, f32[256,512]{1,0:T(8,128)S(1)} %get-tuple-element.14.own_ref, bf16[256,512]{1,0:T(8,128)(2,1)S(1)} %collective-permute-done.6.refs_0_, bf16[256,512]{1,0:T(8,128)(2,1)S(1)} %collective-permute-done.7.refs_1_, bf16[256,512]{1,0:T(8,128)(2,1)S(1)} %collective-permute-done.8.refs_2_), custom_call_target="tpu_custom_call" | custom-call | tf_op jit(solution)/shard_map/finish/pallas_call | solution.py:343
  (6 shorter events, 0.0 us)
Async XLA Ops:
  0.6 18.3 %copy-start.2 = (s32[256]{0:T(256)S(1)}, s32[256]{0:T(256)}, u32[]{:S(2)}) copy-start(s32[256]{0:T(256)} %param.10) | copy-start | bytes 3076
  0.6 2.3 %collective-permute-start.2 = (bf16[512,512]{1,0:T(8,128)(2,1)}, bf16[512,512]{1,0:T(8,128)(2,1)S(1)}, u32[]{:S(2)}, u32[]{:S(2)}) collective-permute-start(bf16[512,512]{1,0:T(8,128)(2,1)} %refs_2_.1), channel_id=1, source_target_pairs={{0,1},{1,0},{2,3},{3,2},{4,5},{5,4},{6,7},{7,6},{8,9},{9,8},{10,11... | collective-permute-start | bytes 1572872 | tf_op jit(solution)/shard_map/ppermute | solution.py:237
  1.2 1.8 %collective-permute-start = (s32[1,512]{1,0:T(1,128)}, s32[1,512]{1,0:T(1,128)S(1)}, u32[]{:S(2)}, u32[]{:S(2)}) collective-permute-start(s32[1,512]{1,0:T(1,128)} %bitcast.14), channel_id=1, source_target_pairs={{0,1},{1,0},{2,3},{3,2},{4,5},{5,4},{6,7},{7,6},{8,9},{9,8},{10,11... | collective-permute-start | bytes 6152 | tf_op jit(solution)/shard_map/ppermute | solution.py:237
  1.2 1.7 %collective-permute-start.1 = (s32[1,512]{1,0:T(1,128)}, s32[1,512]{1,0:T(1,128)S(1)}, u32[]{:S(2)}, u32[]{:S(2)}) collective-permute-start(s32[1,512]{1,0:T(1,128)} %bitcast.16), channel_id=1, source_target_pairs={{0,1},{1,0},{2,3},{3,2},{4,5},{5,4},{6,7},{7,6},{8,9},{9,8},{10,11... | collective-permute-start | bytes 6152 | tf_op jit(solution)/shard_map/ppermute | solution.py:237
  2.9 1.0 %copy-start = (bf16[512,512]{1,0:T(8,128)(2,1)S(1)}, bf16[512,512]{1,0:T(8,128)(2,1)}, u32[]{:S(2)}) copy-start(bf16[512,512]{1,0:T(8,128)(2,1)} %refs_2_.1) | copy-start | bytes 1572868
  4.0 0.7 %copy-start.3 = (s32[512,1]{0,1:T(1,128)S(1)}, s32[512,1]{0,1:T(1,128)}, u32[]{:S(2)}) copy-start(s32[512,1]{0,1:T(1,128)} %param.7) | copy-start | bytes 6148
  4.6 0.7 %copy-start.4 = (s32[512]{0:T(512)S(1)}, s32[512]{0:T(512)}, u32[]{:S(2)}) copy-start(s32[512]{0:T(512)} %param.8) | copy-start | bytes 6148
  6.6 12.3 %collective-permute-start.4 = (bf16[1056,128]{1,0:T(8,128)(2,1)S(1)}, bf16[1056,128]{1,0:T(8,128)(2,1)S(1)}, u32[]{:S(2)}, u32[]{:S(2)}) collective-permute-start(bf16[1056,128]{1,0:T(8,128)(2,1)S(1)} %get-tuple-element.12), channel_id=1, source_target_pairs={{0,2},{1,3},{2,0},{3,1},{4,6},{5,7},{6,4},{7,5},{8,10},{9,11},{10,... | collective-permute-start | bytes 811016 | tf_op jit(solution)/shard_map/ppermute | solution.py:237
  9.5 19.4 %collective-permute-start.3 = (bf16[1056,128]{1,0:T(8,128)(2,1)S(1)}, bf16[1056,128]{1,0:T(8,128)(2,1)S(1)}, u32[]{:S(2)}, u32[]{:S(2)}) collective-permute-start(bf16[1056,128]{1,0:T(8,128)(2,1)S(1)} %get-tuple-element.10), channel_id=1, source_target_pairs={{0,6},{1,7},{2,4},{3,5},{4,2},{5,3},{6,0},{7,1},{8,14},{9,15},{10,... | collective-permute-start | bytes 811016 | tf_op jit(solution)/shard_map/ppermute | solution.py:237
  12.0 24.0 %collective-permute-start.5 = (bf16[1056,128]{1,0:T(8,128)(2,1)S(1)}, bf16[1056,128]{1,0:T(8,128)(2,1)S(1)}, u32[]{:S(2)}, u32[]{:S(2)}) collective-permute-start(bf16[1056,128]{1,0:T(8,128)(2,1)S(1)} %get-tuple-element.13), channel_id=1, source_target_pairs={{0,4},{1,5},{2,6},{3,7},{4,0},{5,1},{6,2},{7,3},{8,12},{9,13},{10,... | collective-permute-start | bytes 811016 | tf_op jit(solution)/shard_map/ppermute | solution.py:237
  36.5 29.5 %copy-start.1 = (f32[256,512]{1,0:T(8,128)S(1)}, f32[256,512]{1,0:T(8,128)}, u32[]{:S(2)}) copy-start(f32[256,512]{1,0:T(8,128)} %stored_ref.1) | copy-start | bytes 1572868
  36.5 29.5 %collective-permute-start.6 = (bf16[256,512]{1,0:T(8,128)(2,1)S(1)}, bf16[256,512]{1,0:T(8,128)(2,1)S(1)}, u32[]{:S(2)}, u32[]{:S(2)}) collective-permute-start(bf16[256,512]{1,0:T(8,128)(2,1)S(1)} %get-tuple-element.15), channel_id=1, source_target_pairs={{0,8},{8,0},{16,24},{24,16},{1,9},{9,1},{17,25},{25,17},{2,10},{10... | collective-permute-start | bytes 786440 | tf_op jit(solution)/shard_map/ppermute | solution.py:237
  38.1 27.9 %collective-permute-start.7 = (bf16[256,512]{1,0:T(8,128)(2,1)S(1)}, bf16[256,512]{1,0:T(8,128)(2,1)S(1)}, u32[]{:S(2)}, u32[]{:S(2)}) collective-permute-start(bf16[256,512]{1,0:T(8,128)(2,1)S(1)} %get-tuple-element.15), channel_id=1, source_target_pairs={{0,16},{8,24},{16,0},{24,8},{1,17},{9,25},{17,1},{25,9},{2,18},{10... | collective-permute-start | bytes 786440 | tf_op jit(solution)/shard_map/ppermute | solution.py:237
  39.6 26.4 %collective-permute-start.8 = (bf16[256,512]{1,0:T(8,128)(2,1)S(1)}, bf16[256,512]{1,0:T(8,128)(2,1)S(1)}, u32[]{:S(2)}, u32[]{:S(2)}) collective-permute-start(bf16[256,512]{1,0:T(8,128)(2,1)S(1)} %get-tuple-element.15), channel_id=1, source_target_pairs={{0,24},{8,16},{16,8},{24,0},{1,25},{9,17},{17,9},{25,1},{2,26},{10... | collective-permute-start | bytes 786440 | tf_op jit(solution)/shard_map/ppermute | solution.py:237

commit v3 on v0

v3 whole, which is shorter than its diff:
```python
import functools

import jax
import jax.numpy as jnp
from jax import lax
from jax.experimental import pallas as pl
from jax.experimental.pallas import tpu as pltpu
from jax.sharding import PartitionSpec as P

epsilon = 1e-06
LANES = 128
INFO_ROWS = 16
CODE_BASE = 128
CORES = 2
SMALL_VMEM = 32 * 1024 * 1024


def whole_vmem():
    return pl.BlockSpec(memory_space=pltpu.VMEM)


def small_params():
    return pltpu.CompilerParams(vmem_limit_bytes=SMALL_VMEM)


def place_rows(owners, owner):
    rows = owner.shape[1]
    hit = lax.broadcasted_iota(jnp.int32, (owners, rows), 0) == owner
    earlier_mask = (
        lax.broadcasted_iota(jnp.int32, (rows, rows), 0)
        < lax.broadcasted_iota(jnp.int32, (rows, rows), 1)
    )
    earlier = jnp.dot(
        hit.astype(jnp.float32).astype(jnp.bfloat16),
        earlier_mask.astype(jnp.float32).astype(jnp.bfloat16),
        preferred_element_type=jnp.float32,
    )
    return jnp.sum(jnp.where(hit, earlier, 0.0), axis=0, keepdims=True).astype(jnp.int32)


def write_messages(source, capacity, index, slot, values, message_refs):
    rows, width = values.shape
    code_row = lax.broadcasted_iota(jnp.int32, (INFO_ROWS, rows), 0)
    codes = jnp.where(
        code_row == 0,
        slot // CODE_BASE + 1,
        jnp.where(code_row == 1, slot % CODE_BASE, 0),
    )
    place = lax.broadcasted_iota(jnp.int32, (len(message_refs) * capacity, rows), 0)
    match = (place == index).astype(jnp.float32).astype(jnp.bfloat16)
    packed = jnp.dot(match, values, preferred_element_type=jnp.float32).astype(jnp.bfloat16)
    info = lax.dot_general(
        codes.astype(jnp.float32).astype(jnp.bfloat16),
        match,
        (((1,), (1,)), ((), ())),
        preferred_element_type=jnp.float32,
    ).astype(jnp.bfloat16)
    for chip, message in enumerate(message_refs):
        low = chip * capacity
        for part in range(width // LANES):
            message[pl.ds((part * CORES + source) * capacity, capacity), :] = packed[
                low : low + capacity, part * LANES : (part + 1) * LANES
            ]
        piece = info[:, low : low + capacity]
        if capacity < LANES:
            piece = jnp.concatenate(
                [piece, jnp.zeros((INFO_ROWS, LANES - capacity), jnp.bfloat16)], axis=1
            )
        start = width // LANES * CORES * capacity + source * INFO_ROWS
        message[pl.ds(start, INFO_ROWS), :] = piece


def pack_kernel(owners, capacity, me_ref, *refs):
    own, other, return_ref, message_refs = refs[0:3], refs[3:6], refs[6], refs[7:-4]
    held, semaphore = refs[-4:-1], refs[-1]
    copies = [
        pltpu.make_async_copy(source, target, semaphore.at[number])
        for number, (source, target) in enumerate(zip(own, held))
    ]
    for copy in copies:
        copy.start()
    for copy in copies:
        copy.wait()
    for source, (owner_ref, slot_ref, rows_ref) in enumerate((held, other)):
        owner = owner_ref[...]
        placed = place_rows(owners, owner)
        if source == 0:
            return_ref[...] = owner * capacity + placed
        peer = owner ^ me_ref[0]
        index = jnp.where(peer % CORES == 0, peer // CORES * capacity + placed, -1)
        write_messages(source, capacity, index, slot_ref[...], rows_ref[...], message_refs)


def load_kernel(blocks, bank_ref, after_ref, held_ref, norm_ref, semaphore):
    clusters, depth, width = held_ref.shape
    block = clusters // blocks
    copies = []
    for number in range(blocks):
        part = pl.ds(number * block, block)
        copies.append(
            pltpu.make_async_copy(bank_ref.at[part], held_ref.at[part], semaphore.at[number])
        )
        copies[-1].start()
    shape = (block, depth, LANES)
    own_lane = lax.broadcasted_iota(jnp.int32, shape, 2) == lax.broadcasted_iota(
        jnp.int32, shape, 1
    )
    for number in range(blocks):
        copies[number].wait()
        part = pl.ds(number * block, block)
        values = held_ref[part].astype(jnp.float32)
        square = jnp.sum(values * values, axis=2, keepdims=True)
        norm_ref[part, :] = jnp.sqrt(jnp.sum(jnp.where(own_lane, square, 0.0), axis=1) + epsilon)


def read_messages(message_refs, capacity, width):
    units, slots = [], []
    count = CORES * capacity
    for message in message_refs:
        values = jnp.concatenate(
            [
                message[pl.ds(part * count, count), :].astype(jnp.float32)
                for part in range(width // LANES)
            ],
            axis=1,
        )
        norm = jnp.sqrt(jnp.sum(values * values, axis=1, keepdims=True) + epsilon)
        units.append((values / norm).astype(jnp.bfloat16))
        for source in range(CORES):
            start = width // LANES * count + source * INFO_ROWS
            info = message[pl.ds(start, INFO_ROWS), :].astype(jnp.float32)
            slots.append((info[0:1, :capacity] - 1.0) * CODE_BASE + info[1:2, :capacity])
    return jnp.concatenate(units, axis=0), jnp.concatenate(slots, axis=1).astype(jnp.int32)


def cluster_onehot(slots, clusters):
    hit = lax.broadcasted_iota(jnp.int32, (clusters, slots.shape[1]), 0) == slots
    return hit.astype(jnp.float32).astype(jnp.bfloat16)


def early_sum_kernel(messages, capacity, *refs):
    message_refs, total_ref = refs[:messages], refs[-1]
    clusters, width = total_ref.shape
    units, slots = read_messages(message_refs, capacity, width)
    total_ref[...] = jnp.dot(
        cluster_onehot(slots, clusters), units, preferred_element_type=jnp.float32
    )


def late_sum_kernel(messages, capacity, *refs):
    message_refs, early_ref = refs[:messages], refs[messages]
    total_ref, sent_ref = refs[-2:]
    clusters, width = total_ref.shape
    units, slots = read_messages(message_refs, capacity, width)
    total = early_ref[...] + jnp.dot(
        cluster_onehot(slots, clusters), units, preferred_element_type=jnp.float32
    )
    total_ref[...] = total
    sent_ref[...] = total.astype(sent_ref.dtype)


def split_exactly(value):
    high = value.astype(jnp.bfloat16)
    rest = value - high.astype(jnp.float32)
    middle = rest.astype(jnp.bfloat16)
    low = (rest - middle.astype(jnp.float32)).astype(jnp.bfloat16)
    return high, middle, low


def score_kernel(
    messages, places, capacity, block, me_ref, bank_ref, norm_ref, members_ref, *refs
):
    message_refs, earlier_refs, best_ref = refs[:messages], refs[messages:-1], refs[-1]
    clusters, depth, width = bank_ref.shape
    units, slots = read_messages(message_refs, capacity, width)
    columns = units.T

    def add_block(number, picked):
        first = number * block
        dots = jnp.dot(
            bank_ref[pl.ds(first, block)].reshape(block * depth, width),
            columns,
            preferred_element_type=jnp.float32,
        )
        wanted = slots - first
        for cluster in range(block):
            picked = jnp.where(
                wanted == cluster, dots[cluster * depth : (cluster + 1) * depth, :], picked
            )
        return picked

    picked = lax.fori_loop(
        0, clusters // block, add_block, jnp.zeros((depth, slots.shape[1]), jnp.float32)
    )
    onehot = cluster_onehot(slots, clusters)
    terms = [
        lax.dot_general(
            term, onehot, (((0,), (0,)), ((), ())), preferred_element_type=jnp.float32
        )[:depth]
        for term in split_exactly(norm_ref[...])
    ]
    chosen_norm = terms[0] + terms[1] + terms[2]
    member_rows = jnp.broadcast_to(
        members_ref[...].astype(jnp.float32), (INFO_ROWS, clusters)
    ).astype(jnp.bfloat16)
    chosen_members = jnp.dot(member_rows, onehot, preferred_element_type=jnp.float32)[0:1]
    place = lax.broadcasted_iota(jnp.int32, picked.shape, 0).astype(jnp.float32)
    cosine = jnp.where(place < chosen_members, picked / chosen_norm, -3.0)
    best = jnp.max(cosine, axis=0, keepdims=True)
    results = [
        best[:, number * capacity : (number + 1) * capacity] for number in range(CORES * messages)
    ]
    if not places:
        for number, value in enumerate(results):
            best_ref[pl.ds(number, 1), :] = value
        return
    for group in reversed(earlier_refs):
        results = [group[pl.ds(number, 1), :] for number in range(group.shape[0])] + results
    for chip, place in enumerate(places):
        for source in range(CORES):
            offset = place * CORES + source
            best_ref[pl.ds(me_ref[0] ^ offset, 1), :] = results[chip * CORES + source]


def finish_kernel(stored_ref, own_ref, *refs):
    out_ref = refs[-1]
    total = stored_ref[...] + own_ref[...]
    for term in refs[:-1]:
        total = total + term[...].astype(jnp.float32)
    out_ref[...] = total / jnp.sqrt(jnp.sum(total * total, axis=1, keepdims=True) + epsilon)


def unpack_kernel(index_ref, best_ref, out_ref):
    owners, capacity = best_ref.shape
    rows = index_ref.shape[1]
    best = jnp.concatenate([best_ref[pl.ds(number, 1), :] for number in range(owners)], axis=1)
    row = lax.broadcasted_iota(jnp.int32, (INFO_ROWS, owners * capacity), 0)
    table = jnp.zeros(row.shape, jnp.float32)
    for number, term in enumerate(split_exactly(best)):
        table = jnp.where(row == number, term.astype(jnp.float32), table)
    place = lax.broadcasted_iota(jnp.int32, (owners * capacity, rows), 0)
    match = (place == index_ref[...]).astype(jnp.float32).astype(jnp.bfloat16)
    spread = jnp.dot(table.astype(jnp.bfloat16), match, preferred_element_type=jnp.float32)
    out_ref[...] = spread[0:1] + spread[1:2] + spread[2:3]


def in_hbm(value):
    return pltpu.with_memory_space_constraint(value, pltpu.HBM)


def exchange(value, axis, offset):
    size = lax.axis_size(axis)
    return lax.ppermute(value, axis, [(device, device ^ offset) for device in range(size)])


def body(arrivals, home_owner, cluster_slot, bank, members, centroid_sum):
    owners = lax.axis_size("own")
    parts = lax.axis_size("grp")
    rows, width = arrivals.shape
    clusters, depth = bank.shape[0], bank.shape[1]
    capacity = 2 * rows // owners
    chips = owners // CORES
    message_rows = (width // LANES * capacity + INFO_ROWS) * CORES
    own_index = lax.axis_index("own").astype(jnp.int32).reshape(1)
    smem = pl.BlockSpec(memory_space=pltpu.SMEM)
    anywhere = pl.BlockSpec(memory_space=pl.ANY)
    message = jax.ShapeDtypeStruct((message_rows, LANES), jnp.bfloat16)
    quarter = chips // 4
    order = [
        list(range(first * quarter, (first + 1) * quarter)) for first in (0, 2, 1, 3)
    ]
    block = min(clusters, 32)

    def vmem_call(kernel, name, out_shape, operands, in_specs=None, scratch_shapes=()):
        out_specs = jax.tree.map(lambda _: whole_vmem(), out_shape)
        return pl.pallas_call(
            kernel,
            out_shape=out_shape,
            in_specs=in_specs or [whole_vmem()] * len(operands),
            out_specs=out_specs,
            scratch_shapes=scratch_shapes,
            compiler_params=small_params(),
            name=name,
        )(*operands)

    own_rows = (home_owner.reshape(1, rows), cluster_slot.reshape(1, rows), arrivals)
    other_rows = [exchange(value, "own", 1) for value in own_rows[::-1]][::-1]
    row = jax.ShapeDtypeStruct((1, rows), jnp.int32)
    return_index, *sent = vmem_call(
        functools.partial(pack_kernel, owners, capacity),
        "pack",
        [row] + [message] * chips,
        [own_index, *[in_hbm(value) for value in own_rows], *other_rows],
        [smem] + [anywhere] * 3 + [whole_vmem()] * 3,
        [
            pltpu.VMEM((1, rows), jnp.int32),
            pltpu.VMEM((1, rows), jnp.int32),
            pltpu.VMEM((rows, width), arrivals.dtype),
            pltpu.SemaphoreType.DMA((3,)),
        ],
    )
    got = [sent[0]] + [exchange(sent[chip], "own", chip * CORES) for chip in range(1, chips)]

    blocks = 8
    held_bank, bank_norm = vmem_call(
        functools.partial(load_kernel, blocks),
        "bank_load",
        [
            pltpu.VMEM(bank.shape, bank.dtype),
            jax.ShapeDtypeStruct((clusters, LANES), jnp.float32),
        ],
        [in_hbm(bank), return_index],
        [anywhere, anywhere],
        [pltpu.SemaphoreType.DMA((blocks,))],
    )
    held_bank = pltpu.with_memory_space_constraint(held_bank, pltpu.VMEM)
    member_row = members.reshape(1, clusters)

    results = []
    sums = jax.ShapeDtypeStruct((clusters, width), jnp.float32)

    def score(chosen):
        last = chosen is order[-1]
        places = sum(order, []) if last else []
        group = [got[chip] for chip in chosen]
        before = results if last else results[-1:]
        operands = [own_index, held_bank, bank_norm, member_row, *group, *before]
        specs = [smem] + [whole_vmem()] * (3 + len(group))
        return vmem_call(
            functools.partial(score_kernel, len(group), places, capacity, block),
            "score",
            jax.ShapeDtypeStruct(
                (owners if last else CORES * len(group), capacity), jnp.float32
            ),
            operands,
            specs + [whole_vmem() if last else anywhere] * len(before),
        )

    for chosen in order[:-1]:
        results.append(score(chosen))
    early_messages = [got[chip] for chip in sum(order[:-1], [])]
    early = vmem_call(
        functools.partial(early_sum_kernel, len(early_messages), capacity),
        "early_sum",
        sums,
        [*early_messages, results[-1]],
        [whole_vmem()] * len(early_messages) + [anywhere],
    )
    late_messages = [got[chip] for chip in order[-1]]
    own_sum, sent_sum = vmem_call(
        functools.partial(late_sum_kernel, len(late_messages), capacity),
        "late_sum",
        [sums, jax.ShapeDtypeStruct((clusters, width), jnp.bfloat16)],
        [*late_messages, early],
    )
    terms = [exchange(sent_sum, "grp", offset) for offset in range(1, parts)]
    best = score(order[-1])
    returned = lax.all_to_all(best, "own", split_axis=0, concat_axis=0, tiled=True)
    best_cosine = vmem_call(unpack_kernel, "unpack", jax.ShapeDtypeStruct((1, rows), jnp.float32), [return_index, returned])
    centroids = vmem_call(finish_kernel, "finish", sums, [centroid_sum, own_sum, *terms])
    return (best_cosine.reshape(rows), centroids)


def solution(mesh):
    return jax.shard_map(
        body,
        mesh=mesh,
        in_specs=(
            P(("grp", "own"), None),
            P(("grp", "own"), None),
            P(("grp", "own")),
            P("own", None, None),
            P("own"),
            P("own", None),
        ),
        out_specs=(P(("grp", "own")), P("own", None)),
        check_vma=False,
    )
```

time: 107 us -> 53 us (0.50)
  matrix products: 29 us -> 0 us
  waiting for transfers between devices: 31.5 us -> 4.93 us
  Pallas kernels: 0 us -> 25.9 us
  between operations: 14.1 us -> 0.75 us
  other arithmetic: 13 us -> 0 us
  blocking collectives: 7.92 us -> 10.7 us
    dot_general x7 -> x0, matrix products: 29 us -> none  [the longest x4 23.9 us: score_tile(): lax.dot_general(query, bank_flat, (((1,), (1,)), ((), ())), preferred_ele...]
    pallas_call x0 -> x10, Pallas kernels: none -> 25.9 us  [vmem_call(): pl.pallas_call(kernel, out_shape=out_shape, in_specs=in_specs or [whole_v...]
    all_to_all x2 -> x0, waiting for transfers between devices: 20.2 us -> none  [the longest x1 18.8 us: body(): lax.all_to_all(send_rows, 'own', split_axis=0, concat_axis=0, tiled=True)]
    psum x1 -> x0, waiting for transfers between devices: 11.3 us -> none  [body(): summed = lax.psum(partial_value, 'grp')]
    ppermute x0 -> x9, starting transfers between devices: none -> 10.5 us  [exchange(): lax.ppermute(value, axis, [(device, device ^ offset) for device in range(...]
    all_to_all x2 -> x0, starting transfers between devices: 10 us -> none  [the longest x1 6.33 us: body(): lax.all_to_all(send_slot, 'own', split_axis=0, concat_axis=0, tiled=True)]
    dot_general x1 -> x0, other arithmetic: 5.11 us -> none  [body(): jnp.einsum('rd,rd->r', bank_flat, bank_flat, preferred_element_type=jnp.f...]
    reduce_sum x5 -> x0, other arithmetic: 5 us -> none  [the longest x1 1.4 us: body(): column_members = jnp.sum(member_hit * members[:, None], axis=0)]
  transfers between devices with their start and end apart: 3 -> 9, of which waited for: 3 -> 2; matrix products, arithmetic and copies ran while one was open for 35% -> 0% of each run, Pallas kernels for 0% -> 42%
where the time goes in v3:
time: 53 us; the launch traced here: 52.8 us
  Pallas kernels  25.9 us (49%)
  blocking collectives  10.7 us (20%)
  starting transfers between devices  10.5 us (20%)
  waiting for transfers between devices  4.93 us (9%)
  between operations  0.75 us (1%)
    pallas_call x10, Pallas kernels, vmem_call(): pl.pallas_call(kernel, out_shape=out_shape, in_specs=in_specs or [whole_v...  25.9 us
    all_to_all x1, blocking collectives, body(): lax.all_to_all(best, 'own', split_axis=0, concat_axis=0, tiled=True)  10.7 us
    ppermute x9, starting transfers between devices, exchange(): lax.ppermute(value, axis, [(device, device ^ offset) for device in range(...  10.5 us
    ppermute x9, waiting for transfers between devices, exchange(): lax.ppermute(value, axis, [(device, device ^ offset) for device in range(...  4.93 us
  transfers between devices with their start and end apart: 9, of which 2 were waited for; matrix products, arithmetic and copies ran while one was open for 0% of the time, Pallas kernels for 42%

profile of v3, /device:TPU:0, one launch (start us, length us, event | category | flops | bytes accessed | tf_op | source)
XLA Modules:
  0.0 52.8 jit_solution(15010795214028289583)
XLA Ops:
  0.6 0.0 copy-start.1
  0.6 0.5 collective-permute-start.2
  1.2 0.1 collective-permute-start
  1.2 0.4 collective-permute-start.1
  1.7 1.2 %collective-permute-done.refs_3_ = s32[1,512]{1,0:T(1,128)S(1)} collective-permute-done((s32[1,512]{1,0:T(1,128)}, s32[1,512]{1,0:T(1,128)S(1)}, u32[]{:S(2)}, u32[]{:S(2)}) %collective-permute-start) | collective-permute-done | bytes 2080 | tf_op jit(solution)/shard_map/ppermute | solution.py:253
  2.9 0.0 collective-permute-done.1.refs_4_
  2.9 0.0 collective-permute-done.2.refs_5_
  2.9 2.4 %pack.1 = (s32[1,512]{1,0:T(1,128)S(1)}, bf16[1056,128]{1,0:T(8,128)(2,1)S(1)}, bf16[1056,128]{1,0:T(8,128)(2,1)S(1)}, bf16[1056,128]{1,0:T(8,128)(2,1)S(1)}, bf16[1056,128]{1,0:T(8,128)(2,1)S(1)}) custom-call(s32[1]{0:T(128)} %bitcast.me_ref, s32[1,512]{1,0:T(1,128)} %bitcast.16, s32[1,512]{1,0:T(1,128)} %bitcast.18, bf16[512,512]{1,0:T(8,128)(2,1)} %refs_2_.1, ...), custom_call_target="tpu_custom_call" | custom-call | tf_op jit(solution)/shard_map/pack/pallas_call | solution.py:276
  5.3 4.0 %collective-permute-start.4 = (bf16[1056,128]{1,0:T(8,128)(2,1)S(1)}, bf16[1056,128]{1,0:T(8,128)(2,1)S(1)}, u32[]{:S(2)}, u32[]{:S(2)}) collective-permute-start(bf16[1056,128]{1,0:T(8,128)(2,1)S(1)} %get-tuple-element.16), channel_id=1, source_target_pairs={{0,4},{1,5},{2,6},{3,7},{4,0},{5,1},{6,2},{7,3},{8,12},{9,13},{10,... | collective-permute-start | bytes 811016 | tf_op jit(solution)/shard_map/ppermute | solution.py:253
  9.3 1.6 %collective-permute-start.5 = (bf16[1056,128]{1,0:T(8,128)(2,1)S(1)}, bf16[1056,128]{1,0:T(8,128)(2,1)S(1)}, u32[]{:S(2)}, u32[]{:S(2)}) collective-permute-start(bf16[1056,128]{1,0:T(8,128)(2,1)S(1)} %get-tuple-element.17), channel_id=1, source_target_pairs={{0,2},{1,3},{2,0},{3,1},{4,6},{5,7},{6,4},{7,5},{8,10},{9,11},{10,... | collective-permute-start | bytes 811016 | tf_op jit(solution)/shard_map/ppermute | solution.py:253
  10.9 0.0 collective-permute-start.3
  10.9 3.8 %bank_load.1 = (bf16[256,32,512]{2,1,0:T(8,128)(2,1)S(1)}, f32[256,128]{1,0:T(8,128)S(1)}) custom-call(bf16[256,32,512]{2,1,0:T(8,128)(2,1)} %bank_ref.1, s32[1,512]{1,0:T(1,128)S(1)} %get-tuple-element.11.after_ref.index_ref), custom_call_target="tpu_custom_call" | custom-call | tf_op jit(solution)/shard_map/bank_load/pallas_call | solution.py:276
  14.7 0.0 copy-done.1
  14.7 4.2 %score.4.refs_1_ = f32[2,128]{1,0:T(2,128)S(1)} custom-call(s32[1]{0:T(128)} %bitcast.me_ref, bf16[256,32,512]{2,1,0:T(8,128)(2,1)S(1)} %get-tuple-element.12.bank_ref, f32[256,128]{1,0:T(8,128)S(1)} %get-tuple-element.13.norm_ref, s32[1,256]{1,0:T(1,128)S(1)} %bitcast.9, bf16[1056,128]{1,0:T(8,128)(2,1)S(1)} %get-tuple-element.15.refs_0_), custom_call_target="tpu_custom_call" | custom-call | tf_op jit(solution)/shard_map/score/pallas_call | solution.py:276
  18.9 3.7 %collective-permute-done.4.refs_0_.refs_1_ = bf16[1056,128]{1,0:T(8,128)(2,1)S(1)} collective-permute-done((bf16[1056,128]{1,0:T(8,128)(2,1)S(1)}, bf16[1056,128]{1,0:T(8,128)(2,1)S(1)}, u32[]{:S(2)}, u32[]{:S(2)}) %collective-permute-start.4) | collective-permute-done | bytes 270368 | tf_op jit(solution)/shard_map/ppermute | solution.py:253
  22.6 4.2 %score.5.refs_1_.refs_2_ = f32[2,128]{1,0:T(2,128)S(1)} custom-call(s32[1]{0:T(128)} %bitcast.me_ref, bf16[256,32,512]{2,1,0:T(8,128)(2,1)S(1)} %get-tuple-element.12.bank_ref, f32[256,128]{1,0:T(8,128)S(1)} %get-tuple-element.13.norm_ref, s32[1,256]{1,0:T(1,128)S(1)} %bitcast.10, bf16[1056,128]{1,0:T(8,128)(2,1)S(1)} %collective-permute-done.4.refs_0_.refs_1_, ...), custom_call_target="tpu_custom_call" | custom-call | tf_op jit(solution)/shard_map/score/pallas_call | solution.py:276
  26.8 0.0 copy-start
  26.8 0.0 collective-permute-done.5.refs_0_.refs_2_
  26.8 4.2 %score.6.refs_3_ = f32[2,128]{1,0:T(2,128)S(1)} custom-call(s32[1]{0:T(128)} %bitcast.me_ref, bf16[256,32,512]{2,1,0:T(8,128)(2,1)S(1)} %get-tuple-element.12.bank_ref, f32[256,128]{1,0:T(8,128)S(1)} %get-tuple-element.13.norm_ref, s32[1,256]{1,0:T(1,128)S(1)} %bitcast.11, bf16[1056,128]{1,0:T(8,128)(2,1)S(1)} %collective-permute-done.5.refs_0_.refs_2_, ...), custom_call_target="tpu_custom_call" | custom-call | tf_op jit(solution)/shard_map/score/pallas_call | solution.py:276
  31.0 0.6 %early_sum.1.refs_1_ = f32[256,512]{1,0:T(8,128)S(1)} custom-call(bf16[1056,128]{1,0:T(8,128)(2,1)S(1)} %get-tuple-element.15.refs_0_, bf16[1056,128]{1,0:T(8,128)(2,1)S(1)} %collective-permute-done.4.refs_0_.refs_1_, bf16[1056,128]{1,0:T(8,128)(2,1)S(1)} %collective-permute-done.5.refs_0_.refs_2_, f32[2,128]{1,0:T(2,128)S(1)} %score.6.refs_3_), custom_call_target="tpu_custom_call" | custom-call | tf_op jit(solution)/shard_map/early_sum/pallas_call | solution.py:276
  31.7 0.0 collective-permute-done.3.refs_0_
  31.7 0.4 late_sum.1
  32.1 3.3 %collective-permute-start.8 = (bf16[256,512]{1,0:T(8,128)(2,1)S(1)}, bf16[256,512]{1,0:T(8,128)(2,1)S(1)}, u32[]{:S(2)}, u32[]{:S(2)}) collective-permute-start(bf16[256,512]{1,0:T(8,128)(2,1)S(1)} %get-tuple-element.19), channel_id=1, source_target_pairs={{0,24},{8,16},{16,8},{24,0},{1,25},{9,17},{17,9},{25,1},{2,26},{10... | collective-permute-start | bytes 786440 | tf_op jit(solution)/shard_map/ppermute | solution.py:253
  35.3 0.5 collective-permute-start.7
  35.8 0.1 collective-permute-start.6
  36.0 4.2 %score.7 = f32[8,128]{1,0:T(8,128)S(1)} custom-call(s32[1]{0:T(128)} %bitcast.me_ref, bf16[256,32,512]{2,1,0:T(8,128)(2,1)S(1)} %get-tuple-element.12.bank_ref, f32[256,128]{1,0:T(8,128)S(1)} %get-tuple-element.13.norm_ref, s32[1,256]{1,0:T(1,128)S(1)} %bitcast.12, bf16[1056,128]{1,0:T(8,128)(2,1)S(1)} %collective-permute-done.3.refs_0_, ...), custom_call_target="tpu_custom_call" | custom-call | tf_op jit(solution)/shard_map/score/pallas_call | solution.py:276
  40.2 10.7 %all_to_all.11 = f32[8,1,128]{2,1,0:T(1,128)S(1)} all-to-all(f32[8,1,128]{2,1,0:T(1,128)S(1)} %bitcast.13), channel_id=1, replica_groups=mesh['grp'=4,'own'=8] {'own'}, dimensions={0} | all-to-all | bytes 8192 | tf_op jit(solution)/shard_map/all_to_all | solution.py:358
  50.9 0.8 %unpack.1 = f32[1,512]{1,0:T(1,128)} custom-call(s32[1,512]{1,0:T(1,128)S(1)} %get-tuple-element.11.after_ref.index_ref, f32[8,128]{1,0:T(8,128)S(1)} %bitcast.14), custom_call_target="tpu_custom_call" | custom-call | tf_op jit(solution)/shard_map/unpack/pallas_call | solution.py:276
  51.7 0.0 collective-permute-done.8.refs_2_
  51.7 0.0 collective-permute-done.7.refs_1_
  51.7 0.0 collective-permute-done.6.refs_0_
  51.8 1.0 %finish.1 = f32[256,512]{1,0:T(8,128)} custom-call(f32[256,512]{1,0:T(8,128)S(1)} %copy-done, f32[256,512]{1,0:T(8,128)S(1)} %get-tuple-element.18.own_ref, bf16[256,512]{1,0:T(8,128)(2,1)S(1)} %collective-permute-done.6.refs_0_, bf16[256,512]{1,0:T(8,128)(2,1)S(1)} %collective-permute-done.7.refs_1_, bf16[256,512]{1,0:T(8,128)(2,1)S(1)} %collective-permute-done.8.refs_2_), custom_call_target="tpu_custom_call" | custom-call | tf_op jit(solution)/shard_map/finish/pallas_call | solution.py:276
  (1 shorter events, 0.0 us)
Async XLA Ops:
  0.6 14.1 %copy-start.1 = (s32[256]{0:T(256)S(1)}, s32[256]{0:T(256)}, u32[]{:S(2)}) copy-start(s32[256]{0:T(256)} %param.10) | copy-start | bytes 3076
  0.6 2.3 %collective-permute-start.2 = (bf16[512,512]{1,0:T(8,128)(2,1)}, bf16[512,512]{1,0:T(8,128)(2,1)S(1)}, u32[]{:S(2)}, u32[]{:S(2)}) collective-permute-start(bf16[512,512]{1,0:T(8,128)(2,1)} %refs_2_.1), channel_id=1, source_target_pairs={{0,1},{1,0},{2,3},{3,2},{4,5},{5,4},{6,7},{7,6},{8,9},{9,8},{10,11... | collective-permute-start | bytes 1572872 | tf_op jit(solution)/shard_map/ppermute | solution.py:253
  1.2 1.8 %collective-permute-start = (s32[1,512]{1,0:T(1,128)}, s32[1,512]{1,0:T(1,128)S(1)}, u32[]{:S(2)}, u32[]{:S(2)}) collective-permute-start(s32[1,512]{1,0:T(1,128)} %bitcast.15), channel_id=1, source_target_pairs={{0,1},{1,0},{2,3},{3,2},{4,5},{5,4},{6,7},{7,6},{8,9},{9,8},{10,11... | collective-permute-start | bytes 6152 | tf_op jit(solution)/shard_map/ppermute | solution.py:253
  1.2 1.7 %collective-permute-start.1 = (s32[1,512]{1,0:T(1,128)}, s32[1,512]{1,0:T(1,128)S(1)}, u32[]{:S(2)}, u32[]{:S(2)}) collective-permute-start(s32[1,512]{1,0:T(1,128)} %bitcast.17), channel_id=1, source_target_pairs={{0,1},{1,0},{2,3},{3,2},{4,5},{5,4},{6,7},{7,6},{8,9},{9,8},{10,11... | collective-permute-start | bytes 6152 | tf_op jit(solution)/shard_map/ppermute | solution.py:253
  5.3 17.3 %collective-permute-start.4 = (bf16[1056,128]{1,0:T(8,128)(2,1)S(1)}, bf16[1056,128]{1,0:T(8,128)(2,1)S(1)}, u32[]{:S(2)}, u32[]{:S(2)}) collective-permute-start(bf16[1056,128]{1,0:T(8,128)(2,1)S(1)} %get-tuple-element.16), channel_id=1, source_target_pairs={{0,4},{1,5},{2,6},{3,7},{4,0},{5,1},{6,2},{7,3},{8,12},{9,13},{10,... | collective-permute-start | bytes 811016 | tf_op jit(solution)/shard_map/ppermute | solution.py:253
  9.3 17.5 %collective-permute-start.5 = (bf16[1056,128]{1,0:T(8,128)(2,1)S(1)}, bf16[1056,128]{1,0:T(8,128)(2,1)S(1)}, u32[]{:S(2)}, u32[]{:S(2)}) collective-permute-start(bf16[1056,128]{1,0:T(8,128)(2,1)S(1)} %get-tuple-element.17), channel_id=1, source_target_pairs={{0,2},{1,3},{2,0},{3,1},{4,6},{5,7},{6,4},{7,5},{8,10},{9,11},{10,... | collective-permute-start | bytes 811016 | tf_op jit(solution)/shard_map/ppermute | solution.py:253
  10.9 20.8 %collective-permute-start.3 = (bf16[1056,128]{1,0:T(8,128)(2,1)S(1)}, bf16[1056,128]{1,0:T(8,128)(2,1)S(1)}, u32[]{:S(2)}, u32[]{:S(2)}) collective-permute-start(bf16[1056,128]{1,0:T(8,128)(2,1)S(1)} %get-tuple-element.14), channel_id=1, source_target_pairs={{0,6},{1,7},{2,4},{3,5},{4,2},{5,3},{6,0},{7,1},{8,14},{9,15},{10,... | collective-permute-start | bytes 811016 | tf_op jit(solution)/shard_map/ppermute | solution.py:253
  26.8 25.0 %copy-start = (f32[256,512]{1,0:T(8,128)S(1)}, f32[256,512]{1,0:T(8,128)}, u32[]{:S(2)}) copy-start(f32[256,512]{1,0:T(8,128)} %stored_ref.1) | copy-start | bytes 1572868
  32.1 19.7 %collective-permute-start.8 = (bf16[256,512]{1,0:T(8,128)(2,1)S(1)}, bf16[256,512]{1,0:T(8,128)(2,1)S(1)}, u32[]{:S(2)}, u32[]{:S(2)}) collective-permute-start(bf16[256,512]{1,0:T(8,128)(2,1)S(1)} %get-tuple-element.19), channel_id=1, source_target_pairs={{0,24},{8,16},{16,8},{24,0},{1,25},{9,17},{17,9},{25,1},{2,26},{10... | collective-permute-start | bytes 786440 | tf_op jit(solution)/shard_map/ppermute | solution.py:253
  35.3 16.4 %collective-permute-start.7 = (bf16[256,512]{1,0:T(8,128)(2,1)S(1)}, bf16[256,512]{1,0:T(8,128)(2,1)S(1)}, u32[]{:S(2)}, u32[]{:S(2)}) collective-permute-start(bf16[256,512]{1,0:T(8,128)(2,1)S(1)} %get-tuple-element.19), channel_id=1, source_target_pairs={{0,16},{8,24},{16,0},{24,8},{1,17},{9,25},{17,1},{25,9},{2,18},{10... | collective-permute-start | bytes 786440 | tf_op jit(solution)/shard_map/ppermute | solution.py:253
  35.8 15.9 %collective-permute-start.6 = (bf16[256,512]{1,0:T(8,128)(2,1)S(1)}, bf16[256,512]{1,0:T(8,128)(2,1)S(1)}, u32[]{:S(2)}, u32[]{:S(2)}) collective-permute-start(bf16[256,512]{1,0:T(8,128)(2,1)S(1)} %get-tuple-element.19), channel_id=1, source_target_pairs={{0,8},{8,0},{16,24},{24,16},{1,9},{9,1},{17,25},{25,17},{2,10},{10... | collective-permute-start | bytes 786440 | tf_op jit(solution)/shard_map/ppermute | solution.py:253

commit v4 on v3

--- a/solution.py
+++ b/solution.py
@@ -11,7 +11,6 @@
 LANES = 128
 INFO_ROWS = 16
 CODE_BASE = 128
-CORES = 2
 SMALL_VMEM = 32 * 1024 * 1024
 
 
@@ -38,7 +37,7 @@
     return jnp.sum(jnp.where(hit, earlier, 0.0), axis=0, keepdims=True).astype(jnp.int32)
 
 
-def write_messages(source, capacity, index, slot, values, message_refs):
+def write_messages(capacity, first, index, slot, values, message_refs):
     rows, width = values.shape
     code_row = lax.broadcasted_iota(jnp.int32, (INFO_ROWS, rows), 0)
     codes = jnp.where(
@@ -46,52 +45,58 @@
         slot // CODE_BASE + 1,
         jnp.where(code_row == 1, slot % CODE_BASE, 0),
     )
-    place = lax.broadcasted_iota(jnp.int32, (len(message_refs) * capacity, rows), 0)
-    match = (place == index).astype(jnp.float32).astype(jnp.bfloat16)
-    packed = jnp.dot(match, values, preferred_element_type=jnp.float32).astype(jnp.bfloat16)
-    info = lax.dot_general(
-        codes.astype(jnp.float32).astype(jnp.bfloat16),
-        match,
-        (((1,), (1,)), ((), ())),
-        preferred_element_type=jnp.float32,
-    ).astype(jnp.bfloat16)
-    for chip, message in enumerate(message_refs):
-        low = chip * capacity
-        for part in range(width // LANES):
-            message[pl.ds((part * CORES + source) * capacity, capacity), :] = packed[
-                low : low + capacity, part * LANES : (part + 1) * LANES
-            ]
-        piece = info[:, low : low + capacity]
-        if capacity < LANES:
-            piece = jnp.concatenate(
-                [piece, jnp.zeros((INFO_ROWS, LANES - capacity), jnp.bfloat16)], axis=1
-            )
-        start = width // LANES * CORES * capacity + source * INFO_ROWS
-        message[pl.ds(start, INFO_ROWS), :] = piece
+    codes = codes.astype(jnp.float32).astype(jnp.bfloat16)
+    peers = max(1, 256 // capacity)
+    for start in range(0, len(message_refs), peers):
+        chosen = message_refs[start : start + peers]
+        place = lax.broadcasted_iota(jnp.int32, (len(chosen) * capacity, rows), 0)
+        match = place + (first + start) * capacity == index
+        match = match.astype(jnp.float32).astype(jnp.bfloat16)
+        packed = jnp.dot(match, values, preferred_element_type=jnp.float32).astype(jnp.bfloat16)
+        info = lax.dot_general(
+            codes, match, (((1,), (1,)), ((), ())), preferred_element_type=jnp.float32
+        )
+        for number, message in enumerate(chosen):
+            low = number * capacity
+            for part in range(width // LANES):
+                message[pl.ds(part * capacity, capacity), :] = packed[
+                    low : low + capacity, part * LANES : (part + 1) * LANES
+                ]
+            piece = info[:, low : low + capacity]
+            if capacity < LANES:
+                piece = jnp.concatenate(
+                    [piece, jnp.zeros((INFO_ROWS, LANES - capacity), jnp.float32)], axis=1
+                )
+            message[pl.ds(width // LANES * capacity, INFO_ROWS), :] = piece.astype(jnp.bfloat16)
 
 
 def pack_kernel(owners, capacity, me_ref, *refs):
-    own, other, return_ref, message_refs = refs[0:3], refs[3:6], refs[6], refs[7:-4]
-    held, semaphore = refs[-4:-1], refs[-1]
+    sources, return_ref, index_ref, held, messages = (
+        refs[:3], refs[3], refs[4], refs[5:8], refs[8:-1]
+    )
+    semaphore = refs[-1]
     copies = [
         pltpu.make_async_copy(source, target, semaphore.at[number])
-        for number, (source, target) in enumerate(zip(own, held))
+        for number, (source, target) in enumerate(zip(sources, held))
     ]
     for copy in copies:
         copy.start()
-    for copy in copies:
+    for copy in copies[:2]:
         copy.wait()
-    for source, (owner_ref, slot_ref, rows_ref) in enumerate((held, other)):
-        owner = owner_ref[...]
-        placed = place_rows(owners, owner)
-        if source == 0:
-            return_ref[...] = owner * capacity + placed
-        peer = owner ^ me_ref[0]
-        index = jnp.where(peer % CORES == 0, peer // CORES * capacity + placed, -1)
-        write_messages(source, capacity, index, slot_ref[...], rows_ref[...], message_refs)
-
-
-def load_kernel(blocks, bank_ref, after_ref, held_ref, norm_ref, semaphore):
+    owner = held[0][...]
+    placed = place_rows(owners, owner)
+    return_ref[...] = owner * capacity + placed
+    index = (owner ^ me_ref[0]) * capacity + placed
+    index_ref[...] = index
+    copies[2].wait()
+    write_messages(capacity, 0, index, held[1][...], held[2][...], messages)
+
+
+def late_pack_kernel(capacity, first, index_ref, slot_ref, rows_ref, after_ref, *messages):
+    write_messages(capacity, first, index_ref[...], slot_ref[...], rows_ref[...], messages)
+
+
+def load_kernel(blocks, bank_ref, packed_ref, held_ref, norm_ref, semaphore):
     clusters, depth, width = held_ref.shape
     block = clusters // blocks
     copies = []
@@ -115,21 +120,18 @@
 
 def read_messages(message_refs, capacity, width):
     units, slots = [], []
-    count = CORES * capacity
     for message in message_refs:
         values = jnp.concatenate(
             [
-                message[pl.ds(part * count, count), :].astype(jnp.float32)
+                message[pl.ds(part * capacity, capacity), :].astype(jnp.float32)
                 for part in range(width // LANES)
             ],
             axis=1,
         )
         norm = jnp.sqrt(jnp.sum(values * values, axis=1, keepdims=True) + epsilon)
         units.append((values / norm).astype(jnp.bfloat16))
-        for source in range(CORES):
-            start = width // LANES * count + source * INFO_ROWS
-            info = message[pl.ds(start, INFO_ROWS), :].astype(jnp.float32)
-            slots.append((info[0:1, :capacity] - 1.0) * CODE_BASE + info[1:2, :capacity])
+        info = message[pl.ds(width // LANES * capacity, INFO_ROWS), :].astype(jnp.float32)
+        slots.append((info[0:1, :capacity] - 1.0) * CODE_BASE + info[1:2, :capacity])
     return jnp.concatenate(units, axis=0), jnp.concatenate(slots, axis=1).astype(jnp.int32)
 
 
@@ -190,7 +192,11 @@
         return picked
 
     picked = lax.fori_loop(
-        0, clusters // block, add_block, jnp.zeros((depth, slots.shape[1]), jnp.float32)
+        0,
+        clusters // block,
+        add_block,
+        jnp.zeros((depth, slots.shape[1]), jnp.float32),
+        unroll=True,
     )
     onehot = cluster_onehot(slots, clusters)
     terms = [
@@ -208,7 +214,7 @@
     cosine = jnp.where(place < chosen_members, picked / chosen_norm, -3.0)
     best = jnp.max(cosine, axis=0, keepdims=True)
     results = [
-        best[:, number * capacity : (number + 1) * capacity] for number in range(CORES * messages)
+        best[:, number * capacity : (number + 1) * capacity] for number in range(messages)
     ]
     if not places:
         for number, value in enumerate(results):
@@ -216,10 +222,8 @@
         return
     for group in reversed(earlier_refs):
         results = [group[pl.ds(number, 1), :] for number in range(group.shape[0])] + results
-    for chip, place in enumerate(places):
-        for source in range(CORES):
-            offset = place * CORES + source
-            best_ref[pl.ds(me_ref[0] ^ offset, 1), :] = results[chip * CORES + source]
+    for value, place in zip(results, places):
+        best_ref[pl.ds(me_ref[0] ^ place, 1), :] = value
 
 
 def finish_kernel(stored_ref, own_ref, *refs):
@@ -259,15 +263,18 @@
     rows, width = arrivals.shape
     clusters, depth = bank.shape[0], bank.shape[1]
     capacity = 2 * rows // owners
-    chips = owners // CORES
-    message_rows = (width // LANES * capacity + INFO_ROWS) * CORES
     own_index = lax.axis_index("own").astype(jnp.int32).reshape(1)
     smem = pl.BlockSpec(memory_space=pltpu.SMEM)
     anywhere = pl.BlockSpec(memory_space=pl.ANY)
-    message = jax.ShapeDtypeStruct((message_rows, LANES), jnp.bfloat16)
-    quarter = chips // 4
-    order = [
-        list(range(first * quarter, (first + 1) * quarter)) for first in (0, 2, 1, 3)
+    message = jax.ShapeDtypeStruct(
+        (width // LANES * capacity + INFO_ROWS, LANES), jnp.bfloat16
+    )
+    half, part = owners // 2, owners // 8
+    groups = [
+        [0, *range(half, half + part)],
+        [*range(half + part, half + 2 * part), *range(1, half)],
+        [*range(half + 2 * part, half + 3 * part)],
+        [*range(half + 3 * part, owners)],
     ]
     block = min(clusters, 32)
 
@@ -280,27 +287,25 @@
             out_specs=out_specs,
             scratch_shapes=scratch_shapes,
             compiler_params=small_params(),
+            cost_estimate=pl.CostEstimate(flops=1, bytes_accessed=1, transcendentals=0),
             name=name,
         )(*operands)
 
-    own_rows = (home_owner.reshape(1, rows), cluster_slot.reshape(1, rows), arrivals)
-    other_rows = [exchange(value, "own", 1) for value in own_rows[::-1]][::-1]
     row = jax.ShapeDtypeStruct((1, rows), jnp.int32)
-    return_index, *sent = vmem_call(
+    late = half + 2 * part
+    return_index, index, _, slots, values, *sent = vmem_call(
         functools.partial(pack_kernel, owners, capacity),
         "pack",
-        [row] + [message] * chips,
-        [own_index, *[in_hbm(value) for value in own_rows], *other_rows],
-        [smem] + [anywhere] * 3 + [whole_vmem()] * 3,
+        [row] * 4 + [jax.ShapeDtypeStruct((rows, width), arrivals.dtype)] + [message] * late,
         [
-            pltpu.VMEM((1, rows), jnp.int32),
-            pltpu.VMEM((1, rows), jnp.int32),
-            pltpu.VMEM((rows, width), arrivals.dtype),
-            pltpu.SemaphoreType.DMA((3,)),
+            own_index,
+            in_hbm(home_owner.reshape(1, rows)),
+            in_hbm(cluster_slot.reshape(1, rows)),
+            in_hbm(arrivals),
         ],
-    )
-    got = [sent[0]] + [exchange(sent[chip], "own", chip * CORES) for chip in range(1, chips)]
-
+        [smem] + [anywhere] * 3,
+        [pltpu.SemaphoreType.DMA((3,))],
+    )
     blocks = 8
     held_bank, bank_norm = vmem_call(
         functools.partial(load_kernel, blocks),
@@ -309,36 +314,48 @@
             pltpu.VMEM(bank.shape, bank.dtype),
             jax.ShapeDtypeStruct((clusters, LANES), jnp.float32),
         ],
-        [in_hbm(bank), return_index],
-        [anywhere, anywhere],
+        [in_hbm(bank), sent[0]],
+        [anywhere] * 2,
         [pltpu.SemaphoreType.DMA((blocks,))],
     )
     held_bank = pltpu.with_memory_space_constraint(held_bank, pltpu.VMEM)
+    got = {peer: exchange(value, "own", peer) if peer else value for peer, value in enumerate(sent)}
+
+    def send_late(chosen, after):
+        packed = vmem_call(
+            functools.partial(late_pack_kernel, capacity, chosen[0]),
+            "late_pack",
+            [message] * len(chosen),
+            [index, slots, values, after],
+            [whole_vmem()] * 3 + [anywhere],
+        )
+        for peer, value in zip(chosen, packed):
+            got[peer] = exchange(value, "own", peer)
+
+    send_late(groups[2], bank_norm)
     member_row = members.reshape(1, clusters)
 
     results = []
     sums = jax.ShapeDtypeStruct((clusters, width), jnp.float32)
 
-    def score(chosen):
-        last = chosen is order[-1]
-        places = sum(order, []) if last else []
-        group = [got[chip] for chip in chosen]
-        before = results if last else results[-1:]
-        operands = [own_index, held_bank, bank_norm, member_row, *group, *before]
-        specs = [smem] + [whole_vmem()] * (3 + len(group))
+    def score(group, places=()):
+        messages = [got[peer] for peer in group]
+        before = results if places else results[-1:]
+        operands = [own_index, held_bank, bank_norm, member_row, *messages, *before]
+        specs = [smem] + [whole_vmem()] * (3 + len(messages))
         return vmem_call(
-            functools.partial(score_kernel, len(group), places, capacity, block),
+            functools.partial(score_kernel, len(messages), places, capacity, block),
             "score",
-            jax.ShapeDtypeStruct(
-                (owners if last else CORES * len(group), capacity), jnp.float32
-            ),
+            jax.ShapeDtypeStruct((owners if places else len(group), capacity), jnp.float32),
             operands,
-            specs + [whole_vmem() if last else anywhere] * len(before),
-        )
-
-    for chosen in order[:-1]:
-        results.append(score(chosen))
-    early_messages = [got[chip] for chip in sum(order[:-1], [])]
+            specs + [whole_vmem() if places else anywhere] * len(before),
+        )
+
+    for group in groups[:-1]:
+        results.append(score(group))
+        if len(results) == 1:
+            send_late(groups[3], results[0])
+    early_messages = [got[peer] for group in groups[:-1] for peer in group]
     early = vmem_call(
         functools.partial(early_sum_kernel, len(early_messages), capacity),
         "early_sum",
@@ -346,7 +363,7 @@
         [*early_messages, results[-1]],
         [whole_vmem()] * len(early_messages) + [anywhere],
     )
-    late_messages = [got[chip] for chip in order[-1]]
+    late_messages = [got[peer] for peer in groups[-1]]
     own_sum, sent_sum = vmem_call(
         functools.partial(late_sum_kernel, len(late_messages), capacity),
         "late_sum",
@@ -354,7 +371,7 @@
         [*late_messages, early],
     )
     terms = [exchange(sent_sum, "grp", offset) for offset in range(1, parts)]
-    best = score(order[-1])
+    best = score(groups[-1], sum(groups, []))
     returned = lax.all_to_all(best, "own", split_axis=0, concat_axis=0, tiled=True)
     best_cosine = vmem_call(unpack_kernel, "unpack", jax.ShapeDtypeStruct((1, rows), jnp.float32), [return_index, returned])
     centroids = vmem_call(finish_kernel, "finish", sums, [centroid_sum, own_sum, *terms])

time: 53 us -> 49.7 us (0.938)
  Pallas kernels: 25.9 us -> 22 us
  starting transfers between devices: 10.5 us -> 12.6 us
  waiting for transfers between devices: 4.93 us -> 4.21 us
  blocking collectives: 10.7 us -> 9.99 us
    pallas_call x10 -> x12, Pallas kernels: 25.9 us -> 22 us  [vmem_call(): pl.pallas_call(kernel, out_shape=out_shape, in_specs=in_specs or [whole_v...]
    ppermute x9 -> x10, starting transfers between devices: 10.5 us -> 12.6 us  [exchange(): lax.ppermute(value, axis, [(device, device ^ offset) for device in range(...]
    ppermute x9 -> x10, waiting for transfers between devices: 4.93 us -> 4.21 us  [exchange(): lax.ppermute(value, axis, [(device, device ^ offset) for device in range(...]
    all_to_all x1, blocking collectives: 10.7 us -> 9.99 us  [body(): lax.all_to_all(best, 'own', split_axis=0, concat_axis=0, tiled=True)]
  transfers between devices with their start and end apart: 9 -> 10, of which waited for: 2 -> 1; matrix products, arithmetic and copies ran while one was open for 0% -> 0% of each run, Pallas kernels for 42% -> 38%
where the time goes in v4:
time: 49.7 us; the launch traced here: 49.5 us
  Pallas kernels  22 us (44%)
  starting transfers between devices  12.6 us (25%)
  blocking collectives  9.99 us (20%)
  waiting for transfers between devices  4.21 us (8%)
  between operations  0.79 us (2%)
    pallas_call x12, Pallas kernels, vmem_call(): pl.pallas_call(kernel, out_shape=out_shape, in_specs=in_specs or [whole_v...  22 us
    ppermute x10, starting transfers between devices, exchange(): lax.ppermute(value, axis, [(device, device ^ offset) for device in range(...  12.6 us
    all_to_all x1, blocking collectives, body(): lax.all_to_all(best, 'own', split_axis=0, concat_axis=0, tiled=True)  9.99 us
    ppermute x10, waiting for transfers between devices, exchange(): lax.ppermute(value, axis, [(device, device ^ offset) for device in range(...  4.21 us
  transfers between devices with their start and end apart: 10, of which 1 were waited for; matrix products, arithmetic and copies ran while one was open for 0% of the time, Pallas kernels for 38%

profile of v4, /device:TPU:0, one launch (start us, length us, event | category | flops | bytes accessed | tf_op | source)
XLA Modules:
  0.0 49.5 jit_solution(17834178946697277121)
XLA Ops:
  0.6 1.8 %pack.1 = (s32[1,512]{1,0:T(1,128)S(1)}, s32[1,512]{1,0:T(1,128)S(1)}, s32[1,512]{1,0:T(1,128)}, s32[1,512]{1,0:T(1,128)S(1)}, bf16[512,512]{1,0:T(8,128)(2,1)S(...) custom-call(s32[1]{0:T(128)} %bitcast.me_ref, ...), custom_call_target="tpu_custom_call" | custom-call | flops 1 | bytes 1 | tf_op jit(solution)/shard_map/pack/pallas_call | solution.py:283
  2.5 4.1 %collective-permute-start = (bf16[528,128]{1,0:T(8,128)(2,1)S(1)}, bf16[528,128]{1,0:T(8,128)(2,1)S(1)}, u32[]{:S(2)}, u32[]{:S(2)}) collective-permute-start(bf16[528,128]{1,0:T(8,128)(2,1)S(1)} %get-tuple-element.23), channel_id=1, source_target_pairs={{0,4},{1,5},{2,6},{3,7},{4,0},{5,1},{6,2},{7,3},{8,12},{9,13},{10,... | collective-permute-start | bytes 405512 | tf_op jit(solution)/shard_map/ppermute | solution.py:257
  6.6 0.0 collective-permute-start.2
  6.6 0.2 collective-permute-start.3
  6.8 1.8 %collective-permute-start.4 = (bf16[528,128]{1,0:T(8,128)(2,1)S(1)}, bf16[528,128]{1,0:T(8,128)(2,1)S(1)}, u32[]{:S(2)}, u32[]{:S(2)}) collective-permute-start(bf16[528,128]{1,0:T(8,128)(2,1)S(1)} %get-tuple-element.26), channel_id=1, source_target_pairs={{0,2},{1,3},{2,0},{3,1},{4,6},{5,7},{6,4},{7,5},{8,10},{9,11},{10,... | collective-permute-start | bytes 405512 | tf_op jit(solution)/shard_map/ppermute | solution.py:257
  8.6 0.0 collective-permute-start.5
  8.6 3.8 %bank_load.1 = (bf16[256,32,512]{2,1,0:T(8,128)(2,1)S(1)}, f32[256,128]{1,0:T(8,128)S(1)}) custom-call(bf16[256,32,512]{2,1,0:T(8,128)(2,1)} %bank_ref.1, bf16[528,128]{1,0:T(8,128)(2,1)S(1)} %get-tuple-element.17.packed_ref.refs_0_), custom_call_target="tpu_custom_call" | custom-call | flops 1 | bytes 1 | tf_op jit(solution)/shard_map/bank_load/pallas_call | solution.py:283
  12.4 0.2 late_pack.3
  12.7 4.2 %collective-permute-done.refs_1_ = bf16[528,128]{1,0:T(8,128)(2,1)S(1)} collective-permute-done((bf16[528,128]{1,0:T(8,128)(2,1)S(1)}, bf16[528,128]{1,0:T(8,128)(2,1)S(1)}, u32[]{:S(2)}, u32[]{:S(2)}) %collective-permute-start) | collective-permute-done | bytes 135200 | tf_op jit(solution)/shard_map/ppermute | solution.py:257
  16.9 2.8 %collective-permute-start.6 = (bf16[528,128]{1,0:T(8,128)(2,1)S(1)}, bf16[528,128]{1,0:T(8,128)(2,1)S(1)}, u32[]{:S(2)}, u32[]{:S(2)}) collective-permute-start(bf16[528,128]{1,0:T(8,128)(2,1)S(1)} %late_pack.3), channel_id=1, source_target_pairs={{0,6},{1,7},{2,4},{3,5},{4,2},{5,3},{6,0},{7,1},{8,14},{9,15},{10,... | collective-permute-start | bytes 405512 | tf_op jit(solution)/shard_map/ppermute | solution.py:257
  19.7 2.8 %score.4.after_ref.refs_4_.refs_1_ = f32[2,128]{1,0:T(2,128)S(1)} custom-call(s32[1]{0:T(128)} %bitcast.me_ref, bf16[256,32,512]{2,1,0:T(8,128)(2,1)S(1)} %get-tuple-element.18.bank_ref, f32[256,128]{1,0:T(8,128)S(1)} %get-tuple-element.19.norm_ref.after_ref, s32[1,256]{1,0:T(1,128)S(1)} %bitcast.10, ...), custom_call_target="tpu_custom_call" | custom-call | flops 1 | bytes 1 | tf_op jit(solution)/shard_map/score/pallas_call | solution.py:283
  22.5 0.2 late_pack.2
  22.7 0.0 collective-permute-done.2.refs_0_.refs_2_
  22.7 0.1 collective-permute-start.1
  22.8 0.0 collective-permute-done.3.refs_1_.refs_3_
  22.8 0.0 collective-permute-done.4.refs_2_.refs_4_
  22.8 0.0 collective-permute-done.5.refs_3_.refs_5_
  22.8 4.9 %score.5.refs_1_.refs_2_ = f32[4,128]{1,0:T(4,128)S(1)} custom-call(s32[1]{0:T(128)} %bitcast.me_ref, bf16[256,32,512]{2,1,0:T(8,128)(2,1)S(1)} %get-tuple-element.18.bank_ref, f32[256,128]{1,0:T(8,128)S(1)} %get-tuple-element.19.norm_ref.after_ref, s32[1,256]{1,0:T(1,128)S(1)} %bitcast.11, bf16[528,128]{1,0:T(8,128)(2,1)S(1)} %collective-permute-done.2.refs_0_.refs_2_, ...), custom_call_target="tpu_custom_call" | custom-call | flops 1 | bytes 1 | tf_op jit(solution)/shard_map/score/pallas_call | solution.py:283
  27.7 0.0 copy-start
  27.7 0.0 collective-permute-done.6.refs_0_.refs_6_
  27.8 2.5 %score.6.refs_3_.refs_7_ = f32[1,128]{1,0:T(1,128)S(1)} custom-call(s32[1]{0:T(128)} %bitcast.me_ref, bf16[256,32,512]{2,1,0:T(8,128)(2,1)S(1)} %get-tuple-element.18.bank_ref, f32[256,128]{1,0:T(8,128)S(1)} %get-tuple-element.19.norm_ref.after_ref, s32[1,256]{1,0:T(1,128)S(1)} %bitcast.12, bf16[528,128]{1,0:T(8,128)(2,1)S(1)} %collective-permute-done.6.refs_0_.refs_6_, ...), custom_call_target="tpu_custom_call" | custom-call | flops 1 | bytes 1 | tf_op jit(solution)/shard_map/score/pallas_call | solution.py:283
  30.3 0.9 %early_sum.1.refs_1_ = f32[256,512]{1,0:T(8,128)S(1)} custom-call(bf16[528,128]{1,0:T(8,128)(2,1)S(1)} %get-tuple-element.17.packed_ref.refs_0_, bf16[528,128]{1,0:T(8,128)(2,1)S(1)} %collective-permute-done.refs_1_, bf16[528,128]{1,0:T(8,128)(2,1)S(1)} %collective-permute-done.2.refs_0_.refs_2_, ...), custom_call_target="tpu_custom_call" | custom-call | flops 1 | bytes 1 | tf_op jit(solution)/shard_map/early_sum/pallas_call | solution.py:283
  31.2 0.0 collective-permute-done.1.refs_0_
  31.2 0.3 late_sum.1
  31.5 2.5 %collective-permute-start.9 = (bf16[256,512]{1,0:T(8,128)(2,1)S(1)}, bf16[256,512]{1,0:T(8,128)(2,1)S(1)}, u32[]{:S(2)}, u32[]{:S(2)}) collective-permute-start(bf16[256,512]{1,0:T(8,128)(2,1)S(1)} %get-tuple-element.29), channel_id=1, source_target_pairs={{0,24},{8,16},{16,8},{24,0},{1,25},{9,17},{17,9},{25,1},{2,26},{10... | collective-permute-start | bytes 786440 | tf_op jit(solution)/shard_map/ppermute | solution.py:257
  34.0 0.5 %collective-permute-start.8 = (bf16[256,512]{1,0:T(8,128)(2,1)S(1)}, bf16[256,512]{1,0:T(8,128)(2,1)S(1)}, u32[]{:S(2)}, u32[]{:S(2)}) collective-permute-start(bf16[256,512]{1,0:T(8,128)(2,1)S(1)} %get-tuple-element.29), channel_id=1, source_target_pairs={{0,16},{8,24},{16,0},{24,8},{1,17},{9,25},{17,1},{25,9},{2,18},{10... | collective-permute-start | bytes 786440 | tf_op jit(solution)/shard_map/ppermute | solution.py:257
  34.6 0.5 %collective-permute-start.7 = (bf16[256,512]{1,0:T(8,128)(2,1)S(1)}, bf16[256,512]{1,0:T(8,128)(2,1)S(1)}, u32[]{:S(2)}, u32[]{:S(2)}) collective-permute-start(bf16[256,512]{1,0:T(8,128)(2,1)S(1)} %get-tuple-element.29), channel_id=1, source_target_pairs={{0,8},{8,0},{16,24},{24,16},{1,9},{9,1},{17,25},{25,17},{2,10},{10... | collective-permute-start | bytes 786440 | tf_op jit(solution)/shard_map/ppermute | solution.py:257
  35.1 2.5 %score.7 = f32[8,128]{1,0:T(8,128)S(1)} custom-call(s32[1]{0:T(128)} %bitcast.me_ref, bf16[256,32,512]{2,1,0:T(8,128)(2,1)S(1)} %get-tuple-element.18.bank_ref, f32[256,128]{1,0:T(8,128)S(1)} %get-tuple-element.19.norm_ref.after_ref, s32[1,256]{1,0:T(1,128)S(1)} %bitcast.13, bf16[528,128]{1,0:T(8,128)(2,1)S(1)} %collective-permute-done.1.refs_0_, ...), custom_call_target="tpu_custom_call" | custom-call | flops 1 | bytes 1 | tf_op jit(solution)/shard_map/score/pallas_call | solution.py:283
  37.6 10.0 %all_to_all.11 = f32[8,1,128]{2,1,0:T(1,128)S(1)} all-to-all(f32[8,1,128]{2,1,0:T(1,128)S(1)} %bitcast.9), channel_id=1, replica_groups=mesh['grp'=4,'own'=8] {'own'}, dimensions={0} | all-to-all | bytes 8192 | tf_op jit(solution)/shard_map/all_to_all | solution.py:375
  47.6 0.8 %unpack.1 = f32[1,512]{1,0:T(1,128)} custom-call(s32[1,512]{1,0:T(1,128)S(1)} %get-tuple-element.16.index_ref, f32[8,128]{1,0:T(8,128)S(1)} %bitcast.14), custom_call_target="tpu_custom_call" | custom-call | flops 1 | bytes 1 | tf_op jit(solution)/shard_map/unpack/pallas_call | solution.py:283
  48.5 0.0 collective-permute-done.9.refs_2_
  48.5 1.0 %finish.1 = f32[256,512]{1,0:T(8,128)} custom-call(f32[256,512]{1,0:T(8,128)S(1)} %copy-done, f32[256,512]{1,0:T(8,128)S(1)} %get-tuple-element.28.own_ref, bf16[256,512]{1,0:T(8,128)(2,1)S(1)} %collective-permute-done.7.refs_0_, bf16[256,512]{1,0:T(8,128)(2,1)S(1)} %collective-permute-done.8.refs_1_, bf16[256,512]{1,0:T(8,128)(2,1)S(1)} %collective-permute-done.9.refs_2_), custom_call_target="tpu_custom_call" | custom-call | flops 1 | bytes 1 | tf_op jit(solution)/shard_map/finish/pallas_call | solution.py:283
  (5 shorter events, 0.0 us)
Async XLA Ops:
  0.6 19.0 %copy-start.1 = (s32[256]{0:T(256)S(1)}, s32[256]{0:T(256)}, u32[]{:S(2)}) copy-start(s32[256]{0:T(256)} %param.10) | copy-start | bytes 3076
  2.5 14.4 %collective-permute-start = (bf16[528,128]{1,0:T(8,128)(2,1)S(1)}, bf16[528,128]{1,0:T(8,128)(2,1)S(1)}, u32[]{:S(2)}, u32[]{:S(2)}) collective-permute-start(bf16[528,128]{1,0:T(8,128)(2,1)S(1)} %get-tuple-element.23), channel_id=1, source_target_pairs={{0,4},{1,5},{2,6},{3,7},{4,0},{5,1},{6,2},{7,3},{8,12},{9,13},{10,... | collective-permute-start | bytes 405512 | tf_op jit(solution)/shard_map/ppermute | solution.py:257
  6.6 16.2 %collective-permute-start.2 = (bf16[528,128]{1,0:T(8,128)(2,1)S(1)}, bf16[528,128]{1,0:T(8,128)(2,1)S(1)}, u32[]{:S(2)}, u32[]{:S(2)}) collective-permute-start(bf16[528,128]{1,0:T(8,128)(2,1)S(1)} %get-tuple-element.24), channel_id=1, source_target_pairs={{0,5},{1,4},{2,7},{3,6},{4,1},{5,0},{6,3},{7,2},{8,13},{9,12},{10,... | collective-permute-start | bytes 405512 | tf_op jit(solution)/shard_map/ppermute | solution.py:257
  6.6 16.2 %collective-permute-start.3 = (bf16[528,128]{1,0:T(8,128)(2,1)S(1)}, bf16[528,128]{1,0:T(8,128)(2,1)S(1)}, u32[]{:S(2)}, u32[]{:S(2)}) collective-permute-start(bf16[528,128]{1,0:T(8,128)(2,1)S(1)} %get-tuple-element.25), channel_id=1, source_target_pairs={{0,1},{1,0},{2,3},{3,2},{4,5},{5,4},{6,7},{7,6},{8,9},{9,8},{10,11... | collective-permute-start | bytes 405512 | tf_op jit(solution)/shard_map/ppermute | solution.py:257
  6.8 16.1 %collective-permute-start.4 = (bf16[528,128]{1,0:T(8,128)(2,1)S(1)}, bf16[528,128]{1,0:T(8,128)(2,1)S(1)}, u32[]{:S(2)}, u32[]{:S(2)}) collective-permute-start(bf16[528,128]{1,0:T(8,128)(2,1)S(1)} %get-tuple-element.26), channel_id=1, source_target_pairs={{0,2},{1,3},{2,0},{3,1},{4,6},{5,7},{6,4},{7,5},{8,10},{9,11},{10,... | collective-permute-start | bytes 405512 | tf_op jit(solution)/shard_map/ppermute | solution.py:257
  8.6 14.2 %collective-permute-start.5 = (bf16[528,128]{1,0:T(8,128)(2,1)S(1)}, bf16[528,128]{1,0:T(8,128)(2,1)S(1)}, u32[]{:S(2)}, u32[]{:S(2)}) collective-permute-start(bf16[528,128]{1,0:T(8,128)(2,1)S(1)} %get-tuple-element.27), channel_id=1, source_target_pairs={{0,3},{1,2},{2,1},{3,0},{4,7},{5,6},{6,5},{7,4},{8,11},{9,10},{10,... | collective-permute-start | bytes 405512 | tf_op jit(solution)/shard_map/ppermute | solution.py:257
  16.9 10.9 %collective-permute-start.6 = (bf16[528,128]{1,0:T(8,128)(2,1)S(1)}, bf16[528,128]{1,0:T(8,128)(2,1)S(1)}, u32[]{:S(2)}, u32[]{:S(2)}) collective-permute-start(bf16[528,128]{1,0:T(8,128)(2,1)S(1)} %late_pack.3), channel_id=1, source_target_pairs={{0,6},{1,7},{2,4},{3,5},{4,2},{5,3},{6,0},{7,1},{8,14},{9,15},{10,... | collective-permute-start | bytes 405512 | tf_op jit(solution)/shard_map/ppermute | solution.py:257
  22.7 8.5 %collective-permute-start.1 = (bf16[528,128]{1,0:T(8,128)(2,1)S(1)}, bf16[528,128]{1,0:T(8,128)(2,1)S(1)}, u32[]{:S(2)}, u32[]{:S(2)}) collective-permute-start(bf16[528,128]{1,0:T(8,128)(2,1)S(1)} %late_pack.2), channel_id=1, source_target_pairs={{0,7},{1,6},{2,5},{3,4},{4,3},{5,2},{6,1},{7,0},{8,15},{9,14},{10,... | collective-permute-start | bytes 405512 | tf_op jit(solution)/shard_map/ppermute | solution.py:257
  27.7 20.8 %copy-start = (f32[256,512]{1,0:T(8,128)S(1)}, f32[256,512]{1,0:T(8,128)}, u32[]{:S(2)}) copy-start(f32[256,512]{1,0:T(8,128)} %stored_ref.1) | copy-start | bytes 1572868
  31.5 16.9 %collective-permute-start.9 = (bf16[256,512]{1,0:T(8,128)(2,1)S(1)}, bf16[256,512]{1,0:T(8,128)(2,1)S(1)}, u32[]{:S(2)}, u32[]{:S(2)}) collective-permute-start(bf16[256,512]{1,0:T(8,128)(2,1)S(1)} %get-tuple-element.29), channel_id=1, source_target_pairs={{0,24},{8,16},{16,8},{24,0},{1,25},{9,17},{17,9},{25,1},{2,26},{10... | collective-permute-start | bytes 786440 | tf_op jit(solution)/shard_map/ppermute | solution.py:257
  34.0 14.4 %collective-permute-start.8 = (bf16[256,512]{1,0:T(8,128)(2,1)S(1)}, bf16[256,512]{1,0:T(8,128)(2,1)S(1)}, u32[]{:S(2)}, u32[]{:S(2)}) collective-permute-start(bf16[256,512]{1,0:T(8,128)(2,1)S(1)} %get-tuple-element.29), channel_id=1, source_target_pairs={{0,16},{8,24},{16,0},{24,8},{1,17},{9,25},{17,1},{25,9},{2,18},{10... | collective-permute-start | bytes 786440 | tf_op jit(solution)/shard_map/ppermute | solution.py:257
  34.6 13.9 %collective-permute-start.7 = (bf16[256,512]{1,0:T(8,128)(2,1)S(1)}, bf16[256,512]{1,0:T(8,128)(2,1)S(1)}, u32[]{:S(2)}, u32[]{:S(2)}) collective-permute-start(bf16[256,512]{1,0:T(8,128)(2,1)S(1)} %get-tuple-element.29), channel_id=1, source_target_pairs={{0,8},{8,0},{16,24},{24,16},{1,9},{9,1},{17,25},{25,17},{2,10},{10... | collective-permute-start | bytes 786440 | tf_op jit(solution)/shard_map/ppermute | solution.py:257

commit v5 on v4

v5 whole, which is shorter than its diff:
```python
import functools

import jax
import jax.numpy as jnp
from jax import lax
from jax.experimental import pallas as pl
from jax.experimental.pallas import tpu as pltpu
from jax.sharding import PartitionSpec as P

epsilon = 1e-06
LANES = 128
INFO_ROWS = 16
CODE_BASE = 128
COSTS = {"score": 10**10}
SMALL_VMEM = 32 * 1024 * 1024


def whole_vmem():
    return pl.BlockSpec(memory_space=pltpu.VMEM)


def small_params():
    return pltpu.CompilerParams(vmem_limit_bytes=SMALL_VMEM)


def place_rows(owners, owner):
    rows = owner.shape[1]
    hit = lax.broadcasted_iota(jnp.int32, (owners, rows), 0) == owner
    earlier_mask = (
        lax.broadcasted_iota(jnp.int32, (rows, rows), 0)
        < lax.broadcasted_iota(jnp.int32, (rows, rows), 1)
    )
    earlier = jnp.dot(
        hit.astype(jnp.float32).astype(jnp.bfloat16),
        earlier_mask.astype(jnp.float32).astype(jnp.bfloat16),
        preferred_element_type=jnp.float32,
    )
    return jnp.sum(jnp.where(hit, earlier, 0.0), axis=0, keepdims=True).astype(jnp.int32)


def block_rows(capacity, width):
    return width // LANES * capacity + INFO_ROWS


def write_blocks(capacity, index, slot, values, targets):
    rows, width = values.shape
    code_row = lax.broadcasted_iota(jnp.int32, (INFO_ROWS, rows), 0)
    codes = jnp.where(
        code_row == 0,
        slot // CODE_BASE + 1,
        jnp.where(code_row == 1, slot % CODE_BASE, 0),
    )
    codes = codes.astype(jnp.float32).astype(jnp.bfloat16)
    peers = len(targets) // 4
    for start in range(0, len(targets), peers):
        place = lax.broadcasted_iota(jnp.int32, (peers * capacity, rows), 0)
        match = place + start * capacity == index
        match = match.astype(jnp.float32).astype(jnp.bfloat16)
        packed = jnp.dot(match, values, preferred_element_type=jnp.float32).astype(jnp.bfloat16)
        info = lax.dot_general(
            codes, match, (((1,), (1,)), ((), ())), preferred_element_type=jnp.float32
        )
        for number, (target, base) in enumerate(targets[start : start + peers]):
            low = number * capacity
            for part in range(width // LANES):
                target[pl.ds(base + part * capacity, capacity), :] = packed[
                    low : low + capacity, part * LANES : (part + 1) * LANES
                ]
            piece = info[:, low : low + capacity]
            if capacity < LANES:
                piece = jnp.concatenate(
                    [piece, jnp.zeros((INFO_ROWS, LANES - capacity), jnp.float32)], axis=1
                )
            target[pl.ds(base + width // LANES * capacity, INFO_ROWS), :] = piece.astype(
                jnp.bfloat16
            )


def pack_kernel(owners, capacity, me_ref, *refs):
    sources, return_ref, messages = refs[:3], refs[3], refs[4:-4]
    held, semaphore = refs[-4:-1], refs[-1]
    copies = [
        pltpu.make_async_copy(source, target, semaphore.at[number])
        for number, (source, target) in enumerate(zip(sources, held))
    ]
    for copy in copies:
        copy.start()
    for copy in copies[:2]:
        copy.wait()
    owner = held[0][...]
    placed = place_rows(owners, owner)
    return_ref[...] = owner * capacity + placed
    copies[2].wait()
    block = block_rows(capacity, held[2].shape[1])
    targets = [
        (message, base) for message in messages for base in range(0, message.shape[0], block)
    ]
    write_blocks(
        capacity, (owner ^ me_ref[0]) * capacity + placed, held[1][...], held[2][...], targets
    )


def pass_kernel(*refs):
    pair_refs, out_ref = refs[:-2], refs[-1]
    rows = pair_refs[0].shape[0] // 2
    for number, pair in enumerate(pair_refs):
        out_ref[pl.ds(number * rows, rows), :] = pair[pl.ds(rows, rows), :]


def read_blocks(blocks, capacity, width):
    units, slots = [], []
    for message, base in blocks:
        values = jnp.concatenate(
            [
                message[pl.ds(base + part * capacity, capacity), :].astype(jnp.float32)
                for part in range(width // LANES)
            ],
            axis=1,
        )
        norm = jnp.sqrt(jnp.sum(values * values, axis=1, keepdims=True) + epsilon)
        units.append((values / norm).astype(jnp.bfloat16))
        info = message[pl.ds(base + width // LANES * capacity, INFO_ROWS), :].astype(jnp.float32)
        slots.append((info[0:1, :capacity] - 1.0) * CODE_BASE + info[1:2, :capacity])
    return jnp.concatenate(units, axis=0), jnp.concatenate(slots, axis=1).astype(jnp.int32)


def cluster_onehot(slots, clusters):
    hit = lax.broadcasted_iota(jnp.int32, (clusters, slots.shape[1]), 0) == slots
    return hit.astype(jnp.float32).astype(jnp.bfloat16)


def split_exactly(value):
    high = value.astype(jnp.bfloat16)
    rest = value - high.astype(jnp.float32)
    middle = rest.astype(jnp.bfloat16)
    low = (rest - middle.astype(jnp.float32)).astype(jnp.bfloat16)
    return high, middle, low


def pick_dots(bank_block, first, columns, slots, picked):
    clusters, depth, width = bank_block.shape
    dots = jnp.dot(
        bank_block.reshape(clusters * depth, width), columns, preferred_element_type=jnp.float32
    )
    wanted = slots - first
    for cluster in range(clusters):
        picked = jnp.where(
            wanted == cluster, dots[cluster * depth : (cluster + 1) * depth, :], picked
        )
    return picked


def best_cosines(picked, onehot, norm, members):
    depth, rows = picked.shape
    terms = [
        lax.dot_general(
            term, onehot, (((0,), (0,)), ((), ())), preferred_element_type=jnp.float32
        )[:depth]
        for term in split_exactly(norm)
    ]
    chosen_norm = terms[0] + terms[1] + terms[2]
    member_rows = jnp.broadcast_to(
        members.astype(jnp.float32), (INFO_ROWS, members.shape[1])
    ).astype(jnp.bfloat16)
    chosen_members = jnp.dot(member_rows, onehot, preferred_element_type=jnp.float32)[0:1]
    place = lax.broadcasted_iota(jnp.int32, picked.shape, 0).astype(jnp.float32)
    cosine = jnp.where(place < chosen_members, picked / chosen_norm, -3.0)
    return jnp.max(cosine, axis=0, keepdims=True)


def first_score_kernel(messages, capacity, block, bank_ref, members_ref, *refs):
    message_refs = refs[:messages]
    held_ref, norm_ref, best_ref, sum_ref, semaphore = refs[messages:]
    clusters, depth, width = held_ref.shape
    copies = []
    for number in range(clusters // block):
        part = pl.ds(number * block, block)
        copies.append(
            pltpu.make_async_copy(bank_ref.at[part], held_ref.at[part], semaphore.at[number])
        )
        copies[-1].start()
    units, slots = read_blocks([(message, 0) for message in message_refs], capacity, width)
    onehot = cluster_onehot(slots, clusters)
    sum_ref[...] = jnp.dot(onehot, units, preferred_element_type=jnp.float32)
    columns = units.T
    picked = jnp.zeros((depth, slots.shape[1]), jnp.float32)
    shape = (block, depth, LANES)
    own_lane = lax.broadcasted_iota(jnp.int32, shape, 2) == lax.broadcasted_iota(
        jnp.int32, shape, 1
    )
    for number in range(clusters // block):
        copies[number].wait()
        part = pl.ds(number * block, block)
        bank_block = held_ref[part]
        picked = pick_dots(bank_block, number * block, columns, slots, picked)
        values = bank_block.astype(jnp.float32)
        square = jnp.sum(values * values, axis=2, keepdims=True)
        norm_ref[part, :] = jnp.sqrt(jnp.sum(jnp.where(own_lane, square, 0.0), axis=1) + epsilon)
    best = best_cosines(picked, onehot, norm_ref[...], members_ref[...])
    for number in range(messages):
        best_ref[pl.ds(number, 1), :] = best[:, number * capacity : (number + 1) * capacity]


def score_group(blocks, capacity, block, bank_ref, norm_ref, members_ref):
    clusters, depth, width = bank_ref.shape
    units, slots = read_blocks(blocks, capacity, width)
    onehot = cluster_onehot(slots, clusters)
    columns = units.T
    picked = jnp.zeros((depth, slots.shape[1]), jnp.float32)
    for number in range(clusters // block):
        bank_block = bank_ref[pl.ds(number * block, block)]
        picked = pick_dots(bank_block, number * block, columns, slots, picked)
    best = best_cosines(picked, onehot, norm_ref[...], members_ref[...])
    results = [
        best[:, number * capacity : (number + 1) * capacity]
        for number in range(len(blocks))
    ]
    return results, onehot, units


def score_kernel(
    messages, bases, match, capacity, block, bank_ref, norm_ref, members_ref, before_ref, *refs
):
    message_refs, refs = refs[:messages], refs[messages:]
    results, onehot, units = score_group(
        [(message, base) for message in message_refs for base in bases],
        capacity,
        block,
        bank_ref,
        norm_ref,
        members_ref,
    )
    best_ref, sum_ref = refs[match : match + 2]
    for number, value in enumerate(results):
        best_ref[pl.ds(number, 1), :] = value
    sum_ref[...] = before_ref[...] + jnp.dot(onehot, units, preferred_element_type=jnp.float32)
    if match:
        index_ref, match_ref = refs[0], refs[3]
        place = lax.broadcasted_iota(jnp.int32, match_ref.shape, 0)
        match_ref[...] = (place == index_ref[...]).astype(jnp.float32).astype(jnp.bfloat16)


def last_sum_kernel(messages, capacity, *refs):
    message_refs, before_ref, total_ref, sent_ref = refs[:messages], *refs[messages:]
    clusters, width = total_ref.shape
    units, slots = read_blocks([(message, 0) for message in message_refs], capacity, width)
    total = before_ref[...] + jnp.dot(
        cluster_onehot(slots, clusters), units, preferred_element_type=jnp.float32
    )
    total_ref[...] = total
    sent_ref[...] = total.astype(sent_ref.dtype)


def last_score_kernel(
    messages, places, capacity, block, me_ref, bank_ref, norm_ref, members_ref, *refs
):
    message_refs, earlier_refs, best_ref = refs[:messages], refs[messages:-1], refs[-1]
    results, _, _ = score_group(
        [(message, 0) for message in message_refs],
        capacity,
        block,
        bank_ref,
        norm_ref,
        members_ref,
    )
    for group in reversed(earlier_refs):
        results = [group[pl.ds(number, 1), :] for number in range(group.shape[0])] + results
    for value, place in zip(results, places):
        best_ref[pl.ds(me_ref[0] ^ place, 1), :] = value


def finish_kernel(pieces, match_ref, best_ref, stored_ref, own_ref, *refs):
    terms, (row_ref, out_ref, held_ref, semaphore) = refs[:-4], refs[-4:]
    rows = own_ref.shape[0] // pieces
    copies = []
    for number in range(pieces):
        part = pl.ds(number * rows, rows)
        total = stored_ref[part, :] + own_ref[part, :]
        for term in terms:
            total = total + term[part, :].astype(jnp.float32)
        held_ref[part, :] = total / jnp.sqrt(
            jnp.sum(total * total, axis=1, keepdims=True) + epsilon
        )
        copies.append(
            pltpu.make_async_copy(held_ref.at[part], out_ref.at[part], semaphore.at[number])
        )
        copies[-1].start()
    owners, capacity = best_ref.shape
    best = jnp.concatenate([best_ref[pl.ds(number, 1), :] for number in range(owners)], axis=1)
    row = lax.broadcasted_iota(jnp.int32, (INFO_ROWS, owners * capacity), 0)
    table = jnp.zeros(row.shape, jnp.float32)
    for number, term in enumerate(split_exactly(best)):
        table = jnp.where(row == number, term.astype(jnp.float32), table)
    spread = jnp.dot(table.astype(jnp.bfloat16), match_ref[...], preferred_element_type=jnp.float32)
    row_ref[...] = spread[0:1] + spread[1:2] + spread[2:3]
    for copy in copies:
        copy.wait()


def in_hbm(value):
    return pltpu.with_memory_space_constraint(value, pltpu.HBM)


def exchange(value, axis, offset):
    size = lax.axis_size(axis)
    return lax.ppermute(value, axis, [(device, device ^ offset) for device in range(size)])


def body(arrivals, home_owner, cluster_slot, bank, members, centroid_sum):
    owners = lax.axis_size("own")
    parts = lax.axis_size("grp")
    rows, width = arrivals.shape
    clusters, depth = bank.shape[0], bank.shape[1]
    capacity = 2 * rows // owners
    own_index = lax.axis_index("own").astype(jnp.int32).reshape(1)
    smem = pl.BlockSpec(memory_space=pltpu.SMEM)
    anywhere = pl.BlockSpec(memory_space=pl.ANY)
    quarter = owners // 4
    block_size = block_rows(capacity, width)
    message = jax.ShapeDtypeStruct((block_size, LANES), jnp.bfloat16)
    pair = jax.ShapeDtypeStruct((2 * block_size, LANES), jnp.bfloat16)
    first, last = list(range(quarter)), list(range(3 * quarter, owners))
    same_core = list(range(quarter, 3 * quarter, 2))[::-1]
    other_core = [peer + 1 for peer in same_core]
    groups = [first, same_core, other_core, last]
    block = min(clusters, 32)

    def vmem_call(
        kernel, name, out_shape, operands, in_specs=None, scratch_shapes=(), out_specs=None
    ):
        out_specs = out_specs or jax.tree.map(lambda _: whole_vmem(), out_shape)
        return pl.pallas_call(
            kernel,
            out_shape=out_shape,
            in_specs=in_specs or [whole_vmem()] * len(operands),
            out_specs=out_specs,
            scratch_shapes=scratch_shapes,
            compiler_params=small_params(),
            cost_estimate=pl.CostEstimate(
                flops=COSTS.get(name, 1), bytes_accessed=1, transcendentals=0
            ),
            name=name,
        )(*operands)

    row = jax.ShapeDtypeStruct((1, rows), jnp.int32)
    return_index, *sent = vmem_call(
        functools.partial(pack_kernel, owners, capacity),
        "pack",
        [row] + [message] * quarter + [pair] * quarter + [message] * quarter,
        [
            own_index,
            in_hbm(home_owner.reshape(1, rows)),
            in_hbm(cluster_slot.reshape(1, rows)),
            in_hbm(arrivals),
        ],
        [smem] + [anywhere] * 3,
        [
            pltpu.VMEM((1, rows), jnp.int32),
            pltpu.VMEM((1, rows), jnp.int32),
            pltpu.VMEM((rows, width), arrivals.dtype),
            pltpu.SemaphoreType.DMA((3,)),
        ],
    )
    order = dict(zip(first + same_core[::-1] + last, sent))
    got = {
        peer: exchange(order[peer], "own", peer) if peer else order[peer]
        for peer in same_core + last + first
    }
    member_row = members.reshape(1, clusters)
    sums = jax.ShapeDtypeStruct((clusters, width), jnp.float32)

    def scores(group):
        return jax.ShapeDtypeStruct((len(group), capacity), jnp.float32)

    held_bank, bank_norm, best, total = vmem_call(
        functools.partial(first_score_kernel, quarter, capacity, block),
        "first_score",
        [
            pltpu.VMEM(bank.shape, bank.dtype),
            jax.ShapeDtypeStruct((clusters, LANES), jnp.float32),
            scores(first),
            sums,
        ],
        [in_hbm(bank), member_row, *[got[peer] for peer in first]],
        [anywhere] + [whole_vmem()] * (1 + quarter),
        [pltpu.SemaphoreType.DMA((clusters // block,))],
    )
    held_bank = pltpu.with_memory_space_constraint(held_bank, pltpu.VMEM)
    pairs = [got[peer] for peer in same_core]
    passed = vmem_call(
        pass_kernel,
        "pass_on",
        jax.ShapeDtypeStruct((quarter * block_size, LANES), jnp.bfloat16),
        [*pairs, best],
        [whole_vmem()] * quarter + [anywhere],
    )
    passed = exchange(passed, "own", 1)
    results = [best]
    one_hot = jax.ShapeDtypeStruct((owners * capacity, rows), jnp.bfloat16)
    middle = [(pairs, [0]), ([passed], list(range(0, quarter * block_size, block_size)))]
    for number, (operands, bases) in enumerate(middle):
        best, total, *match = vmem_call(
            functools.partial(score_kernel, len(operands), bases, number, capacity, block),
            "score",
            [scores(same_core), sums] + [one_hot] * number,
            [held_bank, bank_norm, member_row, total, *operands, *[return_index] * number],
        )
        results.append(best)
    last_messages = [got[peer] for peer in last]
    own_sum, sent_sum = vmem_call(
        functools.partial(last_sum_kernel, quarter, capacity),
        "last_sum",
        [sums, jax.ShapeDtypeStruct((clusters, width), jnp.bfloat16)],
        [*last_messages, total],
    )
    terms = [exchange(sent_sum, "grp", offset) for offset in range(1, parts)]
    best = vmem_call(
        functools.partial(last_score_kernel, quarter, sum(groups, []), capacity, block),
        "last_score",
        jax.ShapeDtypeStruct((owners, capacity), jnp.float32),
        [own_index, held_bank, bank_norm, member_row, *last_messages, *results],
        [smem] + [whole_vmem()] * (3 + quarter + len(results)),
    )
    returned = lax.all_to_all(best, "own", split_axis=0, concat_axis=0, tiled=True)
    pieces = 4
    best_cosine, centroids = vmem_call(
        functools.partial(finish_kernel, pieces),
        "finish",
        [jax.ShapeDtypeStruct((1, rows), jnp.float32), sums],
        [match[0], returned, centroid_sum, own_sum, *terms],
        scratch_shapes=[
            pltpu.VMEM((clusters, width), jnp.float32),
            pltpu.SemaphoreType.DMA((pieces,)),
        ],
        out_specs=[whole_vmem(), anywhere],
    )
    return (best_cosine.reshape(rows), centroids)


def solution(mesh):
    return jax.shard_map(
        body,
        mesh=mesh,
        in_specs=(
            P(("grp", "own"), None),
            P(("grp", "own"), None),
            P(("grp", "own")),
            P("own", None, None),
            P("own"),
            P("own", None),
        ),
        out_specs=(P(("grp", "own")), P("own", None)),
        check_vma=False,
    )
```

time: 49.7 us -> 50.2 us (1.010)
  starting transfers between devices: 12.6 us -> 17.8 us
  waiting for transfers between devices: 4.21 us -> 1.74 us
  blocking collectives: 9.99 us -> 7.92 us
  Pallas kernels: 22 us -> 21 us
  local copies, waits for them, and re-layouts: 0.01 us -> 0.69 us
    ppermute x10 -> x9, starting transfers between devices: 12.6 us -> 17.8 us  [exchange(): lax.ppermute(value, axis, [(device, device ^ offset) for device in range(...]
    ppermute x10 -> x9, waiting for transfers between devices: 4.21 us -> 1.74 us  [exchange(): lax.ppermute(value, axis, [(device, device ^ offset) for device in range(...]
    all_to_all x1, blocking collectives: 9.99 us -> 7.92 us  [body(): lax.all_to_all(best, 'own', split_axis=0, concat_axis=0, tiled=True)]
    pallas_call x12 -> x8, Pallas kernels: 22 us -> 21 us  [vmem_call(): pl.pallas_call(kernel, out_shape=out_shape, in_specs=in_specs or [whole_v...]
    unnamed x4 -> x6, local copies, waits for them, and re-layouts: 0.01 us -> 0.69 us
  transfers between devices with their start and end apart: 10 -> 9, of which waited for: 1 -> 3; matrix products, arithmetic and copies ran while one was open for 0% -> 0% of each run, Pallas kernels for 38% -> 34%
where the time goes in v5:
time: 50.2 us; the launch traced here: 50 us
  Pallas kernels  21 us (42%)
  starting transfers between devices  17.8 us (35%)
  blocking collectives  7.92 us (16%)
  waiting for transfers between devices  1.74 us (3%)
  between operations  0.89 us (2%)
  local copies, waits for them, and re-layouts  0.69 us (1%)
    pallas_call x8, Pallas kernels, vmem_call(): pl.pallas_call(kernel, out_shape=out_shape, in_specs=in_specs or [whole_v...  21 us
    ppermute x9, starting transfers between devices, exchange(): lax.ppermute(value, axis, [(device, device ^ offset) for device in range(...  17.8 us
    all_to_all x1, blocking collectives, body(): lax.all_to_all(best, 'own', split_axis=0, concat_axis=0, tiled=True)  7.92 us
    ppermute x9, waiting for transfers between devices, exchange(): lax.ppermute(value, axis, [(device, device ^ offset) for device in range(...  1.74 us
  transfers between devices with their start and end apart: 9, of which 3 were waited for; matrix products, arithmetic and copies ran while one was open for 0% of the time, Pallas kernels for 34%

profile of v5, /device:TPU:0, one launch (start us, length us, event | category | flops | bytes accessed | tf_op | source)
XLA Modules:
  0.0 50.0 jit_solution(5193111326413577961)
XLA Ops:
  0.6 2.0 %pack.1 = (s32[1,512]{1,0:T(1,128)S(1)}, bf16[528,128]{1,0:T(8,128)(2,1)S(1)}, bf16[528,128]{1,0:T(8,128)(2,1)S(1)}, bf16[1056,128]{1,0:T(8,128)(2,1)S(1)}, bf16...) custom-call(s32[1]{0:T(128)} %bitcast.1.me_ref, s32[1,512]{1,0:T(1,128)} %bitcast.15, ...), custom_call_target="tpu_custom_call" | custom-call | flops 1 | bytes 1 | tf_op jit(solution)/shard_map/pack/pallas_call | solution.py:332
  2.7 4.1 %collective-permute-start.1 = (bf16[1056,128]{1,0:T(8,128)(2,1)S(1)}, bf16[1056,128]{1,0:T(8,128)(2,1)S(1)}, u32[]{:S(2)}, u32[]{:S(2)}) collective-permute-start(bf16[1056,128]{1,0:T(8,128)(2,1)S(1)} %get-tuple-element.27), channel_id=1, source_target_pairs={{0,4},{1,5},{2,6},{3,7},{4,0},{5,1},{6,2},{7,3},{8,12},{9,13},{10,... | collective-permute-start | bytes 811016 | tf_op jit(solution)/shard_map/ppermute | solution.py:306
  6.8 1.6 %collective-permute-start.2 = (bf16[1056,128]{1,0:T(8,128)(2,1)S(1)}, bf16[1056,128]{1,0:T(8,128)(2,1)S(1)}, u32[]{:S(2)}, u32[]{:S(2)}) collective-permute-start(bf16[1056,128]{1,0:T(8,128)(2,1)S(1)} %get-tuple-element.28), channel_id=1, source_target_pairs={{0,2},{1,3},{2,0},{3,1},{4,6},{5,7},{6,4},{7,5},{8,10},{9,11},{10,... | collective-permute-start | bytes 811016 | tf_op jit(solution)/shard_map/ppermute | solution.py:306
  8.4 0.0 collective-permute-start
  8.4 0.0 collective-permute-start.4
  8.4 3.7 %collective-permute-start.5 = (bf16[528,128]{1,0:T(8,128)(2,1)S(1)}, bf16[528,128]{1,0:T(8,128)(2,1)S(1)}, u32[]{:S(2)}, u32[]{:S(2)}) collective-permute-start(bf16[528,128]{1,0:T(8,128)(2,1)S(1)} %get-tuple-element.34), channel_id=1, source_target_pairs={{0,7},{1,6},{2,5},{3,4},{4,3},{5,2},{6,1},{7,0},{8,15},{9,14},{10,... | collective-permute-start | bytes 405512 | tf_op jit(solution)/shard_map/ppermute | solution.py:306
  12.0 0.0 collective-permute-done.refs_1_
  12.0 0.0 copy-start.1
  12.0 0.7 %copy-done.1 = s32[256]{0:T(256)S(1)} copy-done((s32[256]{0:T(256)S(1)}, s32[256]{0:T(256)}, u32[]{:S(2)}) %copy-start.1) | copy-done | bytes 1048
  12.7 7.7 %first_score.1 = (bf16[256,32,512]{2,1,0:T(8,128)(2,1)S(1)}, f32[256,128]{1,0:T(8,128)S(1)}, f32[2,128]{1,0:T(2,128)S(1)}, f32[256,512]{1,0:T(8,128)S(1)}) custom-call(bf16[256,32,512]{2,1,0:T(8,128)(2,1)} %bank_ref.1, s32[1,256]{1,0:T(1,128)S(1)} %bitcast.11, bf16[528,128]{1,0:T(8,128)(2,1)S(1)} %get-tuple-element.22.refs_0_, ...), custom_call_target="tpu_custom_call" | custom-call | flops 1 | bytes 1 | tf_op jit(solution)/shard_map/first_score/pallas_call | solution.py:332
  20.4 0.4 collective-permute-done.1.refs_0_
  20.8 0.0 collective-permute-done.2.refs_1_
  20.8 0.1 collective-permute-start.3
  20.9 2.9 %score.2 = (f32[2,128]{1,0:T(2,128)S(1)}, f32[256,512]{1,0:T(8,128)S(1)}) custom-call(bf16[256,32,512]{2,1,0:T(8,128)(2,1)S(1)} %get-tuple-element.24.bank_ref, f32[256,128]{1,0:T(8,128)S(1)} %get-tuple-element.25.norm_ref, s32[1,256]{1,0:T(1,128)S(1)} %bitcast.12, f32[256,512]{1,0:T(8,128)S(1)} %get-tuple-element.26.before_ref, ...), custom_call_target="tpu_custom_call" | custom-call | flops 10000000000 | bytes 1 | tf_op jit(solution)/shard_map/score/pallas_call | solution.py:332
  23.8 0.0 collective-permute-done.3.refs_0_
  23.8 0.0 copy-start.2
  23.8 3.3 %score.3 = (f32[2,128]{1,0:T(2,128)S(1)}, f32[256,512]{1,0:T(8,128)S(1)}, bf16[1024,512]{1,0:T(8,128)(2,1)S(1)}) custom-call(bf16[256,32,512]{2,1,0:T(8,128)(2,1)S(1)} %get-tuple-element.24.bank_ref, f32[256,128]{1,0:T(8,128)S(1)} %get-tuple-element.25.norm_ref, s32[1,256]{1,0:T(1,128)S(1)} %bitcast.13, f32[256,512]{1,0:T(8,128)S(1)} %get-tuple-element.29.before_ref, ...), custom_call_target="tpu_custom_call" | custom-call | flops 10000000000 | bytes 1 | tf_op jit(solution)/shard_map/score/pallas_call | solution.py:332
  27.1 0.0 copy-start
  27.1 0.0 collective-permute-done.4.refs_0_
  27.1 0.0 collective-permute-done.5.refs_1_
  27.2 0.4 last_sum.1
  27.5 7.8 %collective-permute-start.8 = (bf16[256,512]{1,0:T(8,128)(2,1)S(1)}, bf16[256,512]{1,0:T(8,128)(2,1)S(1)}, u32[]{:S(2)}, u32[]{:S(2)}) collective-permute-start(bf16[256,512]{1,0:T(8,128)(2,1)S(1)} %get-tuple-element.39), channel_id=1, source_target_pairs={{0,24},{8,16},{16,8},{24,0},{1,25},{9,17},{17,9},{25,1},{2,26},{10... | collective-permute-start | bytes 786440 | tf_op jit(solution)/shard_map/ppermute | solution.py:306
  35.3 0.5 %collective-permute-start.7 = (bf16[256,512]{1,0:T(8,128)(2,1)S(1)}, bf16[256,512]{1,0:T(8,128)(2,1)S(1)}, u32[]{:S(2)}, u32[]{:S(2)}) collective-permute-start(bf16[256,512]{1,0:T(8,128)(2,1)S(1)} %get-tuple-element.39), channel_id=1, source_target_pairs={{0,16},{8,24},{16,0},{24,8},{1,17},{9,25},{17,1},{25,9},{2,18},{10... | collective-permute-start | bytes 786440 | tf_op jit(solution)/shard_map/ppermute | solution.py:306
  35.8 0.1 collective-permute-start.6
  36.0 0.0 copy-done.2
  36.0 3.0 %last_score.1 = f32[8,128]{1,0:T(8,128)S(1)} custom-call(s32[1]{0:T(128)} %bitcast.1.me_ref, bf16[256,32,512]{2,1,0:T(8,128)(2,1)S(1)} %get-tuple-element.24.bank_ref, f32[256,128]{1,0:T(8,128)S(1)} %get-tuple-element.25.norm_ref, s32[1,256]{1,0:T(1,128)S(1)} %bitcast.14, bf16[528,128]{1,0:T(8,128)(2,1)S(1)} %collective-permute-done.4.refs_0_, ...), custom_call_target="tpu_custom_call" | custom-call | flops 1 | bytes 1 | tf_op jit(solution)/shard_map/last_score/pallas_call | solution.py:332
  39.0 7.9 %all_to_all.11 = f32[8,1,128]{2,1,0:T(1,128)S(1)} all-to-all(f32[8,1,128]{2,1,0:T(1,128)S(1)} %bitcast.10), channel_id=1, replica_groups=mesh['grp'=4,'own'=8] {'own'}, dimensions={0} | all-to-all | bytes 8192 | tf_op jit(solution)/shard_map/all_to_all | solution.py:424
  46.9 0.0 collective-permute-done.8.refs_2_
  46.9 1.0 %collective-permute-done.7.refs_1_ = bf16[256,512]{1,0:T(8,128)(2,1)S(1)} collective-permute-done((bf16[256,512]{1,0:T(8,128)(2,1)S(1)}, bf16[256,512]{1,0:T(8,128)(2,1)S(1)}, u32[]{:S(2)}, u32[]{:S(2)}) %collective-permute-start.7) | collective-permute-done | bytes 262176 | tf_op jit(solution)/shard_map/ppermute | solution.py:306
  47.9 0.3 collective-permute-done.6.refs_0_
  48.2 0.0 copy-done
  48.2 1.7 %finish.1 = (f32[1,512]{1,0:T(1,128)}, f32[256,512]{1,0:T(8,128)}) custom-call(bf16[1024,512]{1,0:T(8,128)(2,1)S(1)} %get-tuple-element.32.match_ref, f32[8,128]{1,0:T(8,128)S(1)} %bitcast.9, f32[256,512]{1,0:T(8,128)S(1)} %copy-done, f32[256,512]{1,0:T(8,128)S(1)} %get-tuple-element.38.own_ref, bf16[256,512]{1,0:T(8,128)(2,1)S(1)} %collective-permute-done.6.refs_0_, ...), custom_call_target="tpu_custom_call" | custom-call | flops 1 | bytes 1 | tf_op jit(solution)/shard_map/finish/pallas_call | solution.py:332
  (1 shorter events, 0.0 us)
Async XLA Ops:
  2.7 18.1 %collective-permute-start.1 = (bf16[1056,128]{1,0:T(8,128)(2,1)S(1)}, bf16[1056,128]{1,0:T(8,128)(2,1)S(1)}, u32[]{:S(2)}, u32[]{:S(2)}) collective-permute-start(bf16[1056,128]{1,0:T(8,128)(2,1)S(1)} %get-tuple-element.27), channel_id=1, source_target_pairs={{0,4},{1,5},{2,6},{3,7},{4,0},{5,1},{6,2},{7,3},{8,12},{9,13},{10,... | collective-permute-start | bytes 811016 | tf_op jit(solution)/shard_map/ppermute | solution.py:306
  6.8 14.0 %collective-permute-start.2 = (bf16[1056,128]{1,0:T(8,128)(2,1)S(1)}, bf16[1056,128]{1,0:T(8,128)(2,1)S(1)}, u32[]{:S(2)}, u32[]{:S(2)}) collective-permute-start(bf16[1056,128]{1,0:T(8,128)(2,1)S(1)} %get-tuple-element.28), channel_id=1, source_target_pairs={{0,2},{1,3},{2,0},{3,1},{4,6},{5,7},{6,4},{7,5},{8,10},{9,11},{10,... | collective-permute-start | bytes 811016 | tf_op jit(solution)/shard_map/ppermute | solution.py:306
  8.4 3.7 %collective-permute-start = (bf16[528,128]{1,0:T(8,128)(2,1)S(1)}, bf16[528,128]{1,0:T(8,128)(2,1)S(1)}, u32[]{:S(2)}, u32[]{:S(2)}) collective-permute-start(bf16[528,128]{1,0:T(8,128)(2,1)S(1)} %get-tuple-element.23), channel_id=1, source_target_pairs={{0,1},{1,0},{2,3},{3,2},{4,5},{5,4},{6,7},{7,6},{8,9},{9,8},{10,11... | collective-permute-start | bytes 405512 | tf_op jit(solution)/shard_map/ppermute | solution.py:306
  8.4 18.8 %collective-permute-start.4 = (bf16[528,128]{1,0:T(8,128)(2,1)S(1)}, bf16[528,128]{1,0:T(8,128)(2,1)S(1)}, u32[]{:S(2)}, u32[]{:S(2)}) collective-permute-start(bf16[528,128]{1,0:T(8,128)(2,1)S(1)} %get-tuple-element.33), channel_id=1, source_target_pairs={{0,6},{1,7},{2,4},{3,5},{4,2},{5,3},{6,0},{7,1},{8,14},{9,15},{10,... | collective-permute-start | bytes 405512 | tf_op jit(solution)/shard_map/ppermute | solution.py:306
  8.4 18.8 %collective-permute-start.5 = (bf16[528,128]{1,0:T(8,128)(2,1)S(1)}, bf16[528,128]{1,0:T(8,128)(2,1)S(1)}, u32[]{:S(2)}, u32[]{:S(2)}) collective-permute-start(bf16[528,128]{1,0:T(8,128)(2,1)S(1)} %get-tuple-element.34), channel_id=1, source_target_pairs={{0,7},{1,6},{2,5},{3,4},{4,3},{5,2},{6,1},{7,0},{8,15},{9,14},{10,... | collective-permute-start | bytes 405512 | tf_op jit(solution)/shard_map/ppermute | solution.py:306
  12.0 0.7 %copy-start.1 = (s32[256]{0:T(256)S(1)}, s32[256]{0:T(256)}, u32[]{:S(2)}) copy-start(s32[256]{0:T(256)} %param.10) | copy-start | bytes 3076
  20.8 3.0 %collective-permute-start.3 = (bf16[1056,128]{1,0:T(8,128)(2,1)S(1)}, bf16[1056,128]{1,0:T(8,128)(2,1)S(1)}, u32[]{:S(2)}, u32[]{:S(2)}) collective-permute-start(bf16[1056,128]{1,0:T(8,128)(2,1)S(1)} %pass_on.1), channel_id=1, source_target_pairs={{0,1},{1,0},{2,3},{3,2},{4,5},{5,4},{6,7},{7,6},{8,9},{9,8},{10,11... | collective-permute-start | bytes 811016 | tf_op jit(solution)/shard_map/ppermute | solution.py:306
  23.8 12.1 %copy-start.2 = (s32[256]{0:T(256)S(1)}, s32[256]{0:T(256)}, u32[]{:S(2)}) copy-start(s32[256]{0:T(256)} %param.10) | copy-start | bytes 3076
  27.1 21.1 %copy-start = (f32[256,512]{1,0:T(8,128)S(1)}, f32[256,512]{1,0:T(8,128)}, u32[]{:S(2)}) copy-start(f32[256,512]{1,0:T(8,128)} %stored_ref.1) | copy-start | bytes 1572868
  27.5 19.3 %collective-permute-start.8 = (bf16[256,512]{1,0:T(8,128)(2,1)S(1)}, bf16[256,512]{1,0:T(8,128)(2,1)S(1)}, u32[]{:S(2)}, u32[]{:S(2)}) collective-permute-start(bf16[256,512]{1,0:T(8,128)(2,1)S(1)} %get-tuple-element.39), channel_id=1, source_target_pairs={{0,24},{8,16},{16,8},{24,0},{1,25},{9,17},{17,9},{25,1},{2,26},{10... | collective-permute-start | bytes 786440 | tf_op jit(solution)/shard_map/ppermute | solution.py:306
  35.3 12.6 %collective-permute-start.7 = (bf16[256,512]{1,0:T(8,128)(2,1)S(1)}, bf16[256,512]{1,0:T(8,128)(2,1)S(1)}, u32[]{:S(2)}, u32[]{:S(2)}) collective-permute-start(bf16[256,512]{1,0:T(8,128)(2,1)S(1)} %get-tuple-element.39), channel_id=1, source_target_pairs={{0,16},{8,24},{16,0},{24,8},{1,17},{9,25},{17,1},{25,9},{2,18},{10... | collective-permute-start | bytes 786440 | tf_op jit(solution)/shard_map/ppermute | solution.py:306
  35.8 12.4 %collective-permute-start.6 = (bf16[256,512]{1,0:T(8,128)(2,1)S(1)}, bf16[256,512]{1,0:T(8,128)(2,1)S(1)}, u32[]{:S(2)}, u32[]{:S(2)}) collective-permute-start(bf16[256,512]{1,0:T(8,128)(2,1)S(1)} %get-tuple-element.39), channel_id=1, source_target_pairs={{0,8},{8,0},{16,24},{24,16},{1,9},{9,1},{17,25},{25,17},{2,10},{10... | collective-permute-start | bytes 786440 | tf_op jit(solution)/shard_map/ppermute | solution.py:306

commit v6 on v5

--- a/solution.py
+++ b/solution.py
@@ -11,7 +11,7 @@
 LANES = 128
 INFO_ROWS = 16
 CODE_BASE = 128
-COSTS = {"score": 10**10}
+COSTS = {"score": 10**10, "pair_sum": 10**10, "first_sum": 10**10}
 SMALL_VMEM = 32 * 1024 * 1024
 
 
@@ -42,7 +42,7 @@
     return width // LANES * capacity + INFO_ROWS
 
 
-def write_blocks(capacity, index, slot, values, targets):
+def write_blocks(capacity, first_peer, index, slot, values, targets):
     rows, width = values.shape
     code_row = lax.broadcasted_iota(jnp.int32, (INFO_ROWS, rows), 0)
     codes = jnp.where(
@@ -51,16 +51,17 @@
         jnp.where(code_row == 1, slot % CODE_BASE, 0),
     )
     codes = codes.astype(jnp.float32).astype(jnp.bfloat16)
-    peers = len(targets) // 4
+    peers = max(1, 256 // capacity)
     for start in range(0, len(targets), peers):
-        place = lax.broadcasted_iota(jnp.int32, (peers * capacity, rows), 0)
-        match = place + start * capacity == index
+        chosen = targets[start : start + peers]
+        place = lax.broadcasted_iota(jnp.int32, (len(chosen) * capacity, rows), 0)
+        match = place + (first_peer + start) * capacity == index
         match = match.astype(jnp.float32).astype(jnp.bfloat16)
         packed = jnp.dot(match, values, preferred_element_type=jnp.float32).astype(jnp.bfloat16)
         info = lax.dot_general(
             codes, match, (((1,), (1,)), ((), ())), preferred_element_type=jnp.float32
         )
-        for number, (target, base) in enumerate(targets[start : start + peers]):
+        for number, (target, base) in enumerate(chosen):
             low = number * capacity
             for part in range(width // LANES):
                 target[pl.ds(base + part * capacity, capacity), :] = packed[
@@ -76,9 +77,16 @@
             )
 
 
-def pack_kernel(owners, capacity, me_ref, *refs):
-    sources, return_ref, messages = refs[:3], refs[3], refs[4:-4]
-    held, semaphore = refs[-4:-1], refs[-1]
+def blocks_of(messages, capacity, width):
+    size = block_rows(capacity, width)
+    return [(message, base) for message in messages for base in range(0, message.shape[0], size)]
+
+
+def pack_kernel(owners, capacity, first_peers, me_ref, *refs):
+    sources, return_ref, index_ref, held, messages = (
+        refs[:3], refs[3], refs[4], refs[5:8], refs[8:-1]
+    )
+    semaphore = refs[-1]
     copies = [
         pltpu.make_async_copy(source, target, semaphore.at[number])
         for number, (source, target) in enumerate(zip(sources, held))
@@ -90,14 +98,25 @@
     owner = held[0][...]
     placed = place_rows(owners, owner)
     return_ref[...] = owner * capacity + placed
+    index = (owner ^ me_ref[0]) * capacity + placed
+    index_ref[...] = index
     copies[2].wait()
-    block = block_rows(capacity, held[2].shape[1])
-    targets = [
-        (message, base) for message in messages for base in range(0, message.shape[0], block)
-    ]
-    write_blocks(
-        capacity, (owner ^ me_ref[0]) * capacity + placed, held[1][...], held[2][...], targets
-    )
+    targets = blocks_of(messages, capacity, held[2].shape[1])
+    quarter = len(targets) // len(first_peers)
+    for number, first_peer in enumerate(first_peers):
+        write_blocks(
+            capacity,
+            first_peer,
+            index,
+            held[1][...],
+            held[2][...],
+            targets[number * quarter : (number + 1) * quarter],
+        )
+
+
+def late_pack_kernel(capacity, first_peer, index_ref, slot_ref, rows_ref, after_ref, *messages):
+    targets = blocks_of(messages, capacity, rows_ref.shape[1])
+    write_blocks(capacity, first_peer, index_ref[...], slot_ref[...], rows_ref[...], targets)
 
 
 def pass_kernel(*refs):
@@ -170,7 +189,7 @@
 
 def first_score_kernel(messages, capacity, block, bank_ref, members_ref, *refs):
     message_refs = refs[:messages]
-    held_ref, norm_ref, best_ref, sum_ref, semaphore = refs[messages:]
+    held_ref, norm_ref, *best_refs, semaphore = refs[messages:]
     clusters, depth, width = held_ref.shape
     copies = []
     for number in range(clusters // block):
@@ -181,7 +200,6 @@
         copies[-1].start()
     units, slots = read_blocks([(message, 0) for message in message_refs], capacity, width)
     onehot = cluster_onehot(slots, clusters)
-    sum_ref[...] = jnp.dot(onehot, units, preferred_element_type=jnp.float32)
     columns = units.T
     picked = jnp.zeros((depth, slots.shape[1]), jnp.float32)
     shape = (block, depth, LANES)
@@ -197,8 +215,8 @@
         square = jnp.sum(values * values, axis=2, keepdims=True)
         norm_ref[part, :] = jnp.sqrt(jnp.sum(jnp.where(own_lane, square, 0.0), axis=1) + epsilon)
     best = best_cosines(picked, onehot, norm_ref[...], members_ref[...])
-    for number in range(messages):
-        best_ref[pl.ds(number, 1), :] = best[:, number * capacity : (number + 1) * capacity]
+    for number, best_ref in enumerate(best_refs):
+        best_ref[...] = best[:, number * capacity : (number + 1) * capacity]
 
 
 def score_group(blocks, capacity, block, bank_ref, norm_ref, members_ref):
@@ -219,25 +237,50 @@
 
 
 def score_kernel(
-    messages, bases, match, capacity, block, bank_ref, norm_ref, members_ref, before_ref, *refs
+    pairs, capacity, block, bank_ref, norm_ref, members_ref, before_ref, *refs
 ):
-    message_refs, refs = refs[:messages], refs[messages:]
+    pair_refs, passed_ref, refs = refs[:pairs], refs[pairs], refs[pairs + 1 :]
     results, onehot, units = score_group(
-        [(message, base) for message in message_refs for base in bases],
+        [(pair, 0) for pair in pair_refs] + blocks_of([passed_ref], capacity, bank_ref.shape[2]),
         capacity,
         block,
         bank_ref,
         norm_ref,
         members_ref,
     )
-    best_ref, sum_ref = refs[match : match + 2]
-    for number, value in enumerate(results):
-        best_ref[pl.ds(number, 1), :] = value
+    *best_refs, sum_ref = refs
+    for best_ref, value in zip(best_refs, results):
+        best_ref[...] = value
     sum_ref[...] = before_ref[...] + jnp.dot(onehot, units, preferred_element_type=jnp.float32)
-    if match:
-        index_ref, match_ref = refs[0], refs[3]
-        place = lax.broadcasted_iota(jnp.int32, match_ref.shape, 0)
-        match_ref[...] = (place == index_ref[...]).astype(jnp.float32).astype(jnp.bfloat16)
+
+
+def first_sum_kernel(messages, capacity, *refs):
+    message_refs, total_ref = refs[:messages], refs[-1]
+    clusters, width = total_ref.shape
+    units, slots = read_blocks([(message, 0) for message in message_refs], capacity, width)
+    total_ref[...] = jnp.dot(
+        cluster_onehot(slots, clusters), units, preferred_element_type=jnp.float32
+    )
+
+
+def pair_score_kernel(pairs, capacity, block, bank_ref, norm_ref, members_ref, *refs):
+    pair_refs, passed_ref, best_refs = refs[:pairs], refs[pairs], refs[pairs + 1 :]
+    blocks = [(pair, 0) for pair in pair_refs] + blocks_of(
+        [passed_ref], capacity, bank_ref.shape[2]
+    )
+    results, _, _ = score_group(blocks, capacity, block, bank_ref, norm_ref, members_ref)
+    for best_ref, value in zip(best_refs, results):
+        best_ref[...] = value
+
+
+def pair_sum_kernel(pairs, capacity, *refs):
+    pair_refs, passed_ref, before_ref, total_ref = refs[:pairs], *refs[pairs:]
+    clusters, width = total_ref.shape
+    blocks = [(pair, 0) for pair in pair_refs] + blocks_of([passed_ref], capacity, width)
+    units, slots = read_blocks(blocks, capacity, width)
+    total_ref[...] = before_ref[...] + jnp.dot(
+        cluster_onehot(slots, clusters), units, preferred_element_type=jnp.float32
+    )
 
 
 def last_sum_kernel(messages, capacity, *refs):
@@ -263,14 +306,26 @@
         norm_ref,
         members_ref,
     )
-    for group in reversed(earlier_refs):
-        results = [group[pl.ds(number, 1), :] for number in range(group.shape[0])] + results
-    for value, place in zip(results, places):
+    for value, place in zip([ref[...] for ref in earlier_refs] + results, places):
         best_ref[pl.ds(me_ref[0] ^ place, 1), :] = value
 
 
-def finish_kernel(pieces, match_ref, best_ref, stored_ref, own_ref, *refs):
-    terms, (row_ref, out_ref, held_ref, semaphore) = refs[:-4], refs[-4:]
+def unpack_kernel(index_ref, best_ref, out_ref):
+    best = jnp.concatenate(
+        [best_ref[pl.ds(number, 1), :] for number in range(best_ref.shape[0])], axis=1
+    )
+    row = lax.broadcasted_iota(jnp.int32, (INFO_ROWS, best.shape[1]), 0)
+    table = jnp.zeros(row.shape, jnp.float32)
+    for number, term in enumerate(split_exactly(best)):
+        table = jnp.where(row == number, term.astype(jnp.float32), table)
+    place = lax.broadcasted_iota(jnp.int32, (best.shape[1], index_ref.shape[1]), 0)
+    match = (place == index_ref[...]).astype(jnp.float32).astype(jnp.bfloat16)
+    spread = jnp.dot(table.astype(jnp.bfloat16), match, preferred_element_type=jnp.float32)
+    out_ref[...] = spread[0:1] + spread[1:2] + spread[2:3]
+
+
+def finish_kernel(pieces, stored_ref, own_ref, *refs):
+    terms, (out_ref, held_ref, semaphore) = refs[:-3], refs[-3:]
     rows = own_ref.shape[0] // pieces
     copies = []
     for number in range(pieces):
@@ -285,14 +340,6 @@
             pltpu.make_async_copy(held_ref.at[part], out_ref.at[part], semaphore.at[number])
         )
         copies[-1].start()
-    owners, capacity = best_ref.shape
-    best = jnp.concatenate([best_ref[pl.ds(number, 1), :] for number in range(owners)], axis=1)
-    row = lax.broadcasted_iota(jnp.int32, (INFO_ROWS, owners * capacity), 0)
-    table = jnp.zeros(row.shape, jnp.float32)
-    for number, term in enumerate(split_exactly(best)):
-        table = jnp.where(row == number, term.astype(jnp.float32), table)
-    spread = jnp.dot(table.astype(jnp.bfloat16), match_ref[...], preferred_element_type=jnp.float32)
-    row_ref[...] = spread[0:1] + spread[1:2] + spread[2:3]
     for copy in copies:
         copy.wait()
 
@@ -320,9 +367,8 @@
     message = jax.ShapeDtypeStruct((block_size, LANES), jnp.bfloat16)
     pair = jax.ShapeDtypeStruct((2 * block_size, LANES), jnp.bfloat16)
     first, last = list(range(quarter)), list(range(3 * quarter, owners))
-    same_core = list(range(quarter, 3 * quarter, 2))[::-1]
-    other_core = [peer + 1 for peer in same_core]
-    groups = [first, same_core, other_core, last]
+    far_pairs, near_pairs = (list(range(start, start + quarter, 2)) for start in (2 * quarter, quarter))
+    order = first + [peer + core for pairs in (far_pairs, near_pairs) for core in (0, 1) for peer in pairs] + last
     block = min(clusters, 32)
 
     def vmem_call(
@@ -343,10 +389,15 @@
         )(*operands)
 
     row = jax.ShapeDtypeStruct((1, rows), jnp.int32)
-    return_index, *sent = vmem_call(
-        functools.partial(pack_kernel, owners, capacity),
+    pair_count = quarter // 2
+    return_index, index, _, slots, values, *sent = vmem_call(
+        functools.partial(pack_kernel, owners, capacity, (0, 2 * quarter, 3 * quarter)),
         "pack",
-        [row] + [message] * quarter + [pair] * quarter + [message] * quarter,
+        [row] * 4
+        + [jax.ShapeDtypeStruct((rows, width), arrivals.dtype)]
+        + [message] * quarter
+        + [pair] * pair_count
+        + [message] * quarter,
         [
             own_index,
             in_hbm(home_owner.reshape(1, rows)),
@@ -354,85 +405,111 @@
             in_hbm(arrivals),
         ],
         [smem] + [anywhere] * 3,
-        [
-            pltpu.VMEM((1, rows), jnp.int32),
-            pltpu.VMEM((1, rows), jnp.int32),
-            pltpu.VMEM((rows, width), arrivals.dtype),
-            pltpu.SemaphoreType.DMA((3,)),
-        ],
-    )
-    order = dict(zip(first + same_core[::-1] + last, sent))
+        [pltpu.SemaphoreType.DMA((3,))],
+    )
+    packed = dict(zip(first + far_pairs + last, sent))
     got = {
-        peer: exchange(order[peer], "own", peer) if peer else order[peer]
-        for peer in same_core + last + first
+        peer: exchange(packed[peer], "own", peer) if peer else packed[peer]
+        for peer in far_pairs + last + first
     }
     member_row = members.reshape(1, clusters)
     sums = jax.ShapeDtypeStruct((clusters, width), jnp.float32)
 
-    def scores(group):
-        return jax.ShapeDtypeStruct((len(group), capacity), jnp.float32)
-
-    held_bank, bank_norm, best, total = vmem_call(
+    results = [jax.ShapeDtypeStruct((1, capacity), jnp.float32)] * quarter
+    held_bank, bank_norm, *best = vmem_call(
         functools.partial(first_score_kernel, quarter, capacity, block),
         "first_score",
         [
             pltpu.VMEM(bank.shape, bank.dtype),
             jax.ShapeDtypeStruct((clusters, LANES), jnp.float32),
-            scores(first),
-            sums,
+            *results,
         ],
         [in_hbm(bank), member_row, *[got[peer] for peer in first]],
         [anywhere] + [whole_vmem()] * (1 + quarter),
         [pltpu.SemaphoreType.DMA((clusters // block,))],
     )
     held_bank = pltpu.with_memory_space_constraint(held_bank, pltpu.VMEM)
-    pairs = [got[peer] for peer in same_core]
-    passed = vmem_call(
-        pass_kernel,
-        "pass_on",
-        jax.ShapeDtypeStruct((quarter * block_size, LANES), jnp.bfloat16),
-        [*pairs, best],
+    near = vmem_call(
+        functools.partial(late_pack_kernel, capacity, quarter),
+        "late_pack",
+        [pair] * pair_count,
+        [index, slots, values, best[0]],
+        [whole_vmem()] * 3 + [anywhere],
+    )
+    got.update({peer: exchange(value, "own", peer) for peer, value in zip(near_pairs, near)})
+    total = vmem_call(
+        functools.partial(first_sum_kernel, quarter, capacity),
+        "first_sum",
+        sums,
+        [*[got[peer] for peer in first], near[0]],
         [whole_vmem()] * quarter + [anywhere],
     )
-    passed = exchange(passed, "own", 1)
-    results = [best]
-    one_hot = jax.ShapeDtypeStruct((owners * capacity, rows), jnp.bfloat16)
-    middle = [(pairs, [0]), ([passed], list(range(0, quarter * block_size, block_size)))]
-    for number, (operands, bases) in enumerate(middle):
-        best, total, *match = vmem_call(
-            functools.partial(score_kernel, len(operands), bases, number, capacity, block),
-            "score",
-            [scores(same_core), sums] + [one_hot] * number,
-            [held_bank, bank_norm, member_row, total, *operands, *[return_index] * number],
-        )
-        results.append(best)
+    for peers in (far_pairs, near_pairs):
+        pairs = [got[peer] for peer in peers]
+        passed = vmem_call(
+            pass_kernel,
+            "pass_on",
+            jax.ShapeDtypeStruct((pair_count * block_size, LANES), jnp.bfloat16),
+            [*pairs, near[0] if peers is far_pairs else best[-1]],
+            [whole_vmem()] * pair_count + [anywhere],
+        )
+        passed = exchange(passed, "own", 1)
+        if peers is far_pairs:
+            best += vmem_call(
+                functools.partial(pair_score_kernel, pair_count, capacity, block),
+                "score",
+                results,
+                [held_bank, bank_norm, member_row, *pairs, passed],
+            )
+            total = vmem_call(
+                functools.partial(pair_sum_kernel, pair_count, capacity),
+                "pair_sum",
+                sums,
+                [*pairs, passed, total],
+            )
+        else:
+            *found, total = vmem_call(
+                functools.partial(score_kernel, pair_count, capacity, block),
+                "score",
+                results + [sums],
+                [held_bank, bank_norm, member_row, total, *pairs, passed],
+            )
+            best += found
     last_messages = [got[peer] for peer in last]
-    own_sum, sent_sum = vmem_call(
+    total, sent = vmem_call(
         functools.partial(last_sum_kernel, quarter, capacity),
         "last_sum",
         [sums, jax.ShapeDtypeStruct((clusters, width), jnp.bfloat16)],
         [*last_messages, total],
     )
-    terms = [exchange(sent_sum, "grp", offset) for offset in range(1, parts)]
+    terms = [exchange(sent, "grp", offset) for offset in range(1, parts)]
     best = vmem_call(
-        functools.partial(last_score_kernel, quarter, sum(groups, []), capacity, block),
+        functools.partial(
+            last_score_kernel, quarter, order, capacity, block
+        ),
         "last_score",
         jax.ShapeDtypeStruct((owners, capacity), jnp.float32),
-        [own_index, held_bank, bank_norm, member_row, *last_messages, *results],
-        [smem] + [whole_vmem()] * (3 + quarter + len(results)),
+        [own_index, held_bank, bank_norm, member_row, *last_messages, *best],
+        [smem] + [whole_vmem()] * (3 + owners),
     )
     returned = lax.all_to_all(best, "own", split_axis=0, concat_axis=0, tiled=True)
+    best_cosine = vmem_call(
+        unpack_kernel,
+        "unpack",
+        jax.ShapeDtypeStruct((1, rows), jnp.float32),
+        [return_index, returned],
+    )
     pieces = 4
-    best_cosine, centroids = vmem_call(
+    centroids = vmem_call(
         functools.partial(finish_kernel, pieces),
         "finish",
-        [jax.ShapeDtypeStruct((1, rows), jnp.float32), sums],
-        [match[0], returned, centroid_sum, own_sum, *terms],
+        sums,
+        [centroid_sum, total, *terms],
         scratch_shapes=[
             pltpu.VMEM((clusters, width), jnp.float32),
             pltpu.SemaphoreType.DMA((pieces,)),
         ],
-        out_specs=[whole_vmem(), anywhere],
+        out_specs=anywhere,
     )
     return (best_cosine.reshape(rows), centroids)
 

time: 50.2 us -> 54.1 us (1.078)
  waiting for transfers between devices: 1.74 us -> 9.13 us
  starting transfers between devices: 17.8 us -> 11.6 us
  blocking collectives: 7.92 us -> 10.2 us
    ppermute x9 -> x10, waiting for transfers between devices: 1.74 us -> 9.13 us  [exchange(): lax.ppermute(value, axis, [(device, device ^ offset) for device in range(...]
    ppermute x9 -> x10, starting transfers between devices: 17.8 us -> 11.6 us  [exchange(): lax.ppermute(value, axis, [(device, device ^ offset) for device in range(...]
    all_to_all x1, blocking collectives: 7.92 us -> 10.2 us  [body(): lax.all_to_all(best, 'own', split_axis=0, concat_axis=0, tiled=True)]
    pallas_call x8 -> x13, Pallas kernels: 21 us -> 21.4 us  [vmem_call(): pl.pallas_call(kernel, out_shape=out_shape, in_specs=in_specs or [whole_v...]
  transfers between devices with their start and end apart: 9 -> 10, of which waited for: 3 -> 4; matrix products, arithmetic and copies ran while one was open for 0% -> 0% of each run, Pallas kernels for 34% -> 34%
where the time goes in v6:
time: 54.1 us; the launch traced here: 53.9 us
  Pallas kernels  21.4 us (40%)
  starting transfers between devices  11.6 us (21%)
  blocking collectives  10.2 us (19%)
  waiting for transfers between devices  9.13 us (17%)
  between operations  0.93 us (2%)
  local copies, waits for them, and re-layouts  0.69 us (1%)
    pallas_call x13, Pallas kernels, vmem_call(): pl.pallas_call(kernel, out_shape=out_shape, in_specs=in_specs or [whole_v...  21.4 us
    ppermute x10, starting transfers between devices, exchange(): lax.ppermute(value, axis, [(device, device ^ offset) for device in range(...  11.6 us
    all_to_all x1, blocking collectives, body(): lax.all_to_all(best, 'own', split_axis=0, concat_axis=0, tiled=True)  10.2 us
    ppermute x10, waiting for transfers between devices, exchange(): lax.ppermute(value, axis, [(device, device ^ offset) for device in range(...  9.13 us
  transfers between devices with their start and end apart: 10, of which 4 were waited for; matrix products, arithmetic and copies ran while one was open for 0% of the time, Pallas kernels for 34%

profile of v6, /device:TPU:0, one launch (start us, length us, event | category | flops | bytes accessed | tf_op | source)
XLA Modules:
  0.0 53.9 jit_solution(1107486333300897769)
XLA Ops:
  0.6 1.8 %pack.1 = (s32[1,512]{1,0:T(1,128)S(1)}, s32[1,512]{1,0:T(1,128)S(1)}, s32[1,512]{1,0:T(1,128)}, s32[1,512]{1,0:T(1,128)S(1)}, bf16[512,512]{1,0:T(8,128)(2,1)S(...) custom-call(s32[1]{0:T(128)} %bitcast.me_ref, ...), custom_call_target="tpu_custom_call" | custom-call | flops 1 | bytes 1 | tf_op jit(solution)/shard_map/pack/pallas_call | solution.py:378
  2.4 4.1 %collective-permute-start.3 = (bf16[1056,128]{1,0:T(8,128)(2,1)S(1)}, bf16[1056,128]{1,0:T(8,128)(2,1)S(1)}, u32[]{:S(2)}, u32[]{:S(2)}) collective-permute-start(bf16[1056,128]{1,0:T(8,128)(2,1)S(1)} %get-tuple-element.31), channel_id=1, source_target_pairs={{0,4},{1,5},{2,6},{3,7},{4,0},{5,1},{6,2},{7,3},{8,12},{9,13},{10,... | collective-permute-start | bytes 811016 | tf_op jit(solution)/shard_map/ppermute | solution.py:353
  6.5 0.0 collective-permute-start
  6.5 1.3 %collective-permute-start.1 = (bf16[528,128]{1,0:T(8,128)(2,1)S(1)}, bf16[528,128]{1,0:T(8,128)(2,1)S(1)}, u32[]{:S(2)}, u32[]{:S(2)}) collective-permute-start(bf16[528,128]{1,0:T(8,128)(2,1)S(1)} %get-tuple-element.27), channel_id=1, source_target_pairs={{0,6},{1,7},{2,4},{3,5},{4,2},{5,3},{6,0},{7,1},{8,14},{9,15},{10,... | collective-permute-start | bytes 405512 | tf_op jit(solution)/shard_map/ppermute | solution.py:353
  7.9 2.3 %collective-permute-start.2 = (bf16[528,128]{1,0:T(8,128)(2,1)S(1)}, bf16[528,128]{1,0:T(8,128)(2,1)S(1)}, u32[]{:S(2)}, u32[]{:S(2)}) collective-permute-start(bf16[528,128]{1,0:T(8,128)(2,1)S(1)} %get-tuple-element.28), channel_id=1, source_target_pairs={{0,7},{1,6},{2,5},{3,4},{4,3},{5,2},{6,1},{7,0},{8,15},{9,14},{10,... | collective-permute-start | bytes 405512 | tf_op jit(solution)/shard_map/ppermute | solution.py:353
  10.2 0.0 collective-permute-done.refs_1_
  10.2 0.7 %copy-done.1 = s32[256]{0:T(256)S(1)} copy-done((s32[256]{0:T(256)S(1)}, s32[256]{0:T(256)}, u32[]{:S(2)}) %copy-start.1) | copy-done | bytes 1048
  10.9 7.7 %first_score.1 = (bf16[256,32,512]{2,1,0:T(8,128)(2,1)S(1)}, f32[256,128]{1,0:T(8,128)S(1)}, f32[1,128]{1,0:T(1,128)S(1)}, f32[1,128]{1,0:T(1,128)S(1)}) custom-call(bf16[256,32,512]{2,1,0:T(8,128)(2,1)} %bank_ref.1, s32[1,256]{1,0:T(1,128)S(1)} %bitcast.11, bf16[528,128]{1,0:T(8,128)(2,1)S(1)} %get-tuple-element.23.refs_0_, ...), custom_call_target="tpu_custom_call" | custom-call | flops 1 | bytes 1 | tf_op jit(solution)/shard_map/first_score/pallas_call | solution.py:378
  18.6 0.3 late_pack.1.refs_1_.refs_2_
  18.9 0.1 collective-permute-start.5
  19.0 6.5 %collective-permute-done.3.refs_0_ = bf16[1056,128]{1,0:T(8,128)(2,1)S(1)} collective-permute-done((bf16[1056,128]{1,0:T(8,128)(2,1)S(1)}, bf16[1056,128]{1,0:T(8,128)(2,1)S(1)}, u32[]{:S(2)}, u32[]{:S(2)}) %collective-permute-start.3) | collective-permute-done | bytes 270368 | tf_op jit(solution)/shard_map/ppermute | solution.py:353
  25.5 0.1 collective-permute-start.4
  25.6 0.4 first_sum.1.refs_2_
  26.0 1.0 %collective-permute-done.4.refs_1_ = bf16[528,128]{1,0:T(8,128)(2,1)S(1)} collective-permute-done((bf16[528,128]{1,0:T(8,128)(2,1)S(1)}, bf16[528,128]{1,0:T(8,128)(2,1)S(1)}, u32[]{:S(2)}, u32[]{:S(2)}) %collective-permute-start.4) | collective-permute-done | bytes 135200 | tf_op jit(solution)/shard_map/ppermute | solution.py:353
  26.9 2.8 %score.2 = (f32[1,128]{1,0:T(1,128)S(1)}, f32[1,128]{1,0:T(1,128)S(1)}) custom-call(bf16[256,32,512]{2,1,0:T(8,128)(2,1)S(1)} %get-tuple-element.25.bank_ref, f32[256,128]{1,0:T(8,128)S(1)} %get-tuple-element.26.norm_ref, s32[1,256]{1,0:T(1,128)S(1)} %bitcast.12, bf16[1056,128]{1,0:T(8,128)(2,1)S(1)} %collective-permute-done.3.refs_0_, ...), custom_call_target="tpu_custom_call" | custom-call | flops 10000000000 | bytes 1 | tf_op jit(solution)/shard_map/score/pallas_call | solution.py:378
  29.7 0.7 %collective-permute-done.5.refs_0_ = bf16[1056,128]{1,0:T(8,128)(2,1)S(1)} collective-permute-done((bf16[1056,128]{1,0:T(8,128)(2,1)S(1)}, bf16[1056,128]{1,0:T(8,128)(2,1)S(1)}, u32[]{:S(2)}, u32[]{:S(2)}) %collective-permute-start.5) | collective-permute-done | bytes 270368 | tf_op jit(solution)/shard_map/ppermute | solution.py:353
  30.4 0.0 copy-start.2
  30.4 0.1 collective-permute-start.6
  30.5 0.4 pair_sum.1.before_ref
  30.9 0.9 %collective-permute-done.6.refs_1_ = bf16[528,128]{1,0:T(8,128)(2,1)S(1)} collective-permute-done((bf16[528,128]{1,0:T(8,128)(2,1)S(1)}, bf16[528,128]{1,0:T(8,128)(2,1)S(1)}, u32[]{:S(2)}, u32[]{:S(2)}) %collective-permute-start.6) | collective-permute-done | bytes 135200 | tf_op jit(solution)/shard_map/ppermute | solution.py:353
  31.8 2.9 %score.3 = (f32[1,128]{1,0:T(1,128)S(1)}, f32[1,128]{1,0:T(1,128)S(1)}, f32[256,512]{1,0:T(8,128)S(1)}) custom-call(bf16[256,32,512]{2,1,0:T(8,128)(2,1)S(1)} %get-tuple-element.25.bank_ref, f32[256,128]{1,0:T(8,128)S(1)} %get-tuple-element.26.norm_ref, s32[1,256]{1,0:T(1,128)S(1)} %bitcast.13, f32[256,512]{1,0:T(8,128)S(1)} %pair_sum.1.before_ref, ...), custom_call_target="tpu_custom_call" | custom-call | flops 10000000000 | bytes 1 | tf_op jit(solution)/shard_map/score/pallas_call | solution.py:378
  34.7 0.0 collective-permute-done.1.refs_0_
  34.8 0.4 last_sum.1
  35.1 2.6 %collective-permute-start.9 = (bf16[256,512]{1,0:T(8,128)(2,1)S(1)}, bf16[256,512]{1,0:T(8,128)(2,1)S(1)}, u32[]{:S(2)}, u32[]{:S(2)}) collective-permute-start(bf16[256,512]{1,0:T(8,128)(2,1)S(1)} %get-tuple-element.41), channel_id=1, source_target_pairs={{0,24},{8,16},{16,8},{24,0},{1,25},{9,17},{17,9},{25,1},{2,26},{10... | collective-permute-start | bytes 786440 | tf_op jit(solution)/shard_map/ppermute | solution.py:353
  37.7 0.5 collective-permute-start.8
  38.2 0.5 collective-permute-start.7
  38.7 3.0 %last_score.1 = f32[8,128]{1,0:T(8,128)S(1)} custom-call(s32[1]{0:T(128)} %bitcast.me_ref, bf16[256,32,512]{2,1,0:T(8,128)(2,1)S(1)} %get-tuple-element.25.bank_ref, f32[256,128]{1,0:T(8,128)S(1)} %get-tuple-element.26.norm_ref, s32[1,256]{1,0:T(1,128)S(1)} %bitcast.14, bf16[528,128]{1,0:T(8,128)(2,1)S(1)} %collective-permute-done.1.refs_0_, ...), custom_call_target="tpu_custom_call" | custom-call | flops 1 | bytes 1 | tf_op jit(solution)/shard_map/last_score/pallas_call | solution.py:378
  41.7 10.2 %all_to_all.11 = f32[8,1,128]{2,1,0:T(1,128)S(1)} all-to-all(f32[8,1,128]{2,1,0:T(1,128)S(1)} %bitcast.9), channel_id=1, replica_groups=mesh['grp'=4,'own'=8] {'own'}, dimensions={0} | all-to-all | bytes 8192 | tf_op jit(solution)/shard_map/all_to_all | solution.py:495
  51.8 0.8 %unpack.1 = f32[1,512]{1,0:T(1,128)} custom-call(s32[1,512]{1,0:T(1,128)S(1)} %get-tuple-element.22.index_ref, f32[8,128]{1,0:T(8,128)S(1)} %bitcast.10), custom_call_target="tpu_custom_call" | custom-call | flops 1 | bytes 1 | tf_op jit(solution)/shard_map/unpack/pallas_call | solution.py:378
  52.7 0.0 collective-permute-done.9.refs_2_
  52.7 0.0 collective-permute-done.8.refs_1_
  52.7 1.0 %finish.1 = f32[256,512]{1,0:T(8,128)} custom-call(f32[256,512]{1,0:T(8,128)S(1)} %copy-done, f32[256,512]{1,0:T(8,128)S(1)} %get-tuple-element.40.own_ref, bf16[256,512]{1,0:T(8,128)(2,1)S(1)} %collective-permute-done.7.refs_0_, bf16[256,512]{1,0:T(8,128)(2,1)S(1)} %collective-permute-done.8.refs_1_, bf16[256,512]{1,0:T(8,128)(2,1)S(1)} %collective-permute-done.9.refs_2_), custom_call_target="tpu_custom_call" | custom-call | flops 1 | bytes 1 | tf_op jit(solution)/shard_map/finish/pallas_call | solution.py:378
  (8 shorter events, 0.0 us)
Async XLA Ops:
  2.4 23.0 %collective-permute-start.3 = (bf16[1056,128]{1,0:T(8,128)(2,1)S(1)}, bf16[1056,128]{1,0:T(8,128)(2,1)S(1)}, u32[]{:S(2)}, u32[]{:S(2)}) collective-permute-start(bf16[1056,128]{1,0:T(8,128)(2,1)S(1)} %get-tuple-element.31), channel_id=1, source_target_pairs={{0,4},{1,5},{2,6},{3,7},{4,0},{5,1},{6,2},{7,3},{8,12},{9,13},{10,... | collective-permute-start | bytes 811016 | tf_op jit(solution)/shard_map/ppermute | solution.py:353
  6.5 3.7 %collective-permute-start = (bf16[528,128]{1,0:T(8,128)(2,1)S(1)}, bf16[528,128]{1,0:T(8,128)(2,1)S(1)}, u32[]{:S(2)}, u32[]{:S(2)}) collective-permute-start(bf16[528,128]{1,0:T(8,128)(2,1)S(1)} %get-tuple-element.24), channel_id=1, source_target_pairs={{0,1},{1,0},{2,3},{3,2},{4,5},{5,4},{6,7},{7,6},{8,9},{9,8},{10,11... | collective-permute-start | bytes 405512 | tf_op jit(solution)/shard_map/ppermute | solution.py:353
  6.5 28.2 %collective-permute-start.1 = (bf16[528,128]{1,0:T(8,128)(2,1)S(1)}, bf16[528,128]{1,0:T(8,128)(2,1)S(1)}, u32[]{:S(2)}, u32[]{:S(2)}) collective-permute-start(bf16[528,128]{1,0:T(8,128)(2,1)S(1)} %get-tuple-element.27), channel_id=1, source_target_pairs={{0,6},{1,7},{2,4},{3,5},{4,2},{5,3},{6,0},{7,1},{8,14},{9,15},{10,... | collective-permute-start | bytes 405512 | tf_op jit(solution)/shard_map/ppermute | solution.py:353
  7.9 26.9 %collective-permute-start.2 = (bf16[528,128]{1,0:T(8,128)(2,1)S(1)}, bf16[528,128]{1,0:T(8,128)(2,1)S(1)}, u32[]{:S(2)}, u32[]{:S(2)}) collective-permute-start(bf16[528,128]{1,0:T(8,128)(2,1)S(1)} %get-tuple-element.28), channel_id=1, source_target_pairs={{0,7},{1,6},{2,5},{3,4},{4,3},{5,2},{6,1},{7,0},{8,15},{9,14},{10,... | collective-permute-start | bytes 405512 | tf_op jit(solution)/shard_map/ppermute | solution.py:353
  10.2 0.7 %copy-start.1 = (s32[256]{0:T(256)S(1)}, s32[256]{0:T(256)}, u32[]{:S(2)}) copy-start(s32[256]{0:T(256)} %param.10) | copy-start | bytes 3076
  18.9 11.5 %collective-permute-start.5 = (bf16[1056,128]{1,0:T(8,128)(2,1)S(1)}, bf16[1056,128]{1,0:T(8,128)(2,1)S(1)}, u32[]{:S(2)}, u32[]{:S(2)}) collective-permute-start(bf16[1056,128]{1,0:T(8,128)(2,1)S(1)} %late_pack.1.refs_1_.refs_2_), channel_id=1, source_target_pairs={{0,2},{1,3},{2,0},{3,1},{4,6},{5,7},{6,4},{7,5},{8,10},{9,11},{10,... | collective-permute-start | bytes 811016 | tf_op jit(solution)/shard_map/ppermute | solution.py:353
  25.5 1.4 %collective-permute-start.4 = (bf16[528,128]{1,0:T(8,128)(2,1)S(1)}, bf16[528,128]{1,0:T(8,128)(2,1)S(1)}, u32[]{:S(2)}, u32[]{:S(2)}) collective-permute-start(bf16[528,128]{1,0:T(8,128)(2,1)S(1)} %pass_on.2), channel_id=1, source_target_pairs={{0,1},{1,0},{2,3},{3,2},{4,5},{5,4},{6,7},{7,6},{8,9},{9,8},{10,11... | collective-permute-start | bytes 405512 | tf_op jit(solution)/shard_map/ppermute | solution.py:353
  30.4 1.4 %copy-start.2 = (s32[256]{0:T(256)S(1)}, s32[256]{0:T(256)}, u32[]{:S(2)}) copy-start(s32[256]{0:T(256)} %param.10) | copy-start | bytes 3076
  30.4 1.4 %collective-permute-start.6 = (bf16[528,128]{1,0:T(8,128)(2,1)S(1)}, bf16[528,128]{1,0:T(8,128)(2,1)S(1)}, u32[]{:S(2)}, u32[]{:S(2)}) collective-permute-start(bf16[528,128]{1,0:T(8,128)(2,1)S(1)} %pass_on.3), channel_id=1, source_target_pairs={{0,1},{1,0},{2,3},{3,2},{4,5},{5,4},{6,7},{7,6},{8,9},{9,8},{10,11... | collective-permute-start | bytes 405512 | tf_op jit(solution)/shard_map/ppermute | solution.py:353
  34.7 18.0 %copy-start = (f32[256,512]{1,0:T(8,128)S(1)}, f32[256,512]{1,0:T(8,128)}, u32[]{:S(2)}) copy-start(f32[256,512]{1,0:T(8,128)} %stored_ref.1) | copy-start | bytes 1572868
  35.1 17.5 %collective-permute-start.9 = (bf16[256,512]{1,0:T(8,128)(2,1)S(1)}, bf16[256,512]{1,0:T(8,128)(2,1)S(1)}, u32[]{:S(2)}, u32[]{:S(2)}) collective-permute-start(bf16[256,512]{1,0:T(8,128)(2,1)S(1)} %get-tuple-element.41), channel_id=1, source_target_pairs={{0,24},{8,16},{16,8},{24,0},{1,25},{9,17},{17,9},{25,1},{2,26},{10... | collective-permute-start | bytes 786440 | tf_op jit(solution)/shard_map/ppermute | solution.py:353
  37.7 15.0 %collective-permute-start.8 = (bf16[256,512]{1,0:T(8,128)(2,1)S(1)}, bf16[256,512]{1,0:T(8,128)(2,1)S(1)}, u32[]{:S(2)}, u32[]{:S(2)}) collective-permute-start(bf16[256,512]{1,0:T(8,128)(2,1)S(1)} %get-tuple-element.41), channel_id=1, source_target_pairs={{0,16},{8,24},{16,0},{24,8},{1,17},{9,25},{17,1},{25,9},{2,18},{10... | collective-permute-start | bytes 786440 | tf_op jit(solution)/shard_map/ppermute | solution.py:353
  38.2 14.5 %collective-permute-start.7 = (bf16[256,512]{1,0:T(8,128)(2,1)S(1)}, bf16[256,512]{1,0:T(8,128)(2,1)S(1)}, u32[]{:S(2)}, u32[]{:S(2)}) collective-permute-start(bf16[256,512]{1,0:T(8,128)(2,1)S(1)} %get-tuple-element.41), channel_id=1, source_target_pairs={{0,8},{8,0},{16,24},{24,16},{1,9},{9,1},{17,25},{25,17},{2,10},{10... | collective-permute-start | bytes 786440 | tf_op jit(solution)/shard_map/ppermute | solution.py:353

commit v7 on v6

--- a/solution.py
+++ b/solution.py
@@ -11,7 +11,6 @@
 LANES = 128
 INFO_ROWS = 16
 CODE_BASE = 128
-COSTS = {"score": 10**10, "pair_sum": 10**10, "first_sum": 10**10}
 SMALL_VMEM = 32 * 1024 * 1024
 
 
@@ -61,10 +60,10 @@
         info = lax.dot_general(
             codes, match, (((1,), (1,)), ((), ())), preferred_element_type=jnp.float32
         )
-        for number, (target, base) in enumerate(chosen):
+        for number, target in enumerate(chosen):
             low = number * capacity
             for part in range(width // LANES):
-                target[pl.ds(base + part * capacity, capacity), :] = packed[
+                target[pl.ds(part * capacity, capacity), :] = packed[
                     low : low + capacity, part * LANES : (part + 1) * LANES
                 ]
             piece = info[:, low : low + capacity]
@@ -72,17 +71,22 @@
                 piece = jnp.concatenate(
                     [piece, jnp.zeros((INFO_ROWS, LANES - capacity), jnp.float32)], axis=1
                 )
-            target[pl.ds(base + width // LANES * capacity, INFO_ROWS), :] = piece.astype(
+            target[pl.ds(width // LANES * capacity, INFO_ROWS), :] = piece.astype(
                 jnp.bfloat16
             )
 
 
-def blocks_of(messages, capacity, width):
-    size = block_rows(capacity, width)
-    return [(message, base) for message in messages for base in range(0, message.shape[0], size)]
-
-
-def pack_kernel(owners, capacity, first_peers, me_ref, *refs):
+def write_messages(capacity, peers, index, slot, values, messages):
+    start = 0
+    while start < len(peers):
+        stop = start + 1
+        while stop < len(peers) and peers[stop] == peers[stop - 1] + 1:
+            stop += 1
+        write_blocks(capacity, peers[start], index, slot, values, messages[start:stop])
+        start = stop
+
+
+def pack_kernel(owners, capacity, peers, me_ref, *refs):
     sources, return_ref, index_ref, held, messages = (
         refs[:3], refs[3], refs[4], refs[5:8], refs[8:-1]
     )
@@ -101,44 +105,26 @@
     index = (owner ^ me_ref[0]) * capacity + placed
     index_ref[...] = index
     copies[2].wait()
-    targets = blocks_of(messages, capacity, held[2].shape[1])
-    quarter = len(targets) // len(first_peers)
-    for number, first_peer in enumerate(first_peers):
-        write_blocks(
-            capacity,
-            first_peer,
-            index,
-            held[1][...],
-            held[2][...],
-            targets[number * quarter : (number + 1) * quarter],
-        )
-
-
-def late_pack_kernel(capacity, first_peer, index_ref, slot_ref, rows_ref, after_ref, *messages):
-    targets = blocks_of(messages, capacity, rows_ref.shape[1])
-    write_blocks(capacity, first_peer, index_ref[...], slot_ref[...], rows_ref[...], targets)
-
-
-def pass_kernel(*refs):
-    pair_refs, out_ref = refs[:-2], refs[-1]
-    rows = pair_refs[0].shape[0] // 2
-    for number, pair in enumerate(pair_refs):
-        out_ref[pl.ds(number * rows, rows), :] = pair[pl.ds(rows, rows), :]
-
-
-def read_blocks(blocks, capacity, width):
+    write_messages(capacity, peers, index, held[1][...], held[2][...], messages)
+
+
+def late_pack_kernel(capacity, peers, index_ref, slot_ref, rows_ref, after_ref, *messages):
+    write_messages(capacity, peers, index_ref[...], slot_ref[...], rows_ref[...], messages)
+
+
+def read_messages(messages, capacity, width):
     units, slots = [], []
-    for message, base in blocks:
+    for message in messages:
         values = jnp.concatenate(
             [
-                message[pl.ds(base + part * capacity, capacity), :].astype(jnp.float32)
+                message[pl.ds(part * capacity, capacity), :].astype(jnp.float32)
                 for part in range(width // LANES)
             ],
             axis=1,
         )
         norm = jnp.sqrt(jnp.sum(values * values, axis=1, keepdims=True) + epsilon)
         units.append((values / norm).astype(jnp.bfloat16))
-        info = message[pl.ds(base + width // LANES * capacity, INFO_ROWS), :].astype(jnp.float32)
+        info = message[pl.ds(width // LANES * capacity, INFO_ROWS), :].astype(jnp.float32)
         slots.append((info[0:1, :capacity] - 1.0) * CODE_BASE + info[1:2, :capacity])
     return jnp.concatenate(units, axis=0), jnp.concatenate(slots, axis=1).astype(jnp.int32)
 
@@ -189,7 +175,7 @@
 
 def first_score_kernel(messages, capacity, block, bank_ref, members_ref, *refs):
     message_refs = refs[:messages]
-    held_ref, norm_ref, *best_refs, semaphore = refs[messages:]
+    held_ref, norm_ref, sum_ref, *best_refs, semaphore = refs[messages:]
     clusters, depth, width = held_ref.shape
     copies = []
     for number in range(clusters // block):
@@ -198,8 +184,9 @@
             pltpu.make_async_copy(bank_ref.at[part], held_ref.at[part], semaphore.at[number])
         )
         copies[-1].start()
-    units, slots = read_blocks([(message, 0) for message in message_refs], capacity, width)
+    units, slots = read_messages(message_refs, capacity, width)
     onehot = cluster_onehot(slots, clusters)
+    sum_ref[...] = jnp.dot(onehot, units, preferred_element_type=jnp.float32)
     columns = units.T
     picked = jnp.zeros((depth, slots.shape[1]), jnp.float32)
     shape = (block, depth, LANES)
@@ -209,19 +196,20 @@
     for number in range(clusters // block):
         copies[number].wait()
         part = pl.ds(number * block, block)
-        bank_block = held_ref[part]
-        picked = pick_dots(bank_block, number * block, columns, slots, picked)
-        values = bank_block.astype(jnp.float32)
+        values = held_ref[part].astype(jnp.float32)
         square = jnp.sum(values * values, axis=2, keepdims=True)
         norm_ref[part, :] = jnp.sqrt(jnp.sum(jnp.where(own_lane, square, 0.0), axis=1) + epsilon)
+    for number in range(clusters // block):
+        bank_block = held_ref[pl.ds(number * block, block)]
+        picked = pick_dots(bank_block, number * block, columns, slots, picked)
     best = best_cosines(picked, onehot, norm_ref[...], members_ref[...])
     for number, best_ref in enumerate(best_refs):
         best_ref[...] = best[:, number * capacity : (number + 1) * capacity]
 
 
-def score_group(blocks, capacity, block, bank_ref, norm_ref, members_ref):
+def score_group(message_refs, capacity, block, bank_ref, norm_ref, members_ref):
     clusters, depth, width = bank_ref.shape
-    units, slots = read_blocks(blocks, capacity, width)
+    units, slots = read_messages(message_refs, capacity, width)
     onehot = cluster_onehot(slots, clusters)
     columns = units.T
     picked = jnp.zeros((depth, slots.shape[1]), jnp.float32)
@@ -231,22 +219,17 @@
     best = best_cosines(picked, onehot, norm_ref[...], members_ref[...])
     results = [
         best[:, number * capacity : (number + 1) * capacity]
-        for number in range(len(blocks))
+        for number in range(len(message_refs))
     ]
     return results, onehot, units
 
 
 def score_kernel(
-    pairs, capacity, block, bank_ref, norm_ref, members_ref, before_ref, *refs
+    messages, capacity, block, bank_ref, norm_ref, members_ref, before_ref, *refs
 ):
-    pair_refs, passed_ref, refs = refs[:pairs], refs[pairs], refs[pairs + 1 :]
+    message_refs, refs = refs[:messages], refs[messages:]
     results, onehot, units = score_group(
-        [(pair, 0) for pair in pair_refs] + blocks_of([passed_ref], capacity, bank_ref.shape[2]),
-        capacity,
-        block,
-        bank_ref,
-        norm_ref,
-        members_ref,
+        message_refs, capacity, block, bank_ref, norm_ref, members_ref
     )
     *best_refs, sum_ref = refs
     for best_ref, value in zip(best_refs, results):
@@ -254,39 +237,10 @@
     sum_ref[...] = before_ref[...] + jnp.dot(onehot, units, preferred_element_type=jnp.float32)
 
 
-def first_sum_kernel(messages, capacity, *refs):
-    message_refs, total_ref = refs[:messages], refs[-1]
-    clusters, width = total_ref.shape
-    units, slots = read_blocks([(message, 0) for message in message_refs], capacity, width)
-    total_ref[...] = jnp.dot(
-        cluster_onehot(slots, clusters), units, preferred_element_type=jnp.float32
-    )
-
-
-def pair_score_kernel(pairs, capacity, block, bank_ref, norm_ref, members_ref, *refs):
-    pair_refs, passed_ref, best_refs = refs[:pairs], refs[pairs], refs[pairs + 1 :]
-    blocks = [(pair, 0) for pair in pair_refs] + blocks_of(
-        [passed_ref], capacity, bank_ref.shape[2]
-    )
-    results, _, _ = score_group(blocks, capacity, block, bank_ref, norm_ref, members_ref)
-    for best_ref, value in zip(best_refs, results):
-        best_ref[...] = value
-
-
-def pair_sum_kernel(pairs, capacity, *refs):
-    pair_refs, passed_ref, before_ref, total_ref = refs[:pairs], *refs[pairs:]
-    clusters, width = total_ref.shape
-    blocks = [(pair, 0) for pair in pair_refs] + blocks_of([passed_ref], capacity, width)
-    units, slots = read_blocks(blocks, capacity, width)
-    total_ref[...] = before_ref[...] + jnp.dot(
-        cluster_onehot(slots, clusters), units, preferred_element_type=jnp.float32
-    )
-
-
 def last_sum_kernel(messages, capacity, *refs):
     message_refs, before_ref, total_ref, sent_ref = refs[:messages], *refs[messages:]
     clusters, width = total_ref.shape
-    units, slots = read_blocks([(message, 0) for message in message_refs], capacity, width)
+    units, slots = read_messages(message_refs, capacity, width)
     total = before_ref[...] + jnp.dot(
         cluster_onehot(slots, clusters), units, preferred_element_type=jnp.float32
     )
@@ -298,14 +252,7 @@
     messages, places, capacity, block, me_ref, bank_ref, norm_ref, members_ref, *refs
 ):
     message_refs, earlier_refs, best_ref = refs[:messages], refs[messages:-1], refs[-1]
-    results, _, _ = score_group(
-        [(message, 0) for message in message_refs],
-        capacity,
-        block,
-        bank_ref,
-        norm_ref,
-        members_ref,
-    )
+    results, _, _ = score_group(message_refs, capacity, block, bank_ref, norm_ref, members_ref)
     for value, place in zip([ref[...] for ref in earlier_refs] + results, places):
         best_ref[pl.ds(me_ref[0] ^ place, 1), :] = value
 
@@ -362,13 +309,15 @@
     own_index = lax.axis_index("own").astype(jnp.int32).reshape(1)
     smem = pl.BlockSpec(memory_space=pltpu.SMEM)
     anywhere = pl.BlockSpec(memory_space=pl.ANY)
-    quarter = owners // 4
-    block_size = block_rows(capacity, width)
-    message = jax.ShapeDtypeStruct((block_size, LANES), jnp.bfloat16)
-    pair = jax.ShapeDtypeStruct((2 * block_size, LANES), jnp.bfloat16)
-    first, last = list(range(quarter)), list(range(3 * quarter, owners))
-    far_pairs, near_pairs = (list(range(start, start + quarter, 2)) for start in (2 * quarter, quarter))
-    order = first + [peer + core for pairs in (far_pairs, near_pairs) for core in (0, 1) for peer in pairs] + last
+    message = jax.ShapeDtypeStruct((block_rows(capacity, width), LANES), jnp.bfloat16)
+    half, quarter, eighth = owners // 2, owners // 4, owners // 8
+    groups = [
+        list(range(quarter)),
+        list(range(half, half + quarter)),
+        [*range(quarter, quarter + eighth), *range(half + quarter, half + quarter + eighth)],
+        [*range(quarter + eighth, half), *range(half + quarter + eighth, owners)],
+    ]
+    sent_first, last = sum(groups[:3], []), groups[3]
     block = min(clusters, 32)
 
     def vmem_call(
@@ -382,22 +331,17 @@
             out_specs=out_specs,
             scratch_shapes=scratch_shapes,
             compiler_params=small_params(),
-            cost_estimate=pl.CostEstimate(
-                flops=COSTS.get(name, 1), bytes_accessed=1, transcendentals=0
-            ),
+            cost_estimate=pl.CostEstimate(flops=1, bytes_accessed=1, transcendentals=0),
             name=name,
         )(*operands)
 
     row = jax.ShapeDtypeStruct((1, rows), jnp.int32)
-    pair_count = quarter // 2
     return_index, index, _, slots, values, *sent = vmem_call(
-        functools.partial(pack_kernel, owners, capacity, (0, 2 * quarter, 3 * quarter)),
+        functools.partial(pack_kernel, owners, capacity, sent_first),
         "pack",
         [row] * 4
         + [jax.ShapeDtypeStruct((rows, width), arrivals.dtype)]
-        + [message] * quarter
-        + [pair] * pair_count
-        + [message] * quarter,
+        + [message] * len(sent_first),
         [
             own_index,
             in_hbm(home_owner.reshape(1, rows)),
@@ -407,74 +351,44 @@
         [smem] + [anywhere] * 3,
         [pltpu.SemaphoreType.DMA((3,))],
     )
-    packed = dict(zip(first + far_pairs + last, sent))
     got = {
-        peer: exchange(packed[peer], "own", peer) if peer else packed[peer]
-        for peer in far_pairs + last + first
+        peer: exchange(value, "own", peer) if peer else value
+        for peer, value in zip(sent_first, sent)
     }
     member_row = members.reshape(1, clusters)
     sums = jax.ShapeDtypeStruct((clusters, width), jnp.float32)
 
     results = [jax.ShapeDtypeStruct((1, capacity), jnp.float32)] * quarter
-    held_bank, bank_norm, *best = vmem_call(
+    held_bank, bank_norm, total, *best = vmem_call(
         functools.partial(first_score_kernel, quarter, capacity, block),
         "first_score",
         [
             pltpu.VMEM(bank.shape, bank.dtype),
             jax.ShapeDtypeStruct((clusters, LANES), jnp.float32),
+            sums,
             *results,
         ],
-        [in_hbm(bank), member_row, *[got[peer] for peer in first]],
+        [in_hbm(bank), member_row, *[got[peer] for peer in groups[0]]],
         [anywhere] + [whole_vmem()] * (1 + quarter),
         [pltpu.SemaphoreType.DMA((clusters // block,))],
     )
     held_bank = pltpu.with_memory_space_constraint(held_bank, pltpu.VMEM)
-    near = vmem_call(
-        functools.partial(late_pack_kernel, capacity, quarter),
+    late = vmem_call(
+        functools.partial(late_pack_kernel, capacity, last),
         "late_pack",
-        [pair] * pair_count,
-        [index, slots, values, best[0]],
+        [message] * len(last),
+        [index, slots, values, total],
         [whole_vmem()] * 3 + [anywhere],
     )
-    got.update({peer: exchange(value, "own", peer) for peer, value in zip(near_pairs, near)})
-    total = vmem_call(
-        functools.partial(first_sum_kernel, quarter, capacity),
-        "first_sum",
-        sums,
-        [*[got[peer] for peer in first], near[0]],
-        [whole_vmem()] * quarter + [anywhere],
-    )
-    for peers in (far_pairs, near_pairs):
-        pairs = [got[peer] for peer in peers]
-        passed = vmem_call(
-            pass_kernel,
-            "pass_on",
-            jax.ShapeDtypeStruct((pair_count * block_size, LANES), jnp.bfloat16),
-            [*pairs, near[0] if peers is far_pairs else best[-1]],
-            [whole_vmem()] * pair_count + [anywhere],
-        )
-        passed = exchange(passed, "own", 1)
-        if peers is far_pairs:
-            best += vmem_call(
-                functools.partial(pair_score_kernel, pair_count, capacity, block),
-                "score",
-                results,
-                [held_bank, bank_norm, member_row, *pairs, passed],
-            )
-            total = vmem_call(
-                functools.partial(pair_sum_kernel, pair_count, capacity),
-                "pair_sum",
-                sums,
-                [*pairs, passed, total],
-            )
-        else:
-            *found, total = vmem_call(
-                functools.partial(score_kernel, pair_count, capacity, block),
-                "score",
-                results + [sums],
-                [held_bank, bank_norm, member_row, total, *pairs, passed],
-            )
-            best += found
+    got.update({peer: exchange(value, "own", peer) for peer, value in zip(last, late)})
+    for group in groups[1:3]:
+        *found, total = vmem_call(
+            functools.partial(score_kernel, quarter, capacity, block),
+            "score",
+            results + [sums],
+            [held_bank, bank_norm, member_row, total, *[got[peer] for peer in group]],
+        )
+        best += found
     last_messages = [got[peer] for peer in last]
     total, sent = vmem_call(
         functools.partial(last_sum_kernel, quarter, capacity),
@@ -485,7 +399,7 @@
     terms = [exchange(sent, "grp", offset) for offset in range(1, parts)]
     best = vmem_call(
         functools.partial(
-            last_score_kernel, quarter, order, capacity, block
+            last_score_kernel, quarter, sum(groups, []), capacity, block
         ),
         "last_score",
         jax.ShapeDtypeStruct((owners, capacity), jnp.float32),

time: 54.1 us -> 49.8 us (0.921)
  waiting for transfers between devices: 9.13 us -> 2.14 us
  starting transfers between devices: 11.6 us -> 13.9 us
  blocking collectives: 10.2 us -> 12.3 us
  Pallas kernels: 21.4 us -> 19.7 us
    ppermute x10, waiting for transfers between devices: 9.13 us -> 2.14 us  [exchange(): lax.ppermute(value, axis, [(device, device ^ offset) for device in range(...]
    ppermute x10, starting transfers between devices: 11.6 us -> 13.9 us  [exchange(): lax.ppermute(value, axis, [(device, device ^ offset) for device in range(...]
    all_to_all x1, blocking collectives: 10.2 us -> 12.3 us  [body(): lax.all_to_all(best, 'own', split_axis=0, concat_axis=0, tiled=True)]
    pallas_call x13 -> x9, Pallas kernels: 21.4 us -> 19.7 us  [vmem_call(): pl.pallas_call(kernel, out_shape=out_shape, in_specs=in_specs or [whole_v...]
  transfers between devices with their start and end apart: 10 -> 10, of which waited for: 4 -> 2; matrix products, arithmetic and copies ran while one was open for 0% -> 0% of each run, Pallas kernels for 34% -> 33%
where the time goes in v7:
time: 49.8 us; the launch traced here: 49.6 us
  Pallas kernels  19.7 us (40%)
  starting transfers between devices  13.9 us (28%)
  blocking collectives  12.3 us (25%)
  waiting for transfers between devices  2.14 us (4%)
  between operations  0.88 us (2%)
  local copies, waits for them, and re-layouts  0.69 us (1%)
    pallas_call x9, Pallas kernels, vmem_call(): pl.pallas_call(kernel, out_shape=out_shape, in_specs=in_specs or [whole_v...  19.7 us
    ppermute x10, starting transfers between devices, exchange(): lax.ppermute(value, axis, [(device, device ^ offset) for device in range(...  13.9 us
    all_to_all x1, blocking collectives, body(): lax.all_to_all(best, 'own', split_axis=0, concat_axis=0, tiled=True)  12.3 us
    ppermute x10, waiting for transfers between devices, exchange(): lax.ppermute(value, axis, [(device, device ^ offset) for device in range(...  2.14 us
  transfers between devices with their start and end apart: 10, of which 2 were waited for; matrix products, arithmetic and copies ran while one was open for 0% of the time, Pallas kernels for 33%

profile of v7, /device:TPU:0, one launch (start us, length us, event | category | flops | bytes accessed | tf_op | source)
XLA Modules:
  0.0 49.6 jit_solution(17061184952497154691)
XLA Ops:
  0.6 0.0 copy-start.2
  0.6 1.9 %pack.1 = (s32[1,512]{1,0:T(1,128)S(1)}, s32[1,512]{1,0:T(1,128)S(1)}, s32[1,512]{1,0:T(1,128)}, s32[1,512]{1,0:T(1,128)S(1)}, bf16[512,512]{1,0:T(8,128)(2,1)S(...) custom-call(s32[1]{0:T(128)} %bitcast.me_ref, ...), custom_call_target="tpu_custom_call" | custom-call | flops 1 | bytes 1 | tf_op jit(solution)/shard_map/pack/pallas_call | solution.py:327
  2.5 0.5 %collective-permute-start = (bf16[528,128]{1,0:T(8,128)(2,1)S(1)}, bf16[528,128]{1,0:T(8,128)(2,1)S(1)}, u32[]{:S(2)}, u32[]{:S(2)}) collective-permute-start(bf16[528,128]{1,0:T(8,128)(2,1)S(1)} %get-tuple-element.29), channel_id=1, source_target_pairs={{0,1},{1,0},{2,3},{3,2},{4,5},{5,4},{6,7},{7,6},{8,9},{9,8},{10,11... | collective-permute-start | bytes 405512 | tf_op jit(solution)/shard_map/ppermute | solution.py:300
  3.0 3.7 %collective-permute-start.3 = (bf16[528,128]{1,0:T(8,128)(2,1)S(1)}, bf16[528,128]{1,0:T(8,128)(2,1)S(1)}, u32[]{:S(2)}, u32[]{:S(2)}) collective-permute-start(bf16[528,128]{1,0:T(8,128)(2,1)S(1)} %get-tuple-element.40), channel_id=1, source_target_pairs={{0,4},{1,5},{2,6},{3,7},{4,0},{5,1},{6,2},{7,3},{8,12},{9,13},{10,... | collective-permute-start | bytes 405512 | tf_op jit(solution)/shard_map/ppermute | solution.py:300
  6.7 0.1 collective-permute-start.4
  6.8 1.6 %collective-permute-start.5 = (bf16[528,128]{1,0:T(8,128)(2,1)S(1)}, bf16[528,128]{1,0:T(8,128)(2,1)S(1)}, u32[]{:S(2)}, u32[]{:S(2)}) collective-permute-start(bf16[528,128]{1,0:T(8,128)(2,1)S(1)} %get-tuple-element.45), channel_id=1, source_target_pairs={{0,2},{1,3},{2,0},{3,1},{4,6},{5,7},{6,4},{7,5},{8,10},{9,11},{10,... | collective-permute-start | bytes 405512 | tf_op jit(solution)/shard_map/ppermute | solution.py:300
  8.4 2.5 %collective-permute-start.6 = (bf16[528,128]{1,0:T(8,128)(2,1)S(1)}, bf16[528,128]{1,0:T(8,128)(2,1)S(1)}, u32[]{:S(2)}, u32[]{:S(2)}) collective-permute-start(bf16[528,128]{1,0:T(8,128)(2,1)S(1)} %get-tuple-element.46), channel_id=1, source_target_pairs={{0,6},{1,7},{2,4},{3,5},{4,2},{5,3},{6,0},{7,1},{8,14},{9,15},{10,... | collective-permute-start | bytes 405512 | tf_op jit(solution)/shard_map/ppermute | solution.py:300
  10.9 0.0 collective-permute-done.refs_1_
  10.9 0.7 %copy-done.1 = s32[256]{0:T(256)S(1)} copy-done((s32[256]{0:T(256)S(1)}, s32[256]{0:T(256)}, u32[]{:S(2)}) %copy-start.1) | copy-done | bytes 1048
  11.5 6.3 %first_score.1 = (bf16[256,32,512]{2,1,0:T(8,128)(2,1)S(1)}, f32[256,128]{1,0:T(8,128)S(1)}, f32[256,512]{1,0:T(8,128)S(1)}, f32[1,128]{1,0:T(1,128)S(1)}, f32[1,128]{1,0:T(1,128)S(1)}) custom-call(bf16[256,32,512]{2,1,0:T(8,128)(2,1)} %bank_ref.1, s32[1,256]{1,0:T(1,128)S(1)} %bitcast.11, bf16[528,128]{1,0:T(8,128)(2,1)S(1)} %get-tuple-element.28.refs_0_, ...), custom_call_target="tpu_custom_call" | custom-call | flops 1 | bytes 1 | tf_op jit(solution)/shard_map/first_score/pallas_call | solution.py:327
  17.9 0.4 late_pack.1
  18.3 0.1 collective-permute-start.1
  18.4 0.0 collective-permute-done.3.refs_0_
  18.4 1.8 %collective-permute-start.2 = (bf16[528,128]{1,0:T(8,128)(2,1)S(1)}, bf16[528,128]{1,0:T(8,128)(2,1)S(1)}, u32[]{:S(2)}, u32[]{:S(2)}) collective-permute-start(bf16[528,128]{1,0:T(8,128)(2,1)S(1)} %get-tuple-element.37), channel_id=1, source_target_pairs={{0,7},{1,6},{2,5},{3,4},{4,3},{5,2},{6,1},{7,0},{8,15},{9,14},{10,... | collective-permute-start | bytes 405512 | tf_op jit(solution)/shard_map/ppermute | solution.py:300
  20.3 2.0 %collective-permute-done.4.refs_1_ = bf16[528,128]{1,0:T(8,128)(2,1)S(1)} collective-permute-done((bf16[528,128]{1,0:T(8,128)(2,1)S(1)}, bf16[528,128]{1,0:T(8,128)(2,1)S(1)}, u32[]{:S(2)}, u32[]{:S(2)}) %collective-permute-start.4) | collective-permute-done | bytes 135200 | tf_op jit(solution)/shard_map/ppermute | solution.py:300
  22.3 2.9 %score.2 = (f32[1,128]{1,0:T(1,128)S(1)}, f32[1,128]{1,0:T(1,128)S(1)}, f32[256,512]{1,0:T(8,128)S(1)}) custom-call(bf16[256,32,512]{2,1,0:T(8,128)(2,1)S(1)} %get-tuple-element.30.bank_ref, f32[256,128]{1,0:T(8,128)S(1)} %get-tuple-element.31.norm_ref, s32[1,256]{1,0:T(1,128)S(1)} %bitcast.12, f32[256,512]{1,0:T(8,128)S(1)} %get-tuple-element.35.after_ref.before_ref, ...), custom_call_target="tpu_custom_call" | custom-call | flops 1 | bytes 1 | tf_op jit(solution)/shard_map/score/pallas_call | solution.py:327
  25.2 0.0 collective-permute-done.5.refs_0_
  25.2 0.0 collective-permute-done.6.refs_1_
  25.3 0.0 copy-start
  25.3 2.9 %score.3 = (f32[1,128]{1,0:T(1,128)S(1)}, f32[1,128]{1,0:T(1,128)S(1)}, f32[256,512]{1,0:T(8,128)S(1)}) custom-call(bf16[256,32,512]{2,1,0:T(8,128)(2,1)S(1)} %get-tuple-element.30.bank_ref, f32[256,128]{1,0:T(8,128)S(1)} %get-tuple-element.31.norm_ref, s32[1,256]{1,0:T(1,128)S(1)} %bitcast.13, f32[256,512]{1,0:T(8,128)S(1)} %get-tuple-element.44.before_ref, ...), custom_call_target="tpu_custom_call" | custom-call | flops 1 | bytes 1 | tf_op jit(solution)/shard_map/score/pallas_call | solution.py:327
  28.2 0.1 collective-permute-done.1.refs_0_
  28.3 0.0 collective-permute-done.2.refs_1_
  28.3 0.4 last_sum.1
  28.7 2.6 %collective-permute-start.9 = (bf16[256,512]{1,0:T(8,128)(2,1)S(1)}, bf16[256,512]{1,0:T(8,128)(2,1)S(1)}, u32[]{:S(2)}, u32[]{:S(2)}) collective-permute-start(bf16[256,512]{1,0:T(8,128)(2,1)S(1)} %get-tuple-element.51), channel_id=1, source_target_pairs={{0,24},{8,16},{16,8},{24,0},{1,25},{9,17},{17,9},{25,1},{2,26},{10... | collective-permute-start | bytes 786440 | tf_op jit(solution)/shard_map/ppermute | solution.py:300
  31.3 0.5 collective-permute-start.8
  31.7 0.5 collective-permute-start.7
  32.2 3.0 %last_score.1 = f32[8,128]{1,0:T(8,128)S(1)} custom-call(s32[1]{0:T(128)} %bitcast.me_ref, bf16[256,32,512]{2,1,0:T(8,128)(2,1)S(1)} %get-tuple-element.30.bank_ref, f32[256,128]{1,0:T(8,128)S(1)} %get-tuple-element.31.norm_ref, s32[1,256]{1,0:T(1,128)S(1)} %bitcast.14, bf16[528,128]{1,0:T(8,128)(2,1)S(1)} %collective-permute-done.1.refs_0_, ...), custom_call_target="tpu_custom_call" | custom-call | flops 1 | bytes 1 | tf_op jit(solution)/shard_map/last_score/pallas_call | solution.py:327
  35.2 12.3 %all_to_all.11 = f32[8,1,128]{2,1,0:T(1,128)S(1)} all-to-all(f32[8,1,128]{2,1,0:T(1,128)S(1)} %bitcast.9), channel_id=1, replica_groups=mesh['grp'=4,'own'=8] {'own'}, dimensions={0} | all-to-all | bytes 8192 | tf_op jit(solution)/shard_map/all_to_all | solution.py:409
  47.6 0.8 %unpack.1 = f32[1,512]{1,0:T(1,128)} custom-call(s32[1,512]{1,0:T(1,128)S(1)} %get-tuple-element.27.index_ref, f32[8,128]{1,0:T(8,128)S(1)} %bitcast.10), custom_call_target="tpu_custom_call" | custom-call | flops 1 | bytes 1 | tf_op jit(solution)/shard_map/unpack/pallas_call | solution.py:327
  48.4 0.0 collective-permute-done.9.refs_2_
  48.4 0.0 collective-permute-done.8.refs_1_
  48.4 1.0 %finish.1 = f32[256,512]{1,0:T(8,128)} custom-call(f32[256,512]{1,0:T(8,128)S(1)} %copy-done, f32[256,512]{1,0:T(8,128)S(1)} %get-tuple-element.50.own_ref, bf16[256,512]{1,0:T(8,128)(2,1)S(1)} %collective-permute-done.7.refs_0_, bf16[256,512]{1,0:T(8,128)(2,1)S(1)} %collective-permute-done.8.refs_1_, bf16[256,512]{1,0:T(8,128)(2,1)S(1)} %collective-permute-done.9.refs_2_), custom_call_target="tpu_custom_call" | custom-call | flops 1 | bytes 1 | tf_op jit(solution)/shard_map/finish/pallas_call | solution.py:327
  (4 shorter events, 0.0 us)
Async XLA Ops:
  0.6 21.7 %copy-start.2 = (s32[256]{0:T(256)S(1)}, s32[256]{0:T(256)}, u32[]{:S(2)}) copy-start(s32[256]{0:T(256)} %param.10) | copy-start | bytes 3076
  2.5 8.3 %collective-permute-start = (bf16[528,128]{1,0:T(8,128)(2,1)S(1)}, bf16[528,128]{1,0:T(8,128)(2,1)S(1)}, u32[]{:S(2)}, u32[]{:S(2)}) collective-permute-start(bf16[528,128]{1,0:T(8,128)(2,1)S(1)} %get-tuple-element.29), channel_id=1, source_target_pairs={{0,1},{1,0},{2,3},{3,2},{4,5},{5,4},{6,7},{7,6},{8,9},{9,8},{10,11... | collective-permute-start | bytes 405512 | tf_op jit(solution)/shard_map/ppermute | solution.py:300
  3.0 15.4 %collective-permute-start.3 = (bf16[528,128]{1,0:T(8,128)(2,1)S(1)}, bf16[528,128]{1,0:T(8,128)(2,1)S(1)}, u32[]{:S(2)}, u32[]{:S(2)}) collective-permute-start(bf16[528,128]{1,0:T(8,128)(2,1)S(1)} %get-tuple-element.40), channel_id=1, source_target_pairs={{0,4},{1,5},{2,6},{3,7},{4,0},{5,1},{6,2},{7,3},{8,12},{9,13},{10,... | collective-permute-start | bytes 405512 | tf_op jit(solution)/shard_map/ppermute | solution.py:300
  6.7 15.6 %collective-permute-start.4 = (bf16[528,128]{1,0:T(8,128)(2,1)S(1)}, bf16[528,128]{1,0:T(8,128)(2,1)S(1)}, u32[]{:S(2)}, u32[]{:S(2)}) collective-permute-start(bf16[528,128]{1,0:T(8,128)(2,1)S(1)} %get-tuple-element.41), channel_id=1, source_target_pairs={{0,5},{1,4},{2,7},{3,6},{4,1},{5,0},{6,3},{7,2},{8,13},{9,12},{10,... | collective-permute-start | bytes 405512 | tf_op jit(solution)/shard_map/ppermute | solution.py:300
  6.8 18.5 %collective-permute-start.5 = (bf16[528,128]{1,0:T(8,128)(2,1)S(1)}, bf16[528,128]{1,0:T(8,128)(2,1)S(1)}, u32[]{:S(2)}, u32[]{:S(2)}) collective-permute-start(bf16[528,128]{1,0:T(8,128)(2,1)S(1)} %get-tuple-element.45), channel_id=1, source_target_pairs={{0,2},{1,3},{2,0},{3,1},{4,6},{5,7},{6,4},{7,5},{8,10},{9,11},{10,... | collective-permute-start | bytes 405512 | tf_op jit(solution)/shard_map/ppermute | solution.py:300
  8.4 16.9 %collective-permute-start.6 = (bf16[528,128]{1,0:T(8,128)(2,1)S(1)}, bf16[528,128]{1,0:T(8,128)(2,1)S(1)}, u32[]{:S(2)}, u32[]{:S(2)}) collective-permute-start(bf16[528,128]{1,0:T(8,128)(2,1)S(1)} %get-tuple-element.46), channel_id=1, source_target_pairs={{0,6},{1,7},{2,4},{3,5},{4,2},{5,3},{6,0},{7,1},{8,14},{9,15},{10,... | collective-permute-start | bytes 405512 | tf_op jit(solution)/shard_map/ppermute | solution.py:300
  10.9 0.7 %copy-start.1 = (s32[256]{0:T(256)S(1)}, s32[256]{0:T(256)}, u32[]{:S(2)}) copy-start(s32[256]{0:T(256)} %param.10) | copy-start | bytes 3076
  18.3 10.0 %collective-permute-start.1 = (bf16[528,128]{1,0:T(8,128)(2,1)S(1)}, bf16[528,128]{1,0:T(8,128)(2,1)S(1)}, u32[]{:S(2)}, u32[]{:S(2)}) collective-permute-start(bf16[528,128]{1,0:T(8,128)(2,1)S(1)} %get-tuple-element.36), channel_id=1, source_target_pairs={{0,3},{1,2},{2,1},{3,0},{4,7},{5,6},{6,5},{7,4},{8,11},{9,10},{10,... | collective-permute-start | bytes 405512 | tf_op jit(solution)/shard_map/ppermute | solution.py:300
  18.4 9.9 %collective-permute-start.2 = (bf16[528,128]{1,0:T(8,128)(2,1)S(1)}, bf16[528,128]{1,0:T(8,128)(2,1)S(1)}, u32[]{:S(2)}, u32[]{:S(2)}) collective-permute-start(bf16[528,128]{1,0:T(8,128)(2,1)S(1)} %get-tuple-element.37), channel_id=1, source_target_pairs={{0,7},{1,6},{2,5},{3,4},{4,3},{5,2},{6,1},{7,0},{8,15},{9,14},{10,... | collective-permute-start | bytes 405512 | tf_op jit(solution)/shard_map/ppermute | solution.py:300
  25.3 23.2 %copy-start = (f32[256,512]{1,0:T(8,128)S(1)}, f32[256,512]{1,0:T(8,128)}, u32[]{:S(2)}) copy-start(f32[256,512]{1,0:T(8,128)} %stored_ref.1) | copy-start | bytes 1572868
  28.7 19.8 %collective-permute-start.9 = (bf16[256,512]{1,0:T(8,128)(2,1)S(1)}, bf16[256,512]{1,0:T(8,128)(2,1)S(1)}, u32[]{:S(2)}, u32[]{:S(2)}) collective-permute-start(bf16[256,512]{1,0:T(8,128)(2,1)S(1)} %get-tuple-element.51), channel_id=1, source_target_pairs={{0,24},{8,16},{16,8},{24,0},{1,25},{9,17},{17,9},{25,1},{2,26},{10... | collective-permute-start | bytes 786440 | tf_op jit(solution)/shard_map/ppermute | solution.py:300
  31.3 17.2 %collective-permute-start.8 = (bf16[256,512]{1,0:T(8,128)(2,1)S(1)}, bf16[256,512]{1,0:T(8,128)(2,1)S(1)}, u32[]{:S(2)}, u32[]{:S(2)}) collective-permute-start(bf16[256,512]{1,0:T(8,128)(2,1)S(1)} %get-tuple-element.51), channel_id=1, source_target_pairs={{0,16},{8,24},{16,0},{24,8},{1,17},{9,25},{17,1},{25,9},{2,18},{10... | collective-permute-start | bytes 786440 | tf_op jit(solution)/shard_map/ppermute | solution.py:300
  31.7 16.7 %collective-permute-start.7 = (bf16[256,512]{1,0:T(8,128)(2,1)S(1)}, bf16[256,512]{1,0:T(8,128)(2,1)S(1)}, u32[]{:S(2)}, u32[]{:S(2)}) collective-permute-start(bf16[256,512]{1,0:T(8,128)(2,1)S(1)} %get-tuple-element.51), channel_id=1, source_target_pairs={{0,8},{8,0},{16,24},{24,16},{1,9},{9,1},{17,25},{25,17},{2,10},{10... | collective-permute-start | bytes 786440 | tf_op jit(solution)/shard_map/ppermute | solution.py:300

commit v8 on v7

--- a/solution.py
+++ b/solution.py
@@ -313,9 +313,9 @@
     half, quarter, eighth = owners // 2, owners // 4, owners // 8
     groups = [
         list(range(quarter)),
-        list(range(half, half + quarter)),
-        [*range(quarter, quarter + eighth), *range(half + quarter, half + quarter + eighth)],
-        [*range(quarter + eighth, half), *range(half + quarter + eighth, owners)],
+        [*range(half, half + eighth), *range(quarter, quarter + eighth)],
+        [*range(half + eighth, half + quarter), *range(quarter + eighth, half)],
+        list(range(half + quarter, owners)),
     ]
     sent_first, last = sum(groups[:3], []), groups[3]
     block = min(clusters, 32)

time: 49.8 us -> 49.2 us (0.988)
  blocking collectives: 12.3 us -> 13 us
    all_to_all x1, blocking collectives: 12.3 us -> 13 us  [body(): lax.all_to_all(best, 'own', split_axis=0, concat_axis=0, tiled=True)]
  transfers between devices with their start and end apart: 10 -> 10, of which waited for: 2 -> 1; matrix products, arithmetic and copies ran while one was open for 0% -> 0% of each run, Pallas kernels for 33% -> 33%
where the time goes in v8:
time: 49.2 us; the launch traced here: 49 us
  Pallas kernels  19.4 us (39%)
  starting transfers between devices  13.5 us (27%)
  blocking collectives  13 us (26%)
  waiting for transfers between devices  1.67 us (3%)
  between operations  0.74 us (2%)
  local copies, waits for them, and re-layouts  0.69 us (1%)
    pallas_call x9, Pallas kernels, vmem_call(): pl.pallas_call(kernel, out_shape=out_shape, in_specs=in_specs or [whole_v...  19.4 us
    ppermute x10, starting transfers between devices, exchange(): lax.ppermute(value, axis, [(device, device ^ offset) for device in range(...  13.5 us
    all_to_all x1, blocking collectives, body(): lax.all_to_all(best, 'own', split_axis=0, concat_axis=0, tiled=True)  13 us
    ppermute x10, waiting for transfers between devices, exchange(): lax.ppermute(value, axis, [(device, device ^ offset) for device in range(...  1.67 us
  transfers between devices with their start and end apart: 10, of which 1 were waited for; matrix products, arithmetic and copies ran while one was open for 0% of the time, Pallas kernels for 33%

profile of v8, /device:TPU:0, one launch (start us, length us, event | category | flops | bytes accessed | tf_op | source)
XLA Modules:
  0.0 49.0 jit_solution(10768954093663262683)
XLA Ops:
  0.6 0.0 copy-start.2
  0.6 1.9 %pack.1 = (s32[1,512]{1,0:T(1,128)S(1)}, s32[1,512]{1,0:T(1,128)S(1)}, s32[1,512]{1,0:T(1,128)}, s32[1,512]{1,0:T(1,128)S(1)}, bf16[512,512]{1,0:T(8,128)(2,1)S(...) custom-call(s32[1]{0:T(128)} %bitcast.me_ref, ...), custom_call_target="tpu_custom_call" | custom-call | flops 1 | bytes 1 | tf_op jit(solution)/shard_map/pack/pallas_call | solution.py:327
  2.5 0.5 %collective-permute-start = (bf16[528,128]{1,0:T(8,128)(2,1)S(1)}, bf16[528,128]{1,0:T(8,128)(2,1)S(1)}, u32[]{:S(2)}, u32[]{:S(2)}) collective-permute-start(bf16[528,128]{1,0:T(8,128)(2,1)S(1)} %get-tuple-element.29), channel_id=1, source_target_pairs={{0,1},{1,0},{2,3},{3,2},{4,5},{5,4},{6,7},{7,6},{8,9},{9,8},{10,11... | collective-permute-start | bytes 405512 | tf_op jit(solution)/shard_map/ppermute | solution.py:300
  3.0 3.7 %collective-permute-start.3 = (bf16[528,128]{1,0:T(8,128)(2,1)S(1)}, bf16[528,128]{1,0:T(8,128)(2,1)S(1)}, u32[]{:S(2)}, u32[]{:S(2)}) collective-permute-start(bf16[528,128]{1,0:T(8,128)(2,1)S(1)} %get-tuple-element.40), channel_id=1, source_target_pairs={{0,4},{1,5},{2,6},{3,7},{4,0},{5,1},{6,2},{7,3},{8,12},{9,13},{10,... | collective-permute-start | bytes 405512 | tf_op jit(solution)/shard_map/ppermute | solution.py:300
  6.7 1.6 %collective-permute-start.4 = (bf16[528,128]{1,0:T(8,128)(2,1)S(1)}, bf16[528,128]{1,0:T(8,128)(2,1)S(1)}, u32[]{:S(2)}, u32[]{:S(2)}) collective-permute-start(bf16[528,128]{1,0:T(8,128)(2,1)S(1)} %get-tuple-element.41), channel_id=1, source_target_pairs={{0,2},{1,3},{2,0},{3,1},{4,6},{5,7},{6,4},{7,5},{8,10},{9,11},{10,... | collective-permute-start | bytes 405512 | tf_op jit(solution)/shard_map/ppermute | solution.py:300
  8.3 0.0 collective-permute-start.5
  8.3 0.2 collective-permute-start.6
  8.5 0.0 collective-permute-done.refs_1_
  8.5 0.7 %copy-done.1 = s32[256]{0:T(256)S(1)} copy-done((s32[256]{0:T(256)S(1)}, s32[256]{0:T(256)}, u32[]{:S(2)}) %copy-start.1) | copy-done | bytes 1048
  9.2 6.3 %first_score.1 = (bf16[256,32,512]{2,1,0:T(8,128)(2,1)S(1)}, f32[256,128]{1,0:T(8,128)S(1)}, f32[256,512]{1,0:T(8,128)S(1)}, f32[1,128]{1,0:T(1,128)S(1)}, f32[1,128]{1,0:T(1,128)S(1)}) custom-call(bf16[256,32,512]{2,1,0:T(8,128)(2,1)} %bank_ref.1, s32[1,256]{1,0:T(1,128)S(1)} %bitcast.11, bf16[528,128]{1,0:T(8,128)(2,1)S(1)} %get-tuple-element.28.refs_0_, ...), custom_call_target="tpu_custom_call" | custom-call | flops 1 | bytes 1 | tf_op jit(solution)/shard_map/first_score/pallas_call | solution.py:327
  15.6 0.3 late_pack.1
  15.9 3.9 %collective-permute-start.1 = (bf16[528,128]{1,0:T(8,128)(2,1)S(1)}, bf16[528,128]{1,0:T(8,128)(2,1)S(1)}, u32[]{:S(2)}, u32[]{:S(2)}) collective-permute-start(bf16[528,128]{1,0:T(8,128)(2,1)S(1)} %get-tuple-element.36), channel_id=1, source_target_pairs={{0,6},{1,7},{2,4},{3,5},{4,2},{5,3},{6,0},{7,1},{8,14},{9,15},{10,... | collective-permute-start | bytes 405512 | tf_op jit(solution)/shard_map/ppermute | solution.py:300
  19.8 0.0 collective-permute-done.3.refs_0_
  19.8 0.0 collective-permute-start.2
  19.8 0.0 collective-permute-done.4.refs_1_
  19.8 2.9 %score.2 = (f32[1,128]{1,0:T(1,128)S(1)}, f32[1,128]{1,0:T(1,128)S(1)}, f32[256,512]{1,0:T(8,128)S(1)}) custom-call(bf16[256,32,512]{2,1,0:T(8,128)(2,1)S(1)} %get-tuple-element.30.bank_ref, f32[256,128]{1,0:T(8,128)S(1)} %get-tuple-element.31.norm_ref, s32[1,256]{1,0:T(1,128)S(1)} %bitcast.12, f32[256,512]{1,0:T(8,128)S(1)} %get-tuple-element.35.after_ref.before_ref, ...), custom_call_target="tpu_custom_call" | custom-call | flops 1 | bytes 1 | tf_op jit(solution)/shard_map/score/pallas_call | solution.py:327
  22.8 0.0 collective-permute-done.5.refs_0_
  22.8 0.0 collective-permute-done.6.refs_1_
  22.8 0.0 copy-start
  22.8 2.9 %score.3 = (f32[1,128]{1,0:T(1,128)S(1)}, f32[1,128]{1,0:T(1,128)S(1)}, f32[256,512]{1,0:T(8,128)S(1)}) custom-call(bf16[256,32,512]{2,1,0:T(8,128)(2,1)S(1)} %get-tuple-element.30.bank_ref, f32[256,128]{1,0:T(8,128)S(1)} %get-tuple-element.31.norm_ref, s32[1,256]{1,0:T(1,128)S(1)} %bitcast.13, f32[256,512]{1,0:T(8,128)S(1)} %get-tuple-element.44.before_ref, ...), custom_call_target="tpu_custom_call" | custom-call | flops 1 | bytes 1 | tf_op jit(solution)/shard_map/score/pallas_call | solution.py:327
  25.7 0.0 collective-permute-done.1.refs_0_
  25.7 1.6 %collective-permute-done.2.refs_1_ = bf16[528,128]{1,0:T(8,128)(2,1)S(1)} collective-permute-done((bf16[528,128]{1,0:T(8,128)(2,1)S(1)}, bf16[528,128]{1,0:T(8,128)(2,1)S(1)}, u32[]{:S(2)}, u32[]{:S(2)}) %collective-permute-start.2) | collective-permute-done | bytes 135200 | tf_op jit(solution)/shard_map/ppermute | solution.py:300
  27.4 0.4 last_sum.1
  27.8 2.5 %collective-permute-start.9 = (bf16[256,512]{1,0:T(8,128)(2,1)S(1)}, bf16[256,512]{1,0:T(8,128)(2,1)S(1)}, u32[]{:S(2)}, u32[]{:S(2)}) collective-permute-start(bf16[256,512]{1,0:T(8,128)(2,1)S(1)} %get-tuple-element.51), channel_id=1, source_target_pairs={{0,24},{8,16},{16,8},{24,0},{1,25},{9,17},{17,9},{25,1},{2,26},{10... | collective-permute-start | bytes 786440 | tf_op jit(solution)/shard_map/ppermute | solution.py:300
  30.3 0.5 %collective-permute-start.8 = (bf16[256,512]{1,0:T(8,128)(2,1)S(1)}, bf16[256,512]{1,0:T(8,128)(2,1)S(1)}, u32[]{:S(2)}, u32[]{:S(2)}) collective-permute-start(bf16[256,512]{1,0:T(8,128)(2,1)S(1)} %get-tuple-element.51), channel_id=1, source_target_pairs={{0,16},{8,24},{16,0},{24,8},{1,17},{9,25},{17,1},{25,9},{2,18},{10... | collective-permute-start | bytes 786440 | tf_op jit(solution)/shard_map/ppermute | solution.py:300
  30.8 0.5 %collective-permute-start.7 = (bf16[256,512]{1,0:T(8,128)(2,1)S(1)}, bf16[256,512]{1,0:T(8,128)(2,1)S(1)}, u32[]{:S(2)}, u32[]{:S(2)}) collective-permute-start(bf16[256,512]{1,0:T(8,128)(2,1)S(1)} %get-tuple-element.51), channel_id=1, source_target_pairs={{0,8},{8,0},{16,24},{24,16},{1,9},{9,1},{17,25},{25,17},{2,10},{10... | collective-permute-start | bytes 786440 | tf_op jit(solution)/shard_map/ppermute | solution.py:300
  31.3 2.8 %last_score.1 = f32[8,128]{1,0:T(8,128)S(1)} custom-call(s32[1]{0:T(128)} %bitcast.me_ref, bf16[256,32,512]{2,1,0:T(8,128)(2,1)S(1)} %get-tuple-element.30.bank_ref, f32[256,128]{1,0:T(8,128)S(1)} %get-tuple-element.31.norm_ref, s32[1,256]{1,0:T(1,128)S(1)} %bitcast.14, bf16[528,128]{1,0:T(8,128)(2,1)S(1)} %collective-permute-done.1.refs_0_, ...), custom_call_target="tpu_custom_call" | custom-call | flops 1 | bytes 1 | tf_op jit(solution)/shard_map/last_score/pallas_call | solution.py:327
  34.2 13.0 %all_to_all.11 = f32[8,1,128]{2,1,0:T(1,128)S(1)} all-to-all(f32[8,1,128]{2,1,0:T(1,128)S(1)} %bitcast.9), channel_id=1, replica_groups=mesh['grp'=4,'own'=8] {'own'}, dimensions={0} | all-to-all | bytes 8192 | tf_op jit(solution)/shard_map/all_to_all | solution.py:409
  47.1 0.8 %unpack.1 = f32[1,512]{1,0:T(1,128)} custom-call(s32[1,512]{1,0:T(1,128)S(1)} %get-tuple-element.27.index_ref, f32[8,128]{1,0:T(8,128)S(1)} %bitcast.10), custom_call_target="tpu_custom_call" | custom-call | flops 1 | bytes 1 | tf_op jit(solution)/shard_map/unpack/pallas_call | solution.py:327
  48.0 0.0 collective-permute-done.9.refs_2_
  48.0 0.0 collective-permute-done.8.refs_1_
  48.0 1.0 %finish.1 = f32[256,512]{1,0:T(8,128)} custom-call(f32[256,512]{1,0:T(8,128)S(1)} %copy-done, f32[256,512]{1,0:T(8,128)S(1)} %get-tuple-element.50.own_ref, bf16[256,512]{1,0:T(8,128)(2,1)S(1)} %collective-permute-done.7.refs_0_, bf16[256,512]{1,0:T(8,128)(2,1)S(1)} %collective-permute-done.8.refs_1_, bf16[256,512]{1,0:T(8,128)(2,1)S(1)} %collective-permute-done.9.refs_2_), custom_call_target="tpu_custom_call" | custom-call | flops 1 | bytes 1 | tf_op jit(solution)/shard_map/finish/pallas_call | solution.py:327
  (4 shorter events, 0.0 us)
Async XLA Ops:
  0.6 19.2 %copy-start.2 = (s32[256]{0:T(256)S(1)}, s32[256]{0:T(256)}, u32[]{:S(2)}) copy-start(s32[256]{0:T(256)} %param.10) | copy-start | bytes 3076
  2.5 6.0 %collective-permute-start = (bf16[528,128]{1,0:T(8,128)(2,1)S(1)}, bf16[528,128]{1,0:T(8,128)(2,1)S(1)}, u32[]{:S(2)}, u32[]{:S(2)}) collective-permute-start(bf16[528,128]{1,0:T(8,128)(2,1)S(1)} %get-tuple-element.29), channel_id=1, source_target_pairs={{0,1},{1,0},{2,3},{3,2},{4,5},{5,4},{6,7},{7,6},{8,9},{9,8},{10,11... | collective-permute-start | bytes 405512 | tf_op jit(solution)/shard_map/ppermute | solution.py:300
  3.0 16.8 %collective-permute-start.3 = (bf16[528,128]{1,0:T(8,128)(2,1)S(1)}, bf16[528,128]{1,0:T(8,128)(2,1)S(1)}, u32[]{:S(2)}, u32[]{:S(2)}) collective-permute-start(bf16[528,128]{1,0:T(8,128)(2,1)S(1)} %get-tuple-element.40), channel_id=1, source_target_pairs={{0,4},{1,5},{2,6},{3,7},{4,0},{5,1},{6,2},{7,3},{8,12},{9,13},{10,... | collective-permute-start | bytes 405512 | tf_op jit(solution)/shard_map/ppermute | solution.py:300
  6.7 13.1 %collective-permute-start.4 = (bf16[528,128]{1,0:T(8,128)(2,1)S(1)}, bf16[528,128]{1,0:T(8,128)(2,1)S(1)}, u32[]{:S(2)}, u32[]{:S(2)}) collective-permute-start(bf16[528,128]{1,0:T(8,128)(2,1)S(1)} %get-tuple-element.41), channel_id=1, source_target_pairs={{0,2},{1,3},{2,0},{3,1},{4,6},{5,7},{6,4},{7,5},{8,10},{9,11},{10,... | collective-permute-start | bytes 405512 | tf_op jit(solution)/shard_map/ppermute | solution.py:300
  8.3 14.5 %collective-permute-start.5 = (bf16[528,128]{1,0:T(8,128)(2,1)S(1)}, bf16[528,128]{1,0:T(8,128)(2,1)S(1)}, u32[]{:S(2)}, u32[]{:S(2)}) collective-permute-start(bf16[528,128]{1,0:T(8,128)(2,1)S(1)} %get-tuple-element.45), channel_id=1, source_target_pairs={{0,5},{1,4},{2,7},{3,6},{4,1},{5,0},{6,3},{7,2},{8,13},{9,12},{10,... | collective-permute-start | bytes 405512 | tf_op jit(solution)/shard_map/ppermute | solution.py:300
  8.3 14.5 %collective-permute-start.6 = (bf16[528,128]{1,0:T(8,128)(2,1)S(1)}, bf16[528,128]{1,0:T(8,128)(2,1)S(1)}, u32[]{:S(2)}, u32[]{:S(2)}) collective-permute-start(bf16[528,128]{1,0:T(8,128)(2,1)S(1)} %get-tuple-element.46), channel_id=1, source_target_pairs={{0,3},{1,2},{2,1},{3,0},{4,7},{5,6},{6,5},{7,4},{8,11},{9,10},{10,... | collective-permute-start | bytes 405512 | tf_op jit(solution)/shard_map/ppermute | solution.py:300
  8.5 0.7 %copy-start.1 = (s32[256]{0:T(256)S(1)}, s32[256]{0:T(256)}, u32[]{:S(2)}) copy-start(s32[256]{0:T(256)} %param.10) | copy-start | bytes 3076
  15.9 9.9 %collective-permute-start.1 = (bf16[528,128]{1,0:T(8,128)(2,1)S(1)}, bf16[528,128]{1,0:T(8,128)(2,1)S(1)}, u32[]{:S(2)}, u32[]{:S(2)}) collective-permute-start(bf16[528,128]{1,0:T(8,128)(2,1)S(1)} %get-tuple-element.36), channel_id=1, source_target_pairs={{0,6},{1,7},{2,4},{3,5},{4,2},{5,3},{6,0},{7,1},{8,14},{9,15},{10,... | collective-permute-start | bytes 405512 | tf_op jit(solution)/shard_map/ppermute | solution.py:300
  19.8 7.6 %collective-permute-start.2 = (bf16[528,128]{1,0:T(8,128)(2,1)S(1)}, bf16[528,128]{1,0:T(8,128)(2,1)S(1)}, u32[]{:S(2)}, u32[]{:S(2)}) collective-permute-start(bf16[528,128]{1,0:T(8,128)(2,1)S(1)} %get-tuple-element.37), channel_id=1, source_target_pairs={{0,7},{1,6},{2,5},{3,4},{4,3},{5,2},{6,1},{7,0},{8,15},{9,14},{10,... | collective-permute-start | bytes 405512 | tf_op jit(solution)/shard_map/ppermute | solution.py:300
  22.8 25.2 %copy-start = (f32[256,512]{1,0:T(8,128)S(1)}, f32[256,512]{1,0:T(8,128)}, u32[]{:S(2)}) copy-start(f32[256,512]{1,0:T(8,128)} %stored_ref.1) | copy-start | bytes 1572868
  27.8 20.2 %collective-permute-start.9 = (bf16[256,512]{1,0:T(8,128)(2,1)S(1)}, bf16[256,512]{1,0:T(8,128)(2,1)S(1)}, u32[]{:S(2)}, u32[]{:S(2)}) collective-permute-start(bf16[256,512]{1,0:T(8,128)(2,1)S(1)} %get-tuple-element.51), channel_id=1, source_target_pairs={{0,24},{8,16},{16,8},{24,0},{1,25},{9,17},{17,9},{25,1},{2,26},{10... | collective-permute-start | bytes 786440 | tf_op jit(solution)/shard_map/ppermute | solution.py:300
  30.3 17.7 %collective-permute-start.8 = (bf16[256,512]{1,0:T(8,128)(2,1)S(1)}, bf16[256,512]{1,0:T(8,128)(2,1)S(1)}, u32[]{:S(2)}, u32[]{:S(2)}) collective-permute-start(bf16[256,512]{1,0:T(8,128)(2,1)S(1)} %get-tuple-element.51), channel_id=1, source_target_pairs={{0,16},{8,24},{16,0},{24,8},{1,17},{9,25},{17,1},{25,9},{2,18},{10... | collective-permute-start | bytes 786440 | tf_op jit(solution)/shard_map/ppermute | solution.py:300
  30.8 17.2 %collective-permute-start.7 = (bf16[256,512]{1,0:T(8,128)(2,1)S(1)}, bf16[256,512]{1,0:T(8,128)(2,1)S(1)}, u32[]{:S(2)}, u32[]{:S(2)}) collective-permute-start(bf16[256,512]{1,0:T(8,128)(2,1)S(1)} %get-tuple-element.51), channel_id=1, source_target_pairs={{0,8},{8,0},{16,24},{24,16},{1,9},{9,1},{17,25},{25,17},{2,10},{10... | collective-permute-start | bytes 786440 | tf_op jit(solution)/shard_map/ppermute | solution.py:300

commit v9 on v8

--- a/solution.py
+++ b/solution.py
@@ -207,29 +207,27 @@
         best_ref[...] = best[:, number * capacity : (number + 1) * capacity]
 
 
-def score_group(message_refs, capacity, block, bank_ref, norm_ref, members_ref):
-    clusters, depth, width = bank_ref.shape
-    units, slots = read_messages(message_refs, capacity, width)
-    onehot = cluster_onehot(slots, clusters)
-    columns = units.T
+def score_columns(columns, slots, onehot, capacity, block, bank_ref, norm_ref, members_ref):
+    clusters, depth, _ = bank_ref.shape
     picked = jnp.zeros((depth, slots.shape[1]), jnp.float32)
     for number in range(clusters // block):
         bank_block = bank_ref[pl.ds(number * block, block)]
         picked = pick_dots(bank_block, number * block, columns, slots, picked)
     best = best_cosines(picked, onehot, norm_ref[...], members_ref[...])
-    results = [
-        best[:, number * capacity : (number + 1) * capacity]
-        for number in range(len(message_refs))
+    return [
+        best[:, low : low + capacity] for low in range(0, slots.shape[1], capacity)
     ]
-    return results, onehot, units
 
 
 def score_kernel(
     messages, capacity, block, bank_ref, norm_ref, members_ref, before_ref, *refs
 ):
     message_refs, refs = refs[:messages], refs[messages:]
-    results, onehot, units = score_group(
-        message_refs, capacity, block, bank_ref, norm_ref, members_ref
+    clusters, _, width = bank_ref.shape
+    units, slots = read_messages(message_refs, capacity, width)
+    onehot = cluster_onehot(slots, clusters)
+    results = score_columns(
+        units.T, slots, onehot, capacity, block, bank_ref, norm_ref, members_ref
     )
     *best_refs, sum_ref = refs
     for best_ref, value in zip(best_refs, results):
@@ -238,9 +236,13 @@
 
 
 def last_sum_kernel(messages, capacity, *refs):
-    message_refs, before_ref, total_ref, sent_ref = refs[:messages], *refs[messages:]
+    message_refs, before_ref, total_ref, sent_ref, columns_ref, slots_ref = (
+        refs[:messages], *refs[messages:]
+    )
     clusters, width = total_ref.shape
     units, slots = read_messages(message_refs, capacity, width)
+    columns_ref[...] = units.T
+    slots_ref[...] = slots
     total = before_ref[...] + jnp.dot(
         cluster_onehot(slots, clusters), units, preferred_element_type=jnp.float32
     )
@@ -249,10 +251,14 @@
 
 
 def last_score_kernel(
-    messages, places, capacity, block, me_ref, bank_ref, norm_ref, members_ref, *refs
+    places, capacity, block, me_ref, bank_ref, norm_ref, members_ref, columns_ref, slots_ref, *refs
 ):
-    message_refs, earlier_refs, best_ref = refs[:messages], refs[messages:-1], refs[-1]
-    results, _, _ = score_group(message_refs, capacity, block, bank_ref, norm_ref, members_ref)
+    earlier_refs, best_ref = refs[:-1], refs[-1]
+    slots = slots_ref[...]
+    onehot = cluster_onehot(slots, bank_ref.shape[0])
+    results = score_columns(
+        columns_ref[...], slots, onehot, capacity, block, bank_ref, norm_ref, members_ref
+    )
     for value, place in zip([ref[...] for ref in earlier_refs] + results, places):
         best_ref[pl.ds(me_ref[0] ^ place, 1), :] = value
 
@@ -317,7 +323,9 @@
         [*range(half + eighth, half + quarter), *range(quarter + eighth, half)],
         list(range(half + quarter, owners)),
     ]
-    sent_first, last = sum(groups[:3], []), groups[3]
+    sent_first = groups[1][:eighth]
+    sent_next = groups[0] + groups[1][eighth:] + groups[2]
+    last = groups[3]
     block = min(clusters, 32)
 
     def vmem_call(
@@ -351,10 +359,17 @@
         [smem] + [anywhere] * 3,
         [pltpu.SemaphoreType.DMA((3,))],
     )
-    got = {
-        peer: exchange(value, "own", peer) if peer else value
-        for peer, value in zip(sent_first, sent)
-    }
+    got = {peer: exchange(value, "own", peer) for peer, value in zip(sent_first, sent)}
+    packed = vmem_call(
+        functools.partial(late_pack_kernel, capacity, sent_next),
+        "next_pack",
+        [message] * len(sent_next),
+        [index, slots, values, sent[0]],
+        [whole_vmem()] * 3 + [anywhere],
+    )
+    got.update(
+        {peer: exchange(value, "own", peer) if peer else value for peer, value in zip(sent_next, packed)}
+    )
     member_row = members.reshape(1, clusters)
     sums = jax.ShapeDtypeStruct((clusters, width), jnp.float32)
 
@@ -390,21 +405,26 @@
         )
         best += found
     last_messages = [got[peer] for peer in last]
-    total, sent = vmem_call(
+    total, sent, columns, column_slots = vmem_call(
         functools.partial(last_sum_kernel, quarter, capacity),
         "last_sum",
-        [sums, jax.ShapeDtypeStruct((clusters, width), jnp.bfloat16)],
+        [
+            sums,
+            jax.ShapeDtypeStruct((clusters, width), jnp.bfloat16),
+            jax.ShapeDtypeStruct((width, len(last) * capacity), jnp.bfloat16),
+            jax.ShapeDtypeStruct((1, len(last) * capacity), jnp.int32),
+        ],
         [*last_messages, total],
     )
     terms = [exchange(sent, "grp", offset) for offset in range(1, parts)]
     best = vmem_call(
         functools.partial(
-            last_score_kernel, quarter, sum(groups, []), capacity, block
+            last_score_kernel, sum(groups, []), capacity, block
         ),
         "last_score",
         jax.ShapeDtypeStruct((owners, capacity), jnp.float32),
-        [own_index, held_bank, bank_norm, member_row, *last_messages, *best],
-        [smem] + [whole_vmem()] * (3 + owners),
+        [own_index, held_bank, bank_norm, member_row, columns, column_slots, *best],
+        [smem] + [whole_vmem()] * (5 + len(best)),
     )
     returned = lax.all_to_all(best, "own", split_axis=0, concat_axis=0, tiled=True)
     best_cosine = vmem_call(

time: 49.2 us -> 49.4 us (level)
    pallas_call x9 -> x10, Pallas kernels: 19.4 us -> 19.6 us  [vmem_call(): pl.pallas_call(kernel, out_shape=out_shape, in_specs=in_specs or [whole_v...]
  transfers between devices with their start and end apart: 10 -> 10, of which waited for: 1 -> 1; matrix products, arithmetic and copies ran while one was open for 0% -> 0% of each run, Pallas kernels for 33% -> 32%
where the time goes in v9:
time: 49.4 us; the launch traced here: 49.2 us
  Pallas kernels  19.6 us (40%)
  starting transfers between devices  13.5 us (27%)
  blocking collectives  13 us (26%)
  waiting for transfers between devices  1.67 us (3%)
  between operations  0.73 us (1%)
  local copies, waits for them, and re-layouts  0.69 us (1%)
    pallas_call x10, Pallas kernels, vmem_call(): pl.pallas_call(kernel, out_shape=out_shape, in_specs=in_specs or [whole_v...  19.6 us
    ppermute x10, starting transfers between devices, exchange(): lax.ppermute(value, axis, [(device, device ^ offset) for device in range(...  13.5 us
    all_to_all x1, blocking collectives, body(): lax.all_to_all(best, 'own', split_axis=0, concat_axis=0, tiled=True)  13 us
    ppermute x10, waiting for transfers between devices, exchange(): lax.ppermute(value, axis, [(device, device ^ offset) for device in range(...  1.67 us
  transfers between devices with their start and end apart: 10, of which 1 were waited for; matrix products, arithmetic and copies ran while one was open for 0% of the time, Pallas kernels for 32%

profile of v9, /device:TPU:0, one launch (start us, length us, event | category | flops | bytes accessed | tf_op | source)
XLA Modules:
  0.0 49.2 jit_solution(10685222018954017816)
XLA Ops:
  0.6 1.7 %pack.1 = (s32[1,512]{1,0:T(1,128)S(1)}, s32[1,512]{1,0:T(1,128)S(1)}, s32[1,512]{1,0:T(1,128)}, s32[1,512]{1,0:T(1,128)S(1)}, bf16[512,512]{1,0:T(8,128)(2,1)S(1)}, /*index=5*/bf16[528,128]{1,0:T(8,128)(2,1)S(1)}) custom-call(s32[1]{0:T(128)} %bitcast.me_ref, s32[1,512]{1,0:T(1,128)} %bitcast.15, s32[1,512]{1,0:T(1,128)} %bitcast.16, bf16[512,512]{1,0:T(8,128)(2,1)} %refs_2_.1), custom_call_target="tpu_custom_call" | custom-call | flops 1 | bytes 1 | tf_op jit(solution)/shard_map/pack/pallas_call | solution.py:335
  2.3 0.7 %next_pack.1 = (bf16[528,128]{1,0:T(8,128)(2,1)S(1)}, bf16[528,128]{1,0:T(8,128)(2,1)S(1)}, bf16[528,128]{1,0:T(8,128)(2,1)S(1)}, bf16[528,128]{1,0:T(8,128)(2,1)S(1)}, bf16[528,128]{1,0:T(8,128)(2,1)S(1)}) custom-call(s32[1,512]{1,0:T(1,128)S(1)} %get-tuple-element.30.index_ref, s32[1,512]{1,0:T(1,128)S(1)} %get-tuple-element.31.slot_ref, ...), custom_call_target="tpu_custom_call" | custom-call | flops 1 | bytes 1 | tf_op jit(solution)/shard_map/next_pack/pallas_call | solution.py:335
  3.0 0.5 %collective-permute-start = (bf16[528,128]{1,0:T(8,128)(2,1)S(1)}, bf16[528,128]{1,0:T(8,128)(2,1)S(1)}, u32[]{:S(2)}, u32[]{:S(2)}) collective-permute-start(bf16[528,128]{1,0:T(8,128)(2,1)S(1)} %get-tuple-element.35), channel_id=1, source_target_pairs={{0,1},{1,0},{2,3},{3,2},{4,5},{5,4},{6,7},{7,6},{8,9},{9,8},{10,11... | collective-permute-start | bytes 405512 | tf_op jit(solution)/shard_map/ppermute | solution.py:306
  3.5 3.7 %collective-permute-start.3 = (bf16[528,128]{1,0:T(8,128)(2,1)S(1)}, bf16[528,128]{1,0:T(8,128)(2,1)S(1)}, u32[]{:S(2)}, u32[]{:S(2)}) collective-permute-start(bf16[528,128]{1,0:T(8,128)(2,1)S(1)} %get-tuple-element.33.after_ref), channel_id=1, source_target_pairs={{0,4},{1,5},{2,6},{3,7},{4,0},{5,1},{6,2},{7,3},{8,12},{9,13},{10,... | collective-permute-start | bytes 405512 | tf_op jit(solution)/shard_map/ppermute | solution.py:306
  7.2 1.6 %collective-permute-start.4 = (bf16[528,128]{1,0:T(8,128)(2,1)S(1)}, bf16[528,128]{1,0:T(8,128)(2,1)S(1)}, u32[]{:S(2)}, u32[]{:S(2)}) collective-permute-start(bf16[528,128]{1,0:T(8,128)(2,1)S(1)} %get-tuple-element.41), channel_id=1, source_target_pairs={{0,2},{1,3},{2,0},{3,1},{4,6},{5,7},{6,4},{7,5},{8,10},{9,11},{10,... | collective-permute-start | bytes 405512 | tf_op jit(solution)/shard_map/ppermute | solution.py:306
  8.7 0.0 collective-permute-start.5
  8.7 0.2 collective-permute-start.6
  9.0 0.0 collective-permute-done.refs_1_
  9.0 0.7 %copy-done.1 = s32[256]{0:T(256)S(1)} copy-done((s32[256]{0:T(256)S(1)}, s32[256]{0:T(256)}, u32[]{:S(2)}) %copy-start.1) | copy-done | bytes 1048
  9.7 6.3 %first_score.1 = (bf16[256,32,512]{2,1,0:T(8,128)(2,1)S(1)}, f32[256,128]{1,0:T(8,128)S(1)}, f32[256,512]{1,0:T(8,128)S(1)}, f32[1,128]{1,0:T(1,128)S(1)}, f32[1,128]{1,0:T(1,128)S(1)}) custom-call(bf16[256,32,512]{2,1,0:T(8,128)(2,1)} %bank_ref.1, s32[1,256]{1,0:T(1,128)S(1)} %bitcast.11, bf16[528,128]{1,0:T(8,128)(2,1)S(1)} %get-tuple-element.34.refs_0_, ...), custom_call_target="tpu_custom_call" | custom-call | flops 1 | bytes 1 | tf_op jit(solution)/shard_map/first_score/pallas_call | solution.py:335
  16.0 0.3 late_pack.1
  16.3 3.9 %collective-permute-start.1 = (bf16[528,128]{1,0:T(8,128)(2,1)S(1)}, bf16[528,128]{1,0:T(8,128)(2,1)S(1)}, u32[]{:S(2)}, u32[]{:S(2)}) collective-permute-start(bf16[528,128]{1,0:T(8,128)(2,1)S(1)} %get-tuple-element.39), channel_id=1, source_target_pairs={{0,6},{1,7},{2,4},{3,5},{4,2},{5,3},{6,0},{7,1},{8,14},{9,15},{10,... | collective-permute-start | bytes 405512 | tf_op jit(solution)/shard_map/ppermute | solution.py:306
  20.3 0.0 collective-permute-done.3.refs_0_
  20.3 0.0 collective-permute-start.2
  20.3 0.0 collective-permute-done.4.refs_1_
  20.3 0.0 copy-start.2
  20.3 2.9 %score.2 = (f32[1,128]{1,0:T(1,128)S(1)}, f32[1,128]{1,0:T(1,128)S(1)}, f32[256,512]{1,0:T(8,128)S(1)}) custom-call(bf16[256,32,512]{2,1,0:T(8,128)(2,1)S(1)} %get-tuple-element.36.bank_ref, f32[256,128]{1,0:T(8,128)S(1)} %get-tuple-element.37.norm_ref, s32[1,256]{1,0:T(1,128)S(1)} %bitcast.12, f32[256,512]{1,0:T(8,128)S(1)} %get-tuple-element.38.after_ref.before_ref, ...), custom_call_target="tpu_custom_call" | custom-call | flops 1 | bytes 1 | tf_op jit(solution)/shard_map/score/pallas_call | solution.py:335
  23.2 0.0 copy-start
  23.2 2.9 %score.3 = (f32[1,128]{1,0:T(1,128)S(1)}, f32[1,128]{1,0:T(1,128)S(1)}, f32[256,512]{1,0:T(8,128)S(1)}) custom-call(bf16[256,32,512]{2,1,0:T(8,128)(2,1)S(1)} %get-tuple-element.36.bank_ref, f32[256,128]{1,0:T(8,128)S(1)} %get-tuple-element.37.norm_ref, s32[1,256]{1,0:T(1,128)S(1)} %bitcast.13, f32[256,512]{1,0:T(8,128)S(1)} %get-tuple-element.42.before_ref, ...), custom_call_target="tpu_custom_call" | custom-call | flops 1 | bytes 1 | tf_op jit(solution)/shard_map/score/pallas_call | solution.py:335
  26.2 0.0 collective-permute-done.1.refs_0_
  26.2 1.6 %collective-permute-done.2.refs_1_ = bf16[528,128]{1,0:T(8,128)(2,1)S(1)} collective-permute-done((bf16[528,128]{1,0:T(8,128)(2,1)S(1)}, bf16[528,128]{1,0:T(8,128)(2,1)S(1)}, u32[]{:S(2)}, u32[]{:S(2)}) %collective-permute-start.2) | collective-permute-done | bytes 135200 | tf_op jit(solution)/shard_map/ppermute | solution.py:306
  27.8 0.4 last_sum.1
  28.2 2.5 %collective-permute-start.9 = (bf16[256,512]{1,0:T(8,128)(2,1)S(1)}, bf16[256,512]{1,0:T(8,128)(2,1)S(1)}, u32[]{:S(2)}, u32[]{:S(2)}) collective-permute-start(bf16[256,512]{1,0:T(8,128)(2,1)S(1)} %get-tuple-element.55), channel_id=1, source_target_pairs={{0,24},{8,16},{16,8},{24,0},{1,25},{9,17},{17,9},{25,1},{2,26},{10... | collective-permute-start | bytes 786440 | tf_op jit(solution)/shard_map/ppermute | solution.py:306
  30.7 0.5 %collective-permute-start.8 = (bf16[256,512]{1,0:T(8,128)(2,1)S(1)}, bf16[256,512]{1,0:T(8,128)(2,1)S(1)}, u32[]{:S(2)}, u32[]{:S(2)}) collective-permute-start(bf16[256,512]{1,0:T(8,128)(2,1)S(1)} %get-tuple-element.55), channel_id=1, source_target_pairs={{0,16},{8,24},{16,0},{24,8},{1,17},{9,25},{17,1},{25,9},{2,18},{10... | collective-permute-start | bytes 786440 | tf_op jit(solution)/shard_map/ppermute | solution.py:306
  31.2 0.5 %collective-permute-start.7 = (bf16[256,512]{1,0:T(8,128)(2,1)S(1)}, bf16[256,512]{1,0:T(8,128)(2,1)S(1)}, u32[]{:S(2)}, u32[]{:S(2)}) collective-permute-start(bf16[256,512]{1,0:T(8,128)(2,1)S(1)} %get-tuple-element.55), channel_id=1, source_target_pairs={{0,8},{8,0},{16,24},{24,16},{1,9},{9,1},{17,25},{25,17},{2,10},{10... | collective-permute-start | bytes 786440 | tf_op jit(solution)/shard_map/ppermute | solution.py:306
  31.8 2.6 %last_score.1 = f32[8,128]{1,0:T(8,128)S(1)} custom-call(s32[1]{0:T(128)} %bitcast.me_ref, bf16[256,32,512]{2,1,0:T(8,128)(2,1)S(1)} %get-tuple-element.36.bank_ref, f32[256,128]{1,0:T(8,128)S(1)} %get-tuple-element.37.norm_ref, s32[1,256]{1,0:T(1,128)S(1)} %bitcast.14, bf16[512,256]{1,0:T(8,128)(2,1)S(1)} %get-tuple-element.46.columns_ref, ...), custom_call_target="tpu_custom_call" | custom-call | flops 1 | bytes 1 | tf_op jit(solution)/shard_map/last_score/pallas_call | solution.py:335
  34.4 13.0 %all_to_all.11 = f32[8,1,128]{2,1,0:T(1,128)S(1)} all-to-all(f32[8,1,128]{2,1,0:T(1,128)S(1)} %bitcast.9), channel_id=1, replica_groups=mesh['grp'=4,'own'=8] {'own'}, dimensions={0} | all-to-all | bytes 8192 | tf_op jit(solution)/shard_map/all_to_all | solution.py:429
  47.3 0.8 %unpack.1 = f32[1,512]{1,0:T(1,128)} custom-call(s32[1,512]{1,0:T(1,128)S(1)} %get-tuple-element.29.index_ref, f32[8,128]{1,0:T(8,128)S(1)} %bitcast.10), custom_call_target="tpu_custom_call" | custom-call | flops 1 | bytes 1 | tf_op jit(solution)/shard_map/unpack/pallas_call | solution.py:335
  48.2 0.0 collective-permute-done.9.refs_2_
  48.2 0.0 collective-permute-done.8.refs_1_
  48.2 0.0 collective-permute-done.7.refs_0_
  48.2 1.0 %finish.1 = f32[256,512]{1,0:T(8,128)} custom-call(f32[256,512]{1,0:T(8,128)S(1)} %copy-done, f32[256,512]{1,0:T(8,128)S(1)} %get-tuple-element.54.own_ref, bf16[256,512]{1,0:T(8,128)(2,1)S(1)} %collective-permute-done.7.refs_0_, bf16[256,512]{1,0:T(8,128)(2,1)S(1)} %collective-permute-done.8.refs_1_, bf16[256,512]{1,0:T(8,128)(2,1)S(1)} %collective-permute-done.9.refs_2_), custom_call_target="tpu_custom_call" | custom-call | flops 1 | bytes 1 | tf_op jit(solution)/shard_map/finish/pallas_call | solution.py:335
  (5 shorter events, 0.0 us)
Async XLA Ops:
  3.0 6.0 %collective-permute-start = (bf16[528,128]{1,0:T(8,128)(2,1)S(1)}, bf16[528,128]{1,0:T(8,128)(2,1)S(1)}, u32[]{:S(2)}, u32[]{:S(2)}) collective-permute-start(bf16[528,128]{1,0:T(8,128)(2,1)S(1)} %get-tuple-element.35), channel_id=1, source_target_pairs={{0,1},{1,0},{2,3},{3,2},{4,5},{5,4},{6,7},{7,6},{8,9},{9,8},{10,11... | collective-permute-start | bytes 405512 | tf_op jit(solution)/shard_map/ppermute | solution.py:306
  3.5 16.8 %collective-permute-start.3 = (bf16[528,128]{1,0:T(8,128)(2,1)S(1)}, bf16[528,128]{1,0:T(8,128)(2,1)S(1)}, u32[]{:S(2)}, u32[]{:S(2)}) collective-permute-start(bf16[528,128]{1,0:T(8,128)(2,1)S(1)} %get-tuple-element.33.after_ref), channel_id=1, source_target_pairs={{0,4},{1,5},{2,6},{3,7},{4,0},{5,1},{6,2},{7,3},{8,12},{9,13},{10,... | collective-permute-start | bytes 405512 | tf_op jit(solution)/shard_map/ppermute | solution.py:306
  7.2 13.1 %collective-permute-start.4 = (bf16[528,128]{1,0:T(8,128)(2,1)S(1)}, bf16[528,128]{1,0:T(8,128)(2,1)S(1)}, u32[]{:S(2)}, u32[]{:S(2)}) collective-permute-start(bf16[528,128]{1,0:T(8,128)(2,1)S(1)} %get-tuple-element.41), channel_id=1, source_target_pairs={{0,2},{1,3},{2,0},{3,1},{4,6},{5,7},{6,4},{7,5},{8,10},{9,11},{10,... | collective-permute-start | bytes 405512 | tf_op jit(solution)/shard_map/ppermute | solution.py:306
  8.7 14.5 %collective-permute-start.5 = (bf16[528,128]{1,0:T(8,128)(2,1)S(1)}, bf16[528,128]{1,0:T(8,128)(2,1)S(1)}, u32[]{:S(2)}, u32[]{:S(2)}) collective-permute-start(bf16[528,128]{1,0:T(8,128)(2,1)S(1)} %get-tuple-element.43), channel_id=1, source_target_pairs={{0,5},{1,4},{2,7},{3,6},{4,1},{5,0},{6,3},{7,2},{8,13},{9,12},{10,... | collective-permute-start | bytes 405512 | tf_op jit(solution)/shard_map/ppermute | solution.py:306
  8.7 14.5 %collective-permute-start.6 = (bf16[528,128]{1,0:T(8,128)(2,1)S(1)}, bf16[528,128]{1,0:T(8,128)(2,1)S(1)}, u32[]{:S(2)}, u32[]{:S(2)}) collective-permute-start(bf16[528,128]{1,0:T(8,128)(2,1)S(1)} %get-tuple-element.44), channel_id=1, source_target_pairs={{0,3},{1,2},{2,1},{3,0},{4,7},{5,6},{6,5},{7,4},{8,11},{9,10},{10,... | collective-permute-start | bytes 405512 | tf_op jit(solution)/shard_map/ppermute | solution.py:306
  9.0 0.7 %copy-start.1 = (s32[256]{0:T(256)S(1)}, s32[256]{0:T(256)}, u32[]{:S(2)}) copy-start(s32[256]{0:T(256)} %param.10) | copy-start | bytes 3076
  16.3 9.9 %collective-permute-start.1 = (bf16[528,128]{1,0:T(8,128)(2,1)S(1)}, bf16[528,128]{1,0:T(8,128)(2,1)S(1)}, u32[]{:S(2)}, u32[]{:S(2)}) collective-permute-start(bf16[528,128]{1,0:T(8,128)(2,1)S(1)} %get-tuple-element.39), channel_id=1, source_target_pairs={{0,6},{1,7},{2,4},{3,5},{4,2},{5,3},{6,0},{7,1},{8,14},{9,15},{10,... | collective-permute-start | bytes 405512 | tf_op jit(solution)/shard_map/ppermute | solution.py:306
  20.3 7.6 %collective-permute-start.2 = (bf16[528,128]{1,0:T(8,128)(2,1)S(1)}, bf16[528,128]{1,0:T(8,128)(2,1)S(1)}, u32[]{:S(2)}, u32[]{:S(2)}) collective-permute-start(bf16[528,128]{1,0:T(8,128)(2,1)S(1)} %get-tuple-element.40), channel_id=1, source_target_pairs={{0,7},{1,6},{2,5},{3,4},{4,3},{5,2},{6,1},{7,0},{8,15},{9,14},{10,... | collective-permute-start | bytes 405512 | tf_op jit(solution)/shard_map/ppermute | solution.py:306
  20.3 11.5 %copy-start.2 = (s32[256]{0:T(256)S(1)}, s32[256]{0:T(256)}, u32[]{:S(2)}) copy-start(s32[256]{0:T(256)} %param.10) | copy-start | bytes 3076
  23.2 25.0 %copy-start = (f32[256,512]{1,0:T(8,128)S(1)}, f32[256,512]{1,0:T(8,128)}, u32[]{:S(2)}) copy-start(f32[256,512]{1,0:T(8,128)} %stored_ref.1) | copy-start | bytes 1572868
  28.2 20.0 %collective-permute-start.9 = (bf16[256,512]{1,0:T(8,128)(2,1)S(1)}, bf16[256,512]{1,0:T(8,128)(2,1)S(1)}, u32[]{:S(2)}, u32[]{:S(2)}) collective-permute-start(bf16[256,512]{1,0:T(8,128)(2,1)S(1)} %get-tuple-element.55), channel_id=1, source_target_pairs={{0,24},{8,16},{16,8},{24,0},{1,25},{9,17},{17,9},{25,1},{2,26},{10... | collective-permute-start | bytes 786440 | tf_op jit(solution)/shard_map/ppermute | solution.py:306
  30.7 17.4 %collective-permute-start.8 = (bf16[256,512]{1,0:T(8,128)(2,1)S(1)}, bf16[256,512]{1,0:T(8,128)(2,1)S(1)}, u32[]{:S(2)}, u32[]{:S(2)}) collective-permute-start(bf16[256,512]{1,0:T(8,128)(2,1)S(1)} %get-tuple-element.55), channel_id=1, source_target_pairs={{0,16},{8,24},{16,0},{24,8},{1,17},{9,25},{17,1},{25,9},{2,18},{10... | collective-permute-start | bytes 786440 | tf_op jit(solution)/shard_map/ppermute | solution.py:306
  31.2 16.9 %collective-permute-start.7 = (bf16[256,512]{1,0:T(8,128)(2,1)S(1)}, bf16[256,512]{1,0:T(8,128)(2,1)S(1)}, u32[]{:S(2)}, u32[]{:S(2)}) collective-permute-start(bf16[256,512]{1,0:T(8,128)(2,1)S(1)} %get-tuple-element.55), channel_id=1, source_target_pairs={{0,8},{8,0},{16,24},{24,16},{1,9},{9,1},{17,25},{25,17},{2,10},{10... | collective-permute-start | bytes 786440 | tf_op jit(solution)/shard_map/ppermute | solution.py:306

commit v10 on v9

--- a/solution.py
+++ b/solution.py
@@ -323,8 +323,8 @@
         [*range(half + eighth, half + quarter), *range(quarter + eighth, half)],
         list(range(half + quarter, owners)),
     ]
-    sent_first = groups[1][:eighth]
-    sent_next = groups[0] + groups[1][eighth:] + groups[2]
+    sent_first = [*range(half, half + eighth), *range(1, quarter)]
+    sent_next = [0, *sum(groups[1:3], [])[eighth:]]
     last = groups[3]
     block = min(clusters, 32)
 
@@ -363,7 +363,10 @@
     packed = vmem_call(
         functools.partial(late_pack_kernel, capacity, sent_next),
         "next_pack",
-        [message] * len(sent_next),
+        [
+            pltpu.HBM(message.shape, message.dtype) if 0 < peer < half else message
+            for peer in sent_next
+        ],
         [index, slots, values, sent[0]],
         [whole_vmem()] * 3 + [anywhere],
     )

time: 49.4 us -> 48.2 us (0.976)
  blocking collectives: 13 us -> 11.1 us
  Pallas kernels: 19.6 us -> 20.2 us
    all_to_all x1, blocking collectives: 13 us -> 11.1 us  [body(): lax.all_to_all(best, 'own', split_axis=0, concat_axis=0, tiled=True)]
    pallas_call x10, Pallas kernels: 19.6 us -> 20.2 us  [vmem_call(): pl.pallas_call(kernel, out_shape=out_shape, in_specs=in_specs or [whole_v...]
  transfers between devices with their start and end apart: 10 -> 10, of which waited for: 1 -> 1; matrix products, arithmetic and copies ran while one was open for 0% -> 0% of each run, Pallas kernels for 32% -> 36%
where the time goes in v10:
time: 48.2 us; the launch traced here: 48 us
  Pallas kernels  20.2 us (42%)
  starting transfers between devices  13.5 us (28%)
  blocking collectives  11.1 us (23%)
  waiting for transfers between devices  1.69 us (4%)
  between operations  0.73 us (2%)
  local copies, waits for them, and re-layouts  0.69 us (1%)
    pallas_call x10, Pallas kernels, vmem_call(): pl.pallas_call(kernel, out_shape=out_shape, in_specs=in_specs or [whole_v...  20.2 us
    ppermute x10, starting transfers between devices, exchange(): lax.ppermute(value, axis, [(device, device ^ offset) for device in range(...  13.5 us
    all_to_all x1, blocking collectives, body(): lax.all_to_all(best, 'own', split_axis=0, concat_axis=0, tiled=True)  11.1 us
    ppermute x10, waiting for transfers between devices, exchange(): lax.ppermute(value, axis, [(device, device ^ offset) for device in range(...  1.69 us
  transfers between devices with their start and end apart: 10, of which 1 were waited for; matrix products, arithmetic and copies ran while one was open for 0% of the time, Pallas kernels for 36%

profile of v10, /device:TPU:0, one launch (start us, length us, event | category | flops | bytes accessed | tf_op | source)
XLA Modules:
  0.0 48.0 jit_solution(15711340497255060882)
XLA Ops:
  0.6 1.7 %pack.1 = (s32[1,512]{1,0:T(1,128)S(1)}, s32[1,512]{1,0:T(1,128)S(1)}, s32[1,512]{1,0:T(1,128)}, s32[1,512]{1,0:T(1,128)S(1)}, bf16[512,512]{1,0:T(8,128)(2,1)S(...) custom-call(s32[1]{0:T(128)} %bitcast.me_ref, s32[1,512]{1,0:T(1,128)} %bitcast.15, s32[1,512]{1,0:T(1,128)} %bitcast.16, ...), custom_call_target="tpu_custom_call" | custom-call | flops 1 | bytes 1 | tf_op jit(solution)/shard_map/pack/pallas_call | solution.py:335
  2.3 0.5 %collective-permute-start = (bf16[528,128]{1,0:T(8,128)(2,1)S(1)}, bf16[528,128]{1,0:T(8,128)(2,1)S(1)}, u32[]{:S(2)}, u32[]{:S(2)}) collective-permute-start(bf16[528,128]{1,0:T(8,128)(2,1)S(1)} %get-tuple-element.35), channel_id=1, source_target_pairs={{0,1},{1,0},{2,3},{3,2},{4,5},{5,4},{6,7},{7,6},{8,9},{9,8},{10,11... | collective-permute-start | bytes 405512 | tf_op jit(solution)/shard_map/ppermute | solution.py:306
  2.8 3.7 %collective-permute-start.3 = (bf16[528,128]{1,0:T(8,128)(2,1)S(1)}, bf16[528,128]{1,0:T(8,128)(2,1)S(1)}, u32[]{:S(2)}, u32[]{:S(2)}) collective-permute-start(bf16[528,128]{1,0:T(8,128)(2,1)S(1)} %get-tuple-element.33.after_ref), channel_id=1, source_target_pairs={{0,4},{1,5},{2,6},{3,7},{4,0},{5,1},{6,2},{7,3},{8,12},{9,13},{10,... | collective-permute-start | bytes 405512 | tf_op jit(solution)/shard_map/ppermute | solution.py:306
  6.5 1.2 %next_pack.1 = (bf16[528,128]{1,0:T(8,128)(2,1)S(1)}, bf16[528,128]{1,0:T(8,128)(2,1)}, bf16[528,128]{1,0:T(8,128)(2,1)S(1)}, bf16[528,128]{1,0:T(8,128)(2,1)}) custom-call(s32[1,512]{1,0:T(1,128)S(1)} %get-tuple-element.30.index_ref, s32[1,512]{1,0:T(1,128)S(1)} %get-tuple-element.31.slot_ref, bf16[512,512]{1,0:T(8,128)(2,1)S(1)} %get-tuple-element.32.rows_ref, ...), custom_call_target="tpu_custom_call" | custom-call | flops 1 | bytes 1 | tf_op jit(solution)/shard_map/next_pack/pallas_call | solution.py:335
  7.8 1.6 %collective-permute-start.4 = (bf16[528,128]{1,0:T(8,128)(2,1)}, bf16[528,128]{1,0:T(8,128)(2,1)S(1)}, u32[]{:S(2)}, u32[]{:S(2)}) collective-permute-start(bf16[528,128]{1,0:T(8,128)(2,1)} %get-tuple-element.41), channel_id=1, source_target_pairs={{0,2},{1,3},{2,0},{3,1},{4,6},{5,7},{6,4},{7,5},{8,10},{9,11},{10,... | collective-permute-start | bytes 405512 | tf_op jit(solution)/shard_map/ppermute | solution.py:306
  9.3 0.0 collective-permute-start.5
  9.3 0.2 collective-permute-start.6
  9.5 0.0 collective-permute-done.refs_1_
  9.5 0.7 %copy-done.1 = s32[256]{0:T(256)S(1)} copy-done((s32[256]{0:T(256)S(1)}, s32[256]{0:T(256)}, u32[]{:S(2)}) %copy-start.1) | copy-done | bytes 1048
  10.2 6.3 %first_score.1 = (bf16[256,32,512]{2,1,0:T(8,128)(2,1)S(1)}, f32[256,128]{1,0:T(8,128)S(1)}, f32[256,512]{1,0:T(8,128)S(1)}, f32[1,128]{1,0:T(1,128)S(1)}, f32[1,128]{1,0:T(1,128)S(1)}) custom-call(bf16[256,32,512]{2,1,0:T(8,128)(2,1)} %bank_ref.1, s32[1,256]{1,0:T(1,128)S(1)} %bitcast.11, bf16[528,128]{1,0:T(8,128)(2,1)S(1)} %get-tuple-element.34.refs_0_, ...), custom_call_target="tpu_custom_call" | custom-call | flops 1 | bytes 1 | tf_op jit(solution)/shard_map/first_score/pallas_call | solution.py:335
  16.5 0.3 late_pack.1
  16.9 4.0 %collective-permute-start.1 = (bf16[528,128]{1,0:T(8,128)(2,1)S(1)}, bf16[528,128]{1,0:T(8,128)(2,1)S(1)}, u32[]{:S(2)}, u32[]{:S(2)}) collective-permute-start(bf16[528,128]{1,0:T(8,128)(2,1)S(1)} %get-tuple-element.39), channel_id=1, source_target_pairs={{0,6},{1,7},{2,4},{3,5},{4,2},{5,3},{6,0},{7,1},{8,14},{9,15},{10,... | collective-permute-start | bytes 405512 | tf_op jit(solution)/shard_map/ppermute | solution.py:306
  20.8 0.0 collective-permute-done.3.refs_0_
  20.8 0.0 collective-permute-start.2
  20.8 0.0 collective-permute-done.4.refs_1_
  20.8 0.0 copy-start.2
  20.9 2.9 %score.2 = (f32[1,128]{1,0:T(1,128)S(1)}, f32[1,128]{1,0:T(1,128)S(1)}, f32[256,512]{1,0:T(8,128)S(1)}) custom-call(bf16[256,32,512]{2,1,0:T(8,128)(2,1)S(1)} %get-tuple-element.36.bank_ref, f32[256,128]{1,0:T(8,128)S(1)} %get-tuple-element.37.norm_ref, s32[1,256]{1,0:T(1,128)S(1)} %bitcast.12, f32[256,512]{1,0:T(8,128)S(1)} %get-tuple-element.38.after_ref.before_ref, ...), custom_call_target="tpu_custom_call" | custom-call | flops 1 | bytes 1 | tf_op jit(solution)/shard_map/score/pallas_call | solution.py:335
  23.8 0.0 collective-permute-done.5.refs_0_
  23.8 0.0 copy-start
  23.8 2.9 %score.3 = (f32[1,128]{1,0:T(1,128)S(1)}, f32[1,128]{1,0:T(1,128)S(1)}, f32[256,512]{1,0:T(8,128)S(1)}) custom-call(bf16[256,32,512]{2,1,0:T(8,128)(2,1)S(1)} %get-tuple-element.36.bank_ref, f32[256,128]{1,0:T(8,128)S(1)} %get-tuple-element.37.norm_ref, s32[1,256]{1,0:T(1,128)S(1)} %bitcast.13, f32[256,512]{1,0:T(8,128)S(1)} %get-tuple-element.42.before_ref, ...), custom_call_target="tpu_custom_call" | custom-call | flops 1 | bytes 1 | tf_op jit(solution)/shard_map/score/pallas_call | solution.py:335
  26.7 1.7 %collective-permute-done.2.refs_1_ = bf16[528,128]{1,0:T(8,128)(2,1)S(1)} collective-permute-done((bf16[528,128]{1,0:T(8,128)(2,1)S(1)}, bf16[528,128]{1,0:T(8,128)(2,1)S(1)}, u32[]{:S(2)}, u32[]{:S(2)}) %collective-permute-start.2) | collective-permute-done | bytes 135200 | tf_op jit(solution)/shard_map/ppermute | solution.py:306
  28.4 0.4 last_sum.1
  28.8 2.5 %collective-permute-start.9 = (bf16[256,512]{1,0:T(8,128)(2,1)S(1)}, bf16[256,512]{1,0:T(8,128)(2,1)S(1)}, u32[]{:S(2)}, u32[]{:S(2)}) collective-permute-start(bf16[256,512]{1,0:T(8,128)(2,1)S(1)} %get-tuple-element.55), channel_id=1, source_target_pairs={{0,24},{8,16},{16,8},{24,0},{1,25},{9,17},{17,9},{25,1},{2,26},{10... | collective-permute-start | bytes 786440 | tf_op jit(solution)/shard_map/ppermute | solution.py:306
  31.3 0.5 %collective-permute-start.8 = (bf16[256,512]{1,0:T(8,128)(2,1)S(1)}, bf16[256,512]{1,0:T(8,128)(2,1)S(1)}, u32[]{:S(2)}, u32[]{:S(2)}) collective-permute-start(bf16[256,512]{1,0:T(8,128)(2,1)S(1)} %get-tuple-element.55), channel_id=1, source_target_pairs={{0,16},{8,24},{16,0},{24,8},{1,17},{9,25},{17,1},{25,9},{2,18},{10... | collective-permute-start | bytes 786440 | tf_op jit(solution)/shard_map/ppermute | solution.py:306
  31.8 0.5 %collective-permute-start.7 = (bf16[256,512]{1,0:T(8,128)(2,1)S(1)}, bf16[256,512]{1,0:T(8,128)(2,1)S(1)}, u32[]{:S(2)}, u32[]{:S(2)}) collective-permute-start(bf16[256,512]{1,0:T(8,128)(2,1)S(1)} %get-tuple-element.55), channel_id=1, source_target_pairs={{0,8},{8,0},{16,24},{24,16},{1,9},{9,1},{17,25},{25,17},{2,10},{10... | collective-permute-start | bytes 786440 | tf_op jit(solution)/shard_map/ppermute | solution.py:306
  32.4 2.6 %last_score.1 = f32[8,128]{1,0:T(8,128)S(1)} custom-call(s32[1]{0:T(128)} %bitcast.me_ref, bf16[256,32,512]{2,1,0:T(8,128)(2,1)S(1)} %get-tuple-element.36.bank_ref, f32[256,128]{1,0:T(8,128)S(1)} %get-tuple-element.37.norm_ref, s32[1,256]{1,0:T(1,128)S(1)} %bitcast.14, bf16[512,256]{1,0:T(8,128)(2,1)S(1)} %get-tuple-element.46.columns_ref, ...), custom_call_target="tpu_custom_call" | custom-call | flops 1 | bytes 1 | tf_op jit(solution)/shard_map/last_score/pallas_call | solution.py:335
  34.9 11.1 %all_to_all.11 = f32[8,1,128]{2,1,0:T(1,128)S(1)} all-to-all(f32[8,1,128]{2,1,0:T(1,128)S(1)} %bitcast.9), channel_id=1, replica_groups=mesh['grp'=4,'own'=8] {'own'}, dimensions={0} | all-to-all | bytes 8192 | tf_op jit(solution)/shard_map/all_to_all | solution.py:432
  46.1 0.8 %unpack.1 = f32[1,512]{1,0:T(1,128)} custom-call(s32[1,512]{1,0:T(1,128)S(1)} %get-tuple-element.29.index_ref, f32[8,128]{1,0:T(8,128)S(1)} %bitcast.10), custom_call_target="tpu_custom_call" | custom-call | flops 1 | bytes 1 | tf_op jit(solution)/shard_map/unpack/pallas_call | solution.py:335
  46.9 0.0 collective-permute-done.9.refs_2_
  46.9 0.0 collective-permute-done.8.refs_1_
  46.9 0.0 collective-permute-done.7.refs_0_
  46.9 1.0 %finish.1 = f32[256,512]{1,0:T(8,128)} custom-call(f32[256,512]{1,0:T(8,128)S(1)} %copy-done, f32[256,512]{1,0:T(8,128)S(1)} %get-tuple-element.54.own_ref, bf16[256,512]{1,0:T(8,128)(2,1)S(1)} %collective-permute-done.7.refs_0_, bf16[256,512]{1,0:T(8,128)(2,1)S(1)} %collective-permute-done.8.refs_1_, bf16[256,512]{1,0:T(8,128)(2,1)S(1)} %collective-permute-done.9.refs_2_), custom_call_target="tpu_custom_call" | custom-call | flops 1 | bytes 1 | tf_op jit(solution)/shard_map/finish/pallas_call | solution.py:335
  (5 shorter events, 0.0 us)
Async XLA Ops:
  2.3 7.2 %collective-permute-start = (bf16[528,128]{1,0:T(8,128)(2,1)S(1)}, bf16[528,128]{1,0:T(8,128)(2,1)S(1)}, u32[]{:S(2)}, u32[]{:S(2)}) collective-permute-start(bf16[528,128]{1,0:T(8,128)(2,1)S(1)} %get-tuple-element.35), channel_id=1, source_target_pairs={{0,1},{1,0},{2,3},{3,2},{4,5},{5,4},{6,7},{7,6},{8,9},{9,8},{10,11... | collective-permute-start | bytes 405512 | tf_op jit(solution)/shard_map/ppermute | solution.py:306
  2.8 18.0 %collective-permute-start.3 = (bf16[528,128]{1,0:T(8,128)(2,1)S(1)}, bf16[528,128]{1,0:T(8,128)(2,1)S(1)}, u32[]{:S(2)}, u32[]{:S(2)}) collective-permute-start(bf16[528,128]{1,0:T(8,128)(2,1)S(1)} %get-tuple-element.33.after_ref), channel_id=1, source_target_pairs={{0,4},{1,5},{2,6},{3,7},{4,0},{5,1},{6,2},{7,3},{8,12},{9,13},{10,... | collective-permute-start | bytes 405512 | tf_op jit(solution)/shard_map/ppermute | solution.py:306
  7.8 13.1 %collective-permute-start.4 = (bf16[528,128]{1,0:T(8,128)(2,1)}, bf16[528,128]{1,0:T(8,128)(2,1)S(1)}, u32[]{:S(2)}, u32[]{:S(2)}) collective-permute-start(bf16[528,128]{1,0:T(8,128)(2,1)} %get-tuple-element.41), channel_id=1, source_target_pairs={{0,2},{1,3},{2,0},{3,1},{4,6},{5,7},{6,4},{7,5},{8,10},{9,11},{10,... | collective-permute-start | bytes 405512 | tf_op jit(solution)/shard_map/ppermute | solution.py:306
  9.3 14.5 %collective-permute-start.5 = (bf16[528,128]{1,0:T(8,128)(2,1)S(1)}, bf16[528,128]{1,0:T(8,128)(2,1)S(1)}, u32[]{:S(2)}, u32[]{:S(2)}) collective-permute-start(bf16[528,128]{1,0:T(8,128)(2,1)S(1)} %get-tuple-element.43), channel_id=1, source_target_pairs={{0,5},{1,4},{2,7},{3,6},{4,1},{5,0},{6,3},{7,2},{8,13},{9,12},{10,... | collective-permute-start | bytes 405512 | tf_op jit(solution)/shard_map/ppermute | solution.py:306
  9.3 14.5 %collective-permute-start.6 = (bf16[528,128]{1,0:T(8,128)(2,1)}, bf16[528,128]{1,0:T(8,128)(2,1)S(1)}, u32[]{:S(2)}, u32[]{:S(2)}) collective-permute-start(bf16[528,128]{1,0:T(8,128)(2,1)} %get-tuple-element.44), channel_id=1, source_target_pairs={{0,3},{1,2},{2,1},{3,0},{4,7},{5,6},{6,5},{7,4},{8,11},{9,10},{10,... | collective-permute-start | bytes 405512 | tf_op jit(solution)/shard_map/ppermute | solution.py:306
  9.5 0.7 %copy-start.1 = (s32[256]{0:T(256)S(1)}, s32[256]{0:T(256)}, u32[]{:S(2)}) copy-start(s32[256]{0:T(256)} %param.10) | copy-start | bytes 3076
  16.9 9.9 %collective-permute-start.1 = (bf16[528,128]{1,0:T(8,128)(2,1)S(1)}, bf16[528,128]{1,0:T(8,128)(2,1)S(1)}, u32[]{:S(2)}, u32[]{:S(2)}) collective-permute-start(bf16[528,128]{1,0:T(8,128)(2,1)S(1)} %get-tuple-element.39), channel_id=1, source_target_pairs={{0,6},{1,7},{2,4},{3,5},{4,2},{5,3},{6,0},{7,1},{8,14},{9,15},{10,... | collective-permute-start | bytes 405512 | tf_op jit(solution)/shard_map/ppermute | solution.py:306
  20.8 7.6 %collective-permute-start.2 = (bf16[528,128]{1,0:T(8,128)(2,1)S(1)}, bf16[528,128]{1,0:T(8,128)(2,1)S(1)}, u32[]{:S(2)}, u32[]{:S(2)}) collective-permute-start(bf16[528,128]{1,0:T(8,128)(2,1)S(1)} %get-tuple-element.40), channel_id=1, source_target_pairs={{0,7},{1,6},{2,5},{3,4},{4,3},{5,2},{6,1},{7,0},{8,15},{9,14},{10,... | collective-permute-start | bytes 405512 | tf_op jit(solution)/shard_map/ppermute | solution.py:306
  20.8 11.5 %copy-start.2 = (s32[256]{0:T(256)S(1)}, s32[256]{0:T(256)}, u32[]{:S(2)}) copy-start(s32[256]{0:T(256)} %param.10) | copy-start | bytes 3076
  23.8 23.1 %copy-start = (f32[256,512]{1,0:T(8,128)S(1)}, f32[256,512]{1,0:T(8,128)}, u32[]{:S(2)}) copy-start(f32[256,512]{1,0:T(8,128)} %stored_ref.1) | copy-start | bytes 1572868
  28.8 18.1 %collective-permute-start.9 = (bf16[256,512]{1,0:T(8,128)(2,1)S(1)}, bf16[256,512]{1,0:T(8,128)(2,1)S(1)}, u32[]{:S(2)}, u32[]{:S(2)}) collective-permute-start(bf16[256,512]{1,0:T(8,128)(2,1)S(1)} %get-tuple-element.55), channel_id=1, source_target_pairs={{0,24},{8,16},{16,8},{24,0},{1,25},{9,17},{17,9},{25,1},{2,26},{10... | collective-permute-start | bytes 786440 | tf_op jit(solution)/shard_map/ppermute | solution.py:306
  31.3 15.6 %collective-permute-start.8 = (bf16[256,512]{1,0:T(8,128)(2,1)S(1)}, bf16[256,512]{1,0:T(8,128)(2,1)S(1)}, u32[]{:S(2)}, u32[]{:S(2)}) collective-permute-start(bf16[256,512]{1,0:T(8,128)(2,1)S(1)} %get-tuple-element.55), channel_id=1, source_target_pairs={{0,16},{8,24},{16,0},{24,8},{1,17},{9,25},{17,1},{25,9},{2,18},{10... | collective-permute-start | bytes 786440 | tf_op jit(solution)/shard_map/ppermute | solution.py:306
  31.8 15.1 %collective-permute-start.7 = (bf16[256,512]{1,0:T(8,128)(2,1)S(1)}, bf16[256,512]{1,0:T(8,128)(2,1)S(1)}, u32[]{:S(2)}, u32[]{:S(2)}) collective-permute-start(bf16[256,512]{1,0:T(8,128)(2,1)S(1)} %get-tuple-element.55), channel_id=1, source_target_pairs={{0,8},{8,0},{16,24},{24,16},{1,9},{9,1},{17,25},{25,17},{2,10},{10... | collective-permute-start | bytes 786440 | tf_op jit(solution)/shard_map/ppermute | solution.py:306

commit v11 on v9

--- a/solution.py
+++ b/solution.py
@@ -11,6 +11,7 @@
 LANES = 128
 INFO_ROWS = 16
 CODE_BASE = 128
+COSTS = {"score": 10**10, "first_score": 10**10, "next_pack": 10**10}
 SMALL_VMEM = 32 * 1024 * 1024
 
 
@@ -108,8 +109,21 @@
     write_messages(capacity, peers, index, held[1][...], held[2][...], messages)
 
 
-def late_pack_kernel(capacity, peers, index_ref, slot_ref, rows_ref, after_ref, *messages):
+def halves_of(pair_ref):
+    rows = pair_ref.shape[0] // 2
+    return [pair_ref.at[pl.ds(0, rows)], pair_ref.at[pl.ds(rows, rows)]]
+
+
+def next_pack_kernel(capacity, peers, pairs, index_ref, slot_ref, rows_ref, after_ref, *refs):
+    singles = len(refs) - pairs
+    messages = list(refs[:singles]) + [half for pair in refs[singles:] for half in halves_of(pair)]
     write_messages(capacity, peers, index_ref[...], slot_ref[...], rows_ref[...], messages)
+
+
+def pass_kernel(*refs):
+    pair_refs, out_refs = refs[: len(refs) // 2], refs[len(refs) // 2 + 1 :]
+    for pair, out_ref in zip(pair_refs, out_refs):
+        out_ref[...] = halves_of(pair)[1][...]
 
 
 def read_messages(messages, capacity, width):
@@ -223,6 +237,8 @@
     messages, capacity, block, bank_ref, norm_ref, members_ref, before_ref, *refs
 ):
     message_refs, refs = refs[:messages], refs[messages:]
+    size = min(message.shape[0] for message in message_refs)
+    message_refs = [message.at[pl.ds(0, size)] for message in message_refs]
     clusters, _, width = bank_ref.shape
     units, slots = read_messages(message_refs, capacity, width)
     onehot = cluster_onehot(slots, clusters)
@@ -317,14 +333,15 @@
     anywhere = pl.BlockSpec(memory_space=pl.ANY)
     message = jax.ShapeDtypeStruct((block_rows(capacity, width), LANES), jnp.bfloat16)
     half, quarter, eighth = owners // 2, owners // 4, owners // 8
+    same_core = list(range(quarter, half, 2))
     groups = [
         list(range(quarter)),
-        [*range(half, half + eighth), *range(quarter, quarter + eighth)],
-        [*range(half + eighth, half + quarter), *range(quarter + eighth, half)],
+        list(range(half, half + quarter)),
+        same_core + [peer + 1 for peer in same_core],
         list(range(half + quarter, owners)),
     ]
-    sent_first = groups[1][:eighth]
-    sent_next = groups[0] + groups[1][eighth:] + groups[2]
+    sent_first = [*range(1, quarter), *groups[1]]
+    sent_next = [0, *groups[3]]
     last = groups[3]
     block = min(clusters, 32)
 
@@ -339,7 +356,9 @@
             out_specs=out_specs,
             scratch_shapes=scratch_shapes,
             compiler_params=small_params(),
-            cost_estimate=pl.CostEstimate(flops=1, bytes_accessed=1, transcendentals=0),
+            cost_estimate=pl.CostEstimate(
+                flops=COSTS.get(name, 1), bytes_accessed=1, transcendentals=0
+            ),
             name=name,
         )(*operands)
 
@@ -361,15 +380,17 @@
     )
     got = {peer: exchange(value, "own", peer) for peer, value in zip(sent_first, sent)}
     packed = vmem_call(
-        functools.partial(late_pack_kernel, capacity, sent_next),
+        functools.partial(
+            next_pack_kernel, capacity, sent_next + list(range(quarter, half)), eighth
+        ),
         "next_pack",
-        [message] * len(sent_next),
+        [message] * len(sent_next)
+        + [pltpu.HBM((2 * message.shape[0], LANES), message.dtype)] * eighth,
         [index, slots, values, sent[0]],
         [whole_vmem()] * 3 + [anywhere],
     )
-    got.update(
-        {peer: exchange(value, "own", peer) if peer else value for peer, value in zip(sent_next, packed)}
-    )
+    for peer, value in zip(sent_next + same_core, packed):
+        got[peer] = exchange(value, "own", peer) if peer else value
     member_row = members.reshape(1, clusters)
     sums = jax.ShapeDtypeStruct((clusters, width), jnp.float32)
 
@@ -388,15 +409,17 @@
         [pltpu.SemaphoreType.DMA((clusters // block,))],
     )
     held_bank = pltpu.with_memory_space_constraint(held_bank, pltpu.VMEM)
-    late = vmem_call(
-        functools.partial(late_pack_kernel, capacity, last),
-        "late_pack",
-        [message] * len(last),
-        [index, slots, values, total],
-        [whole_vmem()] * 3 + [anywhere],
-    )
-    got.update({peer: exchange(value, "own", peer) for peer, value in zip(last, late)})
     for group in groups[1:3]:
+        if group is groups[2]:
+            passed = vmem_call(
+                pass_kernel,
+                "pass_on",
+                [message] * eighth,
+                [*[got[peer] for peer in same_core], best[-1]],
+                [whole_vmem()] * eighth + [anywhere],
+            )
+            for peer, value in zip(same_core, passed):
+                got[peer + 1] = exchange(value, "own", 1)
         *found, total = vmem_call(
             functools.partial(score_kernel, quarter, capacity, block),
             "score",
@@ -416,7 +439,7 @@
         ],
         [*last_messages, total],
     )
-    terms = [exchange(sent, "grp", offset) for offset in range(1, parts)]
+    terms = [exchange(sent, "grp", offset) for offset in range(1, parts)][::-1]
     best = vmem_call(
         functools.partial(
             last_score_kernel, sum(groups, []), capacity, block

time: 49.4 us -> 53.8 us (1.089)
  waiting for transfers between devices: 1.67 us -> 7.03 us
  blocking collectives: 13 us -> 11.6 us
  starting transfers between devices: 13.5 us -> 14.5 us
  local copies, waits for them, and re-layouts: 0.69 us -> 0.01 us
    ppermute x10, waiting for transfers between devices: 1.67 us -> 7.03 us  [exchange(): lax.ppermute(value, axis, [(device, device ^ offset) for device in range(...]
    all_to_all x1, blocking collectives: 13 us -> 11.6 us  [body(): lax.all_to_all(best, 'own', split_axis=0, concat_axis=0, tiled=True)]
    ppermute x10, starting transfers between devices: 13.5 us -> 14.5 us  [exchange(): lax.ppermute(value, axis, [(device, device ^ offset) for device in range(...]
    unnamed x6 -> x4, local copies, waits for them, and re-layouts: 0.69 us -> 0.01 us
  transfers between devices with their start and end apart: 10 -> 10, of which waited for: 1 -> 5; matrix products, arithmetic and copies ran while one was open for 0% -> 0% of each run, Pallas kernels for 32% -> 31%
where the time goes in v11:
time: 53.8 us; the launch traced here: 53.6 us
  Pallas kernels  19.8 us (37%)
  starting transfers between devices  14.5 us (27%)
  blocking collectives  11.6 us (22%)
  waiting for transfers between devices  7.03 us (13%)
  between operations  0.7 us (1%)
    pallas_call x10, Pallas kernels, vmem_call(): pl.pallas_call(kernel, out_shape=out_shape, in_specs=in_specs or [whole_v...  19.8 us
    ppermute x10, starting transfers between devices, exchange(): lax.ppermute(value, axis, [(device, device ^ offset) for device in range(...  14.5 us
    all_to_all x1, blocking collectives, body(): lax.all_to_all(best, 'own', split_axis=0, concat_axis=0, tiled=True)  11.6 us
    ppermute x10, waiting for transfers between devices, exchange(): lax.ppermute(value, axis, [(device, device ^ offset) for device in range(...  7.03 us
  transfers between devices with their start and end apart: 10, of which 5 were waited for; matrix products, arithmetic and copies ran while one was open for 0% of the time, Pallas kernels for 31%

profile of v11, /device:TPU:0, one launch (start us, length us, event | category | flops | bytes accessed | tf_op | source)
XLA Modules:
  0.0 53.6 jit_solution(15538622260914624386)
XLA Ops:
  0.6 1.7 %pack.1 = (s32[1,512]{1,0:T(1,128)S(1)}, s32[1,512]{1,0:T(1,128)S(1)}, s32[1,512]{1,0:T(1,128)}, s32[1,512]{1,0:T(1,128)S(1)}, bf16[512,512]{1,0:T(8,128)(2,1)S(...) custom-call(s32[1]{0:T(128)} %bitcast.me_ref, s32[1,512]{1,0:T(1,128)} %bitcast.15, ...), custom_call_target="tpu_custom_call" | custom-call | flops 1 | bytes 1 | tf_op jit(solution)/shard_map/pack/pallas_call | solution.py:352
  2.3 4.1 %collective-permute-start.3 = (bf16[528,128]{1,0:T(8,128)(2,1)S(1)}, bf16[528,128]{1,0:T(8,128)(2,1)S(1)}, u32[]{:S(2)}, u32[]{:S(2)}) collective-permute-start(bf16[528,128]{1,0:T(8,128)(2,1)S(1)} %get-tuple-element.39), channel_id=1, source_target_pairs={{0,4},{1,5},{2,6},{3,7},{4,0},{5,1},{6,2},{7,3},{8,12},{9,13},{10,... | collective-permute-start | bytes 405512 | tf_op jit(solution)/shard_map/ppermute | solution.py:322
  6.4 0.0 collective-permute-start.4
  6.4 0.2 collective-permute-start
  6.6 1.3 %next_pack.1 = (bf16[528,128]{1,0:T(8,128)(2,1)S(1)}, bf16[528,128]{1,0:T(8,128)(2,1)S(1)}, bf16[528,128]{1,0:T(8,128)(2,1)S(1)}, bf16[1056,128]{1,0:T(8,128)(2,1)}) custom-call(s32[1,512]{1,0:T(1,128)S(1)} %get-tuple-element.29.index_ref, s32[1,512]{1,0:T(1,128)S(1)} %get-tuple-element.30.slot_ref, bf16[512,512]{1,0:T(8,128)(2,1)S(1)} %get-tuple-element.31.rows_ref, ...), custom_call_target="tpu_custom_call" | custom-call | flops 10000000000 | bytes 1 | tf_op jit(solution)/shard_map/next_pack/pallas_call | solution.py:352
  8.0 1.8 %collective-permute-start.5 = (bf16[1056,128]{1,0:T(8,128)(2,1)}, bf16[1056,128]{1,0:T(8,128)(2,1)S(1)}, u32[]{:S(2)}, u32[]{:S(2)}) collective-permute-start(bf16[1056,128]{1,0:T(8,128)(2,1)} %get-tuple-element.42), channel_id=1, source_target_pairs={{0,2},{1,3},{2,0},{3,1},{4,6},{5,7},{6,4},{7,5},{8,10},{9,11},{10,... | collective-permute-start | bytes 811016 | tf_op jit(solution)/shard_map/ppermute | solution.py:322
  9.8 0.0 collective-permute-done.refs_1_
  9.8 0.0 copy-done.1
  9.8 6.3 %first_score.1 = (bf16[256,32,512]{2,1,0:T(8,128)(2,1)S(1)}, f32[256,128]{1,0:T(8,128)S(1)}, f32[256,512]{1,0:T(8,128)S(1)}, f32[1,128]{1,0:T(1,128)S(1)}, f32[1,128]{1,0:T(1,128)S(1)}) custom-call(bf16[256,32,512]{2,1,0:T(8,128)(2,1)} %bank_ref.1, s32[1,256]{1,0:T(1,128)S(1)} %bitcast.11, bf16[528,128]{1,0:T(8,128)(2,1)S(1)} %get-tuple-element.33.refs_0_, ...), custom_call_target="tpu_custom_call" | custom-call | flops 10000000000 | bytes 1 | tf_op jit(solution)/shard_map/first_score/pallas_call | solution.py:352
  16.1 0.6 %collective-permute-done.3.refs_0_ = bf16[528,128]{1,0:T(8,128)(2,1)S(1)} collective-permute-done((bf16[528,128]{1,0:T(8,128)(2,1)S(1)}, bf16[528,128]{1,0:T(8,128)(2,1)S(1)}, u32[]{:S(2)}, u32[]{:S(2)}) %collective-permute-start.3) | collective-permute-done | bytes 135200 | tf_op jit(solution)/shard_map/ppermute | solution.py:322
  16.7 1.2 %collective-permute-done.4.refs_1_ = bf16[528,128]{1,0:T(8,128)(2,1)S(1)} collective-permute-done((bf16[528,128]{1,0:T(8,128)(2,1)S(1)}, bf16[528,128]{1,0:T(8,128)(2,1)S(1)}, u32[]{:S(2)}, u32[]{:S(2)}) %collective-permute-start.4) | collective-permute-done | bytes 135200 | tf_op jit(solution)/shard_map/ppermute | solution.py:322
  18.0 2.9 %score.2 = (f32[1,128]{1,0:T(1,128)S(1)}, f32[1,128]{1,0:T(1,128)S(1)}, f32[256,512]{1,0:T(8,128)S(1)}) custom-call(bf16[256,32,512]{2,1,0:T(8,128)(2,1)S(1)} %get-tuple-element.34.bank_ref, f32[256,128]{1,0:T(8,128)S(1)} %get-tuple-element.35.norm_ref, s32[1,256]{1,0:T(1,128)S(1)} %bitcast.12, f32[256,512]{1,0:T(8,128)S(1)} %get-tuple-element.38.before_ref, ...), custom_call_target="tpu_custom_call" | custom-call | flops 10000000000 | bytes 1 | tf_op jit(solution)/shard_map/score/pallas_call | solution.py:352
  20.8 0.7 %collective-permute-done.5.refs_0_ = bf16[1056,128]{1,0:T(8,128)(2,1)S(1)} collective-permute-done((bf16[1056,128]{1,0:T(8,128)(2,1)}, bf16[1056,128]{1,0:T(8,128)(2,1)S(1)}, u32[]{:S(2)}, u32[]{:S(2)}) %collective-permute-start.5) | collective-permute-done | bytes 270368 | tf_op jit(solution)/shard_map/ppermute | solution.py:322
  21.5 0.1 collective-permute-start.6
  21.6 4.7 %collective-permute-start.1 = (bf16[528,128]{1,0:T(8,128)(2,1)S(1)}, bf16[528,128]{1,0:T(8,128)(2,1)S(1)}, u32[]{:S(2)}, u32[]{:S(2)}) collective-permute-start(bf16[528,128]{1,0:T(8,128)(2,1)S(1)} %get-tuple-element.36), channel_id=1, source_target_pairs={{0,6},{1,7},{2,4},{3,5},{4,2},{5,3},{6,0},{7,1},{8,14},{9,15},{10,... | collective-permute-start | bytes 405512 | tf_op jit(solution)/shard_map/ppermute | solution.py:322
  26.3 0.1 collective-permute-start.2
  26.3 0.0 collective-permute-done.6.refs_1_
  26.3 2.9 %score.3 = (f32[1,128]{1,0:T(1,128)S(1)}, f32[1,128]{1,0:T(1,128)S(1)}, f32[256,512]{1,0:T(8,128)S(1)}) custom-call(bf16[256,32,512]{2,1,0:T(8,128)(2,1)S(1)} %get-tuple-element.34.bank_ref, f32[256,128]{1,0:T(8,128)S(1)} %get-tuple-element.35.norm_ref, s32[1,256]{1,0:T(1,128)S(1)} %bitcast.13, f32[256,512]{1,0:T(8,128)S(1)} %get-tuple-element.41.before_ref, ...), custom_call_target="tpu_custom_call" | custom-call | flops 10000000000 | bytes 1 | tf_op jit(solution)/shard_map/score/pallas_call | solution.py:352
  29.2 1.3 %collective-permute-done.1.refs_0_ = bf16[528,128]{1,0:T(8,128)(2,1)S(1)} collective-permute-done((bf16[528,128]{1,0:T(8,128)(2,1)S(1)}, bf16[528,128]{1,0:T(8,128)(2,1)S(1)}, u32[]{:S(2)}, u32[]{:S(2)}) %collective-permute-start.1) | collective-permute-done | bytes 135200 | tf_op jit(solution)/shard_map/ppermute | solution.py:322
  30.6 3.2 %collective-permute-done.2.refs_1_ = bf16[528,128]{1,0:T(8,128)(2,1)S(1)} collective-permute-done((bf16[528,128]{1,0:T(8,128)(2,1)S(1)}, bf16[528,128]{1,0:T(8,128)(2,1)S(1)}, u32[]{:S(2)}, u32[]{:S(2)}) %collective-permute-start.2) | collective-permute-done | bytes 135200 | tf_op jit(solution)/shard_map/ppermute | solution.py:322
  33.7 0.4 last_sum.1
  34.1 1.6 %collective-permute-start.9 = (bf16[256,512]{1,0:T(8,128)(2,1)S(1)}, bf16[256,512]{1,0:T(8,128)(2,1)S(1)}, u32[]{:S(2)}, u32[]{:S(2)}) collective-permute-start(bf16[256,512]{1,0:T(8,128)(2,1)S(1)} %get-tuple-element.53), channel_id=1, source_target_pairs={{0,8},{8,0},{16,24},{24,16},{1,9},{9,1},{17,25},{25,17},{2,10},{10... | collective-permute-start | bytes 786440 | tf_op jit(solution)/shard_map/ppermute | solution.py:322
  35.7 1.5 %collective-permute-start.8 = (bf16[256,512]{1,0:T(8,128)(2,1)S(1)}, bf16[256,512]{1,0:T(8,128)(2,1)S(1)}, u32[]{:S(2)}, u32[]{:S(2)}) collective-permute-start(bf16[256,512]{1,0:T(8,128)(2,1)S(1)} %get-tuple-element.53), channel_id=1, source_target_pairs={{0,16},{8,24},{16,0},{24,8},{1,17},{9,25},{17,1},{25,9},{2,18},{10... | collective-permute-start | bytes 786440 | tf_op jit(solution)/shard_map/ppermute | solution.py:322
  37.2 0.5 collective-permute-start.7
  37.7 2.5 %last_score.1 = f32[8,128]{1,0:T(8,128)S(1)} custom-call(s32[1]{0:T(128)} %bitcast.me_ref, bf16[256,32,512]{2,1,0:T(8,128)(2,1)S(1)} %get-tuple-element.34.bank_ref, f32[256,128]{1,0:T(8,128)S(1)} %get-tuple-element.35.norm_ref, s32[1,256]{1,0:T(1,128)S(1)} %bitcast.14, bf16[512,256]{1,0:T(8,128)(2,1)S(1)} %get-tuple-element.45.columns_ref, ...), custom_call_target="tpu_custom_call" | custom-call | flops 1 | bytes 1 | tf_op jit(solution)/shard_map/last_score/pallas_call | solution.py:352
  40.2 11.6 %all_to_all.11 = f32[8,1,128]{2,1,0:T(1,128)S(1)} all-to-all(f32[8,1,128]{2,1,0:T(1,128)S(1)} %bitcast.9), channel_id=1, replica_groups=mesh['grp'=4,'own'=8] {'own'}, dimensions={0} | all-to-all | bytes 8192 | tf_op jit(solution)/shard_map/all_to_all | solution.py:452
  51.7 0.8 %unpack.1 = f32[1,512]{1,0:T(1,128)} custom-call(s32[1,512]{1,0:T(1,128)S(1)} %get-tuple-element.28.index_ref, f32[8,128]{1,0:T(8,128)S(1)} %bitcast.10), custom_call_target="tpu_custom_call" | custom-call | flops 1 | bytes 1 | tf_op jit(solution)/shard_map/unpack/pallas_call | solution.py:352
  52.6 0.0 collective-permute-done.9.refs_2_
  52.6 0.0 collective-permute-done.8.refs_1_
  52.6 0.0 collective-permute-done.7.refs_0_
  52.6 0.0 copy-done
  52.6 1.0 %finish.1 = f32[256,512]{1,0:T(8,128)} custom-call(f32[256,512]{1,0:T(8,128)S(1)} %copy-done, f32[256,512]{1,0:T(8,128)S(1)} %get-tuple-element.52.own_ref, bf16[256,512]{1,0:T(8,128)(2,1)S(1)} %collective-permute-done.7.refs_0_, bf16[256,512]{1,0:T(8,128)(2,1)S(1)} %collective-permute-done.8.refs_1_, bf16[256,512]{1,0:T(8,128)(2,1)S(1)} %collective-permute-done.9.refs_2_), custom_call_target="tpu_custom_call" | custom-call | flops 1 | bytes 1 | tf_op jit(solution)/shard_map/finish/pallas_call | solution.py:352
  (3 shorter events, 0.0 us)
Async XLA Ops:
  2.3 14.4 %collective-permute-start.3 = (bf16[528,128]{1,0:T(8,128)(2,1)S(1)}, bf16[528,128]{1,0:T(8,128)(2,1)S(1)}, u32[]{:S(2)}, u32[]{:S(2)}) collective-permute-start(bf16[528,128]{1,0:T(8,128)(2,1)S(1)} %get-tuple-element.39), channel_id=1, source_target_pairs={{0,4},{1,5},{2,6},{3,7},{4,0},{5,1},{6,2},{7,3},{8,12},{9,13},{10,... | collective-permute-start | bytes 405512 | tf_op jit(solution)/shard_map/ppermute | solution.py:322
  6.4 11.5 %collective-permute-start.4 = (bf16[528,128]{1,0:T(8,128)(2,1)S(1)}, bf16[528,128]{1,0:T(8,128)(2,1)S(1)}, u32[]{:S(2)}, u32[]{:S(2)}) collective-permute-start(bf16[528,128]{1,0:T(8,128)(2,1)S(1)} %get-tuple-element.40), channel_id=1, source_target_pairs={{0,5},{1,4},{2,7},{3,6},{4,1},{5,0},{6,3},{7,2},{8,13},{9,12},{10,... | collective-permute-start | bytes 405512 | tf_op jit(solution)/shard_map/ppermute | solution.py:322
  6.4 3.4 %collective-permute-start = (bf16[528,128]{1,0:T(8,128)(2,1)S(1)}, bf16[528,128]{1,0:T(8,128)(2,1)S(1)}, u32[]{:S(2)}, u32[]{:S(2)}) collective-permute-start(bf16[528,128]{1,0:T(8,128)(2,1)S(1)} %get-tuple-element.32.after_ref), channel_id=1, source_target_pairs={{0,1},{1,0},{2,3},{3,2},{4,5},{5,4},{6,7},{7,6},{8,9},{9,8},{10,11... | collective-permute-start | bytes 405512 | tf_op jit(solution)/shard_map/ppermute | solution.py:322
  6.6 3.2 %copy-start.1 = (s32[256]{0:T(256)S(1)}, s32[256]{0:T(256)}, u32[]{:S(2)}) copy-start(s32[256]{0:T(256)} %param.10) | copy-start | bytes 3076
  8.0 13.5 %collective-permute-start.5 = (bf16[1056,128]{1,0:T(8,128)(2,1)}, bf16[1056,128]{1,0:T(8,128)(2,1)S(1)}, u32[]{:S(2)}, u32[]{:S(2)}) collective-permute-start(bf16[1056,128]{1,0:T(8,128)(2,1)} %get-tuple-element.42), channel_id=1, source_target_pairs={{0,2},{1,3},{2,0},{3,1},{4,6},{5,7},{6,4},{7,5},{8,10},{9,11},{10,... | collective-permute-start | bytes 811016 | tf_op jit(solution)/shard_map/ppermute | solution.py:322
  21.5 4.8 %collective-permute-start.6 = (bf16[528,128]{1,0:T(8,128)(2,1)S(1)}, bf16[528,128]{1,0:T(8,128)(2,1)S(1)}, u32[]{:S(2)}, u32[]{:S(2)}) collective-permute-start(bf16[528,128]{1,0:T(8,128)(2,1)S(1)} %pass_on.1), channel_id=1, source_target_pairs={{0,1},{1,0},{2,3},{3,2},{4,5},{5,4},{6,7},{7,6},{8,9},{9,8},{10,11... | collective-permute-start | bytes 405512 | tf_op jit(solution)/shard_map/ppermute | solution.py:322
  21.6 8.9 %collective-permute-start.1 = (bf16[528,128]{1,0:T(8,128)(2,1)S(1)}, bf16[528,128]{1,0:T(8,128)(2,1)S(1)}, u32[]{:S(2)}, u32[]{:S(2)}) collective-permute-start(bf16[528,128]{1,0:T(8,128)(2,1)S(1)} %get-tuple-element.36), channel_id=1, source_target_pairs={{0,6},{1,7},{2,4},{3,5},{4,2},{5,3},{6,0},{7,1},{8,14},{9,15},{10,... | collective-permute-start | bytes 405512 | tf_op jit(solution)/shard_map/ppermute | solution.py:322
  26.3 7.4 %collective-permute-start.2 = (bf16[528,128]{1,0:T(8,128)(2,1)S(1)}, bf16[528,128]{1,0:T(8,128)(2,1)S(1)}, u32[]{:S(2)}, u32[]{:S(2)}) collective-permute-start(bf16[528,128]{1,0:T(8,128)(2,1)S(1)} %get-tuple-element.37), channel_id=1, source_target_pairs={{0,7},{1,6},{2,5},{3,4},{4,3},{5,2},{6,1},{7,0},{8,15},{9,14},{10,... | collective-permute-start | bytes 405512 | tf_op jit(solution)/shard_map/ppermute | solution.py:322
  29.2 23.4 %copy-start = (f32[256,512]{1,0:T(8,128)S(1)}, f32[256,512]{1,0:T(8,128)}, u32[]{:S(2)}) copy-start(f32[256,512]{1,0:T(8,128)} %stored_ref.1) | copy-start | bytes 1572868
  34.1 18.5 %collective-permute-start.9 = (bf16[256,512]{1,0:T(8,128)(2,1)S(1)}, bf16[256,512]{1,0:T(8,128)(2,1)S(1)}, u32[]{:S(2)}, u32[]{:S(2)}) collective-permute-start(bf16[256,512]{1,0:T(8,128)(2,1)S(1)} %get-tuple-element.53), channel_id=1, source_target_pairs={{0,8},{8,0},{16,24},{24,16},{1,9},{9,1},{17,25},{25,17},{2,10},{10... | collective-permute-start | bytes 786440 | tf_op jit(solution)/shard_map/ppermute | solution.py:322
  35.7 16.9 %collective-permute-start.8 = (bf16[256,512]{1,0:T(8,128)(2,1)S(1)}, bf16[256,512]{1,0:T(8,128)(2,1)S(1)}, u32[]{:S(2)}, u32[]{:S(2)}) collective-permute-start(bf16[256,512]{1,0:T(8,128)(2,1)S(1)} %get-tuple-element.53), channel_id=1, source_target_pairs={{0,16},{8,24},{16,0},{24,8},{1,17},{9,25},{17,1},{25,9},{2,18},{10... | collective-permute-start | bytes 786440 | tf_op jit(solution)/shard_map/ppermute | solution.py:322
  37.2 15.4 %collective-permute-start.7 = (bf16[256,512]{1,0:T(8,128)(2,1)S(1)}, bf16[256,512]{1,0:T(8,128)(2,1)S(1)}, u32[]{:S(2)}, u32[]{:S(2)}) collective-permute-start(bf16[256,512]{1,0:T(8,128)(2,1)S(1)} %get-tuple-element.53), channel_id=1, source_target_pairs={{0,24},{8,16},{16,8},{24,0},{1,25},{9,17},{17,9},{25,1},{2,26},{10... | collective-permute-start | bytes 786440 | tf_op jit(solution)/shard_map/ppermute | solution.py:322

commit v12 on v11

--- a/solution.py
+++ b/solution.py
@@ -11,7 +11,7 @@
 LANES = 128
 INFO_ROWS = 16
 CODE_BASE = 128
-COSTS = {"score": 10**10, "first_score": 10**10, "next_pack": 10**10}
+COSTS = {"score": 10**10, "first_score": 10**10, "next_pack": 10**10, "group_sum": 10**10}
 SMALL_VMEM = 32 * 1024 * 1024
 
 
@@ -233,22 +233,36 @@
     ]
 
 
-def score_kernel(
-    messages, capacity, block, bank_ref, norm_ref, members_ref, before_ref, *refs
-):
-    message_refs, refs = refs[:messages], refs[messages:]
+def group_messages(message_refs):
     size = min(message.shape[0] for message in message_refs)
-    message_refs = [message.at[pl.ds(0, size)] for message in message_refs]
+    return [message.at[pl.ds(0, size)] for message in message_refs]
+
+
+def score_kernel(messages, capacity, block, bank_ref, norm_ref, members_ref, *refs):
+    message_refs, best_refs = group_messages(refs[:messages]), refs[messages:]
     clusters, _, width = bank_ref.shape
     units, slots = read_messages(message_refs, capacity, width)
-    onehot = cluster_onehot(slots, clusters)
     results = score_columns(
-        units.T, slots, onehot, capacity, block, bank_ref, norm_ref, members_ref
-    )
-    *best_refs, sum_ref = refs
+        units.T,
+        slots,
+        cluster_onehot(slots, clusters),
+        capacity,
+        block,
+        bank_ref,
+        norm_ref,
+        members_ref,
+    )
     for best_ref, value in zip(best_refs, results):
         best_ref[...] = value
-    sum_ref[...] = before_ref[...] + jnp.dot(onehot, units, preferred_element_type=jnp.float32)
+
+
+def group_sum_kernel(messages, capacity, *refs):
+    message_refs, before_ref, _, total_ref = group_messages(refs[:messages]), *refs[messages:]
+    clusters, width = total_ref.shape
+    units, slots = read_messages(message_refs, capacity, width)
+    total_ref[...] = before_ref[...] + jnp.dot(
+        cluster_onehot(slots, clusters), units, preferred_element_type=jnp.float32
+    )
 
 
 def last_sum_kernel(messages, capacity, *refs):
@@ -420,13 +434,20 @@
             )
             for peer, value in zip(same_core, passed):
                 got[peer + 1] = exchange(value, "own", 1)
-        *found, total = vmem_call(
+        messages = [got[peer] for peer in group]
+        best += vmem_call(
             functools.partial(score_kernel, quarter, capacity, block),
             "score",
-            results + [sums],
-            [held_bank, bank_norm, member_row, total, *[got[peer] for peer in group]],
-        )
-        best += found
+            results,
+            [held_bank, bank_norm, member_row, *messages],
+        )
+        total = vmem_call(
+            functools.partial(group_sum_kernel, quarter, capacity),
+            "group_sum",
+            sums,
+            [*messages, total, best[-1] if group is groups[2] else best[0]],
+            [whole_vmem()] * (len(messages) + 1) + [anywhere],
+        )
     last_messages = [got[peer] for peer in last]
     total, sent, columns, column_slots = vmem_call(
         functools.partial(last_sum_kernel, quarter, capacity),

time: 53.8 us -> 53.9 us (level)
  waiting for transfers between devices: 7.03 us -> 10.2 us
  starting transfers between devices: 14.5 us -> 11.8 us
  blocking collectives: 11.6 us -> 10.2 us
  Pallas kernels: 19.8 us -> 20.6 us
    ppermute x10, waiting for transfers between devices: 7.03 us -> 10.2 us  [exchange(): lax.ppermute(value, axis, [(device, device ^ offset) for device in range(...]
    ppermute x10, starting transfers between devices: 14.5 us -> 11.8 us  [exchange(): lax.ppermute(value, axis, [(device, device ^ offset) for device in range(...]
    all_to_all x1, blocking collectives: 11.6 us -> 10.2 us  [body(): lax.all_to_all(best, 'own', split_axis=0, concat_axis=0, tiled=True)]
    pallas_call x10 -> x12, Pallas kernels: 19.8 us -> 20.6 us  [vmem_call(): pl.pallas_call(kernel, out_shape=out_shape, in_specs=in_specs or [whole_v...]
  transfers between devices with their start and end apart: 10 -> 10, of which waited for: 5 -> 4; matrix products, arithmetic and copies ran while one was open for 0% -> 0% of each run, Pallas kernels for 31% -> 33%
where the time goes in v12:
time: 53.9 us; the launch traced here: 53.7 us
  Pallas kernels  20.6 us (38%)
  starting transfers between devices  11.8 us (22%)
  waiting for transfers between devices  10.2 us (19%)
  blocking collectives  10.2 us (19%)
  between operations  0.92 us (2%)
    pallas_call x12, Pallas kernels, vmem_call(): pl.pallas_call(kernel, out_shape=out_shape, in_specs=in_specs or [whole_v...  20.6 us
    ppermute x10, starting transfers between devices, exchange(): lax.ppermute(value, axis, [(device, device ^ offset) for device in range(...  11.8 us
    ppermute x10, waiting for transfers between devices, exchange(): lax.ppermute(value, axis, [(device, device ^ offset) for device in range(...  10.2 us
    all_to_all x1, blocking collectives, body(): lax.all_to_all(best, 'own', split_axis=0, concat_axis=0, tiled=True)  10.2 us
  transfers between devices with their start and end apart: 10, of which 4 were waited for; matrix products, arithmetic and copies ran while one was open for 0% of the time, Pallas kernels for 33%

profile of v12, /device:TPU:0, one launch (start us, length us, event | category | flops | bytes accessed | tf_op | source)
XLA Modules:
  0.0 53.7 jit_solution(927738721712513358)
XLA Ops:
  0.6 1.7 %pack.1 = (s32[1,512]{1,0:T(1,128)S(1)}, s32[1,512]{1,0:T(1,128)S(1)}, s32[1,512]{1,0:T(1,128)}, s32[1,512]{1,0:T(1,128)S(1)}, bf16[512,512]{1,0:T(8,128)(2,1)S(...) custom-call(s32[1]{0:T(128)} %bitcast.me_ref, s32[1,512]{1,0:T(1,128)} %bitcast.15, ...), custom_call_target="tpu_custom_call" | custom-call | flops 1 | bytes 1 | tf_op jit(solution)/shard_map/pack/pallas_call | solution.py:366
  2.3 4.1 %collective-permute-start.4 = (bf16[528,128]{1,0:T(8,128)(2,1)S(1)}, bf16[528,128]{1,0:T(8,128)(2,1)S(1)}, u32[]{:S(2)}, u32[]{:S(2)}) collective-permute-start(bf16[528,128]{1,0:T(8,128)(2,1)S(1)} %get-tuple-element.37), channel_id=1, source_target_pairs={{0,4},{1,5},{2,6},{3,7},{4,0},{5,1},{6,2},{7,3},{8,12},{9,13},{10,... | collective-permute-start | bytes 405512 | tf_op jit(solution)/shard_map/ppermute | solution.py:336
  6.4 0.0 collective-permute-start.5
  6.4 0.2 collective-permute-start
  6.6 1.3 %next_pack.1 = (bf16[528,128]{1,0:T(8,128)(2,1)S(1)}, bf16[528,128]{1,0:T(8,128)(2,1)S(1)}, bf16[528,128]{1,0:T(8,128)(2,1)S(1)}, bf16[1056,128]{1,0:T(8,128)(2,1)}) custom-call(s32[1,512]{1,0:T(1,128)S(1)} %get-tuple-element.27.index_ref, s32[1,512]{1,0:T(1,128)S(1)} %get-tuple-element.28.slot_ref, bf16[512,512]{1,0:T(8,128)(2,1)S(1)} %get-tuple-element.29.rows_ref, ...), custom_call_target="tpu_custom_call" | custom-call | flops 10000000000 | bytes 1 | tf_op jit(solution)/shard_map/next_pack/pallas_call | solution.py:366
  8.0 3.9 %collective-permute-start.1 = (bf16[528,128]{1,0:T(8,128)(2,1)S(1)}, bf16[528,128]{1,0:T(8,128)(2,1)S(1)}, u32[]{:S(2)}, u32[]{:S(2)}) collective-permute-start(bf16[528,128]{1,0:T(8,128)(2,1)S(1)} %get-tuple-element.34), channel_id=1, source_target_pairs={{0,6},{1,7},{2,4},{3,5},{4,2},{5,3},{6,0},{7,1},{8,14},{9,15},{10,... | collective-permute-start | bytes 405512 | tf_op jit(solution)/shard_map/ppermute | solution.py:336
  11.8 0.0 collective-permute-start.2
  11.8 0.0 collective-permute-done.refs_1_
  11.8 0.0 collective-permute-start.3
  11.8 6.3 %first_score.1 = (bf16[256,32,512]{2,1,0:T(8,128)(2,1)S(1)}, f32[256,128]{1,0:T(8,128)S(1)}, f32[256,512]{1,0:T(8,128)S(1)}, f32[1,128]{1,0:T(1,128)S(1)}, f32[1,128]{1,0:T(1,128)S(1)}) custom-call(bf16[256,32,512]{2,1,0:T(8,128)(2,1)} %bank_ref.1, s32[1,256]{1,0:T(1,128)S(1)} %bitcast.11, bf16[528,128]{1,0:T(8,128)(2,1)S(1)} %get-tuple-element.31.refs_0_, ...), custom_call_target="tpu_custom_call" | custom-call | flops 10000000000 | bytes 1 | tf_op jit(solution)/shard_map/first_score/pallas_call | solution.py:366
  18.2 4.3 %collective-permute-done.4.refs_0_ = bf16[528,128]{1,0:T(8,128)(2,1)S(1)} collective-permute-done((bf16[528,128]{1,0:T(8,128)(2,1)S(1)}, bf16[528,128]{1,0:T(8,128)(2,1)S(1)}, u32[]{:S(2)}, u32[]{:S(2)}) %collective-permute-start.4) | collective-permute-done | bytes 135200 | tf_op jit(solution)/shard_map/ppermute | solution.py:336
  22.5 1.2 %collective-permute-done.5.refs_1_ = bf16[528,128]{1,0:T(8,128)(2,1)S(1)} collective-permute-done((bf16[528,128]{1,0:T(8,128)(2,1)S(1)}, bf16[528,128]{1,0:T(8,128)(2,1)S(1)}, u32[]{:S(2)}, u32[]{:S(2)}) %collective-permute-start.5) | collective-permute-done | bytes 135200 | tf_op jit(solution)/shard_map/ppermute | solution.py:336
  23.8 2.8 %score.2 = (f32[1,128]{1,0:T(1,128)S(1)}, f32[1,128]{1,0:T(1,128)S(1)}) custom-call(bf16[256,32,512]{2,1,0:T(8,128)(2,1)S(1)} %get-tuple-element.32.bank_ref, f32[256,128]{1,0:T(8,128)S(1)} %get-tuple-element.33.norm_ref, s32[1,256]{1,0:T(1,128)S(1)} %bitcast.12, bf16[528,128]{1,0:T(8,128)(2,1)S(1)} %collective-permute-done.4.refs_0_, ...), custom_call_target="tpu_custom_call" | custom-call | flops 10000000000 | bytes 1 | tf_op jit(solution)/shard_map/score/pallas_call | solution.py:366
  26.6 3.7 %collective-permute-done.3.refs_0_ = bf16[1056,128]{1,0:T(8,128)(2,1)S(1)} collective-permute-done((bf16[1056,128]{1,0:T(8,128)(2,1)}, bf16[1056,128]{1,0:T(8,128)(2,1)S(1)}, u32[]{:S(2)}, u32[]{:S(2)}) %collective-permute-start.3) | collective-permute-done | bytes 270368 | tf_op jit(solution)/shard_map/ppermute | solution.py:336
  30.3 0.1 collective-permute-start.6
  30.4 0.4 group_sum.2.refs_2_
  30.8 0.9 %collective-permute-done.6.refs_1_ = bf16[528,128]{1,0:T(8,128)(2,1)S(1)} collective-permute-done((bf16[528,128]{1,0:T(8,128)(2,1)S(1)}, bf16[528,128]{1,0:T(8,128)(2,1)S(1)}, u32[]{:S(2)}, u32[]{:S(2)}) %collective-permute-start.6) | collective-permute-done | bytes 135200 | tf_op jit(solution)/shard_map/ppermute | solution.py:336
  31.7 2.8 %score.3 = (f32[1,128]{1,0:T(1,128)S(1)}, f32[1,128]{1,0:T(1,128)S(1)}) custom-call(bf16[256,32,512]{2,1,0:T(8,128)(2,1)S(1)} %get-tuple-element.32.bank_ref, f32[256,128]{1,0:T(8,128)S(1)} %get-tuple-element.33.norm_ref, s32[1,256]{1,0:T(1,128)S(1)} %bitcast.13, bf16[1056,128]{1,0:T(8,128)(2,1)S(1)} %collective-permute-done.3.refs_0_, ...), custom_call_target="tpu_custom_call" | custom-call | flops 10000000000 | bytes 1 | tf_op jit(solution)/shard_map/score/pallas_call | solution.py:366
  34.5 0.4 group_sum.3.refs_2_
  34.9 0.0 copy-start
  34.9 0.0 collective-permute-done.1.refs_0_
  34.9 0.0 collective-permute-done.2.refs_1_
  35.0 0.4 last_sum.1
  35.4 1.6 %collective-permute-start.9 = (bf16[256,512]{1,0:T(8,128)(2,1)S(1)}, bf16[256,512]{1,0:T(8,128)(2,1)S(1)}, u32[]{:S(2)}, u32[]{:S(2)}) collective-permute-start(bf16[256,512]{1,0:T(8,128)(2,1)S(1)} %get-tuple-element.49), channel_id=1, source_target_pairs={{0,8},{8,0},{16,24},{24,16},{1,9},{9,1},{17,25},{25,17},{2,10},{10... | collective-permute-start | bytes 786440 | tf_op jit(solution)/shard_map/ppermute | solution.py:336
  37.0 1.5 %collective-permute-start.8 = (bf16[256,512]{1,0:T(8,128)(2,1)S(1)}, bf16[256,512]{1,0:T(8,128)(2,1)S(1)}, u32[]{:S(2)}, u32[]{:S(2)}) collective-permute-start(bf16[256,512]{1,0:T(8,128)(2,1)S(1)} %get-tuple-element.49), channel_id=1, source_target_pairs={{0,16},{8,24},{16,0},{24,8},{1,17},{9,25},{17,1},{25,9},{2,18},{10... | collective-permute-start | bytes 786440 | tf_op jit(solution)/shard_map/ppermute | solution.py:336
  38.5 0.4 collective-permute-start.7
  38.9 2.6 %last_score.1 = f32[8,128]{1,0:T(8,128)S(1)} custom-call(s32[1]{0:T(128)} %bitcast.me_ref, bf16[256,32,512]{2,1,0:T(8,128)(2,1)S(1)} %get-tuple-element.32.bank_ref, f32[256,128]{1,0:T(8,128)S(1)} %get-tuple-element.33.norm_ref, s32[1,256]{1,0:T(1,128)S(1)} %bitcast.14, bf16[512,256]{1,0:T(8,128)(2,1)S(1)} %get-tuple-element.43.columns_ref, ...), custom_call_target="tpu_custom_call" | custom-call | flops 1 | bytes 1 | tf_op jit(solution)/shard_map/last_score/pallas_call | solution.py:366
  41.5 10.2 %all_to_all.11 = f32[8,1,128]{2,1,0:T(1,128)S(1)} all-to-all(f32[8,1,128]{2,1,0:T(1,128)S(1)} %bitcast.9), channel_id=1, replica_groups=mesh['grp'=4,'own'=8] {'own'}, dimensions={0} | all-to-all | bytes 8192 | tf_op jit(solution)/shard_map/all_to_all | solution.py:473
  51.7 0.8 %unpack.1 = f32[1,512]{1,0:T(1,128)} custom-call(s32[1,512]{1,0:T(1,128)S(1)} %get-tuple-element.26.index_ref, f32[8,128]{1,0:T(8,128)S(1)} %bitcast.10), custom_call_target="tpu_custom_call" | custom-call | flops 1 | bytes 1 | tf_op jit(solution)/shard_map/unpack/pallas_call | solution.py:366
  52.5 0.0 collective-permute-done.8.refs_1_
  52.5 0.0 collective-permute-done.7.refs_0_
  52.5 1.0 %finish.1 = f32[256,512]{1,0:T(8,128)} custom-call(f32[256,512]{1,0:T(8,128)S(1)} %copy-done, f32[256,512]{1,0:T(8,128)S(1)} %get-tuple-element.48.own_ref, bf16[256,512]{1,0:T(8,128)(2,1)S(1)} %collective-permute-done.7.refs_0_, bf16[256,512]{1,0:T(8,128)(2,1)S(1)} %collective-permute-done.8.refs_1_, bf16[256,512]{1,0:T(8,128)(2,1)S(1)} %collective-permute-done.9.refs_2_), custom_call_target="tpu_custom_call" | custom-call | flops 1 | bytes 1 | tf_op jit(solution)/shard_map/finish/pallas_call | solution.py:366
  (5 shorter events, 0.0 us)
Async XLA Ops:
  2.3 20.2 %collective-permute-start.4 = (bf16[528,128]{1,0:T(8,128)(2,1)S(1)}, bf16[528,128]{1,0:T(8,128)(2,1)S(1)}, u32[]{:S(2)}, u32[]{:S(2)}) collective-permute-start(bf16[528,128]{1,0:T(8,128)(2,1)S(1)} %get-tuple-element.37), channel_id=1, source_target_pairs={{0,4},{1,5},{2,6},{3,7},{4,0},{5,1},{6,2},{7,3},{8,12},{9,13},{10,... | collective-permute-start | bytes 405512 | tf_op jit(solution)/shard_map/ppermute | solution.py:336
  6.4 17.3 %collective-permute-start.5 = (bf16[528,128]{1,0:T(8,128)(2,1)S(1)}, bf16[528,128]{1,0:T(8,128)(2,1)S(1)}, u32[]{:S(2)}, u32[]{:S(2)}) collective-permute-start(bf16[528,128]{1,0:T(8,128)(2,1)S(1)} %get-tuple-element.38), channel_id=1, source_target_pairs={{0,5},{1,4},{2,7},{3,6},{4,1},{5,0},{6,3},{7,2},{8,13},{9,12},{10,... | collective-permute-start | bytes 405512 | tf_op jit(solution)/shard_map/ppermute | solution.py:336
  6.4 5.4 %collective-permute-start = (bf16[528,128]{1,0:T(8,128)(2,1)S(1)}, bf16[528,128]{1,0:T(8,128)(2,1)S(1)}, u32[]{:S(2)}, u32[]{:S(2)}) collective-permute-start(bf16[528,128]{1,0:T(8,128)(2,1)S(1)} %get-tuple-element.30.after_ref), channel_id=1, source_target_pairs={{0,1},{1,0},{2,3},{3,2},{4,5},{5,4},{6,7},{7,6},{8,9},{9,8},{10,11... | collective-permute-start | bytes 405512 | tf_op jit(solution)/shard_map/ppermute | solution.py:336
  6.6 5.2 %copy-start.1 = (s32[256]{0:T(256)S(1)}, s32[256]{0:T(256)}, u32[]{:S(2)}) copy-start(s32[256]{0:T(256)} %param.10) | copy-start | bytes 3076
  8.0 27.0 %collective-permute-start.1 = (bf16[528,128]{1,0:T(8,128)(2,1)S(1)}, bf16[528,128]{1,0:T(8,128)(2,1)S(1)}, u32[]{:S(2)}, u32[]{:S(2)}) collective-permute-start(bf16[528,128]{1,0:T(8,128)(2,1)S(1)} %get-tuple-element.34), channel_id=1, source_target_pairs={{0,6},{1,7},{2,4},{3,5},{4,2},{5,3},{6,0},{7,1},{8,14},{9,15},{10,... | collective-permute-start | bytes 405512 | tf_op jit(solution)/shard_map/ppermute | solution.py:336
  11.8 23.1 %collective-permute-start.2 = (bf16[528,128]{1,0:T(8,128)(2,1)S(1)}, bf16[528,128]{1,0:T(8,128)(2,1)S(1)}, u32[]{:S(2)}, u32[]{:S(2)}) collective-permute-start(bf16[528,128]{1,0:T(8,128)(2,1)S(1)} %get-tuple-element.35), channel_id=1, source_target_pairs={{0,7},{1,6},{2,5},{3,4},{4,3},{5,2},{6,1},{7,0},{8,15},{9,14},{10,... | collective-permute-start | bytes 405512 | tf_op jit(solution)/shard_map/ppermute | solution.py:336
  11.8 18.5 %collective-permute-start.3 = (bf16[1056,128]{1,0:T(8,128)(2,1)}, bf16[1056,128]{1,0:T(8,128)(2,1)S(1)}, u32[]{:S(2)}, u32[]{:S(2)}) collective-permute-start(bf16[1056,128]{1,0:T(8,128)(2,1)} %get-tuple-element.36), channel_id=1, source_target_pairs={{0,2},{1,3},{2,0},{3,1},{4,6},{5,7},{6,4},{7,5},{8,10},{9,11},{10,... | collective-permute-start | bytes 811016 | tf_op jit(solution)/shard_map/ppermute | solution.py:336
  30.3 1.4 %collective-permute-start.6 = (bf16[528,128]{1,0:T(8,128)(2,1)S(1)}, bf16[528,128]{1,0:T(8,128)(2,1)S(1)}, u32[]{:S(2)}, u32[]{:S(2)}) collective-permute-start(bf16[528,128]{1,0:T(8,128)(2,1)S(1)} %pass_on.1), channel_id=1, source_target_pairs={{0,1},{1,0},{2,3},{3,2},{4,5},{5,4},{6,7},{7,6},{8,9},{9,8},{10,11... | collective-permute-start | bytes 405512 | tf_op jit(solution)/shard_map/ppermute | solution.py:336
  34.9 17.6 %copy-start = (f32[256,512]{1,0:T(8,128)S(1)}, f32[256,512]{1,0:T(8,128)}, u32[]{:S(2)}) copy-start(f32[256,512]{1,0:T(8,128)} %stored_ref.1) | copy-start | bytes 1572868
  35.4 17.1 %collective-permute-start.9 = (bf16[256,512]{1,0:T(8,128)(2,1)S(1)}, bf16[256,512]{1,0:T(8,128)(2,1)S(1)}, u32[]{:S(2)}, u32[]{:S(2)}) collective-permute-start(bf16[256,512]{1,0:T(8,128)(2,1)S(1)} %get-tuple-element.49), channel_id=1, source_target_pairs={{0,8},{8,0},{16,24},{24,16},{1,9},{9,1},{17,25},{25,17},{2,10},{10... | collective-permute-start | bytes 786440 | tf_op jit(solution)/shard_map/ppermute | solution.py:336
  37.0 15.5 %collective-permute-start.8 = (bf16[256,512]{1,0:T(8,128)(2,1)S(1)}, bf16[256,512]{1,0:T(8,128)(2,1)S(1)}, u32[]{:S(2)}, u32[]{:S(2)}) collective-permute-start(bf16[256,512]{1,0:T(8,128)(2,1)S(1)} %get-tuple-element.49), channel_id=1, source_target_pairs={{0,16},{8,24},{16,0},{24,8},{1,17},{9,25},{17,1},{25,9},{2,18},{10... | collective-permute-start | bytes 786440 | tf_op jit(solution)/shard_map/ppermute | solution.py:336
  38.5 14.0 %collective-permute-start.7 = (bf16[256,512]{1,0:T(8,128)(2,1)S(1)}, bf16[256,512]{1,0:T(8,128)(2,1)S(1)}, u32[]{:S(2)}, u32[]{:S(2)}) collective-permute-start(bf16[256,512]{1,0:T(8,128)(2,1)S(1)} %get-tuple-element.49), channel_id=1, source_target_pairs={{0,24},{8,16},{16,8},{24,0},{1,25},{9,17},{17,9},{25,1},{2,26},{10... | collective-permute-start | bytes 786440 | tf_op jit(solution)/shard_map/ppermute | solution.py:336

commit v13 on v10

--- a/solution.py
+++ b/solution.py
@@ -173,9 +173,7 @@
     return jnp.max(cosine, axis=0, keepdims=True)
 
 
-def first_score_kernel(messages, capacity, block, bank_ref, members_ref, *refs):
-    message_refs = refs[:messages]
-    held_ref, norm_ref, sum_ref, *best_refs, semaphore = refs[messages:]
+def load_kernel(block, bank_ref, after_ref, held_ref, norm_ref, semaphore):
     clusters, depth, width = held_ref.shape
     copies = []
     for number in range(clusters // block):
@@ -184,11 +182,6 @@
             pltpu.make_async_copy(bank_ref.at[part], held_ref.at[part], semaphore.at[number])
         )
         copies[-1].start()
-    units, slots = read_messages(message_refs, capacity, width)
-    onehot = cluster_onehot(slots, clusters)
-    sum_ref[...] = jnp.dot(onehot, units, preferred_element_type=jnp.float32)
-    columns = units.T
-    picked = jnp.zeros((depth, slots.shape[1]), jnp.float32)
     shape = (block, depth, LANES)
     own_lane = lax.broadcasted_iota(jnp.int32, shape, 2) == lax.broadcasted_iota(
         jnp.int32, shape, 1
@@ -199,12 +192,6 @@
         values = held_ref[part].astype(jnp.float32)
         square = jnp.sum(values * values, axis=2, keepdims=True)
         norm_ref[part, :] = jnp.sqrt(jnp.sum(jnp.where(own_lane, square, 0.0), axis=1) + epsilon)
-    for number in range(clusters // block):
-        bank_block = held_ref[pl.ds(number * block, block)]
-        picked = pick_dots(bank_block, number * block, columns, slots, picked)
-    best = best_cosines(picked, onehot, norm_ref[...], members_ref[...])
-    for number, best_ref in enumerate(best_refs):
-        best_ref[...] = best[:, number * capacity : (number + 1) * capacity]
 
 
 def score_columns(columns, slots, onehot, capacity, block, bank_ref, norm_ref, members_ref):
@@ -219,9 +206,7 @@
     ]
 
 
-def score_kernel(
-    messages, capacity, block, bank_ref, norm_ref, members_ref, before_ref, *refs
-):
+def score_kernel(messages, capacity, block, bank_ref, norm_ref, members_ref, *refs):
     message_refs, refs = refs[:messages], refs[messages:]
     clusters, _, width = bank_ref.shape
     units, slots = read_messages(message_refs, capacity, width)
@@ -229,10 +214,13 @@
     results = score_columns(
         units.T, slots, onehot, capacity, block, bank_ref, norm_ref, members_ref
     )
-    *best_refs, sum_ref = refs
-    for best_ref, value in zip(best_refs, results):
+    *before_refs, sum_ref = refs[:-messages]
+    for best_ref, value in zip(refs[-messages:], results):
         best_ref[...] = value
-    sum_ref[...] = before_ref[...] + jnp.dot(onehot, units, preferred_element_type=jnp.float32)
+    total = jnp.dot(onehot, units, preferred_element_type=jnp.float32)
+    for before_ref in before_refs:
+        total = before_ref[...] + total
+    sum_ref[...] = total
 
 
 def last_sum_kernel(messages, capacity, *refs):
@@ -377,17 +365,15 @@
     sums = jax.ShapeDtypeStruct((clusters, width), jnp.float32)
 
     results = [jax.ShapeDtypeStruct((1, capacity), jnp.float32)] * quarter
-    held_bank, bank_norm, total, *best = vmem_call(
-        functools.partial(first_score_kernel, quarter, capacity, block),
-        "first_score",
+    held_bank, bank_norm = vmem_call(
+        functools.partial(load_kernel, block),
+        "bank_load",
         [
             pltpu.VMEM(bank.shape, bank.dtype),
             jax.ShapeDtypeStruct((clusters, LANES), jnp.float32),
-            sums,
-            *results,
         ],
-        [in_hbm(bank), member_row, *[got[peer] for peer in groups[0]]],
-        [anywhere] + [whole_vmem()] * (1 + quarter),
+        [in_hbm(bank), got[0]],
+        [anywhere] * 2,
         [pltpu.SemaphoreType.DMA((clusters // block,))],
     )
     held_bank = pltpu.with_memory_space_constraint(held_bank, pltpu.VMEM)
@@ -395,18 +381,20 @@
         functools.partial(late_pack_kernel, capacity, last),
         "late_pack",
         [message] * len(last),
-        [index, slots, values, total],
+        [index, slots, values, bank_norm],
         [whole_vmem()] * 3 + [anywhere],
     )
     got.update({peer: exchange(value, "own", peer) for peer, value in zip(last, late)})
-    for group in groups[1:3]:
-        *found, total = vmem_call(
+    best, before = [], []
+    for group in groups[:3]:
+        total, *found = vmem_call(
             functools.partial(score_kernel, quarter, capacity, block),
             "score",
-            results + [sums],
-            [held_bank, bank_norm, member_row, total, *[got[peer] for peer in group]],
+            [sums] + results,
+            [held_bank, bank_norm, member_row, *[got[peer] for peer in group], *before],
         )
         best += found
+        before = [total]
     last_messages = [got[peer] for peer in last]
     total, sent, columns, column_slots = vmem_call(
         functools.partial(last_sum_kernel, quarter, capacity),
@@ -419,7 +407,7 @@
         ],
         [*last_messages, total],
     )
-    terms = [exchange(sent, "grp", offset) for offset in range(1, parts)]
+    terms = [exchange(sent, "grp", offset) for offset in range(1, parts)][::-1]
     best = vmem_call(
         functools.partial(
             last_score_kernel, sum(groups, []), capacity, block

time: 48.2 us -> 53.4 us (1.11)
  blocking collectives: 11.1 us -> 15.9 us
  starting transfers between devices: 13.5 us -> 15.5 us
  waiting for transfers between devices: 1.69 us -> 0.03 us
  Pallas kernels: 20.2 us -> 20.9 us
  local copies, waits for them, and re-layouts: 0.69 us -> 0.01 us
    all_to_all x1, blocking collectives: 11.1 us -> 15.9 us  [body(): lax.all_to_all(best, 'own', split_axis=0, concat_axis=0, tiled=True)]
    ppermute x10, starting transfers between devices: 13.5 us -> 15.5 us  [exchange(): lax.ppermute(value, axis, [(device, device ^ offset) for device in range(...]
    ppermute x10, waiting for transfers between devices: 1.69 us -> 0.03 us  [exchange(): lax.ppermute(value, axis, [(device, device ^ offset) for device in range(...]
    unnamed x6 -> x4, local copies, waits for them, and re-layouts: 0.69 us -> 0.01 us
    pallas_call x10 -> x11, Pallas kernels: 20.2 us -> 20.9 us  [vmem_call(): pl.pallas_call(kernel, out_shape=out_shape, in_specs=in_specs or [whole_v...]
  transfers between devices with their start and end apart: 10 -> 10, of which waited for: 1 -> 0; matrix products, arithmetic and copies ran while one was open for 0% -> 0% of each run, Pallas kernels for 36% -> 33%
where the time goes in v13:
time: 53.4 us; the launch traced here: 53.3 us
  Pallas kernels  20.9 us (39%)
  blocking collectives  15.9 us (30%)
  starting transfers between devices  15.5 us (29%)
  between operations  0.9 us (2%)
    pallas_call x11, Pallas kernels, vmem_call(): pl.pallas_call(kernel, out_shape=out_shape, in_specs=in_specs or [whole_v...  20.9 us
    all_to_all x1, blocking collectives, body(): lax.all_to_all(best, 'own', split_axis=0, concat_axis=0, tiled=True)  15.9 us
    ppermute x10, starting transfers between devices, exchange(): lax.ppermute(value, axis, [(device, device ^ offset) for device in range(...  15.5 us
  transfers between devices with their start and end apart: 10, of which 0 were waited for; matrix products, arithmetic and copies ran while one was open for 0% of the time, Pallas kernels for 33%

profile of v13, /device:TPU:0, one launch (start us, length us, event | category | flops | bytes accessed | tf_op | source)
XLA Modules:
  0.0 53.3 jit_solution(17521842370459757585)
XLA Ops:
  0.6 1.7 %pack.1 = (s32[1,512]{1,0:T(1,128)S(1)}, s32[1,512]{1,0:T(1,128)S(1)}, s32[1,512]{1,0:T(1,128)}, s32[1,512]{1,0:T(1,128)S(1)}, bf16[512,512]{1,0:T(8,128)(2,1)S(...) custom-call(s32[1]{0:T(128)} %bitcast.me_ref, s32[1,512]{1,0:T(1,128)} %bitcast.15, s32[1,512]{1,0:T(1,128)} %bitcast.16, ...), custom_call_target="tpu_custom_call" | custom-call | flops 1 | bytes 1 | tf_op jit(solution)/shard_map/pack/pallas_call | solution.py:323
  2.3 0.5 collective-permute-start.6
  2.8 3.7 %collective-permute-start.4 = (bf16[528,128]{1,0:T(8,128)(2,1)S(1)}, bf16[528,128]{1,0:T(8,128)(2,1)S(1)}, u32[]{:S(2)}, u32[]{:S(2)}) collective-permute-start(bf16[528,128]{1,0:T(8,128)(2,1)S(1)} %get-tuple-element.33.after_ref), channel_id=1, source_target_pairs={{0,4},{1,5},{2,6},{3,7},{4,0},{5,1},{6,2},{7,3},{8,12},{9,13},{10,... | collective-permute-start | bytes 405512 | tf_op jit(solution)/shard_map/ppermute | solution.py:294
  6.5 1.2 %next_pack.1 = (bf16[528,128]{1,0:T(8,128)(2,1)S(1)}, bf16[528,128]{1,0:T(8,128)(2,1)}, bf16[528,128]{1,0:T(8,128)(2,1)S(1)}, bf16[528,128]{1,0:T(8,128)(2,1)}) custom-call(s32[1,512]{1,0:T(1,128)S(1)} %get-tuple-element.30.index_ref, s32[1,512]{1,0:T(1,128)S(1)} %get-tuple-element.31.slot_ref, bf16[512,512]{1,0:T(8,128)(2,1)S(1)} %get-tuple-element.32.rows_ref, ...), custom_call_target="tpu_custom_call" | custom-call | flops 1 | bytes 1 | tf_op jit(solution)/shard_map/next_pack/pallas_call | solution.py:323
  7.8 0.1 collective-permute-start.2
  7.8 1.6 %collective-permute-start.3 = (bf16[528,128]{1,0:T(8,128)(2,1)}, bf16[528,128]{1,0:T(8,128)(2,1)S(1)}, u32[]{:S(2)}, u32[]{:S(2)}) collective-permute-start(bf16[528,128]{1,0:T(8,128)(2,1)} %get-tuple-element.40), channel_id=1, source_target_pairs={{0,3},{1,2},{2,1},{3,0},{4,7},{5,6},{6,5},{7,4},{8,11},{9,10},{10,... | collective-permute-start | bytes 405512 | tf_op jit(solution)/shard_map/ppermute | solution.py:294
  9.4 0.2 collective-permute-start.5
  9.6 3.8 %bank_load.1 = (bf16[256,32,512]{2,1,0:T(8,128)(2,1)S(1)}, f32[256,128]{1,0:T(8,128)S(1)}) custom-call(bf16[256,32,512]{2,1,0:T(8,128)(2,1)} %bank_ref.1, bf16[528,128]{1,0:T(8,128)(2,1)S(1)} %get-tuple-element.34.after_ref.refs_0_), custom_call_target="tpu_custom_call" | custom-call | flops 1 | bytes 1 | tf_op jit(solution)/shard_map/bank_load/pallas_call | solution.py:323
  13.4 0.3 late_pack.1
  13.7 0.0 collective-permute-done.6.refs_1_
  13.7 3.9 %collective-permute-start = (bf16[528,128]{1,0:T(8,128)(2,1)S(1)}, bf16[528,128]{1,0:T(8,128)(2,1)S(1)}, u32[]{:S(2)}, u32[]{:S(2)}) collective-permute-start(bf16[528,128]{1,0:T(8,128)(2,1)S(1)} %get-tuple-element.37), channel_id=1, source_target_pairs={{0,6},{1,7},{2,4},{3,5},{4,2},{5,3},{6,0},{7,1},{8,14},{9,15},{10,... | collective-permute-start | bytes 405512 | tf_op jit(solution)/shard_map/ppermute | solution.py:294
  17.7 0.0 collective-permute-done.4.refs_0_
  17.7 2.1 %collective-permute-start.1 = (bf16[528,128]{1,0:T(8,128)(2,1)S(1)}, bf16[528,128]{1,0:T(8,128)(2,1)S(1)}, u32[]{:S(2)}, u32[]{:S(2)}) collective-permute-start(bf16[528,128]{1,0:T(8,128)(2,1)S(1)} %get-tuple-element.38), channel_id=1, source_target_pairs={{0,7},{1,6},{2,5},{3,4},{4,3},{5,2},{6,1},{7,0},{8,15},{9,14},{10,... | collective-permute-start | bytes 405512 | tf_op jit(solution)/shard_map/ppermute | solution.py:294
  19.8 2.9 %score.3 = (f32[256,512]{1,0:T(8,128)S(1)}, f32[1,128]{1,0:T(1,128)S(1)}, f32[1,128]{1,0:T(1,128)S(1)}) custom-call(bf16[256,32,512]{2,1,0:T(8,128)(2,1)S(1)} %get-tuple-element.35.bank_ref, f32[256,128]{1,0:T(8,128)S(1)} %get-tuple-element.36.after_ref.norm_ref, s32[1,256]{1,0:T(1,128)S(1)} %bitcast.11, ...), custom_call_target="tpu_custom_call" | custom-call | flops 1 | bytes 1 | tf_op jit(solution)/shard_map/score/pallas_call | solution.py:323
  22.7 0.0 collective-permute-done.5.refs_1_
  22.7 2.9 %score.4 = (f32[256,512]{1,0:T(8,128)S(1)}, f32[1,128]{1,0:T(1,128)S(1)}, f32[1,128]{1,0:T(1,128)S(1)}) custom-call(bf16[256,32,512]{2,1,0:T(8,128)(2,1)S(1)} %get-tuple-element.35.bank_ref, f32[256,128]{1,0:T(8,128)S(1)} %get-tuple-element.36.after_ref.norm_ref, s32[1,256]{1,0:T(1,128)S(1)} %bitcast.12, ...), custom_call_target="tpu_custom_call" | custom-call | flops 1 | bytes 1 | tf_op jit(solution)/shard_map/score/pallas_call | solution.py:323
  25.6 0.0 collective-permute-done.2.refs_0_
  25.6 0.0 copy-start
  25.6 2.9 %score.5 = (f32[256,512]{1,0:T(8,128)S(1)}, f32[1,128]{1,0:T(1,128)S(1)}, f32[1,128]{1,0:T(1,128)S(1)}) custom-call(bf16[256,32,512]{2,1,0:T(8,128)(2,1)S(1)} %get-tuple-element.35.bank_ref, f32[256,128]{1,0:T(8,128)S(1)} %get-tuple-element.36.after_ref.norm_ref, s32[1,256]{1,0:T(1,128)S(1)} %bitcast.13, ...), custom_call_target="tpu_custom_call" | custom-call | flops 1 | bytes 1 | tf_op jit(solution)/shard_map/score/pallas_call | solution.py:323
  28.6 0.0 collective-permute-done.refs_0_
  28.6 0.0 collective-permute-done.1.refs_1_
  28.6 0.4 last_sum.1
  29.0 1.6 %collective-permute-start.9 = (bf16[256,512]{1,0:T(8,128)(2,1)S(1)}, bf16[256,512]{1,0:T(8,128)(2,1)S(1)}, u32[]{:S(2)}, u32[]{:S(2)}) collective-permute-start(bf16[256,512]{1,0:T(8,128)(2,1)S(1)} %get-tuple-element.55), channel_id=1, source_target_pairs={{0,8},{8,0},{16,24},{24,16},{1,9},{9,1},{17,25},{25,17},{2,10},{10... | collective-permute-start | bytes 786440 | tf_op jit(solution)/shard_map/ppermute | solution.py:294
  30.5 1.5 %collective-permute-start.8 = (bf16[256,512]{1,0:T(8,128)(2,1)S(1)}, bf16[256,512]{1,0:T(8,128)(2,1)S(1)}, u32[]{:S(2)}, u32[]{:S(2)}) collective-permute-start(bf16[256,512]{1,0:T(8,128)(2,1)S(1)} %get-tuple-element.55), channel_id=1, source_target_pairs={{0,16},{8,24},{16,0},{24,8},{1,17},{9,25},{17,1},{25,9},{2,18},{10... | collective-permute-start | bytes 786440 | tf_op jit(solution)/shard_map/ppermute | solution.py:294
  32.1 0.5 collective-permute-start.7
  32.5 2.8 %last_score.1 = f32[8,128]{1,0:T(8,128)S(1)} custom-call(s32[1]{0:T(128)} %bitcast.me_ref, bf16[256,32,512]{2,1,0:T(8,128)(2,1)S(1)} %get-tuple-element.35.bank_ref, f32[256,128]{1,0:T(8,128)S(1)} %get-tuple-element.36.after_ref.norm_ref, s32[1,256]{1,0:T(1,128)S(1)} %bitcast.14, bf16[512,256]{1,0:T(8,128)(2,1)S(1)} %get-tuple-element.46.columns_ref, ...), custom_call_target="tpu_custom_call" | custom-call | flops 1 | bytes 1 | tf_op jit(solution)/shard_map/last_score/pallas_call | solution.py:323
  35.3 15.9 %all_to_all.11 = f32[8,1,128]{2,1,0:T(1,128)S(1)} all-to-all(f32[8,1,128]{2,1,0:T(1,128)S(1)} %bitcast.9), channel_id=1, replica_groups=mesh['grp'=4,'own'=8] {'own'}, dimensions={0} | all-to-all | bytes 8192 | tf_op jit(solution)/shard_map/all_to_all | solution.py:420
  51.2 0.8 %unpack.1 = f32[1,512]{1,0:T(1,128)} custom-call(s32[1,512]{1,0:T(1,128)S(1)} %get-tuple-element.29.index_ref, f32[8,128]{1,0:T(8,128)S(1)} %bitcast.10), custom_call_target="tpu_custom_call" | custom-call | flops 1 | bytes 1 | tf_op jit(solution)/shard_map/unpack/pallas_call | solution.py:323
  52.1 0.0 collective-permute-done.9.refs_2_
  52.1 0.0 collective-permute-done.8.refs_1_
  52.1 0.0 collective-permute-done.7.refs_0_
  52.1 1.0 %finish.1 = f32[256,512]{1,0:T(8,128)} custom-call(f32[256,512]{1,0:T(8,128)S(1)} %copy-done, f32[256,512]{1,0:T(8,128)S(1)} %get-tuple-element.54.own_ref, bf16[256,512]{1,0:T(8,128)(2,1)S(1)} %collective-permute-done.7.refs_0_, bf16[256,512]{1,0:T(8,128)(2,1)S(1)} %collective-permute-done.8.refs_1_, bf16[256,512]{1,0:T(8,128)(2,1)S(1)} %collective-permute-done.9.refs_2_), custom_call_target="tpu_custom_call" | custom-call | flops 1 | bytes 1 | tf_op jit(solution)/shard_map/finish/pallas_call | solution.py:323
  (4 shorter events, 0.0 us)
Async XLA Ops:
  0.6 19.1 %copy-start.1 = (s32[256]{0:T(256)S(1)}, s32[256]{0:T(256)}, u32[]{:S(2)}) copy-start(s32[256]{0:T(256)} %param.10) | copy-start | bytes 3076
  2.3 11.4 %collective-permute-start.6 = (bf16[528,128]{1,0:T(8,128)(2,1)S(1)}, bf16[528,128]{1,0:T(8,128)(2,1)S(1)}, u32[]{:S(2)}, u32[]{:S(2)}) collective-permute-start(bf16[528,128]{1,0:T(8,128)(2,1)S(1)} %get-tuple-element.42), channel_id=1, source_target_pairs={{0,1},{1,0},{2,3},{3,2},{4,5},{5,4},{6,7},{7,6},{8,9},{9,8},{10,11... | collective-permute-start | bytes 405512 | tf_op jit(solution)/shard_map/ppermute | solution.py:294
  2.8 14.8 %collective-permute-start.4 = (bf16[528,128]{1,0:T(8,128)(2,1)S(1)}, bf16[528,128]{1,0:T(8,128)(2,1)S(1)}, u32[]{:S(2)}, u32[]{:S(2)}) collective-permute-start(bf16[528,128]{1,0:T(8,128)(2,1)S(1)} %get-tuple-element.33.after_ref), channel_id=1, source_target_pairs={{0,4},{1,5},{2,6},{3,7},{4,0},{5,1},{6,2},{7,3},{8,12},{9,13},{10,... | collective-permute-start | bytes 405512 | tf_op jit(solution)/shard_map/ppermute | solution.py:294
  7.8 17.9 %collective-permute-start.2 = (bf16[528,128]{1,0:T(8,128)(2,1)S(1)}, bf16[528,128]{1,0:T(8,128)(2,1)S(1)}, u32[]{:S(2)}, u32[]{:S(2)}) collective-permute-start(bf16[528,128]{1,0:T(8,128)(2,1)S(1)} %get-tuple-element.39), channel_id=1, source_target_pairs={{0,5},{1,4},{2,7},{3,6},{4,1},{5,0},{6,3},{7,2},{8,13},{9,12},{10,... | collective-permute-start | bytes 405512 | tf_op jit(solution)/shard_map/ppermute | solution.py:294
  7.8 17.8 %collective-permute-start.3 = (bf16[528,128]{1,0:T(8,128)(2,1)}, bf16[528,128]{1,0:T(8,128)(2,1)S(1)}, u32[]{:S(2)}, u32[]{:S(2)}) collective-permute-start(bf16[528,128]{1,0:T(8,128)(2,1)} %get-tuple-element.40), channel_id=1, source_target_pairs={{0,3},{1,2},{2,1},{3,0},{4,7},{5,6},{6,5},{7,4},{8,11},{9,10},{10,... | collective-permute-start | bytes 405512 | tf_op jit(solution)/shard_map/ppermute | solution.py:294
  9.4 13.3 %collective-permute-start.5 = (bf16[528,128]{1,0:T(8,128)(2,1)}, bf16[528,128]{1,0:T(8,128)(2,1)S(1)}, u32[]{:S(2)}, u32[]{:S(2)}) collective-permute-start(bf16[528,128]{1,0:T(8,128)(2,1)} %get-tuple-element.41), channel_id=1, source_target_pairs={{0,2},{1,3},{2,0},{3,1},{4,6},{5,7},{6,4},{7,5},{8,10},{9,11},{10,... | collective-permute-start | bytes 405512 | tf_op jit(solution)/shard_map/ppermute | solution.py:294
  13.7 14.8 %collective-permute-start = (bf16[528,128]{1,0:T(8,128)(2,1)S(1)}, bf16[528,128]{1,0:T(8,128)(2,1)S(1)}, u32[]{:S(2)}, u32[]{:S(2)}) collective-permute-start(bf16[528,128]{1,0:T(8,128)(2,1)S(1)} %get-tuple-element.37), channel_id=1, source_target_pairs={{0,6},{1,7},{2,4},{3,5},{4,2},{5,3},{6,0},{7,1},{8,14},{9,15},{10,... | collective-permute-start | bytes 405512 | tf_op jit(solution)/shard_map/ppermute | solution.py:294
  17.7 10.9 %collective-permute-start.1 = (bf16[528,128]{1,0:T(8,128)(2,1)S(1)}, bf16[528,128]{1,0:T(8,128)(2,1)S(1)}, u32[]{:S(2)}, u32[]{:S(2)}) collective-permute-start(bf16[528,128]{1,0:T(8,128)(2,1)S(1)} %get-tuple-element.38), channel_id=1, source_target_pairs={{0,7},{1,6},{2,5},{3,4},{4,3},{5,2},{6,1},{7,0},{8,15},{9,14},{10,... | collective-permute-start | bytes 405512 | tf_op jit(solution)/shard_map/ppermute | solution.py:294
  25.6 26.4 %copy-start = (f32[256,512]{1,0:T(8,128)S(1)}, f32[256,512]{1,0:T(8,128)}, u32[]{:S(2)}) copy-start(f32[256,512]{1,0:T(8,128)} %stored_ref.1) | copy-start | bytes 1572868
  29.0 23.1 %collective-permute-start.9 = (bf16[256,512]{1,0:T(8,128)(2,1)S(1)}, bf16[256,512]{1,0:T(8,128)(2,1)S(1)}, u32[]{:S(2)}, u32[]{:S(2)}) collective-permute-start(bf16[256,512]{1,0:T(8,128)(2,1)S(1)} %get-tuple-element.55), channel_id=1, source_target_pairs={{0,8},{8,0},{16,24},{24,16},{1,9},{9,1},{17,25},{25,17},{2,10},{10... | collective-permute-start | bytes 786440 | tf_op jit(solution)/shard_map/ppermute | solution.py:294
  30.5 21.5 %collective-permute-start.8 = (bf16[256,512]{1,0:T(8,128)(2,1)S(1)}, bf16[256,512]{1,0:T(8,128)(2,1)S(1)}, u32[]{:S(2)}, u32[]{:S(2)}) collective-permute-start(bf16[256,512]{1,0:T(8,128)(2,1)S(1)} %get-tuple-element.55), channel_id=1, source_target_pairs={{0,16},{8,24},{16,0},{24,8},{1,17},{9,25},{17,1},{25,9},{2,18},{10... | collective-permute-start | bytes 786440 | tf_op jit(solution)/shard_map/ppermute | solution.py:294
  32.1 20.0 %collective-permute-start.7 = (bf16[256,512]{1,0:T(8,128)(2,1)S(1)}, bf16[256,512]{1,0:T(8,128)(2,1)S(1)}, u32[]{:S(2)}, u32[]{:S(2)}) collective-permute-start(bf16[256,512]{1,0:T(8,128)(2,1)S(1)} %get-tuple-element.55), channel_id=1, source_target_pairs={{0,24},{8,16},{16,8},{24,0},{1,25},{9,17},{17,9},{25,1},{2,26},{10... | collective-permute-start | bytes 786440 | tf_op jit(solution)/shard_map/ppermute | solution.py:294

commit v14 on v10

--- a/solution.py
+++ b/solution.py
@@ -419,7 +419,7 @@
         ],
         [*last_messages, total],
     )
-    terms = [exchange(sent, "grp", offset) for offset in range(1, parts)]
+    terms = [exchange(sent, "grp", offset) for offset in range(1, parts)][::-1]
     best = vmem_call(
         functools.partial(
             last_score_kernel, sum(groups, []), capacity, block

time: 48.2 us -> 48.2 us (level)
  no operation moved by 1% of the time
where the time goes in v14:
time: 48.2 us; the launch traced here: 48 us
  Pallas kernels  20.2 us (42%)
  starting transfers between devices  13.5 us (28%)
  blocking collectives  11.2 us (23%)
  waiting for transfers between devices  1.69 us (4%)
  between operations  0.73 us (2%)
  local copies, waits for them, and re-layouts  0.69 us (1%)
    pallas_call x10, Pallas kernels, vmem_call(): pl.pallas_call(kernel, out_shape=out_shape, in_specs=in_specs or [whole_v...  20.2 us
    ppermute x10, starting transfers between devices, exchange(): lax.ppermute(value, axis, [(device, device ^ offset) for device in range(...  13.5 us
    all_to_all x1, blocking collectives, body(): lax.all_to_all(best, 'own', split_axis=0, concat_axis=0, tiled=True)  11.2 us
    ppermute x10, waiting for transfers between devices, exchange(): lax.ppermute(value, axis, [(device, device ^ offset) for device in range(...  1.69 us
  transfers between devices with their start and end apart: 10, of which 1 were waited for; matrix products, arithmetic and copies ran while one was open for 0% of the time, Pallas kernels for 36%

profile of v14, /device:TPU:0, one launch (start us, length us, event | category | flops | bytes accessed | tf_op | source)
XLA Modules:
  0.0 48.0 jit_solution(3717232540577986387)
XLA Ops:
  0.6 1.7 %pack.1 = (s32[1,512]{1,0:T(1,128)S(1)}, s32[1,512]{1,0:T(1,128)S(1)}, s32[1,512]{1,0:T(1,128)}, s32[1,512]{1,0:T(1,128)S(1)}, bf16[512,512]{1,0:T(8,128)(2,1)S(...) custom-call(s32[1]{0:T(128)} %bitcast.me_ref, s32[1,512]{1,0:T(1,128)} %bitcast.15, s32[1,512]{1,0:T(1,128)} %bitcast.16, ...), custom_call_target="tpu_custom_call" | custom-call | flops 1 | bytes 1 | tf_op jit(solution)/shard_map/pack/pallas_call | solution.py:335
  2.3 0.5 %collective-permute-start = (bf16[528,128]{1,0:T(8,128)(2,1)S(1)}, bf16[528,128]{1,0:T(8,128)(2,1)S(1)}, u32[]{:S(2)}, u32[]{:S(2)}) collective-permute-start(bf16[528,128]{1,0:T(8,128)(2,1)S(1)} %get-tuple-element.35), channel_id=1, source_target_pairs={{0,1},{1,0},{2,3},{3,2},{4,5},{5,4},{6,7},{7,6},{8,9},{9,8},{10,11... | collective-permute-start | bytes 405512 | tf_op jit(solution)/shard_map/ppermute | solution.py:306
  2.8 3.7 %collective-permute-start.3 = (bf16[528,128]{1,0:T(8,128)(2,1)S(1)}, bf16[528,128]{1,0:T(8,128)(2,1)S(1)}, u32[]{:S(2)}, u32[]{:S(2)}) collective-permute-start(bf16[528,128]{1,0:T(8,128)(2,1)S(1)} %get-tuple-element.33.after_ref), channel_id=1, source_target_pairs={{0,4},{1,5},{2,6},{3,7},{4,0},{5,1},{6,2},{7,3},{8,12},{9,13},{10,... | collective-permute-start | bytes 405512 | tf_op jit(solution)/shard_map/ppermute | solution.py:306
  6.5 1.2 %next_pack.1 = (bf16[528,128]{1,0:T(8,128)(2,1)S(1)}, bf16[528,128]{1,0:T(8,128)(2,1)}, bf16[528,128]{1,0:T(8,128)(2,1)S(1)}, bf16[528,128]{1,0:T(8,128)(2,1)}) custom-call(s32[1,512]{1,0:T(1,128)S(1)} %get-tuple-element.30.index_ref, s32[1,512]{1,0:T(1,128)S(1)} %get-tuple-element.31.slot_ref, bf16[512,512]{1,0:T(8,128)(2,1)S(1)} %get-tuple-element.32.rows_ref, ...), custom_call_target="tpu_custom_call" | custom-call | flops 1 | bytes 1 | tf_op jit(solution)/shard_map/next_pack/pallas_call | solution.py:335
  7.8 1.6 %collective-permute-start.4 = (bf16[528,128]{1,0:T(8,128)(2,1)}, bf16[528,128]{1,0:T(8,128)(2,1)S(1)}, u32[]{:S(2)}, u32[]{:S(2)}) collective-permute-start(bf16[528,128]{1,0:T(8,128)(2,1)} %get-tuple-element.41), channel_id=1, source_target_pairs={{0,2},{1,3},{2,0},{3,1},{4,6},{5,7},{6,4},{7,5},{8,10},{9,11},{10,... | collective-permute-start | bytes 405512 | tf_op jit(solution)/shard_map/ppermute | solution.py:306
  9.3 0.0 collective-permute-start.5
  9.3 0.2 collective-permute-start.6
  9.5 0.0 collective-permute-done.refs_1_
  9.5 0.7 %copy-done.1 = s32[256]{0:T(256)S(1)} copy-done((s32[256]{0:T(256)S(1)}, s32[256]{0:T(256)}, u32[]{:S(2)}) %copy-start.1) | copy-done | bytes 1048
  10.2 6.3 %first_score.1 = (bf16[256,32,512]{2,1,0:T(8,128)(2,1)S(1)}, f32[256,128]{1,0:T(8,128)S(1)}, f32[256,512]{1,0:T(8,128)S(1)}, f32[1,128]{1,0:T(1,128)S(1)}, f32[1,128]{1,0:T(1,128)S(1)}) custom-call(bf16[256,32,512]{2,1,0:T(8,128)(2,1)} %bank_ref.1, s32[1,256]{1,0:T(1,128)S(1)} %bitcast.11, bf16[528,128]{1,0:T(8,128)(2,1)S(1)} %get-tuple-element.34.refs_0_, ...), custom_call_target="tpu_custom_call" | custom-call | flops 1 | bytes 1 | tf_op jit(solution)/shard_map/first_score/pallas_call | solution.py:335
  16.5 0.3 late_pack.1
  16.9 4.0 %collective-permute-start.1 = (bf16[528,128]{1,0:T(8,128)(2,1)S(1)}, bf16[528,128]{1,0:T(8,128)(2,1)S(1)}, u32[]{:S(2)}, u32[]{:S(2)}) collective-permute-start(bf16[528,128]{1,0:T(8,128)(2,1)S(1)} %get-tuple-element.39), channel_id=1, source_target_pairs={{0,6},{1,7},{2,4},{3,5},{4,2},{5,3},{6,0},{7,1},{8,14},{9,15},{10,... | collective-permute-start | bytes 405512 | tf_op jit(solution)/shard_map/ppermute | solution.py:306
  20.8 0.0 collective-permute-done.3.refs_0_
  20.8 0.0 collective-permute-start.2
  20.8 0.0 collective-permute-done.4.refs_1_
  20.8 0.0 copy-start.2
  20.9 2.9 %score.2 = (f32[1,128]{1,0:T(1,128)S(1)}, f32[1,128]{1,0:T(1,128)S(1)}, f32[256,512]{1,0:T(8,128)S(1)}) custom-call(bf16[256,32,512]{2,1,0:T(8,128)(2,1)S(1)} %get-tuple-element.36.bank_ref, f32[256,128]{1,0:T(8,128)S(1)} %get-tuple-element.37.norm_ref, s32[1,256]{1,0:T(1,128)S(1)} %bitcast.12, f32[256,512]{1,0:T(8,128)S(1)} %get-tuple-element.38.after_ref.before_ref, ...), custom_call_target="tpu_custom_call" | custom-call | flops 1 | bytes 1 | tf_op jit(solution)/shard_map/score/pallas_call | solution.py:335
  23.8 0.0 collective-permute-done.5.refs_0_
  23.8 0.0 collective-permute-done.6.refs_1_
  23.8 0.0 copy-start
  23.8 2.9 %score.3 = (f32[1,128]{1,0:T(1,128)S(1)}, f32[1,128]{1,0:T(1,128)S(1)}, f32[256,512]{1,0:T(8,128)S(1)}) custom-call(bf16[256,32,512]{2,1,0:T(8,128)(2,1)S(1)} %get-tuple-element.36.bank_ref, f32[256,128]{1,0:T(8,128)S(1)} %get-tuple-element.37.norm_ref, s32[1,256]{1,0:T(1,128)S(1)} %bitcast.13, f32[256,512]{1,0:T(8,128)S(1)} %get-tuple-element.42.before_ref, ...), custom_call_target="tpu_custom_call" | custom-call | flops 1 | bytes 1 | tf_op jit(solution)/shard_map/score/pallas_call | solution.py:335
  26.7 1.7 %collective-permute-done.2.refs_1_ = bf16[528,128]{1,0:T(8,128)(2,1)S(1)} collective-permute-done((bf16[528,128]{1,0:T(8,128)(2,1)S(1)}, bf16[528,128]{1,0:T(8,128)(2,1)S(1)}, u32[]{:S(2)}, u32[]{:S(2)}) %collective-permute-start.2) | collective-permute-done | bytes 135200 | tf_op jit(solution)/shard_map/ppermute | solution.py:306
  28.4 0.4 last_sum.1
  28.8 1.6 %collective-permute-start.9 = (bf16[256,512]{1,0:T(8,128)(2,1)S(1)}, bf16[256,512]{1,0:T(8,128)(2,1)S(1)}, u32[]{:S(2)}, u32[]{:S(2)}) collective-permute-start(bf16[256,512]{1,0:T(8,128)(2,1)S(1)} %get-tuple-element.55), channel_id=1, source_target_pairs={{0,8},{8,0},{16,24},{24,16},{1,9},{9,1},{17,25},{25,17},{2,10},{10... | collective-permute-start | bytes 786440 | tf_op jit(solution)/shard_map/ppermute | solution.py:306
  30.4 1.5 %collective-permute-start.8 = (bf16[256,512]{1,0:T(8,128)(2,1)S(1)}, bf16[256,512]{1,0:T(8,128)(2,1)S(1)}, u32[]{:S(2)}, u32[]{:S(2)}) collective-permute-start(bf16[256,512]{1,0:T(8,128)(2,1)S(1)} %get-tuple-element.55), channel_id=1, source_target_pairs={{0,16},{8,24},{16,0},{24,8},{1,17},{9,25},{17,1},{25,9},{2,18},{10... | collective-permute-start | bytes 786440 | tf_op jit(solution)/shard_map/ppermute | solution.py:306
  31.9 0.5 collective-permute-start.7
  32.4 2.6 %last_score.1 = f32[8,128]{1,0:T(8,128)S(1)} custom-call(s32[1]{0:T(128)} %bitcast.me_ref, bf16[256,32,512]{2,1,0:T(8,128)(2,1)S(1)} %get-tuple-element.36.bank_ref, f32[256,128]{1,0:T(8,128)S(1)} %get-tuple-element.37.norm_ref, s32[1,256]{1,0:T(1,128)S(1)} %bitcast.14, bf16[512,256]{1,0:T(8,128)(2,1)S(1)} %get-tuple-element.46.columns_ref, ...), custom_call_target="tpu_custom_call" | custom-call | flops 1 | bytes 1 | tf_op jit(solution)/shard_map/last_score/pallas_call | solution.py:335
  34.9 11.2 %all_to_all.11 = f32[8,1,128]{2,1,0:T(1,128)S(1)} all-to-all(f32[8,1,128]{2,1,0:T(1,128)S(1)} %bitcast.9), channel_id=1, replica_groups=mesh['grp'=4,'own'=8] {'own'}, dimensions={0} | all-to-all | bytes 8192 | tf_op jit(solution)/shard_map/all_to_all | solution.py:432
  46.1 0.8 %unpack.1 = f32[1,512]{1,0:T(1,128)} custom-call(s32[1,512]{1,0:T(1,128)S(1)} %get-tuple-element.29.index_ref, f32[8,128]{1,0:T(8,128)S(1)} %bitcast.10), custom_call_target="tpu_custom_call" | custom-call | flops 1 | bytes 1 | tf_op jit(solution)/shard_map/unpack/pallas_call | solution.py:335
  46.9 0.0 collective-permute-done.8.refs_1_
  46.9 0.0 collective-permute-done.7.refs_0_
  47.0 1.0 %finish.1 = f32[256,512]{1,0:T(8,128)} custom-call(f32[256,512]{1,0:T(8,128)S(1)} %copy-done, f32[256,512]{1,0:T(8,128)S(1)} %get-tuple-element.54.own_ref, bf16[256,512]{1,0:T(8,128)(2,1)S(1)} %collective-permute-done.7.refs_0_, bf16[256,512]{1,0:T(8,128)(2,1)S(1)} %collective-permute-done.8.refs_1_, bf16[256,512]{1,0:T(8,128)(2,1)S(1)} %collective-permute-done.9.refs_2_), custom_call_target="tpu_custom_call" | custom-call | flops 1 | bytes 1 | tf_op jit(solution)/shard_map/finish/pallas_call | solution.py:335
  (5 shorter events, 0.0 us)
Async XLA Ops:
  2.3 7.2 %collective-permute-start = (bf16[528,128]{1,0:T(8,128)(2,1)S(1)}, bf16[528,128]{1,0:T(8,128)(2,1)S(1)}, u32[]{:S(2)}, u32[]{:S(2)}) collective-permute-start(bf16[528,128]{1,0:T(8,128)(2,1)S(1)} %get-tuple-element.35), channel_id=1, source_target_pairs={{0,1},{1,0},{2,3},{3,2},{4,5},{5,4},{6,7},{7,6},{8,9},{9,8},{10,11... | collective-permute-start | bytes 405512 | tf_op jit(solution)/shard_map/ppermute | solution.py:306
  2.8 18.0 %collective-permute-start.3 = (bf16[528,128]{1,0:T(8,128)(2,1)S(1)}, bf16[528,128]{1,0:T(8,128)(2,1)S(1)}, u32[]{:S(2)}, u32[]{:S(2)}) collective-permute-start(bf16[528,128]{1,0:T(8,128)(2,1)S(1)} %get-tuple-element.33.after_ref), channel_id=1, source_target_pairs={{0,4},{1,5},{2,6},{3,7},{4,0},{5,1},{6,2},{7,3},{8,12},{9,13},{10,... | collective-permute-start | bytes 405512 | tf_op jit(solution)/shard_map/ppermute | solution.py:306
  7.8 13.1 %collective-permute-start.4 = (bf16[528,128]{1,0:T(8,128)(2,1)}, bf16[528,128]{1,0:T(8,128)(2,1)S(1)}, u32[]{:S(2)}, u32[]{:S(2)}) collective-permute-start(bf16[528,128]{1,0:T(8,128)(2,1)} %get-tuple-element.41), channel_id=1, source_target_pairs={{0,2},{1,3},{2,0},{3,1},{4,6},{5,7},{6,4},{7,5},{8,10},{9,11},{10,... | collective-permute-start | bytes 405512 | tf_op jit(solution)/shard_map/ppermute | solution.py:306
  9.3 14.5 %collective-permute-start.5 = (bf16[528,128]{1,0:T(8,128)(2,1)S(1)}, bf16[528,128]{1,0:T(8,128)(2,1)S(1)}, u32[]{:S(2)}, u32[]{:S(2)}) collective-permute-start(bf16[528,128]{1,0:T(8,128)(2,1)S(1)} %get-tuple-element.43), channel_id=1, source_target_pairs={{0,5},{1,4},{2,7},{3,6},{4,1},{5,0},{6,3},{7,2},{8,13},{9,12},{10,... | collective-permute-start | bytes 405512 | tf_op jit(solution)/shard_map/ppermute | solution.py:306
  9.3 14.5 %collective-permute-start.6 = (bf16[528,128]{1,0:T(8,128)(2,1)}, bf16[528,128]{1,0:T(8,128)(2,1)S(1)}, u32[]{:S(2)}, u32[]{:S(2)}) collective-permute-start(bf16[528,128]{1,0:T(8,128)(2,1)} %get-tuple-element.44), channel_id=1, source_target_pairs={{0,3},{1,2},{2,1},{3,0},{4,7},{5,6},{6,5},{7,4},{8,11},{9,10},{10,... | collective-permute-start | bytes 405512 | tf_op jit(solution)/shard_map/ppermute | solution.py:306
  9.5 0.7 %copy-start.1 = (s32[256]{0:T(256)S(1)}, s32[256]{0:T(256)}, u32[]{:S(2)}) copy-start(s32[256]{0:T(256)} %param.10) | copy-start | bytes 3076
  16.9 9.9 %collective-permute-start.1 = (bf16[528,128]{1,0:T(8,128)(2,1)S(1)}, bf16[528,128]{1,0:T(8,128)(2,1)S(1)}, u32[]{:S(2)}, u32[]{:S(2)}) collective-permute-start(bf16[528,128]{1,0:T(8,128)(2,1)S(1)} %get-tuple-element.39), channel_id=1, source_target_pairs={{0,6},{1,7},{2,4},{3,5},{4,2},{5,3},{6,0},{7,1},{8,14},{9,15},{10,... | collective-permute-start | bytes 405512 | tf_op jit(solution)/shard_map/ppermute | solution.py:306
  20.8 7.6 %collective-permute-start.2 = (bf16[528,128]{1,0:T(8,128)(2,1)S(1)}, bf16[528,128]{1,0:T(8,128)(2,1)S(1)}, u32[]{:S(2)}, u32[]{:S(2)}) collective-permute-start(bf16[528,128]{1,0:T(8,128)(2,1)S(1)} %get-tuple-element.40), channel_id=1, source_target_pairs={{0,7},{1,6},{2,5},{3,4},{4,3},{5,2},{6,1},{7,0},{8,15},{9,14},{10,... | collective-permute-start | bytes 405512 | tf_op jit(solution)/shard_map/ppermute | solution.py:306
  20.8 11.5 %copy-start.2 = (s32[256]{0:T(256)S(1)}, s32[256]{0:T(256)}, u32[]{:S(2)}) copy-start(s32[256]{0:T(256)} %param.10) | copy-start | bytes 3076
  23.8 23.1 %copy-start = (f32[256,512]{1,0:T(8,128)S(1)}, f32[256,512]{1,0:T(8,128)}, u32[]{:S(2)}) copy-start(f32[256,512]{1,0:T(8,128)} %stored_ref.1) | copy-start | bytes 1572868
  28.8 18.1 %collective-permute-start.9 = (bf16[256,512]{1,0:T(8,128)(2,1)S(1)}, bf16[256,512]{1,0:T(8,128)(2,1)S(1)}, u32[]{:S(2)}, u32[]{:S(2)}) collective-permute-start(bf16[256,512]{1,0:T(8,128)(2,1)S(1)} %get-tuple-element.55), channel_id=1, source_target_pairs={{0,8},{8,0},{16,24},{24,16},{1,9},{9,1},{17,25},{25,17},{2,10},{10... | collective-permute-start | bytes 786440 | tf_op jit(solution)/shard_map/ppermute | solution.py:306
  30.4 16.6 %collective-permute-start.8 = (bf16[256,512]{1,0:T(8,128)(2,1)S(1)}, bf16[256,512]{1,0:T(8,128)(2,1)S(1)}, u32[]{:S(2)}, u32[]{:S(2)}) collective-permute-start(bf16[256,512]{1,0:T(8,128)(2,1)S(1)} %get-tuple-element.55), channel_id=1, source_target_pairs={{0,16},{8,24},{16,0},{24,8},{1,17},{9,25},{17,1},{25,9},{2,18},{10... | collective-permute-start | bytes 786440 | tf_op jit(solution)/shard_map/ppermute | solution.py:306
  31.9 15.0 %collective-permute-start.7 = (bf16[256,512]{1,0:T(8,128)(2,1)S(1)}, bf16[256,512]{1,0:T(8,128)(2,1)S(1)}, u32[]{:S(2)}, u32[]{:S(2)}) collective-permute-start(bf16[256,512]{1,0:T(8,128)(2,1)S(1)} %get-tuple-element.55), channel_id=1, source_target_pairs={{0,24},{8,16},{16,8},{24,0},{1,25},{9,17},{17,9},{25,1},{2,26},{10... | collective-permute-start | bytes 786440 | tf_op jit(solution)/shard_map/ppermute | solution.py:306

commit v15 on v14

--- a/solution.py
+++ b/solution.py
@@ -419,7 +419,8 @@
         ],
         [*last_messages, total],
     )
-    terms = [exchange(sent, "grp", offset) for offset in range(1, parts)][::-1]
+    offsets = sorted(range(1, parts), key=lambda offset: (offset.bit_count() == 1, offset))
+    terms = [exchange(sent, "grp", offset) for offset in offsets]
     best = vmem_call(
         functools.partial(
             last_score_kernel, sum(groups, []), capacity, block

time: 48.2 us -> 48.2 us (level)
  no operation moved by 1% of the time
where the time goes in v15:
time: 48.2 us; the launch traced here: 48 us
  Pallas kernels  20.2 us (42%)
  starting transfers between devices  13.5 us (28%)
  blocking collectives  11.2 us (23%)
  waiting for transfers between devices  1.69 us (4%)
  between operations  0.73 us (2%)
  local copies, waits for them, and re-layouts  0.69 us (1%)
    pallas_call x10, Pallas kernels, vmem_call(): pl.pallas_call(kernel, out_shape=out_shape, in_specs=in_specs or [whole_v...  20.2 us
    ppermute x10, starting transfers between devices, exchange(): lax.ppermute(value, axis, [(device, device ^ offset) for device in range(...  13.5 us
    all_to_all x1, blocking collectives, body(): lax.all_to_all(best, 'own', split_axis=0, concat_axis=0, tiled=True)  11.2 us
    ppermute x10, waiting for transfers between devices, exchange(): lax.ppermute(value, axis, [(device, device ^ offset) for device in range(...  1.69 us
  transfers between devices with their start and end apart: 10, of which 1 were waited for; matrix products, arithmetic and copies ran while one was open for 0% of the time, Pallas kernels for 36%

profile of v15, /device:TPU:0, one launch (start us, length us, event | category | flops | bytes accessed | tf_op | source)
XLA Modules:
  0.0 48.0 jit_solution(4502390814306177227)
XLA Ops:
  0.6 1.7 %pack.1 = (s32[1,512]{1,0:T(1,128)S(1)}, s32[1,512]{1,0:T(1,128)S(1)}, s32[1,512]{1,0:T(1,128)}, s32[1,512]{1,0:T(1,128)S(1)}, bf16[512,512]{1,0:T(8,128)(2,1)S(...) custom-call(s32[1]{0:T(128)} %bitcast.me_ref, s32[1,512]{1,0:T(1,128)} %bitcast.15, s32[1,512]{1,0:T(1,128)} %bitcast.16, ...), custom_call_target="tpu_custom_call" | custom-call | flops 1 | bytes 1 | tf_op jit(solution)/shard_map/pack/pallas_call | solution.py:335
  2.3 0.5 %collective-permute-start = (bf16[528,128]{1,0:T(8,128)(2,1)S(1)}, bf16[528,128]{1,0:T(8,128)(2,1)S(1)}, u32[]{:S(2)}, u32[]{:S(2)}) collective-permute-start(bf16[528,128]{1,0:T(8,128)(2,1)S(1)} %get-tuple-element.35), channel_id=1, source_target_pairs={{0,1},{1,0},{2,3},{3,2},{4,5},{5,4},{6,7},{7,6},{8,9},{9,8},{10,11... | collective-permute-start | bytes 405512 | tf_op jit(solution)/shard_map/ppermute | solution.py:306
  2.8 3.7 %collective-permute-start.3 = (bf16[528,128]{1,0:T(8,128)(2,1)S(1)}, bf16[528,128]{1,0:T(8,128)(2,1)S(1)}, u32[]{:S(2)}, u32[]{:S(2)}) collective-permute-start(bf16[528,128]{1,0:T(8,128)(2,1)S(1)} %get-tuple-element.33.after_ref), channel_id=1, source_target_pairs={{0,4},{1,5},{2,6},{3,7},{4,0},{5,1},{6,2},{7,3},{8,12},{9,13},{10,... | collective-permute-start | bytes 405512 | tf_op jit(solution)/shard_map/ppermute | solution.py:306
  6.5 1.2 %next_pack.1 = (bf16[528,128]{1,0:T(8,128)(2,1)S(1)}, bf16[528,128]{1,0:T(8,128)(2,1)}, bf16[528,128]{1,0:T(8,128)(2,1)S(1)}, bf16[528,128]{1,0:T(8,128)(2,1)}) custom-call(s32[1,512]{1,0:T(1,128)S(1)} %get-tuple-element.30.index_ref, s32[1,512]{1,0:T(1,128)S(1)} %get-tuple-element.31.slot_ref, bf16[512,512]{1,0:T(8,128)(2,1)S(1)} %get-tuple-element.32.rows_ref, ...), custom_call_target="tpu_custom_call" | custom-call | flops 1 | bytes 1 | tf_op jit(solution)/shard_map/next_pack/pallas_call | solution.py:335
  7.8 1.6 %collective-permute-start.4 = (bf16[528,128]{1,0:T(8,128)(2,1)}, bf16[528,128]{1,0:T(8,128)(2,1)S(1)}, u32[]{:S(2)}, u32[]{:S(2)}) collective-permute-start(bf16[528,128]{1,0:T(8,128)(2,1)} %get-tuple-element.41), channel_id=1, source_target_pairs={{0,2},{1,3},{2,0},{3,1},{4,6},{5,7},{6,4},{7,5},{8,10},{9,11},{10,... | collective-permute-start | bytes 405512 | tf_op jit(solution)/shard_map/ppermute | solution.py:306
  9.3 0.0 collective-permute-start.5
  9.3 0.2 collective-permute-start.6
  9.5 0.0 collective-permute-done.refs_1_
  9.5 0.7 %copy-done.1 = s32[256]{0:T(256)S(1)} copy-done((s32[256]{0:T(256)S(1)}, s32[256]{0:T(256)}, u32[]{:S(2)}) %copy-start.1) | copy-done | bytes 1048
  10.2 6.3 %first_score.1 = (bf16[256,32,512]{2,1,0:T(8,128)(2,1)S(1)}, f32[256,128]{1,0:T(8,128)S(1)}, f32[256,512]{1,0:T(8,128)S(1)}, f32[1,128]{1,0:T(1,128)S(1)}, f32[1,128]{1,0:T(1,128)S(1)}) custom-call(bf16[256,32,512]{2,1,0:T(8,128)(2,1)} %bank_ref.1, s32[1,256]{1,0:T(1,128)S(1)} %bitcast.11, bf16[528,128]{1,0:T(8,128)(2,1)S(1)} %get-tuple-element.34.refs_0_, ...), custom_call_target="tpu_custom_call" | custom-call | flops 1 | bytes 1 | tf_op jit(solution)/shard_map/first_score/pallas_call | solution.py:335
  16.5 0.3 late_pack.1
  16.9 4.0 %collective-permute-start.1 = (bf16[528,128]{1,0:T(8,128)(2,1)S(1)}, bf16[528,128]{1,0:T(8,128)(2,1)S(1)}, u32[]{:S(2)}, u32[]{:S(2)}) collective-permute-start(bf16[528,128]{1,0:T(8,128)(2,1)S(1)} %get-tuple-element.39), channel_id=1, source_target_pairs={{0,6},{1,7},{2,4},{3,5},{4,2},{5,3},{6,0},{7,1},{8,14},{9,15},{10,... | collective-permute-start | bytes 405512 | tf_op jit(solution)/shard_map/ppermute | solution.py:306
  20.8 0.0 collective-permute-done.3.refs_0_
  20.8 0.0 collective-permute-start.2
  20.8 0.0 collective-permute-done.4.refs_1_
  20.8 0.0 copy-start.2
  20.9 2.9 %score.2 = (f32[1,128]{1,0:T(1,128)S(1)}, f32[1,128]{1,0:T(1,128)S(1)}, f32[256,512]{1,0:T(8,128)S(1)}) custom-call(bf16[256,32,512]{2,1,0:T(8,128)(2,1)S(1)} %get-tuple-element.36.bank_ref, f32[256,128]{1,0:T(8,128)S(1)} %get-tuple-element.37.norm_ref, s32[1,256]{1,0:T(1,128)S(1)} %bitcast.12, f32[256,512]{1,0:T(8,128)S(1)} %get-tuple-element.38.after_ref.before_ref, ...), custom_call_target="tpu_custom_call" | custom-call | flops 1 | bytes 1 | tf_op jit(solution)/shard_map/score/pallas_call | solution.py:335
  23.8 0.0 collective-permute-done.5.refs_0_
  23.8 0.0 collective-permute-done.6.refs_1_
  23.8 0.0 copy-start
  23.8 2.9 %score.3 = (f32[1,128]{1,0:T(1,128)S(1)}, f32[1,128]{1,0:T(1,128)S(1)}, f32[256,512]{1,0:T(8,128)S(1)}) custom-call(bf16[256,32,512]{2,1,0:T(8,128)(2,1)S(1)} %get-tuple-element.36.bank_ref, f32[256,128]{1,0:T(8,128)S(1)} %get-tuple-element.37.norm_ref, s32[1,256]{1,0:T(1,128)S(1)} %bitcast.13, f32[256,512]{1,0:T(8,128)S(1)} %get-tuple-element.42.before_ref, ...), custom_call_target="tpu_custom_call" | custom-call | flops 1 | bytes 1 | tf_op jit(solution)/shard_map/score/pallas_call | solution.py:335
  26.7 0.0 collective-permute-done.1.refs_0_
  26.7 1.7 %collective-permute-done.2.refs_1_ = bf16[528,128]{1,0:T(8,128)(2,1)S(1)} collective-permute-done((bf16[528,128]{1,0:T(8,128)(2,1)S(1)}, bf16[528,128]{1,0:T(8,128)(2,1)S(1)}, u32[]{:S(2)}, u32[]{:S(2)}) %collective-permute-start.2) | collective-permute-done | bytes 135200 | tf_op jit(solution)/shard_map/ppermute | solution.py:306
  28.4 0.4 last_sum.1
  28.8 1.6 %collective-permute-start.9 = (bf16[256,512]{1,0:T(8,128)(2,1)S(1)}, bf16[256,512]{1,0:T(8,128)(2,1)S(1)}, u32[]{:S(2)}, u32[]{:S(2)}) collective-permute-start(bf16[256,512]{1,0:T(8,128)(2,1)S(1)} %get-tuple-element.55), channel_id=1, source_target_pairs={{0,16},{8,24},{16,0},{24,8},{1,17},{9,25},{17,1},{25,9},{2,18},{10... | collective-permute-start | bytes 786440 | tf_op jit(solution)/shard_map/ppermute | solution.py:306
  30.4 1.5 %collective-permute-start.8 = (bf16[256,512]{1,0:T(8,128)(2,1)S(1)}, bf16[256,512]{1,0:T(8,128)(2,1)S(1)}, u32[]{:S(2)}, u32[]{:S(2)}) collective-permute-start(bf16[256,512]{1,0:T(8,128)(2,1)S(1)} %get-tuple-element.55), channel_id=1, source_target_pairs={{0,8},{8,0},{16,24},{24,16},{1,9},{9,1},{17,25},{25,17},{2,10},{10... | collective-permute-start | bytes 786440 | tf_op jit(solution)/shard_map/ppermute | solution.py:306
  31.9 0.5 collective-permute-start.7
  32.4 2.6 %last_score.1 = f32[8,128]{1,0:T(8,128)S(1)} custom-call(s32[1]{0:T(128)} %bitcast.me_ref, bf16[256,32,512]{2,1,0:T(8,128)(2,1)S(1)} %get-tuple-element.36.bank_ref, f32[256,128]{1,0:T(8,128)S(1)} %get-tuple-element.37.norm_ref, s32[1,256]{1,0:T(1,128)S(1)} %bitcast.14, bf16[512,256]{1,0:T(8,128)(2,1)S(1)} %get-tuple-element.46.columns_ref, ...), custom_call_target="tpu_custom_call" | custom-call | flops 1 | bytes 1 | tf_op jit(solution)/shard_map/last_score/pallas_call | solution.py:335
  34.9 11.2 %all_to_all.11 = f32[8,1,128]{2,1,0:T(1,128)S(1)} all-to-all(f32[8,1,128]{2,1,0:T(1,128)S(1)} %bitcast.9), channel_id=1, replica_groups=mesh['grp'=4,'own'=8] {'own'}, dimensions={0} | all-to-all | bytes 8192 | tf_op jit(solution)/shard_map/all_to_all | solution.py:433
  46.1 0.8 %unpack.1 = f32[1,512]{1,0:T(1,128)} custom-call(s32[1,512]{1,0:T(1,128)S(1)} %get-tuple-element.29.index_ref, f32[8,128]{1,0:T(8,128)S(1)} %bitcast.10), custom_call_target="tpu_custom_call" | custom-call | flops 1 | bytes 1 | tf_op jit(solution)/shard_map/unpack/pallas_call | solution.py:335
  46.9 0.0 collective-permute-done.9.refs_2_
  47.0 1.0 %finish.1 = f32[256,512]{1,0:T(8,128)} custom-call(f32[256,512]{1,0:T(8,128)S(1)} %copy-done, f32[256,512]{1,0:T(8,128)S(1)} %get-tuple-element.54.own_ref, bf16[256,512]{1,0:T(8,128)(2,1)S(1)} %collective-permute-done.7.refs_0_, bf16[256,512]{1,0:T(8,128)(2,1)S(1)} %collective-permute-done.8.refs_1_, bf16[256,512]{1,0:T(8,128)(2,1)S(1)} %collective-permute-done.9.refs_2_), custom_call_target="tpu_custom_call" | custom-call | flops 1 | bytes 1 | tf_op jit(solution)/shard_map/finish/pallas_call | solution.py:335
  (5 shorter events, 0.0 us)
Async XLA Ops:
  2.3 7.2 %collective-permute-start = (bf16[528,128]{1,0:T(8,128)(2,1)S(1)}, bf16[528,128]{1,0:T(8,128)(2,1)S(1)}, u32[]{:S(2)}, u32[]{:S(2)}) collective-permute-start(bf16[528,128]{1,0:T(8,128)(2,1)S(1)} %get-tuple-element.35), channel_id=1, source_target_pairs={{0,1},{1,0},{2,3},{3,2},{4,5},{5,4},{6,7},{7,6},{8,9},{9,8},{10,11... | collective-permute-start | bytes 405512 | tf_op jit(solution)/shard_map/ppermute | solution.py:306
  2.8 18.0 %collective-permute-start.3 = (bf16[528,128]{1,0:T(8,128)(2,1)S(1)}, bf16[528,128]{1,0:T(8,128)(2,1)S(1)}, u32[]{:S(2)}, u32[]{:S(2)}) collective-permute-start(bf16[528,128]{1,0:T(8,128)(2,1)S(1)} %get-tuple-element.33.after_ref), channel_id=1, source_target_pairs={{0,4},{1,5},{2,6},{3,7},{4,0},{5,1},{6,2},{7,3},{8,12},{9,13},{10,... | collective-permute-start | bytes 405512 | tf_op jit(solution)/shard_map/ppermute | solution.py:306
  7.8 13.1 %collective-permute-start.4 = (bf16[528,128]{1,0:T(8,128)(2,1)}, bf16[528,128]{1,0:T(8,128)(2,1)S(1)}, u32[]{:S(2)}, u32[]{:S(2)}) collective-permute-start(bf16[528,128]{1,0:T(8,128)(2,1)} %get-tuple-element.41), channel_id=1, source_target_pairs={{0,2},{1,3},{2,0},{3,1},{4,6},{5,7},{6,4},{7,5},{8,10},{9,11},{10,... | collective-permute-start | bytes 405512 | tf_op jit(solution)/shard_map/ppermute | solution.py:306
  9.3 14.5 %collective-permute-start.5 = (bf16[528,128]{1,0:T(8,128)(2,1)S(1)}, bf16[528,128]{1,0:T(8,128)(2,1)S(1)}, u32[]{:S(2)}, u32[]{:S(2)}) collective-permute-start(bf16[528,128]{1,0:T(8,128)(2,1)S(1)} %get-tuple-element.43), channel_id=1, source_target_pairs={{0,5},{1,4},{2,7},{3,6},{4,1},{5,0},{6,3},{7,2},{8,13},{9,12},{10,... | collective-permute-start | bytes 405512 | tf_op jit(solution)/shard_map/ppermute | solution.py:306
  9.3 14.5 %collective-permute-start.6 = (bf16[528,128]{1,0:T(8,128)(2,1)}, bf16[528,128]{1,0:T(8,128)(2,1)S(1)}, u32[]{:S(2)}, u32[]{:S(2)}) collective-permute-start(bf16[528,128]{1,0:T(8,128)(2,1)} %get-tuple-element.44), channel_id=1, source_target_pairs={{0,3},{1,2},{2,1},{3,0},{4,7},{5,6},{6,5},{7,4},{8,11},{9,10},{10,... | collective-permute-start | bytes 405512 | tf_op jit(solution)/shard_map/ppermute | solution.py:306
  9.5 0.7 %copy-start.1 = (s32[256]{0:T(256)S(1)}, s32[256]{0:T(256)}, u32[]{:S(2)}) copy-start(s32[256]{0:T(256)} %param.10) | copy-start | bytes 3076
  16.9 9.9 %collective-permute-start.1 = (bf16[528,128]{1,0:T(8,128)(2,1)S(1)}, bf16[528,128]{1,0:T(8,128)(2,1)S(1)}, u32[]{:S(2)}, u32[]{:S(2)}) collective-permute-start(bf16[528,128]{1,0:T(8,128)(2,1)S(1)} %get-tuple-element.39), channel_id=1, source_target_pairs={{0,6},{1,7},{2,4},{3,5},{4,2},{5,3},{6,0},{7,1},{8,14},{9,15},{10,... | collective-permute-start | bytes 405512 | tf_op jit(solution)/shard_map/ppermute | solution.py:306
  20.8 7.6 %collective-permute-start.2 = (bf16[528,128]{1,0:T(8,128)(2,1)S(1)}, bf16[528,128]{1,0:T(8,128)(2,1)S(1)}, u32[]{:S(2)}, u32[]{:S(2)}) collective-permute-start(bf16[528,128]{1,0:T(8,128)(2,1)S(1)} %get-tuple-element.40), channel_id=1, source_target_pairs={{0,7},{1,6},{2,5},{3,4},{4,3},{5,2},{6,1},{7,0},{8,15},{9,14},{10,... | collective-permute-start | bytes 405512 | tf_op jit(solution)/shard_map/ppermute | solution.py:306
  20.8 11.5 %copy-start.2 = (s32[256]{0:T(256)S(1)}, s32[256]{0:T(256)}, u32[]{:S(2)}) copy-start(s32[256]{0:T(256)} %param.10) | copy-start | bytes 3076
  23.8 23.1 %copy-start = (f32[256,512]{1,0:T(8,128)S(1)}, f32[256,512]{1,0:T(8,128)}, u32[]{:S(2)}) copy-start(f32[256,512]{1,0:T(8,128)} %stored_ref.1) | copy-start | bytes 1572868
  28.8 18.1 %collective-permute-start.9 = (bf16[256,512]{1,0:T(8,128)(2,1)S(1)}, bf16[256,512]{1,0:T(8,128)(2,1)S(1)}, u32[]{:S(2)}, u32[]{:S(2)}) collective-permute-start(bf16[256,512]{1,0:T(8,128)(2,1)S(1)} %get-tuple-element.55), channel_id=1, source_target_pairs={{0,16},{8,24},{16,0},{24,8},{1,17},{9,25},{17,1},{25,9},{2,18},{10... | collective-permute-start | bytes 786440 | tf_op jit(solution)/shard_map/ppermute | solution.py:306
  30.4 16.5 %collective-permute-start.8 = (bf16[256,512]{1,0:T(8,128)(2,1)S(1)}, bf16[256,512]{1,0:T(8,128)(2,1)S(1)}, u32[]{:S(2)}, u32[]{:S(2)}) collective-permute-start(bf16[256,512]{1,0:T(8,128)(2,1)S(1)} %get-tuple-element.55), channel_id=1, source_target_pairs={{0,8},{8,0},{16,24},{24,16},{1,9},{9,1},{17,25},{25,17},{2,10},{10... | collective-permute-start | bytes 786440 | tf_op jit(solution)/shard_map/ppermute | solution.py:306
  31.9 15.0 %collective-permute-start.7 = (bf16[256,512]{1,0:T(8,128)(2,1)S(1)}, bf16[256,512]{1,0:T(8,128)(2,1)S(1)}, u32[]{:S(2)}, u32[]{:S(2)}) collective-permute-start(bf16[256,512]{1,0:T(8,128)(2,1)S(1)} %get-tuple-element.55), channel_id=1, source_target_pairs={{0,24},{8,16},{16,8},{24,0},{1,25},{9,17},{17,9},{25,1},{2,26},{10... | collective-permute-start | bytes 786440 | tf_op jit(solution)/shard_map/ppermute | solution.py:306

commit v16 on v14

--- a/solution.py
+++ b/solution.py
@@ -236,7 +236,7 @@
 
 
 def last_sum_kernel(messages, capacity, *refs):
-    message_refs, before_ref, total_ref, sent_ref, columns_ref, slots_ref = (
+    message_refs, before_ref, total_ref, sent_ref, far_ref, columns_ref, slots_ref = (
         refs[:messages], *refs[messages:]
     )
     clusters, width = total_ref.shape
@@ -248,6 +248,7 @@
     )
     total_ref[...] = total
     sent_ref[...] = total.astype(sent_ref.dtype)
+    far_ref[...] = total.astype(far_ref.dtype)
 
 
 def last_score_kernel(
@@ -408,18 +409,22 @@
         )
         best += found
     last_messages = [got[peer] for peer in last]
-    total, sent, columns, column_slots = vmem_call(
+    total, sent, sent_far, columns, column_slots = vmem_call(
         functools.partial(last_sum_kernel, quarter, capacity),
         "last_sum",
         [
             sums,
             jax.ShapeDtypeStruct((clusters, width), jnp.bfloat16),
+            pltpu.HBM((clusters, width), jnp.bfloat16),
             jax.ShapeDtypeStruct((width, len(last) * capacity), jnp.bfloat16),
             jax.ShapeDtypeStruct((1, len(last) * capacity), jnp.int32),
         ],
         [*last_messages, total],
     )
-    terms = [exchange(sent, "grp", offset) for offset in range(1, parts)][::-1]
+    terms = [
+        exchange(sent if offset.bit_count() == 1 else sent_far, "grp", offset)
+        for offset in range(1, parts)
+    ][::-1]
     best = vmem_call(
         functools.partial(
             last_score_kernel, sum(groups, []), capacity, block

time: 48.2 us -> 48.8 us (1.012)
  Pallas kernels: 20.2 us -> 20.9 us
    pallas_call x10, Pallas kernels: 20.2 us -> 20.9 us  [vmem_call(): pl.pallas_call(kernel, out_shape=out_shape, in_specs=in_specs or [whole_v...]
  transfers between devices with their start and end apart: 10 -> 10, of which waited for: 1 -> 1; matrix products, arithmetic and copies ran while one was open for 0% -> 0% of each run, Pallas kernels for 36% -> 35%
where the time goes in v16:
time: 48.8 us; the launch traced here: 48.6 us
  Pallas kernels  20.9 us (43%)
  starting transfers between devices  13.4 us (27%)
  blocking collectives  11.1 us (23%)
  waiting for transfers between devices  1.69 us (3%)
  between operations  0.72 us (1%)
  local copies, waits for them, and re-layouts  0.69 us (1%)
    pallas_call x10, Pallas kernels, vmem_call(): pl.pallas_call(kernel, out_shape=out_shape, in_specs=in_specs or [whole_v...  20.9 us
    ppermute x10, starting transfers between devices, exchange(): lax.ppermute(value, axis, [(device, device ^ offset) for device in range(...  13.4 us
    all_to_all x1, blocking collectives, body(): lax.all_to_all(best, 'own', split_axis=0, concat_axis=0, tiled=True)  11.1 us
    ppermute x10, waiting for transfers between devices, exchange(): lax.ppermute(value, axis, [(device, device ^ offset) for device in range(...  1.69 us
  transfers between devices with their start and end apart: 10, of which 1 were waited for; matrix products, arithmetic and copies ran while one was open for 0% of the time, Pallas kernels for 35%

profile of v16, /device:TPU:0, one launch (start us, length us, event | category | flops | bytes accessed | tf_op | source)
XLA Modules:
  0.0 48.6 jit_solution(8941477802853278076)
XLA Ops:
  0.6 1.7 %pack.1 = (s32[1,512]{1,0:T(1,128)S(1)}, s32[1,512]{1,0:T(1,128)S(1)}, s32[1,512]{1,0:T(1,128)}, s32[1,512]{1,0:T(1,128)S(1)}, bf16[512,512]{1,0:T(8,128)(2,1)S(...) custom-call(s32[1]{0:T(128)} %bitcast.me_ref, s32[1,512]{1,0:T(1,128)} %bitcast.15, s32[1,512]{1,0:T(1,128)} %bitcast.16, ...), custom_call_target="tpu_custom_call" | custom-call | flops 1 | bytes 1 | tf_op jit(solution)/shard_map/pack/pallas_call | solution.py:336
  2.3 0.5 %collective-permute-start = (bf16[528,128]{1,0:T(8,128)(2,1)S(1)}, bf16[528,128]{1,0:T(8,128)(2,1)S(1)}, u32[]{:S(2)}, u32[]{:S(2)}) collective-permute-start(bf16[528,128]{1,0:T(8,128)(2,1)S(1)} %get-tuple-element.36), channel_id=1, source_target_pairs={{0,1},{1,0},{2,3},{3,2},{4,5},{5,4},{6,7},{7,6},{8,9},{9,8},{10,11... | collective-permute-start | bytes 405512 | tf_op jit(solution)/shard_map/ppermute | solution.py:307
  2.8 3.7 %collective-permute-start.3 = (bf16[528,128]{1,0:T(8,128)(2,1)S(1)}, bf16[528,128]{1,0:T(8,128)(2,1)S(1)}, u32[]{:S(2)}, u32[]{:S(2)}) collective-permute-start(bf16[528,128]{1,0:T(8,128)(2,1)S(1)} %get-tuple-element.34.after_ref), channel_id=1, source_target_pairs={{0,4},{1,5},{2,6},{3,7},{4,0},{5,1},{6,2},{7,3},{8,12},{9,13},{10,... | collective-permute-start | bytes 405512 | tf_op jit(solution)/shard_map/ppermute | solution.py:307
  6.5 1.2 %next_pack.1 = (bf16[528,128]{1,0:T(8,128)(2,1)S(1)}, bf16[528,128]{1,0:T(8,128)(2,1)}, bf16[528,128]{1,0:T(8,128)(2,1)S(1)}, bf16[528,128]{1,0:T(8,128)(2,1)}) custom-call(s32[1,512]{1,0:T(1,128)S(1)} %get-tuple-element.31.index_ref, s32[1,512]{1,0:T(1,128)S(1)} %get-tuple-element.32.slot_ref, bf16[512,512]{1,0:T(8,128)(2,1)S(1)} %get-tuple-element.33.rows_ref, ...), custom_call_target="tpu_custom_call" | custom-call | flops 1 | bytes 1 | tf_op jit(solution)/shard_map/next_pack/pallas_call | solution.py:336
  7.8 1.6 %collective-permute-start.4 = (bf16[528,128]{1,0:T(8,128)(2,1)}, bf16[528,128]{1,0:T(8,128)(2,1)S(1)}, u32[]{:S(2)}, u32[]{:S(2)}) collective-permute-start(bf16[528,128]{1,0:T(8,128)(2,1)} %get-tuple-element.42), channel_id=1, source_target_pairs={{0,2},{1,3},{2,0},{3,1},{4,6},{5,7},{6,4},{7,5},{8,10},{9,11},{10,... | collective-permute-start | bytes 405512 | tf_op jit(solution)/shard_map/ppermute | solution.py:307
  9.3 0.0 collective-permute-start.5
  9.3 0.2 collective-permute-start.6
  9.5 0.0 collective-permute-done.refs_1_
  9.5 0.7 %copy-done.1 = s32[256]{0:T(256)S(1)} copy-done((s32[256]{0:T(256)S(1)}, s32[256]{0:T(256)}, u32[]{:S(2)}) %copy-start.1) | copy-done | bytes 1048
  10.2 6.3 %first_score.1 = (bf16[256,32,512]{2,1,0:T(8,128)(2,1)S(1)}, f32[256,128]{1,0:T(8,128)S(1)}, f32[256,512]{1,0:T(8,128)S(1)}, f32[1,128]{1,0:T(1,128)S(1)}, f32[1,128]{1,0:T(1,128)S(1)}) custom-call(bf16[256,32,512]{2,1,0:T(8,128)(2,1)} %bank_ref.1, s32[1,256]{1,0:T(1,128)S(1)} %bitcast.11, bf16[528,128]{1,0:T(8,128)(2,1)S(1)} %get-tuple-element.35.refs_0_, ...), custom_call_target="tpu_custom_call" | custom-call | flops 1 | bytes 1 | tf_op jit(solution)/shard_map/first_score/pallas_call | solution.py:336
  16.5 0.3 late_pack.1
  16.9 4.0 %collective-permute-start.1 = (bf16[528,128]{1,0:T(8,128)(2,1)S(1)}, bf16[528,128]{1,0:T(8,128)(2,1)S(1)}, u32[]{:S(2)}, u32[]{:S(2)}) collective-permute-start(bf16[528,128]{1,0:T(8,128)(2,1)S(1)} %get-tuple-element.40), channel_id=1, source_target_pairs={{0,6},{1,7},{2,4},{3,5},{4,2},{5,3},{6,0},{7,1},{8,14},{9,15},{10,... | collective-permute-start | bytes 405512 | tf_op jit(solution)/shard_map/ppermute | solution.py:307
  20.8 0.0 collective-permute-done.3.refs_0_
  20.8 0.0 collective-permute-start.2
  20.8 0.0 collective-permute-done.4.refs_1_
  20.8 0.0 copy-start.2
  20.9 2.9 %score.2 = (f32[1,128]{1,0:T(1,128)S(1)}, f32[1,128]{1,0:T(1,128)S(1)}, f32[256,512]{1,0:T(8,128)S(1)}) custom-call(bf16[256,32,512]{2,1,0:T(8,128)(2,1)S(1)} %get-tuple-element.37.bank_ref, f32[256,128]{1,0:T(8,128)S(1)} %get-tuple-element.38.norm_ref, s32[1,256]{1,0:T(1,128)S(1)} %bitcast.12, f32[256,512]{1,0:T(8,128)S(1)} %get-tuple-element.39.after_ref.before_ref, ...), custom_call_target="tpu_custom_call" | custom-call | flops 1 | bytes 1 | tf_op jit(solution)/shard_map/score/pallas_call | solution.py:336
  23.8 0.0 collective-permute-done.5.refs_0_
  23.8 0.0 copy-start
  23.8 2.9 %score.3 = (f32[1,128]{1,0:T(1,128)S(1)}, f32[1,128]{1,0:T(1,128)S(1)}, f32[256,512]{1,0:T(8,128)S(1)}) custom-call(bf16[256,32,512]{2,1,0:T(8,128)(2,1)S(1)} %get-tuple-element.37.bank_ref, f32[256,128]{1,0:T(8,128)S(1)} %get-tuple-element.38.norm_ref, s32[1,256]{1,0:T(1,128)S(1)} %bitcast.13, f32[256,512]{1,0:T(8,128)S(1)} %get-tuple-element.43.before_ref, ...), custom_call_target="tpu_custom_call" | custom-call | flops 1 | bytes 1 | tf_op jit(solution)/shard_map/score/pallas_call | solution.py:336
  26.7 1.7 %collective-permute-done.2.refs_1_ = bf16[528,128]{1,0:T(8,128)(2,1)S(1)} collective-permute-done((bf16[528,128]{1,0:T(8,128)(2,1)S(1)}, bf16[528,128]{1,0:T(8,128)(2,1)S(1)}, u32[]{:S(2)}, u32[]{:S(2)}) %collective-permute-start.2) | collective-permute-done | bytes 135200 | tf_op jit(solution)/shard_map/ppermute | solution.py:307
  28.4 1.1 %last_sum.1 = (f32[256,512]{1,0:T(8,128)S(1)}, bf16[256,512]{1,0:T(8,128)(2,1)S(1)}, bf16[256,512]{1,0:T(8,128)(2,1)}, bf16[512,256]{1,0:T(8,128)(2,1)S(1)}, s32[1,256]{1,0:T(1,128)S(1)}) custom-call(bf16[528,128]{1,0:T(8,128)(2,1)S(1)} %collective-permute-done.1.refs_0_, bf16[528,128]{1,0:T(8,128)(2,1)S(1)} %collective-permute-done.2.refs_1_, ...), custom_call_target="tpu_custom_call" | custom-call | flops 1 | bytes 1 | tf_op jit(solution)/shard_map/last_sum/pallas_call | solution.py:336
  29.5 2.5 %collective-permute-start.7 = (bf16[256,512]{1,0:T(8,128)(2,1)}, bf16[256,512]{1,0:T(8,128)(2,1)S(1)}, u32[]{:S(2)}, u32[]{:S(2)}) collective-permute-start(bf16[256,512]{1,0:T(8,128)(2,1)} %get-tuple-element.56), channel_id=1, source_target_pairs={{0,24},{8,16},{16,8},{24,0},{1,25},{9,17},{17,9},{25,1},{2,26},{10... | collective-permute-start | bytes 786440 | tf_op jit(solution)/shard_map/ppermute | solution.py:307
  32.0 0.5 %collective-permute-start.9 = (bf16[256,512]{1,0:T(8,128)(2,1)S(1)}, bf16[256,512]{1,0:T(8,128)(2,1)S(1)}, u32[]{:S(2)}, u32[]{:S(2)}) collective-permute-start(bf16[256,512]{1,0:T(8,128)(2,1)S(1)} %get-tuple-element.57), channel_id=1, source_target_pairs={{0,8},{8,0},{16,24},{24,16},{1,9},{9,1},{17,25},{25,17},{2,10},{10... | collective-permute-start | bytes 786440 | tf_op jit(solution)/shard_map/ppermute | solution.py:307
  32.5 0.5 %collective-permute-start.8 = (bf16[256,512]{1,0:T(8,128)(2,1)S(1)}, bf16[256,512]{1,0:T(8,128)(2,1)S(1)}, u32[]{:S(2)}, u32[]{:S(2)}) collective-permute-start(bf16[256,512]{1,0:T(8,128)(2,1)S(1)} %get-tuple-element.57), channel_id=1, source_target_pairs={{0,16},{8,24},{16,0},{24,8},{1,17},{9,25},{17,1},{25,9},{2,18},{10... | collective-permute-start | bytes 786440 | tf_op jit(solution)/shard_map/ppermute | solution.py:307
  33.0 2.6 %last_score.1 = f32[8,128]{1,0:T(8,128)S(1)} custom-call(s32[1]{0:T(128)} %bitcast.me_ref, bf16[256,32,512]{2,1,0:T(8,128)(2,1)S(1)} %get-tuple-element.37.bank_ref, f32[256,128]{1,0:T(8,128)S(1)} %get-tuple-element.38.norm_ref, s32[1,256]{1,0:T(1,128)S(1)} %bitcast.14, bf16[512,256]{1,0:T(8,128)(2,1)S(1)} %get-tuple-element.47.columns_ref, ...), custom_call_target="tpu_custom_call" | custom-call | flops 1 | bytes 1 | tf_op jit(solution)/shard_map/last_score/pallas_call | solution.py:336
  35.6 11.1 %all_to_all.11 = f32[8,1,128]{2,1,0:T(1,128)S(1)} all-to-all(f32[8,1,128]{2,1,0:T(1,128)S(1)} %bitcast.9), channel_id=1, replica_groups=mesh['grp'=4,'own'=8] {'own'}, dimensions={0} | all-to-all | bytes 8192 | tf_op jit(solution)/shard_map/all_to_all | solution.py:437
  46.7 0.8 %unpack.1 = f32[1,512]{1,0:T(1,128)} custom-call(s32[1,512]{1,0:T(1,128)S(1)} %get-tuple-element.30.index_ref, f32[8,128]{1,0:T(8,128)S(1)} %bitcast.10), custom_call_target="tpu_custom_call" | custom-call | flops 1 | bytes 1 | tf_op jit(solution)/shard_map/unpack/pallas_call | solution.py:336
  47.6 0.0 collective-permute-done.7.refs_0_
  47.6 0.0 collective-permute-done.9.refs_2_
  47.6 0.0 collective-permute-done.8.refs_1_
  47.6 1.0 %finish.1 = f32[256,512]{1,0:T(8,128)} custom-call(f32[256,512]{1,0:T(8,128)S(1)} %copy-done, f32[256,512]{1,0:T(8,128)S(1)} %get-tuple-element.55.own_ref, bf16[256,512]{1,0:T(8,128)(2,1)S(1)} %collective-permute-done.7.refs_0_, bf16[256,512]{1,0:T(8,128)(2,1)S(1)} %collective-permute-done.8.refs_1_, bf16[256,512]{1,0:T(8,128)(2,1)S(1)} %collective-permute-done.9.refs_2_), custom_call_target="tpu_custom_call" | custom-call | flops 1 | bytes 1 | tf_op jit(solution)/shard_map/finish/pallas_call | solution.py:336
  (5 shorter events, 0.0 us)
Async XLA Ops:
  2.3 7.2 %collective-permute-start = (bf16[528,128]{1,0:T(8,128)(2,1)S(1)}, bf16[528,128]{1,0:T(8,128)(2,1)S(1)}, u32[]{:S(2)}, u32[]{:S(2)}) collective-permute-start(bf16[528,128]{1,0:T(8,128)(2,1)S(1)} %get-tuple-element.36), channel_id=1, source_target_pairs={{0,1},{1,0},{2,3},{3,2},{4,5},{5,4},{6,7},{7,6},{8,9},{9,8},{10,11... | collective-permute-start | bytes 405512 | tf_op jit(solution)/shard_map/ppermute | solution.py:307
  2.8 18.0 %collective-permute-start.3 = (bf16[528,128]{1,0:T(8,128)(2,1)S(1)}, bf16[528,128]{1,0:T(8,128)(2,1)S(1)}, u32[]{:S(2)}, u32[]{:S(2)}) collective-permute-start(bf16[528,128]{1,0:T(8,128)(2,1)S(1)} %get-tuple-element.34.after_ref), channel_id=1, source_target_pairs={{0,4},{1,5},{2,6},{3,7},{4,0},{5,1},{6,2},{7,3},{8,12},{9,13},{10,... | collective-permute-start | bytes 405512 | tf_op jit(solution)/shard_map/ppermute | solution.py:307
  7.8 13.1 %collective-permute-start.4 = (bf16[528,128]{1,0:T(8,128)(2,1)}, bf16[528,128]{1,0:T(8,128)(2,1)S(1)}, u32[]{:S(2)}, u32[]{:S(2)}) collective-permute-start(bf16[528,128]{1,0:T(8,128)(2,1)} %get-tuple-element.42), channel_id=1, source_target_pairs={{0,2},{1,3},{2,0},{3,1},{4,6},{5,7},{6,4},{7,5},{8,10},{9,11},{10,... | collective-permute-start | bytes 405512 | tf_op jit(solution)/shard_map/ppermute | solution.py:307
  9.3 14.5 %collective-permute-start.5 = (bf16[528,128]{1,0:T(8,128)(2,1)S(1)}, bf16[528,128]{1,0:T(8,128)(2,1)S(1)}, u32[]{:S(2)}, u32[]{:S(2)}) collective-permute-start(bf16[528,128]{1,0:T(8,128)(2,1)S(1)} %get-tuple-element.44), channel_id=1, source_target_pairs={{0,5},{1,4},{2,7},{3,6},{4,1},{5,0},{6,3},{7,2},{8,13},{9,12},{10,... | collective-permute-start | bytes 405512 | tf_op jit(solution)/shard_map/ppermute | solution.py:307
  9.3 14.5 %collective-permute-start.6 = (bf16[528,128]{1,0:T(8,128)(2,1)}, bf16[528,128]{1,0:T(8,128)(2,1)S(1)}, u32[]{:S(2)}, u32[]{:S(2)}) collective-permute-start(bf16[528,128]{1,0:T(8,128)(2,1)} %get-tuple-element.45), channel_id=1, source_target_pairs={{0,3},{1,2},{2,1},{3,0},{4,7},{5,6},{6,5},{7,4},{8,11},{9,10},{10,... | collective-permute-start | bytes 405512 | tf_op jit(solution)/shard_map/ppermute | solution.py:307
  9.5 0.7 %copy-start.1 = (s32[256]{0:T(256)S(1)}, s32[256]{0:T(256)}, u32[]{:S(2)}) copy-start(s32[256]{0:T(256)} %param.10) | copy-start | bytes 3076
  16.9 9.9 %collective-permute-start.1 = (bf16[528,128]{1,0:T(8,128)(2,1)S(1)}, bf16[528,128]{1,0:T(8,128)(2,1)S(1)}, u32[]{:S(2)}, u32[]{:S(2)}) collective-permute-start(bf16[528,128]{1,0:T(8,128)(2,1)S(1)} %get-tuple-element.40), channel_id=1, source_target_pairs={{0,6},{1,7},{2,4},{3,5},{4,2},{5,3},{6,0},{7,1},{8,14},{9,15},{10,... | collective-permute-start | bytes 405512 | tf_op jit(solution)/shard_map/ppermute | solution.py:307
  20.8 7.6 %collective-permute-start.2 = (bf16[528,128]{1,0:T(8,128)(2,1)S(1)}, bf16[528,128]{1,0:T(8,128)(2,1)S(1)}, u32[]{:S(2)}, u32[]{:S(2)}) collective-permute-start(bf16[528,128]{1,0:T(8,128)(2,1)S(1)} %get-tuple-element.41), channel_id=1, source_target_pairs={{0,7},{1,6},{2,5},{3,4},{4,3},{5,2},{6,1},{7,0},{8,15},{9,14},{10,... | collective-permute-start | bytes 405512 | tf_op jit(solution)/shard_map/ppermute | solution.py:307
  20.8 12.2 %copy-start.2 = (s32[256]{0:T(256)S(1)}, s32[256]{0:T(256)}, u32[]{:S(2)}) copy-start(s32[256]{0:T(256)} %param.10) | copy-start | bytes 3076
  23.8 23.8 %copy-start = (f32[256,512]{1,0:T(8,128)S(1)}, f32[256,512]{1,0:T(8,128)}, u32[]{:S(2)}) copy-start(f32[256,512]{1,0:T(8,128)} %stored_ref.1) | copy-start | bytes 1572868
  29.5 18.1 %collective-permute-start.7 = (bf16[256,512]{1,0:T(8,128)(2,1)}, bf16[256,512]{1,0:T(8,128)(2,1)S(1)}, u32[]{:S(2)}, u32[]{:S(2)}) collective-permute-start(bf16[256,512]{1,0:T(8,128)(2,1)} %get-tuple-element.56), channel_id=1, source_target_pairs={{0,24},{8,16},{16,8},{24,0},{1,25},{9,17},{17,9},{25,1},{2,26},{10... | collective-permute-start | bytes 786440 | tf_op jit(solution)/shard_map/ppermute | solution.py:307
  32.0 15.6 %collective-permute-start.9 = (bf16[256,512]{1,0:T(8,128)(2,1)S(1)}, bf16[256,512]{1,0:T(8,128)(2,1)S(1)}, u32[]{:S(2)}, u32[]{:S(2)}) collective-permute-start(bf16[256,512]{1,0:T(8,128)(2,1)S(1)} %get-tuple-element.57), channel_id=1, source_target_pairs={{0,8},{8,0},{16,24},{24,16},{1,9},{9,1},{17,25},{25,17},{2,10},{10... | collective-permute-start | bytes 786440 | tf_op jit(solution)/shard_map/ppermute | solution.py:307
  32.5 15.1 %collective-permute-start.8 = (bf16[256,512]{1,0:T(8,128)(2,1)S(1)}, bf16[256,512]{1,0:T(8,128)(2,1)S(1)}, u32[]{:S(2)}, u32[]{:S(2)}) collective-permute-start(bf16[256,512]{1,0:T(8,128)(2,1)S(1)} %get-tuple-element.57), channel_id=1, source_target_pairs={{0,16},{8,24},{16,0},{24,8},{1,17},{9,25},{17,1},{25,9},{2,18},{10... | collective-permute-start | bytes 786440 | tf_op jit(solution)/shard_map/ppermute | solution.py:307

commit v17 on v10

--- a/solution.py
+++ b/solution.py
@@ -364,7 +364,7 @@
         functools.partial(late_pack_kernel, capacity, sent_next),
         "next_pack",
         [
-            pltpu.HBM(message.shape, message.dtype) if 0 < peer < half else message
+            pltpu.HBM(message.shape, message.dtype) if peer else message
             for peer in sent_next
         ],
         [index, slots, values, sent[0]],

time: 48.2 us -> 48.2 us (level)
  no operation moved by 1% of the time
where the time goes in v17:
time: 48.2 us; the launch traced here: 48 us
  Pallas kernels  20.2 us (42%)
  starting transfers between devices  13.5 us (28%)
  blocking collectives  11.2 us (23%)
  waiting for transfers between devices  1.68 us (3%)
  between operations  0.73 us (2%)
  local copies, waits for them, and re-layouts  0.69 us (1%)
    pallas_call x10, Pallas kernels, vmem_call(): pl.pallas_call(kernel, out_shape=out_shape, in_specs=in_specs or [whole_v...  20.2 us
    ppermute x10, starting transfers between devices, exchange(): lax.ppermute(value, axis, [(device, device ^ offset) for device in range(...  13.5 us
    all_to_all x1, blocking collectives, body(): lax.all_to_all(best, 'own', split_axis=0, concat_axis=0, tiled=True)  11.2 us
    ppermute x10, waiting for transfers between devices, exchange(): lax.ppermute(value, axis, [(device, device ^ offset) for device in range(...  1.68 us
  transfers between devices with their start and end apart: 10, of which 1 were waited for; matrix products, arithmetic and copies ran while one was open for 0% of the time, Pallas kernels for 36%

profile of v17, /device:TPU:0, one launch (start us, length us, event | category | flops | bytes accessed | tf_op | source)
XLA Modules:
  0.0 48.0 jit_solution(17926890083608554204)
XLA Ops:
  0.6 1.7 %pack.1 = (s32[1,512]{1,0:T(1,128)S(1)}, s32[1,512]{1,0:T(1,128)S(1)}, s32[1,512]{1,0:T(1,128)}, s32[1,512]{1,0:T(1,128)S(1)}, bf16[512,512]{1,0:T(8,128)(2,1)S(...) custom-call(s32[1]{0:T(128)} %bitcast.me_ref, s32[1,512]{1,0:T(1,128)} %bitcast.15, s32[1,512]{1,0:T(1,128)} %bitcast.16, ...), custom_call_target="tpu_custom_call" | custom-call | flops 1 | bytes 1 | tf_op jit(solution)/shard_map/pack/pallas_call | solution.py:335
  2.3 0.5 %collective-permute-start = (bf16[528,128]{1,0:T(8,128)(2,1)S(1)}, bf16[528,128]{1,0:T(8,128)(2,1)S(1)}, u32[]{:S(2)}, u32[]{:S(2)}) collective-permute-start(bf16[528,128]{1,0:T(8,128)(2,1)S(1)} %get-tuple-element.35), channel_id=1, source_target_pairs={{0,1},{1,0},{2,3},{3,2},{4,5},{5,4},{6,7},{7,6},{8,9},{9,8},{10,11... | collective-permute-start | bytes 405512 | tf_op jit(solution)/shard_map/ppermute | solution.py:306
  2.8 3.7 %collective-permute-start.3 = (bf16[528,128]{1,0:T(8,128)(2,1)S(1)}, bf16[528,128]{1,0:T(8,128)(2,1)S(1)}, u32[]{:S(2)}, u32[]{:S(2)}) collective-permute-start(bf16[528,128]{1,0:T(8,128)(2,1)S(1)} %get-tuple-element.33.after_ref), channel_id=1, source_target_pairs={{0,4},{1,5},{2,6},{3,7},{4,0},{5,1},{6,2},{7,3},{8,12},{9,13},{10,... | collective-permute-start | bytes 405512 | tf_op jit(solution)/shard_map/ppermute | solution.py:306
  6.5 1.3 %next_pack.1 = (bf16[528,128]{1,0:T(8,128)(2,1)S(1)}, bf16[528,128]{1,0:T(8,128)(2,1)}, bf16[528,128]{1,0:T(8,128)(2,1)}, bf16[528,128]{1,0:T(8,128)(2,1)}) custom-call(s32[1,512]{1,0:T(1,128)S(1)} %get-tuple-element.30.index_ref, s32[1,512]{1,0:T(1,128)S(1)} %get-tuple-element.31.slot_ref, bf16[512,512]{1,0:T(8,128)(2,1)S(1)} %get-tuple-element.32.rows_ref, ...), custom_call_target="tpu_custom_call" | custom-call | flops 1 | bytes 1 | tf_op jit(solution)/shard_map/next_pack/pallas_call | solution.py:335
  7.8 1.6 %collective-permute-start.4 = (bf16[528,128]{1,0:T(8,128)(2,1)}, bf16[528,128]{1,0:T(8,128)(2,1)S(1)}, u32[]{:S(2)}, u32[]{:S(2)}) collective-permute-start(bf16[528,128]{1,0:T(8,128)(2,1)} %get-tuple-element.41), channel_id=1, source_target_pairs={{0,2},{1,3},{2,0},{3,1},{4,6},{5,7},{6,4},{7,5},{8,10},{9,11},{10,... | collective-permute-start | bytes 405512 | tf_op jit(solution)/shard_map/ppermute | solution.py:306
  9.3 0.0 collective-permute-start.5
  9.3 0.2 collective-permute-start.6
  9.5 0.0 collective-permute-done.refs_1_
  9.5 0.7 %copy-done.1 = s32[256]{0:T(256)S(1)} copy-done((s32[256]{0:T(256)S(1)}, s32[256]{0:T(256)}, u32[]{:S(2)}) %copy-start.1) | copy-done | bytes 1048
  10.2 6.3 %first_score.1 = (bf16[256,32,512]{2,1,0:T(8,128)(2,1)S(1)}, f32[256,128]{1,0:T(8,128)S(1)}, f32[256,512]{1,0:T(8,128)S(1)}, f32[1,128]{1,0:T(1,128)S(1)}, f32[1,128]{1,0:T(1,128)S(1)}) custom-call(bf16[256,32,512]{2,1,0:T(8,128)(2,1)} %bank_ref.1, s32[1,256]{1,0:T(1,128)S(1)} %bitcast.11, bf16[528,128]{1,0:T(8,128)(2,1)S(1)} %get-tuple-element.34.refs_0_, ...), custom_call_target="tpu_custom_call" | custom-call | flops 1 | bytes 1 | tf_op jit(solution)/shard_map/first_score/pallas_call | solution.py:335
  16.6 0.3 late_pack.1
  16.9 4.0 %collective-permute-start.1 = (bf16[528,128]{1,0:T(8,128)(2,1)S(1)}, bf16[528,128]{1,0:T(8,128)(2,1)S(1)}, u32[]{:S(2)}, u32[]{:S(2)}) collective-permute-start(bf16[528,128]{1,0:T(8,128)(2,1)S(1)} %get-tuple-element.39), channel_id=1, source_target_pairs={{0,6},{1,7},{2,4},{3,5},{4,2},{5,3},{6,0},{7,1},{8,14},{9,15},{10,... | collective-permute-start | bytes 405512 | tf_op jit(solution)/shard_map/ppermute | solution.py:306
  20.9 0.0 collective-permute-done.3.refs_0_
  20.9 0.0 collective-permute-start.2
  20.9 0.0 collective-permute-done.4.refs_1_
  20.9 0.0 copy-start.2
  20.9 2.9 %score.2 = (f32[1,128]{1,0:T(1,128)S(1)}, f32[1,128]{1,0:T(1,128)S(1)}, f32[256,512]{1,0:T(8,128)S(1)}) custom-call(bf16[256,32,512]{2,1,0:T(8,128)(2,1)S(1)} %get-tuple-element.36.bank_ref, f32[256,128]{1,0:T(8,128)S(1)} %get-tuple-element.37.norm_ref, s32[1,256]{1,0:T(1,128)S(1)} %bitcast.12, f32[256,512]{1,0:T(8,128)S(1)} %get-tuple-element.38.after_ref.before_ref, ...), custom_call_target="tpu_custom_call" | custom-call | flops 1 | bytes 1 | tf_op jit(solution)/shard_map/score/pallas_call | solution.py:335
  23.8 0.0 collective-permute-done.5.refs_0_
  23.8 0.0 collective-permute-done.6.refs_1_
  23.8 0.0 copy-start
  23.8 2.9 %score.3 = (f32[1,128]{1,0:T(1,128)S(1)}, f32[1,128]{1,0:T(1,128)S(1)}, f32[256,512]{1,0:T(8,128)S(1)}) custom-call(bf16[256,32,512]{2,1,0:T(8,128)(2,1)S(1)} %get-tuple-element.36.bank_ref, f32[256,128]{1,0:T(8,128)S(1)} %get-tuple-element.37.norm_ref, s32[1,256]{1,0:T(1,128)S(1)} %bitcast.13, f32[256,512]{1,0:T(8,128)S(1)} %get-tuple-element.42.before_ref, ...), custom_call_target="tpu_custom_call" | custom-call | flops 1 | bytes 1 | tf_op jit(solution)/shard_map/score/pallas_call | solution.py:335
  26.8 0.0 collective-permute-done.1.refs_0_
  26.8 1.7 %collective-permute-done.2.refs_1_ = bf16[528,128]{1,0:T(8,128)(2,1)S(1)} collective-permute-done((bf16[528,128]{1,0:T(8,128)(2,1)S(1)}, bf16[528,128]{1,0:T(8,128)(2,1)S(1)}, u32[]{:S(2)}, u32[]{:S(2)}) %collective-permute-start.2) | collective-permute-done | bytes 135200 | tf_op jit(solution)/shard_map/ppermute | solution.py:306
  28.4 0.4 last_sum.1
  28.8 2.5 %collective-permute-start.9 = (bf16[256,512]{1,0:T(8,128)(2,1)S(1)}, bf16[256,512]{1,0:T(8,128)(2,1)S(1)}, u32[]{:S(2)}, u32[]{:S(2)}) collective-permute-start(bf16[256,512]{1,0:T(8,128)(2,1)S(1)} %get-tuple-element.55), channel_id=1, source_target_pairs={{0,24},{8,16},{16,8},{24,0},{1,25},{9,17},{17,9},{25,1},{2,26},{10... | collective-permute-start | bytes 786440 | tf_op jit(solution)/shard_map/ppermute | solution.py:306
  31.3 0.5 %collective-permute-start.8 = (bf16[256,512]{1,0:T(8,128)(2,1)S(1)}, bf16[256,512]{1,0:T(8,128)(2,1)S(1)}, u32[]{:S(2)}, u32[]{:S(2)}) collective-permute-start(bf16[256,512]{1,0:T(8,128)(2,1)S(1)} %get-tuple-element.55), channel_id=1, source_target_pairs={{0,16},{8,24},{16,0},{24,8},{1,17},{9,25},{17,1},{25,9},{2,18},{10... | collective-permute-start | bytes 786440 | tf_op jit(solution)/shard_map/ppermute | solution.py:306
  31.9 0.5 %collective-permute-start.7 = (bf16[256,512]{1,0:T(8,128)(2,1)S(1)}, bf16[256,512]{1,0:T(8,128)(2,1)S(1)}, u32[]{:S(2)}, u32[]{:S(2)}) collective-permute-start(bf16[256,512]{1,0:T(8,128)(2,1)S(1)} %get-tuple-element.55), channel_id=1, source_target_pairs={{0,8},{8,0},{16,24},{24,16},{1,9},{9,1},{17,25},{25,17},{2,10},{10... | collective-permute-start | bytes 786440 | tf_op jit(solution)/shard_map/ppermute | solution.py:306
  32.4 2.6 %last_score.1 = f32[8,128]{1,0:T(8,128)S(1)} custom-call(s32[1]{0:T(128)} %bitcast.me_ref, bf16[256,32,512]{2,1,0:T(8,128)(2,1)S(1)} %get-tuple-element.36.bank_ref, f32[256,128]{1,0:T(8,128)S(1)} %get-tuple-element.37.norm_ref, s32[1,256]{1,0:T(1,128)S(1)} %bitcast.14, bf16[512,256]{1,0:T(8,128)(2,1)S(1)} %get-tuple-element.46.columns_ref, ...), custom_call_target="tpu_custom_call" | custom-call | flops 1 | bytes 1 | tf_op jit(solution)/shard_map/last_score/pallas_call | solution.py:335
  35.0 11.2 %all_to_all.11 = f32[8,1,128]{2,1,0:T(1,128)S(1)} all-to-all(f32[8,1,128]{2,1,0:T(1,128)S(1)} %bitcast.9), channel_id=1, replica_groups=mesh['grp'=4,'own'=8] {'own'}, dimensions={0} | all-to-all | bytes 8192 | tf_op jit(solution)/shard_map/all_to_all | solution.py:432
  46.1 0.8 %unpack.1 = f32[1,512]{1,0:T(1,128)} custom-call(s32[1,512]{1,0:T(1,128)S(1)} %get-tuple-element.29.index_ref, f32[8,128]{1,0:T(8,128)S(1)} %bitcast.10), custom_call_target="tpu_custom_call" | custom-call | flops 1 | bytes 1 | tf_op jit(solution)/shard_map/unpack/pallas_call | solution.py:335
  46.9 0.0 collective-permute-done.9.refs_2_
  47.0 1.0 %finish.1 = f32[256,512]{1,0:T(8,128)} custom-call(f32[256,512]{1,0:T(8,128)S(1)} %copy-done, f32[256,512]{1,0:T(8,128)S(1)} %get-tuple-element.54.own_ref, bf16[256,512]{1,0:T(8,128)(2,1)S(1)} %collective-permute-done.7.refs_0_, bf16[256,512]{1,0:T(8,128)(2,1)S(1)} %collective-permute-done.8.refs_1_, bf16[256,512]{1,0:T(8,128)(2,1)S(1)} %collective-permute-done.9.refs_2_), custom_call_target="tpu_custom_call" | custom-call | flops 1 | bytes 1 | tf_op jit(solution)/shard_map/finish/pallas_call | solution.py:335
  (5 shorter events, 0.0 us)
Async XLA Ops:
  2.3 7.2 %collective-permute-start = (bf16[528,128]{1,0:T(8,128)(2,1)S(1)}, bf16[528,128]{1,0:T(8,128)(2,1)S(1)}, u32[]{:S(2)}, u32[]{:S(2)}) collective-permute-start(bf16[528,128]{1,0:T(8,128)(2,1)S(1)} %get-tuple-element.35), channel_id=1, source_target_pairs={{0,1},{1,0},{2,3},{3,2},{4,5},{5,4},{6,7},{7,6},{8,9},{9,8},{10,11... | collective-permute-start | bytes 405512 | tf_op jit(solution)/shard_map/ppermute | solution.py:306
  2.8 18.0 %collective-permute-start.3 = (bf16[528,128]{1,0:T(8,128)(2,1)S(1)}, bf16[528,128]{1,0:T(8,128)(2,1)S(1)}, u32[]{:S(2)}, u32[]{:S(2)}) collective-permute-start(bf16[528,128]{1,0:T(8,128)(2,1)S(1)} %get-tuple-element.33.after_ref), channel_id=1, source_target_pairs={{0,4},{1,5},{2,6},{3,7},{4,0},{5,1},{6,2},{7,3},{8,12},{9,13},{10,... | collective-permute-start | bytes 405512 | tf_op jit(solution)/shard_map/ppermute | solution.py:306
  7.8 13.1 %collective-permute-start.4 = (bf16[528,128]{1,0:T(8,128)(2,1)}, bf16[528,128]{1,0:T(8,128)(2,1)S(1)}, u32[]{:S(2)}, u32[]{:S(2)}) collective-permute-start(bf16[528,128]{1,0:T(8,128)(2,1)} %get-tuple-element.41), channel_id=1, source_target_pairs={{0,2},{1,3},{2,0},{3,1},{4,6},{5,7},{6,4},{7,5},{8,10},{9,11},{10,... | collective-permute-start | bytes 405512 | tf_op jit(solution)/shard_map/ppermute | solution.py:306
  9.3 14.5 %collective-permute-start.5 = (bf16[528,128]{1,0:T(8,128)(2,1)}, bf16[528,128]{1,0:T(8,128)(2,1)S(1)}, u32[]{:S(2)}, u32[]{:S(2)}) collective-permute-start(bf16[528,128]{1,0:T(8,128)(2,1)} %get-tuple-element.43), channel_id=1, source_target_pairs={{0,5},{1,4},{2,7},{3,6},{4,1},{5,0},{6,3},{7,2},{8,13},{9,12},{10,... | collective-permute-start | bytes 405512 | tf_op jit(solution)/shard_map/ppermute | solution.py:306
  9.3 14.5 %collective-permute-start.6 = (bf16[528,128]{1,0:T(8,128)(2,1)}, bf16[528,128]{1,0:T(8,128)(2,1)S(1)}, u32[]{:S(2)}, u32[]{:S(2)}) collective-permute-start(bf16[528,128]{1,0:T(8,128)(2,1)} %get-tuple-element.44), channel_id=1, source_target_pairs={{0,3},{1,2},{2,1},{3,0},{4,7},{5,6},{6,5},{7,4},{8,11},{9,10},{10,... | collective-permute-start | bytes 405512 | tf_op jit(solution)/shard_map/ppermute | solution.py:306
  9.5 0.7 %copy-start.1 = (s32[256]{0:T(256)S(1)}, s32[256]{0:T(256)}, u32[]{:S(2)}) copy-start(s32[256]{0:T(256)} %param.10) | copy-start | bytes 3076
  16.9 9.9 %collective-permute-start.1 = (bf16[528,128]{1,0:T(8,128)(2,1)S(1)}, bf16[528,128]{1,0:T(8,128)(2,1)S(1)}, u32[]{:S(2)}, u32[]{:S(2)}) collective-permute-start(bf16[528,128]{1,0:T(8,128)(2,1)S(1)} %get-tuple-element.39), channel_id=1, source_target_pairs={{0,6},{1,7},{2,4},{3,5},{4,2},{5,3},{6,0},{7,1},{8,14},{9,15},{10,... | collective-permute-start | bytes 405512 | tf_op jit(solution)/shard_map/ppermute | solution.py:306
  20.9 7.6 %collective-permute-start.2 = (bf16[528,128]{1,0:T(8,128)(2,1)S(1)}, bf16[528,128]{1,0:T(8,128)(2,1)S(1)}, u32[]{:S(2)}, u32[]{:S(2)}) collective-permute-start(bf16[528,128]{1,0:T(8,128)(2,1)S(1)} %get-tuple-element.40), channel_id=1, source_target_pairs={{0,7},{1,6},{2,5},{3,4},{4,3},{5,2},{6,1},{7,0},{8,15},{9,14},{10,... | collective-permute-start | bytes 405512 | tf_op jit(solution)/shard_map/ppermute | solution.py:306
  20.9 11.5 %copy-start.2 = (s32[256]{0:T(256)S(1)}, s32[256]{0:T(256)}, u32[]{:S(2)}) copy-start(s32[256]{0:T(256)} %param.10) | copy-start | bytes 3076
  23.8 23.1 %copy-start = (f32[256,512]{1,0:T(8,128)S(1)}, f32[256,512]{1,0:T(8,128)}, u32[]{:S(2)}) copy-start(f32[256,512]{1,0:T(8,128)} %stored_ref.1) | copy-start | bytes 1572868
  28.8 18.1 %collective-permute-start.9 = (bf16[256,512]{1,0:T(8,128)(2,1)S(1)}, bf16[256,512]{1,0:T(8,128)(2,1)S(1)}, u32[]{:S(2)}, u32[]{:S(2)}) collective-permute-start(bf16[256,512]{1,0:T(8,128)(2,1)S(1)} %get-tuple-element.55), channel_id=1, source_target_pairs={{0,24},{8,16},{16,8},{24,0},{1,25},{9,17},{17,9},{25,1},{2,26},{10... | collective-permute-start | bytes 786440 | tf_op jit(solution)/shard_map/ppermute | solution.py:306
  31.3 15.6 %collective-permute-start.8 = (bf16[256,512]{1,0:T(8,128)(2,1)S(1)}, bf16[256,512]{1,0:T(8,128)(2,1)S(1)}, u32[]{:S(2)}, u32[]{:S(2)}) collective-permute-start(bf16[256,512]{1,0:T(8,128)(2,1)S(1)} %get-tuple-element.55), channel_id=1, source_target_pairs={{0,16},{8,24},{16,0},{24,8},{1,17},{9,25},{17,1},{25,9},{2,18},{10... | collective-permute-start | bytes 786440 | tf_op jit(solution)/shard_map/ppermute | solution.py:306
  31.9 15.1 %collective-permute-start.7 = (bf16[256,512]{1,0:T(8,128)(2,1)S(1)}, bf16[256,512]{1,0:T(8,128)(2,1)S(1)}, u32[]{:S(2)}, u32[]{:S(2)}) collective-permute-start(bf16[256,512]{1,0:T(8,128)(2,1)S(1)} %get-tuple-element.55), channel_id=1, source_target_pairs={{0,8},{8,0},{16,24},{24,16},{1,9},{9,1},{17,25},{25,17},{2,10},{10... | collective-permute-start | bytes 786440 | tf_op jit(solution)/shard_map/ppermute | solution.py:306

commit v18 on v10

--- a/solution.py
+++ b/solution.py
@@ -394,7 +394,7 @@
     late = vmem_call(
         functools.partial(late_pack_kernel, capacity, last),
         "late_pack",
-        [message] * len(last),
+        [message] * eighth + [pltpu.HBM(message.shape, message.dtype)] * (len(last) - eighth),
         [index, slots, values, total],
         [whole_vmem()] * 3 + [anywhere],
     )

time: 48.2 us -> 48.8 us (1.012)
  Pallas kernels: 20.2 us -> 20.9 us
    pallas_call x10, Pallas kernels: 20.2 us -> 20.9 us  [vmem_call(): pl.pallas_call(kernel, out_shape=out_shape, in_specs=in_specs or [whole_v...]
  transfers between devices with their start and end apart: 10 -> 10, of which waited for: 1 -> 1; matrix products, arithmetic and copies ran while one was open for 0% -> 0% of each run, Pallas kernels for 36% -> 37%
where the time goes in v18:
time: 48.8 us; the launch traced here: 48.6 us
  Pallas kernels  20.9 us (43%)
  starting transfers between devices  13.4 us (27%)
  blocking collectives  10.9 us (22%)
  waiting for transfers between devices  1.89 us (4%)
  between operations  0.72 us (1%)
  local copies, waits for them, and re-layouts  0.69 us (1%)
    pallas_call x10, Pallas kernels, vmem_call(): pl.pallas_call(kernel, out_shape=out_shape, in_specs=in_specs or [whole_v...  20.9 us
    ppermute x10, starting transfers between devices, exchange(): lax.ppermute(value, axis, [(device, device ^ offset) for device in range(...  13.4 us
    all_to_all x1, blocking collectives, body(): lax.all_to_all(best, 'own', split_axis=0, concat_axis=0, tiled=True)  10.9 us
    ppermute x10, waiting for transfers between devices, exchange(): lax.ppermute(value, axis, [(device, device ^ offset) for device in range(...  1.89 us
  transfers between devices with their start and end apart: 10, of which 1 were waited for; matrix products, arithmetic and copies ran while one was open for 0% of the time, Pallas kernels for 37%

profile of v18, /device:TPU:0, one launch (start us, length us, event | category | flops | bytes accessed | tf_op | source)
XLA Modules:
  0.0 48.6 jit_solution(11345907392581329767)
XLA Ops:
  0.6 1.7 %pack.1 = (s32[1,512]{1,0:T(1,128)S(1)}, s32[1,512]{1,0:T(1,128)S(1)}, s32[1,512]{1,0:T(1,128)}, s32[1,512]{1,0:T(1,128)S(1)}, bf16[512,512]{1,0:T(8,128)(2,1)S(...) custom-call(s32[1]{0:T(128)} %bitcast.me_ref, s32[1,512]{1,0:T(1,128)} %bitcast.15, s32[1,512]{1,0:T(1,128)} %bitcast.16, ...), custom_call_target="tpu_custom_call" | custom-call | flops 1 | bytes 1 | tf_op jit(solution)/shard_map/pack/pallas_call | solution.py:335
  2.3 0.5 %collective-permute-start = (bf16[528,128]{1,0:T(8,128)(2,1)S(1)}, bf16[528,128]{1,0:T(8,128)(2,1)S(1)}, u32[]{:S(2)}, u32[]{:S(2)}) collective-permute-start(bf16[528,128]{1,0:T(8,128)(2,1)S(1)} %get-tuple-element.35), channel_id=1, source_target_pairs={{0,1},{1,0},{2,3},{3,2},{4,5},{5,4},{6,7},{7,6},{8,9},{9,8},{10,11... | collective-permute-start | bytes 405512 | tf_op jit(solution)/shard_map/ppermute | solution.py:306
  2.8 3.7 %collective-permute-start.3 = (bf16[528,128]{1,0:T(8,128)(2,1)S(1)}, bf16[528,128]{1,0:T(8,128)(2,1)S(1)}, u32[]{:S(2)}, u32[]{:S(2)}) collective-permute-start(bf16[528,128]{1,0:T(8,128)(2,1)S(1)} %get-tuple-element.33.after_ref), channel_id=1, source_target_pairs={{0,4},{1,5},{2,6},{3,7},{4,0},{5,1},{6,2},{7,3},{8,12},{9,13},{10,... | collective-permute-start | bytes 405512 | tf_op jit(solution)/shard_map/ppermute | solution.py:306
  6.5 1.2 %next_pack.1 = (bf16[528,128]{1,0:T(8,128)(2,1)S(1)}, bf16[528,128]{1,0:T(8,128)(2,1)}, bf16[528,128]{1,0:T(8,128)(2,1)S(1)}, bf16[528,128]{1,0:T(8,128)(2,1)}) custom-call(s32[1,512]{1,0:T(1,128)S(1)} %get-tuple-element.30.index_ref, s32[1,512]{1,0:T(1,128)S(1)} %get-tuple-element.31.slot_ref, bf16[512,512]{1,0:T(8,128)(2,1)S(1)} %get-tuple-element.32.rows_ref, ...), custom_call_target="tpu_custom_call" | custom-call | flops 1 | bytes 1 | tf_op jit(solution)/shard_map/next_pack/pallas_call | solution.py:335
  7.8 1.6 %collective-permute-start.4 = (bf16[528,128]{1,0:T(8,128)(2,1)}, bf16[528,128]{1,0:T(8,128)(2,1)S(1)}, u32[]{:S(2)}, u32[]{:S(2)}) collective-permute-start(bf16[528,128]{1,0:T(8,128)(2,1)} %get-tuple-element.41), channel_id=1, source_target_pairs={{0,2},{1,3},{2,0},{3,1},{4,6},{5,7},{6,4},{7,5},{8,10},{9,11},{10,... | collective-permute-start | bytes 405512 | tf_op jit(solution)/shard_map/ppermute | solution.py:306
  9.3 0.0 collective-permute-start.5
  9.3 0.2 collective-permute-start.6
  9.5 0.0 collective-permute-done.refs_1_
  9.5 0.7 %copy-done.1 = s32[256]{0:T(256)S(1)} copy-done((s32[256]{0:T(256)S(1)}, s32[256]{0:T(256)}, u32[]{:S(2)}) %copy-start.1) | copy-done | bytes 1048
  10.2 6.3 %first_score.1 = (bf16[256,32,512]{2,1,0:T(8,128)(2,1)S(1)}, f32[256,128]{1,0:T(8,128)S(1)}, f32[256,512]{1,0:T(8,128)S(1)}, f32[1,128]{1,0:T(1,128)S(1)}, f32[1,128]{1,0:T(1,128)S(1)}) custom-call(bf16[256,32,512]{2,1,0:T(8,128)(2,1)} %bank_ref.1, s32[1,256]{1,0:T(1,128)S(1)} %bitcast.11, bf16[528,128]{1,0:T(8,128)(2,1)S(1)} %get-tuple-element.34.refs_0_, ...), custom_call_target="tpu_custom_call" | custom-call | flops 1 | bytes 1 | tf_op jit(solution)/shard_map/first_score/pallas_call | solution.py:335
  16.5 1.0 %late_pack.1 = (bf16[528,128]{1,0:T(8,128)(2,1)S(1)}, bf16[528,128]{1,0:T(8,128)(2,1)}) custom-call(s32[1,512]{1,0:T(1,128)S(1)} %get-tuple-element.30.index_ref, s32[1,512]{1,0:T(1,128)S(1)} %get-tuple-element.31.slot_ref, bf16[512,512]{1,0:T(8,128)(2,1)S(1)} %get-tuple-element.32.rows_ref, f32[256,512]{1,0:T(8,128)S(1)} %get-tuple-element.38.after_ref.before_ref), custom_call_target="tpu_custom_call" | custom-call | flops 1 | bytes 1 | tf_op jit(solution)/shard_map/late_pack/pallas_call | solution.py:335
  17.5 3.9 %collective-permute-start.1 = (bf16[528,128]{1,0:T(8,128)(2,1)S(1)}, bf16[528,128]{1,0:T(8,128)(2,1)S(1)}, u32[]{:S(2)}, u32[]{:S(2)}) collective-permute-start(bf16[528,128]{1,0:T(8,128)(2,1)S(1)} %get-tuple-element.39), channel_id=1, source_target_pairs={{0,6},{1,7},{2,4},{3,5},{4,2},{5,3},{6,0},{7,1},{8,14},{9,15},{10,... | collective-permute-start | bytes 405512 | tf_op jit(solution)/shard_map/ppermute | solution.py:306
  21.4 0.0 collective-permute-done.3.refs_0_
  21.4 0.0 collective-permute-start.2
  21.4 0.0 collective-permute-done.4.refs_1_
  21.4 0.0 copy-start.2
  21.5 2.9 %score.2 = (f32[1,128]{1,0:T(1,128)S(1)}, f32[1,128]{1,0:T(1,128)S(1)}, f32[256,512]{1,0:T(8,128)S(1)}) custom-call(bf16[256,32,512]{2,1,0:T(8,128)(2,1)S(1)} %get-tuple-element.36.bank_ref, f32[256,128]{1,0:T(8,128)S(1)} %get-tuple-element.37.norm_ref, s32[1,256]{1,0:T(1,128)S(1)} %bitcast.12, f32[256,512]{1,0:T(8,128)S(1)} %get-tuple-element.38.after_ref.before_ref, ...), custom_call_target="tpu_custom_call" | custom-call | flops 1 | bytes 1 | tf_op jit(solution)/shard_map/score/pallas_call | solution.py:335
  24.4 0.0 collective-permute-done.5.refs_0_
  24.4 0.0 copy-start
  24.4 2.9 %score.3 = (f32[1,128]{1,0:T(1,128)S(1)}, f32[1,128]{1,0:T(1,128)S(1)}, f32[256,512]{1,0:T(8,128)S(1)}) custom-call(bf16[256,32,512]{2,1,0:T(8,128)(2,1)S(1)} %get-tuple-element.36.bank_ref, f32[256,128]{1,0:T(8,128)S(1)} %get-tuple-element.37.norm_ref, s32[1,256]{1,0:T(1,128)S(1)} %bitcast.13, f32[256,512]{1,0:T(8,128)S(1)} %get-tuple-element.42.before_ref, ...), custom_call_target="tpu_custom_call" | custom-call | flops 1 | bytes 1 | tf_op jit(solution)/shard_map/score/pallas_call | solution.py:335
  27.4 0.0 collective-permute-done.1.refs_0_
  27.4 1.9 %collective-permute-done.2.refs_1_ = bf16[528,128]{1,0:T(8,128)(2,1)S(1)} collective-permute-done((bf16[528,128]{1,0:T(8,128)(2,1)}, bf16[528,128]{1,0:T(8,128)(2,1)S(1)}, u32[]{:S(2)}, u32[]{:S(2)}) %collective-permute-start.2) | collective-permute-done | bytes 135200 | tf_op jit(solution)/shard_map/ppermute | solution.py:306
  29.2 0.4 last_sum.1
  29.6 2.5 %collective-permute-start.9 = (bf16[256,512]{1,0:T(8,128)(2,1)S(1)}, bf16[256,512]{1,0:T(8,128)(2,1)S(1)}, u32[]{:S(2)}, u32[]{:S(2)}) collective-permute-start(bf16[256,512]{1,0:T(8,128)(2,1)S(1)} %get-tuple-element.55), channel_id=1, source_target_pairs={{0,24},{8,16},{16,8},{24,0},{1,25},{9,17},{17,9},{25,1},{2,26},{10... | collective-permute-start | bytes 786440 | tf_op jit(solution)/shard_map/ppermute | solution.py:306
  32.1 0.5 %collective-permute-start.8 = (bf16[256,512]{1,0:T(8,128)(2,1)S(1)}, bf16[256,512]{1,0:T(8,128)(2,1)S(1)}, u32[]{:S(2)}, u32[]{:S(2)}) collective-permute-start(bf16[256,512]{1,0:T(8,128)(2,1)S(1)} %get-tuple-element.55), channel_id=1, source_target_pairs={{0,16},{8,24},{16,0},{24,8},{1,17},{9,25},{17,1},{25,9},{2,18},{10... | collective-permute-start | bytes 786440 | tf_op jit(solution)/shard_map/ppermute | solution.py:306
  32.6 0.5 %collective-permute-start.7 = (bf16[256,512]{1,0:T(8,128)(2,1)S(1)}, bf16[256,512]{1,0:T(8,128)(2,1)S(1)}, u32[]{:S(2)}, u32[]{:S(2)}) collective-permute-start(bf16[256,512]{1,0:T(8,128)(2,1)S(1)} %get-tuple-element.55), channel_id=1, source_target_pairs={{0,8},{8,0},{16,24},{24,16},{1,9},{9,1},{17,25},{25,17},{2,10},{10... | collective-permute-start | bytes 786440 | tf_op jit(solution)/shard_map/ppermute | solution.py:306
  33.2 2.6 %last_score.1 = f32[8,128]{1,0:T(8,128)S(1)} custom-call(s32[1]{0:T(128)} %bitcast.me_ref, bf16[256,32,512]{2,1,0:T(8,128)(2,1)S(1)} %get-tuple-element.36.bank_ref, f32[256,128]{1,0:T(8,128)S(1)} %get-tuple-element.37.norm_ref, s32[1,256]{1,0:T(1,128)S(1)} %bitcast.14, bf16[512,256]{1,0:T(8,128)(2,1)S(1)} %get-tuple-element.46.columns_ref, ...), custom_call_target="tpu_custom_call" | custom-call | flops 1 | bytes 1 | tf_op jit(solution)/shard_map/last_score/pallas_call | solution.py:335
  35.7 10.9 %all_to_all.11 = f32[8,1,128]{2,1,0:T(1,128)S(1)} all-to-all(f32[8,1,128]{2,1,0:T(1,128)S(1)} %bitcast.9), channel_id=1, replica_groups=mesh['grp'=4,'own'=8] {'own'}, dimensions={0} | all-to-all | bytes 8192 | tf_op jit(solution)/shard_map/all_to_all | solution.py:432
  46.7 0.8 %unpack.1 = f32[1,512]{1,0:T(1,128)} custom-call(s32[1,512]{1,0:T(1,128)S(1)} %get-tuple-element.29.index_ref, f32[8,128]{1,0:T(8,128)S(1)} %bitcast.10), custom_call_target="tpu_custom_call" | custom-call | flops 1 | bytes 1 | tf_op jit(solution)/shard_map/unpack/pallas_call | solution.py:335
  47.5 0.0 collective-permute-done.9.refs_2_
  47.5 0.0 collective-permute-done.8.refs_1_
  47.5 1.0 %finish.1 = f32[256,512]{1,0:T(8,128)} custom-call(f32[256,512]{1,0:T(8,128)S(1)} %copy-done, f32[256,512]{1,0:T(8,128)S(1)} %get-tuple-element.54.own_ref, bf16[256,512]{1,0:T(8,128)(2,1)S(1)} %collective-permute-done.7.refs_0_, bf16[256,512]{1,0:T(8,128)(2,1)S(1)} %collective-permute-done.8.refs_1_, bf16[256,512]{1,0:T(8,128)(2,1)S(1)} %collective-permute-done.9.refs_2_), custom_call_target="tpu_custom_call" | custom-call | flops 1 | bytes 1 | tf_op jit(solution)/shard_map/finish/pallas_call | solution.py:335
  (5 shorter events, 0.0 us)
Async XLA Ops:
  2.3 7.2 %collective-permute-start = (bf16[528,128]{1,0:T(8,128)(2,1)S(1)}, bf16[528,128]{1,0:T(8,128)(2,1)S(1)}, u32[]{:S(2)}, u32[]{:S(2)}) collective-permute-start(bf16[528,128]{1,0:T(8,128)(2,1)S(1)} %get-tuple-element.35), channel_id=1, source_target_pairs={{0,1},{1,0},{2,3},{3,2},{4,5},{5,4},{6,7},{7,6},{8,9},{9,8},{10,11... | collective-permute-start | bytes 405512 | tf_op jit(solution)/shard_map/ppermute | solution.py:306
  2.8 18.6 %collective-permute-start.3 = (bf16[528,128]{1,0:T(8,128)(2,1)S(1)}, bf16[528,128]{1,0:T(8,128)(2,1)S(1)}, u32[]{:S(2)}, u32[]{:S(2)}) collective-permute-start(bf16[528,128]{1,0:T(8,128)(2,1)S(1)} %get-tuple-element.33.after_ref), channel_id=1, source_target_pairs={{0,4},{1,5},{2,6},{3,7},{4,0},{5,1},{6,2},{7,3},{8,12},{9,13},{10,... | collective-permute-start | bytes 405512 | tf_op jit(solution)/shard_map/ppermute | solution.py:306
  7.8 13.7 %collective-permute-start.4 = (bf16[528,128]{1,0:T(8,128)(2,1)}, bf16[528,128]{1,0:T(8,128)(2,1)S(1)}, u32[]{:S(2)}, u32[]{:S(2)}) collective-permute-start(bf16[528,128]{1,0:T(8,128)(2,1)} %get-tuple-element.41), channel_id=1, source_target_pairs={{0,2},{1,3},{2,0},{3,1},{4,6},{5,7},{6,4},{7,5},{8,10},{9,11},{10,... | collective-permute-start | bytes 405512 | tf_op jit(solution)/shard_map/ppermute | solution.py:306
  9.3 15.1 %collective-permute-start.5 = (bf16[528,128]{1,0:T(8,128)(2,1)S(1)}, bf16[528,128]{1,0:T(8,128)(2,1)S(1)}, u32[]{:S(2)}, u32[]{:S(2)}) collective-permute-start(bf16[528,128]{1,0:T(8,128)(2,1)S(1)} %get-tuple-element.43), channel_id=1, source_target_pairs={{0,5},{1,4},{2,7},{3,6},{4,1},{5,0},{6,3},{7,2},{8,13},{9,12},{10,... | collective-permute-start | bytes 405512 | tf_op jit(solution)/shard_map/ppermute | solution.py:306
  9.3 15.1 %collective-permute-start.6 = (bf16[528,128]{1,0:T(8,128)(2,1)}, bf16[528,128]{1,0:T(8,128)(2,1)S(1)}, u32[]{:S(2)}, u32[]{:S(2)}) collective-permute-start(bf16[528,128]{1,0:T(8,128)(2,1)} %get-tuple-element.44), channel_id=1, source_target_pairs={{0,3},{1,2},{2,1},{3,0},{4,7},{5,6},{6,5},{7,4},{8,11},{9,10},{10,... | collective-permute-start | bytes 405512 | tf_op jit(solution)/shard_map/ppermute | solution.py:306
  9.5 0.7 %copy-start.1 = (s32[256]{0:T(256)S(1)}, s32[256]{0:T(256)}, u32[]{:S(2)}) copy-start(s32[256]{0:T(256)} %param.10) | copy-start | bytes 3076
  17.5 9.8 %collective-permute-start.1 = (bf16[528,128]{1,0:T(8,128)(2,1)S(1)}, bf16[528,128]{1,0:T(8,128)(2,1)S(1)}, u32[]{:S(2)}, u32[]{:S(2)}) collective-permute-start(bf16[528,128]{1,0:T(8,128)(2,1)S(1)} %get-tuple-element.39), channel_id=1, source_target_pairs={{0,6},{1,7},{2,4},{3,5},{4,2},{5,3},{6,0},{7,1},{8,14},{9,15},{10,... | collective-permute-start | bytes 405512 | tf_op jit(solution)/shard_map/ppermute | solution.py:306
  21.4 7.8 %collective-permute-start.2 = (bf16[528,128]{1,0:T(8,128)(2,1)}, bf16[528,128]{1,0:T(8,128)(2,1)S(1)}, u32[]{:S(2)}, u32[]{:S(2)}) collective-permute-start(bf16[528,128]{1,0:T(8,128)(2,1)} %get-tuple-element.40), channel_id=1, source_target_pairs={{0,7},{1,6},{2,5},{3,4},{4,3},{5,2},{6,1},{7,0},{8,15},{9,14},{10,... | collective-permute-start | bytes 405512 | tf_op jit(solution)/shard_map/ppermute | solution.py:306
  21.4 11.7 %copy-start.2 = (s32[256]{0:T(256)S(1)}, s32[256]{0:T(256)}, u32[]{:S(2)}) copy-start(s32[256]{0:T(256)} %param.10) | copy-start | bytes 3076
  24.4 23.1 %copy-start = (f32[256,512]{1,0:T(8,128)S(1)}, f32[256,512]{1,0:T(8,128)}, u32[]{:S(2)}) copy-start(f32[256,512]{1,0:T(8,128)} %stored_ref.1) | copy-start | bytes 1572868
  29.6 17.9 %collective-permute-start.9 = (bf16[256,512]{1,0:T(8,128)(2,1)S(1)}, bf16[256,512]{1,0:T(8,128)(2,1)S(1)}, u32[]{:S(2)}, u32[]{:S(2)}) collective-permute-start(bf16[256,512]{1,0:T(8,128)(2,1)S(1)} %get-tuple-element.55), channel_id=1, source_target_pairs={{0,24},{8,16},{16,8},{24,0},{1,25},{9,17},{17,9},{25,1},{2,26},{10... | collective-permute-start | bytes 786440 | tf_op jit(solution)/shard_map/ppermute | solution.py:306
  32.1 15.4 %collective-permute-start.8 = (bf16[256,512]{1,0:T(8,128)(2,1)S(1)}, bf16[256,512]{1,0:T(8,128)(2,1)S(1)}, u32[]{:S(2)}, u32[]{:S(2)}) collective-permute-start(bf16[256,512]{1,0:T(8,128)(2,1)S(1)} %get-tuple-element.55), channel_id=1, source_target_pairs={{0,16},{8,24},{16,0},{24,8},{1,17},{9,25},{17,1},{25,9},{2,18},{10... | collective-permute-start | bytes 786440 | tf_op jit(solution)/shard_map/ppermute | solution.py:306
  32.6 14.9 %collective-permute-start.7 = (bf16[256,512]{1,0:T(8,128)(2,1)S(1)}, bf16[256,512]{1,0:T(8,128)(2,1)S(1)}, u32[]{:S(2)}, u32[]{:S(2)}) collective-permute-start(bf16[256,512]{1,0:T(8,128)(2,1)S(1)} %get-tuple-element.55), channel_id=1, source_target_pairs={{0,8},{8,0},{16,24},{24,16},{1,9},{9,1},{17,25},{25,17},{2,10},{10... | collective-permute-start | bytes 786440 | tf_op jit(solution)/shard_map/ppermute | solution.py:306
